TPU v7x, 512 devices: a whole 4x4x16 slice. The times are simulated.
512 devices in a mesh: heads: 8 (over x, z_hi), tokens: 64 (over y, z_lo, core).
Axes of the slice: x: 4, y: 4, z: 16 (z_hi: 2, z_lo: 8; z = z_hi * 8 + z_lo), core: 2. Of those that a mesh axis runs over, the one named last changes fastest.
Arguments:
- queries: bfloat16 [128, 64, 576], P('heads', 'tokens'), may hold values from -40 to 40
- latent_keys: bfloat16 [65536, 576], P('tokens'), may hold values from -4 to 4
- index_queries: bfloat16 [64, 64, 128], P(None, 'heads'), may hold values from -4 to 4
- index_keys: bfloat16 [65536, 128], P('tokens'), may hold values from -8 to 8
- index_weights: float32 [64, 64], P(None, 'heads'), may hold values from 0 to 1.2
- positions: int32 [64], replicated, may hold values from 32768 to 65535
Outputs:
- index_query_grad: float32 [64, 64, 128], P(None, 'heads')
- index_weight_grad: float32 [64, 64], P(None, 'heads')
- index_key_grad: float32 [65536, 128], P('tokens')
All inputs are finite; a program needn't handle non-finite values.
Results may differ from a plain program's by a relative error of at most 0.0026.
Values may be sent and summed in bfloat16 or wider, within the bound.
No kernel may reach another device: no remote copies, remote signals or barrier semaphores. Data moves between devices by JAX's collectives and lax.ppermute only.
A program may use at most 64 MiB of HBM per device.

v0:
```python
import jax
import jax.numpy as jnp
from jax import lax
from jax.sharding import PartitionSpec as P

H = 128


softmax_scale = 192.0 ** (-0.5)
masked_value = -1e30


def sent_to_all(value, axis):
    devices = lax.axis_size(axis)
    return lax.all_to_all(
        jnp.broadcast_to(value[None], (devices, *value.shape)), axis, 0, 0, tiled=True
    )


def gathered_once(value, axis):
    leaves = jax.tree.leaves(value)
    order = sorted(range(len(leaves)), key=lambda k: -leaves[k].size)
    width = (1, *leaves[order[0]].shape)[-1]
    lines = [
        jnp.pad(leaves[k].reshape(-1), (0, -leaves[k].size % width)).reshape(-1, width)
        for k in order
    ]
    both, at, found = (sent_to_all(jnp.concatenate(lines), axis), 0, {})
    for k, line in zip(order, lines):
        slab = both[:, at : at + len(line)].reshape(len(both), -1)
        found[k] = slab[:, : leaves[k].size].reshape(-1, *leaves[k].shape)
        at += len(line)
    numbers = iter(range(len(leaves)))
    return jax.tree.map(lambda _: found[next(numbers)], value)


def folded_in_pairs(pieces, combine):
    while len(jax.tree.leaves(pieces)[0]) > 1:
        pieces = jax.vmap(combine)(
            *(jax.tree.map(lambda part: part[side::2], pieces) for side in (0, 1))
        )
    return jax.tree.map(lambda part: part[0], pieces)


def combined_all(value, axis, combine):
    pieces = gathered_once(value, axis)
    return folded_in_pairs(pieces, combine)


def cut_along(value, dim, devices):
    before, after = (value.shape[:dim], value.shape[dim + 1 :])
    return jnp.moveaxis(value.reshape(*before, devices, -1, *after), dim, 0)


def one_scatter(arrays, axis, dims):
    devices = lax.axis_size(axis)
    parts = [cut_along(a, dim, devices) for a, dim in zip(arrays, dims)]
    lines = jnp.concatenate([b.reshape(devices, -1) for b in parts], axis=1)
    rows = max(16, -(-lines.shape[1] // 1024) * 8)
    lines = jnp.pad(lines, ((0, 0), (0, rows * 128 - lines.shape[1]))).reshape(-1, 128)
    vector, at, outs = (lax.psum_scatter(lines, axis, tiled=True).reshape(-1), 0, [])
    for b in parts:
        part = b[0]
        outs.append(vector[at : at + part.size].reshape(part.shape))
        at += part.size
    return tuple(outs)


def in_order(parts, dim):
    dims = list(parts.shape[1:])
    dims[dim] *= parts.shape[0]
    return jnp.moveaxis(parts, 0, dim).reshape(dims)


def gathered_copies(value, axis, dim):
    parts = sent_to_all(value, axis)
    return in_order(parts, dim)


def padded_to(lines, devices):
    spare = -len(lines) % devices
    return jnp.pad(lines, [(0, spare)] + [(0, 0)] * (lines.ndim - 1))


def sent_and_summed(value, axis, dim):
    parts = cut_along(value, dim, lax.axis_size(axis))
    arrived = lax.all_to_all(parts, axis, split_axis=0, concat_axis=0, tiled=True)
    return arrived.sum(axis=0)


def nested_sum(value, axes):
    lines = value.reshape(-1, value.shape[-1])
    padded = padded_to(lines, lax.axis_size(axes))
    whole = gathered_copies(sent_and_summed(padded, axes, 0), axes, 0)
    return lax.slice_in_dim(whole, 0, len(lines)).reshape(value.shape)


def block_size(heads_here, row_limit):
    chosen = 1
    for option in range(1, heads_here + 1):
        if heads_here % option == 0 and option <= row_limit:
            chosen = option
    return chosen


def joined_stats(first_pair, second_pair):
    maximum = jnp.maximum(first_pair[0], second_pair[0])
    totals = first_pair[1] * jnp.exp(first_pair[0] - maximum) + second_pair[1] * jnp.exp(
        second_pair[0] - maximum
    )
    return (maximum, totals)


def global_stats(local_max, local_total):
    maximum, totals = combined_all((local_max, local_total), "tokens", joined_stats)
    return (maximum, totals)


def logit_grad(summed_target, logits, visible, loss_scale):
    target = summed_target / H
    masked = jnp.where(visible, logits, masked_value)
    local_max = jnp.max(masked, axis=1)
    local_total = jnp.sum(jnp.exp(masked - local_max[:, None]), axis=1)
    maximum, totals = global_stats(local_max, local_total)
    index_probs = jnp.exp(masked - maximum[:, None]) / totals[:, None]
    return loss_scale * (index_probs - target)


def local(queries, latent_keys, index_queries, index_keys, index_weights, positions):
    key_count = latent_keys.shape[0]
    loss_scale = key_count * lax.axis_size("tokens") // 8
    offset = lax.axis_index("tokens") * key_count
    key_index = offset + jnp.arange(key_count, dtype=jnp.int32)
    visible = key_index[None, :] <= positions[:, None]
    gathered = lax.all_gather(queries, "tokens", axis=1, tiled=True)
    head_count, query_count, width_qk = gathered.shape
    per_block = block_size(head_count, max(1, 512 // query_count))
    head_blocks = gathered.reshape(head_count // per_block, per_block, query_count, width_qk)

    def block_scores(head_block):
        scores = (
            jnp.einsum("hqd,kd->hqk", head_block, latent_keys, preferred_element_type=jnp.float32)
            * softmax_scale
        )
        return jnp.where(visible[None], scores, masked_value)

    def block_stats(head_block):
        scores = block_scores(head_block)
        maximum = jnp.max(scores, axis=2)
        return (maximum, jnp.sum(jnp.exp(scores - maximum[..., None]), axis=2))

    local_max, local_total = lax.map(block_stats, head_blocks)
    head_max, head_total = global_stats(local_max, local_total)

    def accumulate(running, inputs):
        head_block, maximum, totals = inputs
        scores = block_scores(head_block)
        probabilities = jnp.exp(scores - maximum[..., None]) / totals[..., None]
        return (running + jnp.sum(probabilities, axis=0), None)

    partial_target, _ = lax.scan(
        accumulate,
        jnp.zeros((query_count, key_count), jnp.float32),
        (head_blocks, head_max, head_total),
    )
    index_scale = index_queries.shape[2] ** (-0.5)
    active = (
        jnp.einsum("qjd,kd->qjk", index_queries, index_keys, preferred_element_type=jnp.float32)
        * index_scale
    )
    rectified = jnp.maximum(active, 0.0)
    partial_logits = jnp.sum(index_weights[:, :, None] * rectified, axis=1)
    row_count = query_count // lax.axis_size("heads")
    share_target, share_logits = one_scatter((partial_target, partial_logits), "heads", (0, 0))
    first_row = lax.axis_index("heads") * row_count
    share_visible = lax.dynamic_slice_in_dim(visible, first_row, row_count, 0)
    share_grad = logit_grad(share_target, share_logits, share_visible, loss_scale)
    dlogit = gathered_copies(share_grad, "heads", 0)
    gate_grad = (dlogit[:, None, :] * index_weights[:, :, None] * (active > 0.0)).astype(
        jnp.bfloat16
    )
    query_local = (
        jnp.einsum("qjk,kd->qjd", gate_grad, index_keys, preferred_element_type=jnp.float32)
        * index_scale
    )
    weight_local = jnp.sum(dlogit[:, None, :] * rectified, axis=2)
    query_grad, weight_grad = (
        nested_sum(query_local, "tokens"),
        nested_sum(weight_local, "tokens"),
    )
    key_local = (
        jnp.einsum("qjk,qjd->kd", gate_grad, index_queries, preferred_element_type=jnp.float32)
        * index_scale
    )
    key_grad = lax.psum(key_local, "heads")
    return (query_grad, weight_grad, key_grad)


def solution(mesh):
    placed = (
        P("heads", "tokens", None),
        P("tokens", None),
        P(None, "heads", None),
        P("tokens", None),
        P(None, "heads"),
        P(),
    )
    return jax.shard_map(
        local,
        mesh=mesh,
        in_specs=placed,
        out_specs=(P(None, "heads", None), P(None, "heads"), P("tokens", None)),
        check_vma=False,
    )
```

profile of v0, /device:TPU:1, one launch (start us, length us, event | category | flops | bytes accessed | tf_op | source)
XLA Modules:
  0.0 615.3 jit_solution(9117610947227083281)
XLA Ops:
  8.0 128.1 %all-gather.2.cloned.1.call-done = bf16[16,64,576]{2,0,1:T(8,128)(2,1)} async-done(((bf16[16,1,576]{2,0,1:T(8,128)(2,1)}), bf16[16,64,576]{2,0,1:T(8,128)(2,1)}) %all-gather.2.cloned.1.call-update) | async-done | bytes 1179664 | tf_op jit(solution)/shard_map/all_gather | solution.py:135
  136.0 1.6 copy.14
  137.7 3.7 while.24
  137.8 1.1 fusion.30
  139.7 1.1 fusion.30
  141.4 1.0 copy-done.2
  142.6 1.5 reshape.94
  144.1 7.3 %all-to-all-start = ((f32[64,1,2048]{2,1,0:T(1,128)}), f32[64,1,2048]{2,1,0:T(1,128)S(1)}, u32[]{:S(2)}, u32[]{:S(2)}) async-start(f32[64,1,2048]{2,1,0:T(1,128)} %reshape.94), calls=%async_computation | async-start | bytes 1048576 | tf_op jit(solution)/shard_map/all_to_all | solution.py:15
  151.6 1.6 multiply_reduce_fusion.1
  154.2 26.9 %all-to-all-done = f32[64,1,2048]{2,1,0:T(1,128)S(1)} async-done(((f32[64,1,2048]{2,1,0:T(1,128)}), f32[64,1,2048]{2,1,0:T(1,128)S(1)}, u32[]{:S(2)}, u32[]{:S(2)}) %all-to-all-start) | async-done | bytes 524320 | tf_op jit(solution)/shard_map/all_to_all | solution.py:15
  182.3 2.9 reduce.1
  185.3 1.4 reshape.95
  186.7 1.3 slice_bitcast_fusion.1
  188.2 6.0 while.25
  188.4 2.8 fusion.33
  191.4 2.8 fusion.33
  195.4 106.3 %reduce-scatter.2.cloned.1.call-done = f32[128,128]{1,0:T(8,128)} async-done(((f32[1024,128]{1,0:T(8,128)}), f32[128,128]{1,0:T(8,128)}) %reduce-scatter.2.cloned.1.call-update) | async-done | bytes 65552 | tf_op jit(solution)/shard_map/reduce_scatter | solution.py:61
  303.5 7.3 %all-to-all-start.1 = ((f32[64,2,8]{2,1,0:T(2,128)}), f32[64,2,8]{2,1,0:T(2,128)S(1)}, u32[]{:S(2)}, u32[]{:S(2)}) async-start(f32[64,2,8]{2,1,0:T(2,128)} %broadcast_in_dim.77), calls=%async_computation.2 | async-start | bytes 131072 | tf_op jit(solution)/shard_map/all_to_all | solution.py:15
  310.8 12.8 %all-to-all-done.1 = f32[64,2,8]{2,1,0:T(2,128)S(1)} async-done(((f32[64,2,8]{2,1,0:T(2,128)}), f32[64,2,8]{2,1,0:T(2,128)S(1)}, u32[]{:S(2)}, u32[]{:S(2)}) %all-to-all-start.1) | async-done | bytes 4128 | tf_op jit(solution)/shard_map/all_to_all | solution.py:15
  324.3 24.4 %all_to_all.35 = f32[8,8,1024]{2,1,0:T(8,128)S(1)} all-to-all(f32[8,8,1024]{2,1,0:T(8,128)S(1)} %broadcast_in_dim.78), channel_id=1, replica_groups=mesh['heads'=8,'tokens'=64] {'heads'}, dimensions={0} | all-to-all | bytes 524288 | tf_op jit(solution)/shard_map/all_to_all | solution.py:15
  349.7 13.4 %all-to-all-start.5 = ((f32[64,1,8]{2,1,0:T(1,128)}), f32[64,1,8]{2,1,0:T(1,128)S(1)}, u32[]{:S(2)}, u32[]{:S(2)}) async-start(f32[64,1,8]{2,1,0:T(1,128)} %bitcast.15), calls=%async_computation.6 | async-start | bytes 65536 | tf_op jit(solution)/shard_map/all_to_all | solution.py:87
  363.2 1.2 convolution_multiply_fusion
  364.4 11.0 %all-to-all-done.5 = f32[64,1,8]{2,1,0:T(1,128)S(1)} async-done(((f32[64,1,8]{2,1,0:T(1,128)}), f32[64,1,8]{2,1,0:T(1,128)S(1)}, u32[]{:S(2)}, u32[]{:S(2)}) %all-to-all-start.5) | async-done | bytes 2080 | tf_op jit(solution)/shard_map/all_to_all | solution.py:87
  375.3 4.9 all-to-all-start.3
  380.3 19.3 %all-to-all-done.3 = f32[64,8,128]{2,1,0:T(8,128)S(1)} async-done(((f32[64,8,128]{2,1,0:T(8,128)}), f32[64,8,128]{2,1,0:T(8,128)S(1)}, u32[]{:S(2)}, u32[]{:S(2)}) %all-to-all-start.3) | async-done | bytes 262176 | tf_op jit(solution)/shard_map/all_to_all | solution.py:87
  400.2 6.9 %all-to-all-start.6 = ((f32[64,1,8]{2,1,0:T(1,128)}), f32[64,1,8]{2,1,0:T(1,128)S(1)}, u32[]{:S(2)}, u32[]{:S(2)}) async-start(f32[64,1,8]{2,1,0:T(1,128)} %broadcast_in_dim.80), calls=%async_computation.7 | async-start | bytes 65536 | tf_op jit(solution)/shard_map/all_to_all | solution.py:15
  407.2 12.1 %all-to-all-done.6 = f32[64,1,8]{2,1,0:T(1,128)S(1)} async-done(((f32[64,1,8]{2,1,0:T(1,128)}), f32[64,1,8]{2,1,0:T(1,128)S(1)}, u32[]{:S(2)}, u32[]{:S(2)}) %all-to-all-start.6) | async-done | bytes 2080 | tf_op jit(solution)/shard_map/all_to_all | solution.py:15
  420.0 4.7 all-to-all-start.4
  424.8 1.5 fusion.15
  427.0 17.1 %all-to-all-done.4 = f32[64,8,128]{2,1,0:T(8,128)S(1)} async-done(((f32[64,8,128]{2,1,0:T(8,128)}), f32[64,8,128]{2,1,0:T(8,128)S(1)}, u32[]{:S(2)}, u32[]{:S(2)}) %all-to-all-start.4) | async-done | bytes 262176 | tf_op jit(solution)/shard_map/all_to_all | solution.py:15
  444.1 162.1 %all-reduce.2.cloned.1.call-done = f32[1024,128]{1,0:T(8,128)} async-done(((f32[1024,128]{1,0:T(8,128)}), f32[1024,128]{1,0:T(8,128)}) %all-reduce.2.cloned.1.call-update) | async-done | bytes 524304 | tf_op jit(solution)/shard_map/psum | solution.py:195
  606.9 1.9 copy.43
  (95 shorter events, 12.8 us)
Async XLA Ops:
  7.2 144.4 %copy-start = (bf16[1024,128]{1,0:T(8,128)(2,1)S(1)}, bf16[1024,128]{1,0:T(8,128)(2,1)}, u32[]{:S(2)}) copy-start(bf16[1024,128]{1,0:T(8,128)(2,1)} %param.13) | copy-start | bytes 786436
  7.2 130.5 %copy-start.7 = (bf16[1024,576]{0,1:T(8,128)(2,1)S(1)}, bf16[1024,576]{0,1:T(8,128)(2,1)}, u32[]{:S(2)}) copy-start(bf16[1024,576]{0,1:T(8,128)(2,1)} %param.11) | copy-start | bytes 3538948
  7.2 130.5 %copy-start.5 = (s32[64]{0:T(128)S(1)}, s32[64]{0:T(128)}, u32[]{:S(2)}) copy-start(s32[64]{0:T(128)} %param.15) | copy-start | bytes 772
  7.2 128.8 %all-gather.2.cloned.1.call-start = ((), (), s32[]{:S(2)}) async-start(), calls=%async_computation.8 | async-start | bytes 1331200 | tf_op jit(solution)/shard_map/all_gather | solution.py:135
  141.4 1.1 copy-start.2
  141.4 10.1 %copy-start.6 = (f32[64,8]{0,1:T(8,128)S(1)}, f32[64,8]{0,1:T(8,128)}, u32[]{:S(2)}) copy-start(f32[64,8]{0,1:T(8,128)} %param.14) | copy-start | bytes 6148
  141.4 10.1 %copy-start.3 = (bf16[64,8,128]{2,1,0:T(8,128)(2,1)S(1)}, bf16[64,8,128]{2,1,0:T(8,128)(2,1)}, u32[]{:S(2)}) copy-start(bf16[64,8,128]{2,1,0:T(8,128)(2,1)} %param.12) | copy-start | bytes 393220
  144.1 37.0 %all-to-all-start = ((f32[64,1,2048]{2,1,0:T(1,128)}), f32[64,1,2048]{2,1,0:T(1,128)S(1)}, u32[]{:S(2)}, u32[]{:S(2)}) async-start(f32[64,1,2048]{2,1,0:T(1,128)} %reshape.94), calls=%async_computation | async-start | bytes 1048576 | tf_op jit(solution)/shard_map/all_to_all | solution.py:15
  151.4 150.2 %reduce-scatter.2.cloned.1.call-start = ((), (), s32[]{:S(2)}) async-start(), calls=%async_computation.9 | async-start | bytes 589824 | tf_op jit(solution)/shard_map/reduce_scatter | solution.py:61
  181.0 0.8 copy-start.1
  303.5 20.2 %all-to-all-start.1 = ((f32[64,2,8]{2,1,0:T(2,128)}), f32[64,2,8]{2,1,0:T(2,128)S(1)}, u32[]{:S(2)}, u32[]{:S(2)}) async-start(f32[64,2,8]{2,1,0:T(2,128)} %broadcast_in_dim.77), calls=%async_computation.2 | async-start | bytes 131072 | tf_op jit(solution)/shard_map/all_to_all | solution.py:15
  349.7 25.6 %all-to-all-start.5 = ((f32[64,1,8]{2,1,0:T(1,128)}), f32[64,1,8]{2,1,0:T(1,128)S(1)}, u32[]{:S(2)}, u32[]{:S(2)}) async-start(f32[64,1,8]{2,1,0:T(1,128)} %bitcast.15), calls=%async_computation.6 | async-start | bytes 65536 | tf_op jit(solution)/shard_map/all_to_all | solution.py:87
  363.1 61.6 %copy-start.4 = (bf16[64,8,128]{2,1,0:T(8,128)(2,1)S(1)}, bf16[64,8,128]{2,1,0:T(8,128)(2,1)}, u32[]{:S(2)}) copy-start(bf16[64,8,128]{2,1,0:T(8,128)(2,1)} %param.12) | copy-start | bytes 393220
  375.3 24.3 %all-to-all-start.3 = ((f32[64,8,128]{2,1,0:T(8,128)}), f32[64,8,128]{2,1,0:T(8,128)S(1)}, u32[]{:S(2)}, u32[]{:S(2)}) async-start(f32[64,8,128]{2,1,0:T(8,128)} %convolution_multiply_fusion), calls=%async_computation.4 | async-start | bytes 524288 | tf_op jit(solution)/shard_map/all_to_all | solution.py:87
  400.2 19.1 %all-to-all-start.6 = ((f32[64,1,8]{2,1,0:T(1,128)}), f32[64,1,8]{2,1,0:T(1,128)S(1)}, u32[]{:S(2)}, u32[]{:S(2)}) async-start(f32[64,1,8]{2,1,0:T(1,128)} %broadcast_in_dim.80), calls=%async_computation.7 | async-start | bytes 65536 | tf_op jit(solution)/shard_map/all_to_all | solution.py:15
  420.0 24.1 %all-to-all-start.4 = ((f32[64,8,128]{2,1,0:T(8,128)}), f32[64,8,128]{2,1,0:T(8,128)S(1)}, u32[]{:S(2)}, u32[]{:S(2)}) async-start(f32[64,8,128]{2,1,0:T(8,128)} %broadcast_in_dim.79), calls=%async_computation.5 | async-start | bytes 524288 | tf_op jit(solution)/shard_map/all_to_all | solution.py:15
  424.7 181.5 %all-reduce.2.cloned.1.call-start = ((), (), s32[]{:S(2)}) async-start(), calls=%async_computation.10 | async-start | bytes 1048576 | tf_op jit(solution)/shard_map/psum | solution.py:195
Sparse Core Ops, SparseCore 0:
  10.2 125.8 all-gather.1
  195.4 106.1 reduce-scatter.1
  429.3 176.8 all-reduce.1
where the time goes:
time: 616 us; the launch traced here: 615 us
  waiting for transfers between devices  496 us (81%)
  starting transfers between devices  44.7 us (7%)
  blocking collectives  24.4 us (4%)
  local copies, waits for them, and re-layouts  16 us (3%)
  between operations  14.1 us (2%)
  matrix products  12.1 us (2%)
  other arithmetic  7.47 us (1%)
    psum x1, waiting for transfers between devices, local(): key_grad = lax.psum(key_local, 'heads')  162 us
    all_gather x1, waiting for transfers between devices, local(): gathered = lax.all_gather(queries, 'tokens', axis=1, tiled=True)  128 us
    reduce_scatter x1, waiting for transfers between devices, one_scatter(): lax.psum_scatter(lines, axis, tiled=True).reshape(-1)  106 us
    all_to_all x4, waiting for transfers between devices, sent_to_all(): lax.all_to_all(jnp.broadcast_to(value[None], (devices, *value.shape)), ax...  68.9 us
    all_to_all x2, waiting for transfers between devices, sent_and_summed(): lax.all_to_all(parts, axis, split_axis=0, concat_axis=0, tiled=True)  30.3 us
    all_to_all x4, starting transfers between devices, sent_to_all(): lax.all_to_all(jnp.broadcast_to(value[None], (devices, *value.shape)), ax...  26.3 us
    all_to_all x1, blocking collectives, sent_to_all(): lax.all_to_all(jnp.broadcast_to(value[None], (devices, *value.shape)), ax...  24.4 us
    all_to_all x2, starting transfers between devices, sent_and_summed(): lax.all_to_all(parts, axis, split_axis=0, concat_axis=0, tiled=True)  18.3 us
  transfers between devices with their start and end apart: 9, of which 9 were waited for; matrix products, arithmetic and copies ran while one was open for 1% of the time, Pallas kernels for 0%

commit v1 on v0

v1 whole, which is shorter than its diff:
```python
import jax
import jax.numpy as jnp
from jax import lax
from jax.sharding import PartitionSpec as P

H = 128
NX, NZH = 4, 2
NY, NZ, NC = 4, 8, 2

softmax_scale = 192.0 ** (-0.5)
masked_value = -1e30


def token_at(y, z, c):
    return (y * NZ + z) * NC + c


def head_at(x, z):
    return x * NZH + z


groups_z = [[token_at(y, z, c) for z in range(NZ)] for y in range(NY) for c in range(NC)]
groups_yc = [[token_at(y, z, c) for y in range(NY) for c in range(NC)] for z in range(NZ)]
groups_x = [[head_at(x, z) for x in range(NX)] for z in range(NZH)]
pairs_zh = [(head_at(x, z), head_at(x, 1 - z)) for x in range(NX) for z in range(NZH)]


def pairs_x(flip):
    return [(head_at(x, z), head_at(x ^ flip, z)) for x in range(NX) for z in range(NZH)]


def exchanged(parts, axis, groups):
    return lax.all_to_all(parts, axis, 0, 0, tiled=True, axis_index_groups=groups)


def gathered(value, axis, groups):
    copies = jnp.broadcast_to(value[None], (len(groups[0]), *value.shape))
    return exchanged(copies, axis, groups)


def x_scatter_sum(parts, x):
    total = lax.dynamic_index_in_dim(parts, x, 0, keepdims=False)
    for flip in range(1, NX):
        piece = lax.dynamic_index_in_dim(parts, x ^ flip, 0, keepdims=False)
        total = total + lax.ppermute(piece, "heads", pairs_x(flip))
    return total


def x_gather(piece, x):
    whole = jnp.broadcast_to(piece[None], (NX, *piece.shape))
    for flip in range(1, NX):
        other = lax.ppermute(piece, "heads", pairs_x(flip))
        whole = lax.dynamic_update_index_in_dim(whole, other, x ^ flip, 0)
    return whole


def both_zh(value):
    return value + lax.ppermute(value, "heads", pairs_zh)


def joined(stats):
    maximum = jnp.max(stats[:, 0], axis=0)
    total = jnp.sum(stats[:, 1] * jnp.exp(stats[:, 0] - maximum), axis=0)
    return jnp.stack([maximum, total])


def local(queries, latent_keys, index_queries, index_keys, index_weights, positions):
    heads_here, width = queries.shape[0], queries.shape[2]
    key_count = latent_keys.shape[0]
    query_count, index_heads, index_width = index_queries.shape
    loss_scale = key_count * lax.axis_size("tokens") // 8
    x = lax.axis_index("heads") // NZH
    key_index = lax.axis_index("tokens") * key_count + jnp.arange(key_count, dtype=jnp.int32)
    share_rows = query_count // NX

    along_z = gathered(queries.reshape(heads_here, width), "tokens", groups_z)
    rows = gathered(along_z, "tokens", groups_yc).reshape(-1, width)

    index_scale = index_width ** (-0.5)
    active = (
        jnp.einsum("qjd,kd->qjk", index_queries, index_keys, preferred_element_type=jnp.float32)
        * index_scale
    )
    rectified = jnp.maximum(active, 0.0)
    partial_logits = jnp.sum(index_weights[:, :, None] * rectified, axis=1)
    logits = both_zh(x_scatter_sum(partial_logits.reshape(NX, share_rows, key_count), x))
    share_positions = lax.dynamic_slice_in_dim(positions, x * share_rows, share_rows, 0)
    logits = jnp.where(key_index[None, :] <= share_positions[:, None], logits, masked_value)
    index_max = jnp.max(logits, axis=1)
    index_total = jnp.sum(jnp.exp(logits - index_max[:, None]), axis=1)

    row_positions = positions.reshape(NY, NZ, NC).transpose(0, 2, 1).reshape(query_count)
    visible = key_index[None, :] <= row_positions[:, None]
    scores = (
        jnp.einsum("rd,kd->rk", rows, latent_keys, preferred_element_type=jnp.float32)
        * softmax_scale
    ).reshape(query_count, heads_here, key_count)
    scores = jnp.where(visible[:, None, :], scores, masked_value)
    local_max = jnp.max(scores, axis=2)
    exponent = jnp.exp(scores - local_max[..., None])
    local_total = jnp.sum(exponent, axis=2)

    def lines(main, index):
        return jnp.concatenate([main.reshape(-1, 128), jnp.pad(index, (0, 128 - share_rows))[None]])

    stats = jnp.stack([lines(local_max, index_max), lines(local_total, index_total)])
    stats = joined(gathered(stats, "tokens", groups_z))
    stats = joined(gathered(stats, "tokens", groups_yc))
    maximum = stats[0, :-1].reshape(query_count, heads_here)
    total = stats[1, :-1].reshape(query_count, heads_here)
    index_max, index_total = stats[0, -1, :share_rows], stats[1, -1, :share_rows]

    weight = jnp.exp(local_max - maximum) / total
    partial_target = jnp.sum(exponent * weight[..., None], axis=1)
    partial_target = partial_target.reshape(NY, NC, NZ, key_count).transpose(0, 2, 1, 3)
    partial_target = partial_target.reshape(NX, share_rows, key_count)
    target = both_zh(exchanged(partial_target, "heads", groups_x).sum(axis=0)) / H
    index_probs = jnp.exp(logits - index_max[:, None]) / index_total[:, None]
    share_grad = loss_scale * (index_probs - target)
    dlogit = gathered(share_grad, "heads", groups_x).reshape(query_count, key_count)

    gate = (dlogit[:, None, :] * index_weights[:, :, None] * (active > 0.0)).astype(jnp.bfloat16)
    query_local = (
        jnp.einsum("qjk,kd->qjd", gate, index_keys, preferred_element_type=jnp.float32)
        * index_scale
    ).reshape(-1, 128)
    weight_local = jnp.sum(dlogit[:, None, :] * rectified, axis=2).reshape(-1, 128)
    key_local = (
        jnp.einsum("qjk,qjd->kd", gate, index_queries, preferred_element_type=jnp.float32)
        * index_scale
    )

    both = jnp.concatenate([query_local, weight_local])
    piece_rows = -(-len(both) // (NY * NC * 8)) * 8
    both = jnp.pad(both, ((0, piece_rows * NY * NC - len(both)), (0, 0)))
    piece = exchanged(both.reshape(NY * NC, piece_rows, 128), "tokens", groups_yc).sum(axis=0)
    piece = gathered(piece, "tokens", groups_z).sum(axis=0)
    both = gathered(piece, "tokens", groups_yc).reshape(-1, 128)
    query_lines = query_count * index_heads * index_width // 128
    query_grad = both[:query_lines].reshape(query_count, index_heads, index_width)
    weight_grad = both[query_lines : query_lines + query_count * index_heads // 128]
    weight_grad = weight_grad.reshape(query_count, index_heads)

    key_piece = both_zh(x_scatter_sum(key_local.reshape(NX, key_count // NX, index_width), x))
    key_grad = x_gather(key_piece, x).reshape(key_count, index_width)
    return (query_grad, weight_grad, key_grad)


def solution(mesh):
    placed = (
        P("heads", "tokens", None),
        P("tokens", None),
        P(None, "heads", None),
        P("tokens", None),
        P(None, "heads"),
        P(),
    )
    return jax.shard_map(
        local,
        mesh=mesh,
        in_specs=placed,
        out_specs=(P(None, "heads", None), P(None, "heads"), P("tokens", None)),
        check_vma=False,
    )
```

time: 616 us -> 221 us (0.36)
  the two profiles are of different devices: /device:TPU:1 before, /device:TPU:160 now
where the time goes in v1:
time: 221 us; the launch traced here: 220 us
  starting transfers between devices  88.3 us (40%)
  waiting for transfers between devices  48 us (22%)
  blocking collectives  43.3 us (20%)
  local copies, waits for them, and re-layouts  16.1 us (7%)
  other arithmetic  14.8 us (7%)
  matrix products  8.15 us (4%)
    all_to_all x4, blocking collectives, exchanged(): lax.all_to_all(parts, axis, 0, 0, tiled=True, axis_index_groups=groups)  43.3 us
    all_to_all x5, starting transfers between devices, exchanged(): lax.all_to_all(parts, axis, 0, 0, tiled=True, axis_index_groups=groups)  33.5 us
    ppermute x3, waiting for transfers between devices, both_zh(): return value + lax.ppermute(value, 'heads', pairs_zh)  30.9 us
    ppermute x3, starting transfers between devices, both_zh(): return value + lax.ppermute(value, 'heads', pairs_zh)  25.1 us
    ppermute x6, starting transfers between devices, x_scatter_sum(): total = total + lax.ppermute(piece, 'heads', pairs_x(flip))  19.8 us
    all_to_all x5, waiting for transfers between devices, exchanged(): lax.all_to_all(parts, axis, 0, 0, tiled=True, axis_index_groups=groups)  13.3 us
    ppermute x3, starting transfers between devices, x_gather(): other = lax.ppermute(piece, 'heads', pairs_x(flip))  9.82 us
    broadcast_in_dim x7, local copies, waits for them, and re-layouts, gathered(): copies = jnp.broadcast_to(value[None], (len(groups[0]), *value.shape))  6.51 us
  transfers between devices with their start and end apart: 17, of which 8 were waited for; matrix products, arithmetic and copies ran while one was open for 8% of the time, Pallas kernels for 0%

profile of v1, /device:TPU:160, one launch (start us, length us, event | category | flops | bytes accessed | tf_op | source)
XLA Modules:
  0.0 219.6 jit_solution(16723321404875774238)
XLA Ops:
  2.1 10.8 %all-to-all-start = ((bf16[8,16,576]{2,1,0:T(8,128)(2,1)}), bf16[8,16,576]{2,1,0:T(8,128)(2,1)}, u32[]{:S(2)}, u32[]{:S(2)}) async-start(bf16[8,16,576]{2,1,0:T(8,128)(2,1)} %broadcast_in_dim.100), calls=%async_computation | async-start | bytes 327680 | tf_op jit(solution)/shard_map/all_to_all | solution.py:33
  14.3 1.9 multiply_reduce_fusion.2
  16.9 3.4 %collective-permute-start = (f32[16,1024]{1,0:T(8,128)}, f32[16,1024]{1,0:T(8,128)}, u32[]{:S(2)}, u32[]{:S(2)}) collective-permute-start(f32[16,1024]{1,0:T(8,128)} %get-tuple-element.23), channel_id=1, source_target_pairs={{0,128},{64,192},{128,0},{192,64},{256,384},{320,448},{384,256},{4... | collective-permute-start | bytes 196616 | tf_op jit(solution)/shard_map/ppermute | solution.py:45
  20.3 4.0 %collective-permute-start.2 = (f32[16,1024]{1,0:T(8,128)}, f32[16,1024]{1,0:T(8,128)}, u32[]{:S(2)}, u32[]{:S(2)}) collective-permute-start(f32[16,1024]{1,0:T(8,128)} %get-tuple-element.24), channel_id=1, source_target_pairs={{0,384},{64,448},{128,256},{192,320},{256,128},{320,192},{384,0},{... | collective-permute-start | bytes 196616 | tf_op jit(solution)/shard_map/ppermute | solution.py:45
  24.3 2.6 %collective-permute-start.1 = (f32[16,1024]{1,0:T(8,128)}, f32[16,1024]{1,0:T(8,128)}, u32[]{:S(2)}, u32[]{:S(2)}) collective-permute-start(f32[16,1024]{1,0:T(8,128)} %get-tuple-element.25), channel_id=1, source_target_pairs={{0,256},{64,320},{128,384},{192,448},{256,0},{320,64},{384,128},{4... | collective-permute-start | bytes 196616 | tf_op jit(solution)/shard_map/ppermute | solution.py:45
  26.9 2.1 broadcast_in_dim.101
  29.0 4.5 %all-to-all-start.1 = ((bf16[8,8,16,576]{3,2,1,0:T(8,128)(2,1)}), bf16[8,8,16,576]{3,2,1,0:T(8,128)(2,1)}, u32[]{:S(2)}, u32[]{:S(2)}) async-start(bf16[8,8,16,576]{3,2,1,0:T(8,128)(2,1)} %broadcast_in_dim.101), calls=%async_computation.1 | async-start | bytes 2621440 | tf_op jit(solution)/shard_map/all_to_all | solution.py:33
  37.8 8.2 %collective-permute-start.3 = (f32[16,1024]{1,0:T(8,128)}, f32[16,1024]{1,0:T(8,128)S(1)}, u32[]{:S(2)}, u32[]{:S(2)}) collective-permute-start(f32[16,1024]{1,0:T(8,128)} %fusion.9), channel_id=1, source_target_pairs={{0,64},{64,0},{128,192},{192,128},{256,320},{320,256},{384,448},{4... | collective-permute-start | bytes 196616 | tf_op jit(solution)/shard_map/ppermute | solution.py:58
  47.6 9.8 %collective-permute-done.3 = f32[16,1024]{1,0:T(8,128)S(1)} collective-permute-done((f32[16,1024]{1,0:T(8,128)}, f32[16,1024]{1,0:T(8,128)S(1)}, u32[]{:S(2)}, u32[]{:S(2)}) %collective-permute-start.3) | collective-permute-done | bytes 65568 | tf_op jit(solution)/shard_map/ppermute | solution.py:58
  59.2 3.4 %fusion = (f32[1024]{0:T(1024)S(1)}, f32[1024,1024]{1,0:T(8,128)S(1)}) fusion(pred[64,1024]{1,0:T(8,128)(4,1)S(1)} %broadcast_compare_fusion, bf16[1024,576]{1,0:T(8,128)(2,1)} %bitcast.9, bf16[1024,576]{0,1:T(8,128)(2,1)S(1)} %copy-done), kind=kOutput, calls=%fused_computation.3 | convolution fusion | flops 1211104256 | bytes 6623232 | tf_op jit(solution)/shard_map/rd,kd->rk/dot_general | solution.py:95
  64.7 12.6 %all_to_all.45 = f32[8,2,9,128]{3,1,2,0:T(2,128)S(1)} all-to-all(f32[8,2,9,128]{3,1,2,0:T(2,128)S(1)} %broadcast_in_dim.105), channel_id=1, replica_groups={{0,2,4,6,8,10,12,14},{1,3,5,7,9,11,13,15},{16,18,20,22,24,26,28,30},{17..., dimensions={0} | all-to-all | bytes 147456 | tf_op jit(solution)/shard_map/all_to_all | solution.py:33
  78.1 4.4 %all-to-all-start.3 = ((f32[8,2,9,128]{3,1,2,0:T(2,128)}), f32[8,2,9,128]{3,1,2,0:T(2,128)S(1)}, u32[]{:S(2)}, u32[]{:S(2)}) async-start(f32[8,2,9,128]{3,1,2,0:T(2,128)} %broadcast_in_dim.106), calls=%async_computation.3 | async-start | bytes 147456 | tf_op jit(solution)/shard_map/all_to_all | solution.py:33
  82.6 5.6 %all-to-all-done.3 = f32[8,2,9,128]{3,1,2,0:T(2,128)S(1)} async-done(((f32[8,2,9,128]{3,1,2,0:T(2,128)}), f32[8,2,9,128]{3,1,2,0:T(2,128)S(1)}, u32[]{:S(2)}, u32[]{:S(2)}) %all-to-all-start.3) | async-done | bytes 73760 | tf_op jit(solution)/shard_map/all_to_all | solution.py:33
  88.5 3.2 %multiply_reduce_fusion = f32[64,1024]{1,0:T(8,128)S(1)} fusion(f32[64,16]{1,0:T(8,128)S(1)} %exponential_divide_fusion, f32[64,16]{1,0:T(8,128)S(1)} %sub.75, pred[64,1024]{1,0:T(8,128)(4,1)S(1)} %broadcast_compare_fusion, f32[1024,1024]{1,0:T(8,128)} %copy-done.1), kind=kLoop, calls=%fused_computation | loop fusion | flops 4128768 | bytes 4530176 | tf_op jit(solution)/shard_map/reduce_sum | solution.py:114
  92.0 10.6 %all_to_all.46 = f32[4,16,1024]{2,1,0:T(8,128)S(1)} all-to-all(f32[4,16,1024]{2,1,0:T(8,128)S(1)} %copy.54), channel_id=1, replica_groups={{0,128,256,384},{64,192,320,448},{1,129,257,385},{65,193,321,449},{2,13..., dimensions={0} | all-to-all | bytes 524288 | tf_op jit(solution)/shard_map/all_to_all | solution.py:33
  103.3 8.3 %collective-permute-start.4 = (f32[16,1024]{1,0:T(8,128)}, f32[16,1024]{1,0:T(8,128)S(1)}, u32[]{:S(2)}, u32[]{:S(2)}) collective-permute-start(f32[16,1024]{1,0:T(8,128)} %reduce_sum.96), channel_id=1, source_target_pairs={{0,64},{64,0},{128,192},{192,128},{256,320},{320,256},{384,448},{4... | collective-permute-start | bytes 196616 | tf_op jit(solution)/shard_map/ppermute | solution.py:58
  111.7 7.0 %collective-permute-done.4 = f32[16,1024]{1,0:T(8,128)S(1)} collective-permute-done((f32[16,1024]{1,0:T(8,128)}, f32[16,1024]{1,0:T(8,128)S(1)}, u32[]{:S(2)}, u32[]{:S(2)}) %collective-permute-start.4) | collective-permute-done | bytes 65568 | tf_op jit(solution)/shard_map/ppermute | solution.py:58
  119.7 9.1 %all_to_all.47 = f32[4,16,1024]{2,1,0:T(8,128)S(1)} all-to-all(f32[4,16,1024]{2,1,0:T(8,128)S(1)} %broadcast_in_dim.108), channel_id=1, replica_groups={{0,128,256,384},{64,192,320,448},{1,129,257,385},{65,193,321,449},{2,13..., dimensions={0} | all-to-all | bytes 524288 | tf_op jit(solution)/shard_map/all_to_all | solution.py:33
  132.7 11.0 %all_to_all.48 = f32[8,72,128]{2,1,0:T(8,128)} all-to-all(f32[8,72,128]{2,1,0:T(8,128)S(1)} %bitcast.112), channel_id=1, replica_groups={{0,1,16,17,32,33,48,49},{2,3,18,19,34,35,50,51},{4,5,20,21,36,37,52,53}..., dimensions={0} | all-to-all | bytes 589824 | tf_op jit(solution)/shard_map/all_to_all | solution.py:33
  146.8 10.4 %all-to-all-start.7 = ((f32[8,72,128]{2,1,0:T(8,128)}), f32[8,72,128]{2,1,0:T(8,128)}, u32[]{:S(2)}, u32[]{:S(2)}) async-start(f32[8,72,128]{2,1,0:T(8,128)} %broadcast_in_dim.109), calls=%async_computation.7 | async-start | bytes 589824 | tf_op jit(solution)/shard_map/all_to_all | solution.py:33
  157.2 1.7 fusion.1
  158.9 2.5 %collective-permute-start.5 = (f32[256,128]{1,0:T(8,128)S(1)}, f32[256,128]{1,0:T(8,128)S(1)}, u32[]{:S(2)}, u32[]{:S(2)}) collective-permute-start(f32[256,128]{1,0:T(8,128)S(1)} %get-tuple-element.20), channel_id=1, source_target_pairs={{0,128},{64,192},{128,0},{192,64},{256,384},{320,448},{384,256},{4... | collective-permute-start | bytes 393224 | tf_op jit(solution)/shard_map/ppermute | solution.py:45
  161.4 2.7 %collective-permute-start.7 = (f32[256,128]{1,0:T(8,128)S(1)}, f32[256,128]{1,0:T(8,128)S(1)}, u32[]{:S(2)}, u32[]{:S(2)}) collective-permute-start(f32[256,128]{1,0:T(8,128)S(1)} %get-tuple-element.21), channel_id=1, source_target_pairs={{0,384},{64,448},{128,256},{192,320},{256,128},{320,192},{384,0},{... | collective-permute-start | bytes 393224 | tf_op jit(solution)/shard_map/ppermute | solution.py:45
  164.1 4.6 %collective-permute-start.6 = (f32[256,128]{1,0:T(8,128)S(1)}, f32[256,128]{1,0:T(8,128)S(1)}, u32[]{:S(2)}, u32[]{:S(2)}) collective-permute-start(f32[256,128]{1,0:T(8,128)S(1)} %get-tuple-element.22), channel_id=1, source_target_pairs={{0,256},{64,320},{128,384},{192,448},{256,0},{320,64},{384,128},{4... | collective-permute-start | bytes 393224 | tf_op jit(solution)/shard_map/ppermute | solution.py:45
  168.7 2.1 collective-permute-done.7
  172.5 8.6 %collective-permute-start.8 = (f32[256,128]{1,0:T(8,128)S(1)}, f32[256,128]{1,0:T(8,128)S(1)}, u32[]{:S(2)}, u32[]{:S(2)}) collective-permute-start(f32[256,128]{1,0:T(8,128)S(1)} %fusion.7), channel_id=1, source_target_pairs={{0,64},{64,0},{128,192},{192,128},{256,320},{320,256},{384,448},{4... | collective-permute-start | bytes 393224 | tf_op jit(solution)/shard_map/ppermute | solution.py:58
  181.1 14.2 %collective-permute-done.8 = f32[256,128]{1,0:T(8,128)S(1)} collective-permute-done((f32[256,128]{1,0:T(8,128)S(1)}, f32[256,128]{1,0:T(8,128)S(1)}, u32[]{:S(2)}, u32[]{:S(2)}) %collective-permute-start.8) | collective-permute-done | bytes 131104 | tf_op jit(solution)/shard_map/ppermute | solution.py:58
  195.3 2.9 %collective-permute-start.9 = (f32[256,128]{1,0:T(8,128)S(1)}, f32[256,128]{1,0:T(8,128)S(1)}, u32[]{:S(2)}, u32[]{:S(2)}) collective-permute-start(f32[256,128]{1,0:T(8,128)S(1)} %add.84), channel_id=1, source_target_pairs={{0,128},{64,192},{128,0},{192,64},{256,384},{320,448},{384,256},{4... | collective-permute-start | bytes 393224 | tf_op jit(solution)/shard_map/ppermute | solution.py:52
  198.2 3.8 %collective-permute-start.11 = (f32[256,128]{1,0:T(8,128)S(1)}, f32[256,128]{1,0:T(8,128)S(1)}, u32[]{:S(2)}, u32[]{:S(2)}) collective-permute-start(f32[256,128]{1,0:T(8,128)S(1)} %add.84), channel_id=1, source_target_pairs={{0,384},{64,448},{128,256},{192,320},{256,128},{320,192},{384,0},{... | collective-permute-start | bytes 393224 | tf_op jit(solution)/shard_map/ppermute | solution.py:52
  202.1 3.1 %collective-permute-start.10 = (f32[256,128]{1,0:T(8,128)S(1)}, f32[256,128]{1,0:T(8,128)S(1)}, u32[]{:S(2)}, u32[]{:S(2)}) collective-permute-start(f32[256,128]{1,0:T(8,128)S(1)} %add.84), channel_id=1, source_target_pairs={{0,256},{64,320},{128,384},{192,448},{256,0},{320,64},{384,128},{4... | collective-permute-start | bytes 393224 | tf_op jit(solution)/shard_map/ppermute | solution.py:52
  206.9 3.4 %all-to-all-start.8 = ((f32[8,72,128]{2,1,0:T(8,128)}), f32[8,72,128]{2,1,0:T(8,128)S(1)}, u32[]{:S(2)}, u32[]{:S(2)}) async-start(f32[8,72,128]{2,1,0:T(8,128)} %broadcast_in_dim.110), calls=%async_computation.8 | async-start | bytes 589824 | tf_op jit(solution)/shard_map/all_to_all | solution.py:33
  210.5 7.7 %all-to-all-done.8 = f32[8,72,128]{2,1,0:T(8,128)S(1)} async-done(((f32[8,72,128]{2,1,0:T(8,128)}), f32[8,72,128]{2,1,0:T(8,128)S(1)}, u32[]{:S(2)}, u32[]{:S(2)}) %all-to-all-start.8) | async-done | bytes 294944 | tf_op jit(solution)/shard_map/all_to_all | solution.py:33
  (82 shorter events, 28.5 us)
Async XLA Ops:
  0.6 58.6 %copy-start = (bf16[1024,576]{0,1:T(8,128)(2,1)S(1)}, bf16[1024,576]{0,1:T(8,128)(2,1)}, u32[]{:S(2)}) copy-start(bf16[1024,576]{0,1:T(8,128)(2,1)} %param.7) | copy-start | bytes 3538948
  2.1 24.7 %all-to-all-start = ((bf16[8,16,576]{2,1,0:T(8,128)(2,1)}), bf16[8,16,576]{2,1,0:T(8,128)(2,1)}, u32[]{:S(2)}, u32[]{:S(2)}) async-start(bf16[8,16,576]{2,1,0:T(8,128)(2,1)} %broadcast_in_dim.100), calls=%async_computation | async-start | bytes 327680 | tf_op jit(solution)/shard_map/all_to_all | solution.py:33
  16.9 19.4 %collective-permute-start = (f32[16,1024]{1,0:T(8,128)}, f32[16,1024]{1,0:T(8,128)}, u32[]{:S(2)}, u32[]{:S(2)}) collective-permute-start(f32[16,1024]{1,0:T(8,128)} %get-tuple-element.23), channel_id=1, source_target_pairs={{0,128},{64,192},{128,0},{192,64},{256,384},{320,448},{384,256},{4... | collective-permute-start | bytes 196616 | tf_op jit(solution)/shard_map/ppermute | solution.py:45
  20.3 16.0 %collective-permute-start.2 = (f32[16,1024]{1,0:T(8,128)}, f32[16,1024]{1,0:T(8,128)}, u32[]{:S(2)}, u32[]{:S(2)}) collective-permute-start(f32[16,1024]{1,0:T(8,128)} %get-tuple-element.24), channel_id=1, source_target_pairs={{0,384},{64,448},{128,256},{192,320},{256,128},{320,192},{384,0},{... | collective-permute-start | bytes 196616 | tf_op jit(solution)/shard_map/ppermute | solution.py:45
  24.3 12.0 %collective-permute-start.1 = (f32[16,1024]{1,0:T(8,128)}, f32[16,1024]{1,0:T(8,128)}, u32[]{:S(2)}, u32[]{:S(2)}) collective-permute-start(f32[16,1024]{1,0:T(8,128)} %get-tuple-element.25), channel_id=1, source_target_pairs={{0,256},{64,320},{128,384},{192,448},{256,0},{320,64},{384,128},{4... | collective-permute-start | bytes 196616 | tf_op jit(solution)/shard_map/ppermute | solution.py:45
  29.0 30.2 %all-to-all-start.1 = ((bf16[8,8,16,576]{3,2,1,0:T(8,128)(2,1)}), bf16[8,8,16,576]{3,2,1,0:T(8,128)(2,1)}, u32[]{:S(2)}, u32[]{:S(2)}) async-start(bf16[8,8,16,576]{3,2,1,0:T(8,128)(2,1)} %broadcast_in_dim.101), calls=%async_computation.1 | async-start | bytes 2621440 | tf_op jit(solution)/shard_map/all_to_all | solution.py:33
  37.8 19.5 %collective-permute-start.3 = (f32[16,1024]{1,0:T(8,128)}, f32[16,1024]{1,0:T(8,128)S(1)}, u32[]{:S(2)}, u32[]{:S(2)}) collective-permute-start(f32[16,1024]{1,0:T(8,128)} %fusion.9), channel_id=1, source_target_pairs={{0,64},{64,0},{128,192},{192,128},{256,320},{320,256},{384,448},{4... | collective-permute-start | bytes 196616 | tf_op jit(solution)/shard_map/ppermute | solution.py:58
  58.4 0.6 copy-start.2
  62.7 1.9 copy-start.1
  78.1 10.1 %all-to-all-start.3 = ((f32[8,2,9,128]{3,1,2,0:T(2,128)}), f32[8,2,9,128]{3,1,2,0:T(2,128)S(1)}, u32[]{:S(2)}, u32[]{:S(2)}) async-start(f32[8,2,9,128]{3,1,2,0:T(2,128)} %broadcast_in_dim.106), calls=%async_computation.3 | async-start | bytes 147456 | tf_op jit(solution)/shard_map/all_to_all | solution.py:33
  103.3 26.4 %copy-start.4 = (bf16[1024,128]{1,0:T(8,128)(2,1)S(1)}, bf16[1024,128]{1,0:T(8,128)(2,1)}, u32[]{:S(2)}) copy-start(bf16[1024,128]{1,0:T(8,128)(2,1)} %param.9) | copy-start | bytes 786436
  103.3 26.4 %copy-start.5 = (f32[64,8]{1,0:T(8,128)S(1)}, f32[64,8]{1,0:T(8,128)}, u32[]{:S(2)}) copy-start(f32[64,8]{1,0:T(8,128)} %copy.46) | copy-start | bytes 6148
  103.3 15.3 %collective-permute-start.4 = (f32[16,1024]{1,0:T(8,128)}, f32[16,1024]{1,0:T(8,128)S(1)}, u32[]{:S(2)}, u32[]{:S(2)}) collective-permute-start(f32[16,1024]{1,0:T(8,128)} %reduce_sum.96), channel_id=1, source_target_pairs={{0,64},{64,0},{128,192},{192,128},{256,320},{320,256},{384,448},{4... | collective-permute-start | bytes 196616 | tf_op jit(solution)/shard_map/ppermute | solution.py:58
  146.8 58.4 %all-to-all-start.7 = ((f32[8,72,128]{2,1,0:T(8,128)}), f32[8,72,128]{2,1,0:T(8,128)}, u32[]{:S(2)}, u32[]{:S(2)}) async-start(f32[8,72,128]{2,1,0:T(8,128)} %broadcast_in_dim.109), calls=%async_computation.7 | async-start | bytes 589824 | tf_op jit(solution)/shard_map/all_to_all | solution.py:33
  158.9 9.8 %collective-permute-start.5 = (f32[256,128]{1,0:T(8,128)S(1)}, f32[256,128]{1,0:T(8,128)S(1)}, u32[]{:S(2)}, u32[]{:S(2)}) collective-permute-start(f32[256,128]{1,0:T(8,128)S(1)} %get-tuple-element.20), channel_id=1, source_target_pairs={{0,128},{64,192},{128,0},{192,64},{256,384},{320,448},{384,256},{4... | collective-permute-start | bytes 393224 | tf_op jit(solution)/shard_map/ppermute | solution.py:45
  161.4 9.5 %collective-permute-start.7 = (f32[256,128]{1,0:T(8,128)S(1)}, f32[256,128]{1,0:T(8,128)S(1)}, u32[]{:S(2)}, u32[]{:S(2)}) collective-permute-start(f32[256,128]{1,0:T(8,128)S(1)} %get-tuple-element.21), channel_id=1, source_target_pairs={{0,384},{64,448},{128,256},{192,320},{256,128},{320,192},{384,0},{... | collective-permute-start | bytes 393224 | tf_op jit(solution)/shard_map/ppermute | solution.py:45
  164.1 8.4 %collective-permute-start.6 = (f32[256,128]{1,0:T(8,128)S(1)}, f32[256,128]{1,0:T(8,128)S(1)}, u32[]{:S(2)}, u32[]{:S(2)}) collective-permute-start(f32[256,128]{1,0:T(8,128)S(1)} %get-tuple-element.22), channel_id=1, source_target_pairs={{0,256},{64,320},{128,384},{192,448},{256,0},{320,64},{384,128},{4... | collective-permute-start | bytes 393224 | tf_op jit(solution)/shard_map/ppermute | solution.py:45
  172.5 22.8 %collective-permute-start.8 = (f32[256,128]{1,0:T(8,128)S(1)}, f32[256,128]{1,0:T(8,128)S(1)}, u32[]{:S(2)}, u32[]{:S(2)}) collective-permute-start(f32[256,128]{1,0:T(8,128)S(1)} %fusion.7), channel_id=1, source_target_pairs={{0,64},{64,0},{128,192},{192,128},{256,320},{320,256},{384,448},{4... | collective-permute-start | bytes 393224 | tf_op jit(solution)/shard_map/ppermute | solution.py:58
  195.3 9.8 %collective-permute-start.9 = (f32[256,128]{1,0:T(8,128)S(1)}, f32[256,128]{1,0:T(8,128)S(1)}, u32[]{:S(2)}, u32[]{:S(2)}) collective-permute-start(f32[256,128]{1,0:T(8,128)S(1)} %add.84), channel_id=1, source_target_pairs={{0,128},{64,192},{128,0},{192,64},{256,384},{320,448},{384,256},{4... | collective-permute-start | bytes 393224 | tf_op jit(solution)/shard_map/ppermute | solution.py:52
  198.2 12.2 %collective-permute-start.11 = (f32[256,128]{1,0:T(8,128)S(1)}, f32[256,128]{1,0:T(8,128)S(1)}, u32[]{:S(2)}, u32[]{:S(2)}) collective-permute-start(f32[256,128]{1,0:T(8,128)S(1)} %add.84), channel_id=1, source_target_pairs={{0,384},{64,448},{128,256},{192,320},{256,128},{320,192},{384,0},{... | collective-permute-start | bytes 393224 | tf_op jit(solution)/shard_map/ppermute | solution.py:52
  202.1 8.4 %collective-permute-start.10 = (f32[256,128]{1,0:T(8,128)S(1)}, f32[256,128]{1,0:T(8,128)S(1)}, u32[]{:S(2)}, u32[]{:S(2)}) collective-permute-start(f32[256,128]{1,0:T(8,128)S(1)} %add.84), channel_id=1, source_target_pairs={{0,256},{64,320},{128,384},{192,448},{256,0},{320,64},{384,128},{4... | collective-permute-start | bytes 393224 | tf_op jit(solution)/shard_map/ppermute | solution.py:52
  206.9 11.2 %all-to-all-start.8 = ((f32[8,72,128]{2,1,0:T(8,128)}), f32[8,72,128]{2,1,0:T(8,128)S(1)}, u32[]{:S(2)}, u32[]{:S(2)}) async-start(f32[8,72,128]{2,1,0:T(8,128)} %broadcast_in_dim.110), calls=%async_computation.8 | async-start | bytes 589824 | tf_op jit(solution)/shard_map/all_to_all | solution.py:33
  210.5 9.2 %copy-start.3 = (f32[4,256,128]{2,1,0:T(8,128)}, f32[4,256,128]{2,1,0:T(8,128)S(1)}, u32[]{:S(2)}) copy-start(f32[4,256,128]{2,1,0:T(8,128)S(1)} %bitcast_dynamic-update-slice_fusion) | copy-start | bytes 1572868

commit v2 on v1

v2 whole, which is shorter than its diff:
```python
import jax
import jax.numpy as jnp
from jax import lax
from jax.experimental import pallas as pl
from jax.experimental.pallas import tpu as pltpu
from jax.sharding import PartitionSpec as P

H = 128
NX, NZH = 4, 2
NY, NZ, NC = 4, 8, 2
NYC = NY * NC
GRAD_SCALE = 8192.0

softmax_scale = 192.0 ** (-0.5)
masked_value = -1e30
f32, bf16 = jnp.float32, jnp.bfloat16


def token_at(y, z, c):
    return (y * NZ + z) * NC + c


def head_at(x, z):
    return x * NZH + z


groups_z = [[token_at(y, z, c) for z in range(NZ)] for y in range(NY) for c in range(NC)]
groups_yc = [[token_at(y, z, c) for y in range(NY) for c in range(NC)] for z in range(NZ)]
groups_x = [[head_at(x, z) for x in range(NX)] for z in range(NZH)]
pairs_zh = [(head_at(x, z), head_at(x, 1 - z)) for x in range(NX) for z in range(NZH)]


def pairs_x(flip):
    return [(head_at(x, z), head_at(x ^ flip, z)) for x in range(NX) for z in range(NZH)]


def exchanged(parts, axis, groups):
    return lax.all_to_all(parts, axis, 0, 0, tiled=True, axis_index_groups=groups)


def gathered(value, axis, groups):
    copies = jnp.broadcast_to(value[None], (len(groups[0]), *value.shape))
    return exchanged(copies, axis, groups)


def diagonal(rows, lanes):
    return lax.broadcasted_iota(jnp.int32, (rows, lanes), 0) == lax.broadcasted_iota(
        jnp.int32, (rows, lanes), 1
    )


def as_row(column, lanes=128):
    return jnp.sum(jnp.where(diagonal(column.shape[0], lanes), column, 0.0), axis=0, keepdims=True)


def as_column(row, rows):
    return jnp.sum(jnp.where(diagonal(rows, row.shape[1]), row, 0.0), axis=1, keepdims=True)


def call(kernel, out_shape, grid=None, in_specs=None, out_specs=None, flops=0, moved=0):
    whole = {}
    if grid is not None:
        whole = dict(grid=grid, in_specs=in_specs, out_specs=out_specs)
    return pl.pallas_call(
        kernel,
        out_shape=out_shape,
        compiler_params=pltpu.CompilerParams(vmem_limit_bytes=48 << 20),
        cost_estimate=pl.CostEstimate(flops=flops, bytes_accessed=moved, transcendentals=0),
        **whole,
    )


def score_kernel(limit_ref, q_ref, k_ref, e_ref, m_ref, l_ref):
    b = pl.program_id(0)
    rows, keys = e_ref.shape
    heads = rows // NZ
    s = jnp.dot(q_ref[...], k_ref[...], preferred_element_type=f32) * softmax_scale
    row = lax.broadcasted_iota(jnp.int32, (rows, 1), 0)
    limit = jnp.zeros((rows, 1), jnp.int32)
    for z in range(NZ):
        here = (row >= z * heads) & (row < (z + 1) * heads)
        limit = jnp.where(here, limit_ref[b * NZ + z], limit)
    key = lax.broadcasted_iota(jnp.int32, (1, keys), 1)
    s = jnp.where(key <= limit, s, masked_value)
    m = jnp.max(s, axis=1, keepdims=True)
    e = jnp.exp(s - m)
    e_ref[...] = e
    m_ref[pl.ds(b, 1), :] = as_row(m)
    l_ref[pl.ds(b, 1), :] = as_row(jnp.sum(e, axis=1, keepdims=True))


def message_parts(ref, tokens, heads):
    block = ref[tokens * heads :, :].astype(f32)
    w = block[:, :heads] + block[:, heads : 2 * heads] + block[:, 2 * heads : 3 * heads]
    return ref[: tokens * heads, :], w


def index_dot(iq, ik):
    return lax.dot_general(iq, ik, (((1,), (1,)), ((), ())), preferred_element_type=f32)


def logits_kernel(heads, scale, limit_ref, ik_ref, *refs):
    messages, (logits_ref, stat_ref) = refs[:-2], refs[-2:]
    tokens, keys = logits_ref.shape
    ik = ik_ref[...]
    logits = jnp.zeros((tokens, keys), f32)
    for message in messages:
        for part in range(message.shape[0]):
            iq, w = message_parts(message.at[part], tokens, heads)
            active = index_dot(iq, ik)
            for j in range(heads):
                here = active[j * tokens : (j + 1) * tokens] * scale
                logits = logits + w[:, j : j + 1] * jnp.maximum(here, 0.0)
    key = lax.broadcasted_iota(jnp.int32, (1, keys), 1)
    logits = jnp.where(key <= limit_ref[...], logits, masked_value)
    m = jnp.max(logits, axis=1, keepdims=True)
    l = jnp.sum(jnp.exp(logits - m), axis=1, keepdims=True)
    logits_ref[...] = logits
    stat_ref[...] = jnp.concatenate([as_row(m), as_row(l), jnp.zeros((6, 128), f32)], axis=0)


def joined(stats):
    def one(m, l):
        top = jnp.max(m, axis=0)
        return top, jnp.sum(l * jnp.exp(m - top), axis=0)

    return (*one(stats[:, 0:8], stats[:, 8:16]), *one(stats[:, 16:17], stats[:, 17:18]))


def join_kernel(stats_ref, out_ref):
    lines = jnp.concatenate([*joined(stats_ref[...]), jnp.zeros((6, 128), f32)], axis=0)
    out_ref[...] = jnp.broadcast_to(lines[None], out_ref.shape)


def target_kernel(stats_ref, m_ref, e_ref, out_ref):
    b = pl.program_id(0)
    rows, keys = e_ref.shape
    m = stats_ref[:, pl.ds(b, 1), :]
    l = stats_ref[:, pl.ds(b + 8, 1), :]
    top = jnp.max(m, axis=0)
    total = jnp.sum(l * jnp.exp(m - top), axis=0)
    weight = as_column(jnp.exp(m_ref[pl.ds(b, 1), :] - top) / total, rows)
    part = jnp.sum((e_ref[...] * weight).reshape(NZ, rows // NZ, keys), axis=1)
    out_ref[...] = jnp.broadcast_to(part[None], out_ref.shape)


def grad_kernel(heads, scale, one_ref, two_ref, logits_ref, stats_ref, message_ref, ik_ref, d_ref, out_ref):
    tokens, keys = logits_ref.shape
    stats = stats_ref[...]
    _, _, top, total = joined(stats)
    probs = jnp.exp(logits_ref[...] - as_column(top, tokens)) / as_column(total, tokens)
    dlogit = GRAD_SCALE * (probs - (one_ref[...] + two_ref[...]) / H)
    d_ref[...] = dlogit
    iq, w = message_parts(message_ref, tokens, heads)
    ik = ik_ref[...]
    active = index_dot(iq, ik)
    row = lax.broadcasted_iota(jnp.int32, (tokens, 128), 0)
    place = row // (NC * NZ) * (NC * NZ) + row % NZ * NC + row // NZ % NC
    places = place == lax.broadcasted_iota(jnp.int32, (tokens, 128), 1)
    out_ref[tokens * heads :, :] = jnp.zeros((out_ref.shape[0] - tokens * heads, 128), f32)
    for j in range(heads):
        here = active[j * tokens : (j + 1) * tokens]
        gate = jnp.where(here > 0.0, dlogit * w[:, j : j + 1], 0.0).astype(bf16)
        grad = jnp.dot(gate, ik, preferred_element_type=f32) * scale
        for b in range(NYC):
            first = (b // NC) * (NZ * NC) + b % NC
            lines = pl.ds(first * heads + j, NZ, stride=NC * heads)
            out_ref[lines, :] = grad[b * NZ : (b + 1) * NZ]
        weight_grad = jnp.sum(dlogit * jnp.maximum(here * scale, 0.0), axis=1, keepdims=True)
        out_ref[tokens * heads + j : tokens * heads + j + 1, :] = jnp.sum(
            jnp.where(places, weight_grad, 0.0), axis=0, keepdims=True
        )


def key_kernel(heads, scale, d_ref, ik_ref, *refs):
    messages, out_ref = refs[:-1], refs[-1]
    tokens, keys = d_ref.shape
    dlogit, ik = d_ref[...], ik_ref[...]
    total = jnp.zeros((ik.shape[1], keys), f32)
    for message in messages:
        for part in range(message.shape[0]):
            iq, w = message_parts(message.at[part], tokens, heads)
            active = index_dot(iq, ik)
            gates = []
            for j in range(heads):
                here = active[j * tokens : (j + 1) * tokens]
                gates.append(jnp.where(here > 0.0, dlogit * w[:, j : j + 1], 0.0).astype(bf16))
            gate = jnp.concatenate(gates, axis=0)
            total = total + jnp.dot(iq.T, gate, preferred_element_type=f32)
    out_ref[...] = total.T * scale


def sum_kernel(parts_ref, out_ref):
    out_ref[...] = jnp.broadcast_to(jnp.sum(parts_ref[...], axis=0)[None], out_ref.shape)


def in_order(value):
    return jnp.swapaxes(value.reshape(NY, NZ, NC, *value.shape[1:]), 1, 2).reshape(value.shape)


def local(queries, latent_keys, index_queries, index_keys, index_weights, positions):
    heads_here, width = queries.shape[0], queries.shape[2]
    key_count = latent_keys.shape[0]
    query_count, index_heads, index_width = index_queries.shape
    index_scale = index_width ** (-0.5)
    shape = jax.ShapeDtypeStruct
    limit = in_order(positions - lax.axis_index("tokens") * key_count)

    along_z = gathered(queries.reshape(heads_here, width), "tokens", groups_z)

    high = lax.reduce_precision(index_weights, 8, 7)
    middle = lax.reduce_precision(index_weights - high, 8, 7)
    low = index_weights - high - middle
    lines = jnp.pad(in_order(jnp.concatenate([high, middle, low], axis=1)), ((0, 0), (0, 128 - 3 * index_heads)))
    by_head = in_order(index_queries).transpose(1, 0, 2)
    by_head = by_head.reshape(index_heads * query_count, index_width)
    mine = jnp.concatenate([by_head, lines.astype(bf16)])
    pair = jnp.stack([mine, lax.ppermute(mine, "heads", pairs_zh)])
    messages = [pair] + [lax.ppermute(pair, "heads", pairs_x(flip)) for flip in range(1, NX)]

    rows = gathered(along_z, "tokens", groups_yc).reshape(-1, width)
    row_count = rows.shape[0]
    block = row_count // NYC

    index_flops = 2 * query_count * index_heads * NX * NZH * key_count * index_width
    logits, index_stats = call(
        lambda *refs: logits_kernel(index_heads, index_scale, *refs),
        (shape((query_count, key_count), f32), shape((8, 128), f32)),
        flops=index_flops,
        moved=2 << 20,
    )(limit[:, None], index_keys, *messages)

    score_flops = 2 * row_count * key_count * width
    exponent, local_max, local_total = call(
        score_kernel,
        (shape((row_count, key_count), f32), shape((NYC, block), f32), shape((NYC, block), f32)),
        grid=(NYC,),
        in_specs=[
            pl.BlockSpec(memory_space=pltpu.SMEM),
            pl.BlockSpec((block, width), lambda b: (b, 0)),
            pl.BlockSpec((width, key_count), lambda b: (0, 0)),
        ],
        out_specs=[
            pl.BlockSpec((block, key_count), lambda b: (b, 0)),
            pl.BlockSpec((NYC, block), lambda b: (0, 0)),
            pl.BlockSpec((NYC, block), lambda b: (0, 0)),
        ],
        flops=score_flops,
        moved=7 << 20,
    )(limit, rows, latent_keys.T)

    stats = jnp.concatenate([local_max, local_total, index_stats])
    stats = gathered(stats, "tokens", groups_z)
    stats = call(join_kernel, shape((NYC, *stats.shape[1:]), f32))(stats)
    stats = exchanged(stats, "tokens", groups_yc)

    partial = call(
        target_kernel,
        shape((NX, query_count, key_count), f32),
        grid=(NYC,),
        in_specs=[
            pl.BlockSpec(stats.shape, lambda b: (0, 0, 0)),
            pl.BlockSpec((NYC, block), lambda b: (0, 0)),
            pl.BlockSpec((block, key_count), lambda b: (b, 0)),
        ],
        out_specs=pl.BlockSpec((NX, NZ, key_count), lambda b: (0, b, 0)),
        moved=5 << 20,
    )(stats, local_max, exponent)
    over_x = exchanged(partial, "heads", groups_x).sum(axis=0)
    other = lax.ppermute(over_x, "heads", pairs_zh)

    query_lines = query_count * index_heads
    piece_rows = -(-(query_lines + index_heads) // (NYC * 8)) * 8
    dlogit, both = call(
        lambda *refs: grad_kernel(index_heads, index_scale, *refs),
        (shape((query_count, key_count), f32), shape((piece_rows * NYC, 128), f32)),
        flops=index_flops // 4,
        moved=2 << 20,
    )(over_x, other, logits, stats, mine, index_keys)

    piece = exchanged(both.reshape(NYC, piece_rows, 128), "tokens", groups_yc)
    piece = call(sum_kernel, shape((NZ, piece_rows, 128), f32))(piece)
    piece = exchanged(piece, "tokens", groups_z)
    piece = call(sum_kernel, shape((NYC, piece_rows, 128), f32))(piece)
    both = exchanged(piece, "tokens", groups_yc).reshape(-1, 128)
    query_grad = both[:query_lines].reshape(query_count, index_heads, index_width)
    weight_grad = both[query_lines : query_lines + index_heads, :query_count].T

    key_grad = call(
        lambda *refs: key_kernel(index_heads, index_scale, *refs),
        shape((key_count, index_width), f32),
        flops=2 * index_flops,
        moved=3 << 20,
    )(dlogit, index_keys, *messages)
    return (query_grad, weight_grad, key_grad)


def solution(mesh):
    placed = (
        P("heads", "tokens", None),
        P("tokens", None),
        P(None, "heads", None),
        P("tokens", None),
        P(None, "heads"),
        P(),
    )
    return jax.shard_map(
        local,
        mesh=mesh,
        in_specs=placed,
        out_specs=(P(None, "heads", None), P(None, "heads"), P("tokens", None)),
        check_vma=False,
    )
```

time: 221 us -> 217 us (0.982)
  the two profiles are of different devices: /device:TPU:160 before, /device:TPU:1 now
where the time goes in v2:
time: 217 us
  blocking collectives  96.8 us (45%)
  waiting for transfers between devices  52.3 us (24%)
  starting transfers between devices  40 us (18%)
  Pallas kernels  20.6 us (9%)
  local copies, waits for them, and re-layouts  5.96 us (3%)
    all_to_all x6, blocking collectives, exchanged(): lax.all_to_all(parts, axis, 0, 0, tiled=True, axis_index_groups=groups)  96.8 us
    ppermute x1, waiting for transfers between devices, local(): other = lax.ppermute(over_x, 'heads', pairs_zh)  25.5 us
    ppermute x1, waiting for transfers between devices, local(): pair = jnp.stack([mine, lax.ppermute(mine, 'heads', pairs_zh)])  15.8 us
    all_to_all x2, starting transfers between devices, exchanged(): lax.all_to_all(parts, axis, 0, 0, tiled=True, axis_index_groups=groups)  14.6 us
    ppermute x3, waiting for transfers between devices, local(): lax.ppermute(pair, 'heads', pairs_x(flip))  9.99 us
    ppermute x3, starting transfers between devices, local(): lax.ppermute(pair, 'heads', pairs_x(flip))  8.98 us
    ppermute x1, starting transfers between devices, local(): other = lax.ppermute(over_x, 'heads', pairs_zh)  8.48 us
    ppermute x1, starting transfers between devices, local(): pair = jnp.stack([mine, lax.ppermute(mine, 'heads', pairs_zh)])  7.94 us
  transfers between devices with their start and end apart: 7, of which 5 were waited for; matrix products, arithmetic and copies ran while one was open for 0% of the time, Pallas kernels for 5%

profile of v2, /device:TPU:1, one launch (start us, length us, event | category | flops | bytes accessed | tf_op | source)
XLA Modules:
  0.0 216.6 jit_solution(14914807742393354696)
XLA Ops:
  0.6 0.7 broadcast_in_dim.9
  1.4 23.5 %all_to_all.40 = bf16[8,16,576]{2,1,0:T(8,128)(2,1)S(1)} all-to-all(bf16[8,16,576]{2,1,0:T(8,128)(2,1)S(1)} %broadcast_in_dim.9), channel_id=1, replica_groups={{0,2,4,6,8,10,12,14},{1,3,5,7,9,11,13,15},{16,18,20,22,24,26,28,30},{17..., dimensions={0} | all-to-all | bytes 294912 | tf_op jit(solution)/shard_map/all_to_all | solution.py:38
  24.9 1.2 broadcast_in_dim.10
  26.1 7.8 %all-to-all-start.1 = ((bf16[8,8,16,576]{3,2,1,0:T(8,128)(2,1)}), bf16[8,8,16,576]{3,2,1,0:T(8,128)(2,1)S(1)}, u32[]{:S(2)}, u32[]{:S(2)}) async-start(bf16[8,8,16,576]{3,2,1,0:T(8,128)(2,1)} %broadcast_in_dim.10), calls=%async_computation.1 | async-start | bytes 2621440 | tf_op jit(solution)/shard_map/all_to_all | solution.py:38
  33.9 0.1 copy.24
  34.1 7.9 %collective-permute-start = (bf16[576,128]{1,0:T(8,128)(2,1)S(1)}, bf16[576,128]{1,0:T(8,128)(2,1)S(1)}, u32[]{:S(2)}, u32[]{:S(2)}) collective-permute-start(bf16[576,128]{1,0:T(8,128)(2,1)S(1)} %get-tuple-element.18.refs_4_), channel_id=1, source_target_pairs={{0,64},{64,0},{128,192},{192,128},{256,320},{320,256},{384,448},{4... | collective-permute-start | bytes 442376 | tf_op jit(solution)/shard_map/ppermute | solution.py:218
  42.1 15.8 %collective-permute-done = bf16[576,128]{1,0:T(8,128)(2,1)S(1)} collective-permute-done((bf16[576,128]{1,0:T(8,128)(2,1)S(1)}, bf16[576,128]{1,0:T(8,128)(2,1)S(1)}, u32[]{:S(2)}, u32[]{:S(2)}) %collective-permute-start) | collective-permute-done | bytes 147488 | tf_op jit(solution)/shard_map/ppermute | solution.py:218
  57.9 4.4 %collective-permute-start.3 = (bf16[2,576,128]{2,1,0:T(8,128)(2,1)S(1)}, bf16[2,576,128]{2,1,0:T(8,128)(2,1)}, u32[]{:S(2)}, u32[]{:S(2)}) collective-permute-start(bf16[2,576,128]{2,1,0:T(8,128)(2,1)S(1)} %pad_maximum_fusion.refs_2_), channel_id=1, source_target_pairs={{0,384},{64,448},{128,256},{192,320},{256,128},{320,192},{384,0},{... | collective-permute-start | bytes 884744 | tf_op jit(solution)/shard_map/ppermute | solution.py:219
  62.3 2.4 %collective-permute-start.2 = (bf16[2,576,128]{2,1,0:T(8,128)(2,1)S(1)}, bf16[2,576,128]{2,1,0:T(8,128)(2,1)}, u32[]{:S(2)}, u32[]{:S(2)}) collective-permute-start(bf16[2,576,128]{2,1,0:T(8,128)(2,1)S(1)} %pad_maximum_fusion.refs_2_), channel_id=1, source_target_pairs={{0,256},{64,320},{128,384},{192,448},{256,0},{320,64},{384,128},{4... | collective-permute-start | bytes 884744 | tf_op jit(solution)/shard_map/ppermute | solution.py:219
  64.8 2.2 collective-permute-start.1
  66.9 0.1 reshape.44
  67.1 0.1 copy.21
  67.3 6.5 %collective-permute-done.3.refs_5_ = bf16[2,576,128]{2,1,0:T(8,128)(2,1)} collective-permute-done((bf16[2,576,128]{2,1,0:T(8,128)(2,1)S(1)}, bf16[2,576,128]{2,1,0:T(8,128)(2,1)}, u32[]{:S(2)}, u32[]{:S(2)}) %collective-permute-start.3) | collective-permute-done | bytes 294944 | tf_op jit(solution)/shard_map/ppermute | solution.py:219
  73.8 3.5 %collective-permute-done.1.refs_3_ = bf16[2,576,128]{2,1,0:T(8,128)(2,1)} collective-permute-done((bf16[2,576,128]{2,1,0:T(8,128)(2,1)S(1)}, bf16[2,576,128]{2,1,0:T(8,128)(2,1)}, u32[]{:S(2)}, u32[]{:S(2)}) %collective-permute-start.1) | collective-permute-done | bytes 294944 | tf_op jit(solution)/shard_map/ppermute | solution.py:219
  77.3 4.7 %shard_map.86 = (f32[64,1024]{1,0:T(8,128)S(1)}, f32[8,128]{1,0:T(8,128)S(1)}) custom-call(s32[64,1]{1,0:T(8,128)S(1)} %broadcast_in_dim_reshape.5.refs_0_, bf16[1024,128]{1,0:T(8,128)(2,1)S(1)} %copy-done.1, bf16[2,576,128]{2,1,0:T(8,128)(2,1)S(1)} %pad_maximum_fusion.refs_2_, bf16[2,576,128]{2,1,0:T(8,128)(2,1)} %collective-permute-done.1.refs_3_, ...), custom_call_target="tpu_custom_call" | custom-call | flops 1073741824 | bytes 2097152 | tf_op jit(solution)/shard_map/pallas_call | solution.py:226
  82.0 6.4 %shard_map.85 = (f32[1024,1024]{1,0:T(8,128)}, f32[8,128]{1,0:T(8,128)S(1)}, f32[8,128]{1,0:T(8,128)S(1)}) custom-call(s32[64]{0:T(128)S(1)} %reshape.45.limit_ref, bf16[1024,576]{1,0:T(8,128)(2,1)S(1)} %bitcast.25, bf16[576,1024]{1,0:T(8,128)(2,1)S(1)} %bitcast.27), custom_call_target="tpu_custom_call" | custom-call | flops 1207959552 | bytes 7340032 | tf_op jit(solution)/shard_map/pallas_call | solution.py:234
  88.5 14.0 %all_to_all.41.stats_ref = f32[8,24,128]{2,1,0:T(8,128)S(1)} all-to-all(f32[8,24,128]{2,1,0:T(8,128)S(1)} %broadcast_in_dim.22), channel_id=1, replica_groups={{0,2,4,6,8,10,12,14},{1,3,5,7,9,11,13,15},{16,18,20,22,24,26,28,30},{17..., dimensions={0} | all-to-all | bytes 196608 | tf_op jit(solution)/shard_map/all_to_all | solution.py:38
  102.5 12.2 %all_to_all.42.stats_ref.refs_3_ = f32[8,24,128]{2,1,0:T(8,128)S(1)} all-to-all(f32[8,24,128]{2,1,0:T(8,128)S(1)} %shard_map.87), channel_id=1, replica_groups={{0,1,16,17,32,33,48,49},{2,3,18,19,34,35,50,51},{4,5,20,21,36,37,52,53}..., dimensions={0} | all-to-all | bytes 196608 | tf_op jit(solution)/shard_map/all_to_all | solution.py:38
  114.7 2.2 %copy-done = f32[1024,1024]{1,0:T(8,128)S(1)} copy-done((f32[1024,1024]{1,0:T(8,128)S(1)}, f32[1024,1024]{1,0:T(8,128)}, u32[]{:S(2)}) %copy-start) | copy-done | bytes 4194328
  116.9 1.7 shard_map.88
  118.6 17.8 %all_to_all.43 = f32[4,64,1024]{2,1,0:T(8,128)S(1)} all-to-all(f32[4,64,1024]{2,1,0:T(8,128)S(1)} %shard_map.88), channel_id=1, replica_groups={{0,128,256,384},{64,192,320,448},{1,129,257,385},{65,193,321,449},{2,13..., dimensions={0} | all-to-all | bytes 2097152 | tf_op jit(solution)/shard_map/all_to_all | solution.py:38
  136.6 8.5 %collective-permute-start.4 = (f32[64,1024]{1,0:T(8,128)S(1)}, f32[64,1024]{1,0:T(8,128)S(1)}, u32[]{:S(2)}, u32[]{:S(2)}) collective-permute-start(f32[64,1024]{1,0:T(8,128)S(1)} %reduce_sum.9.refs_0_), channel_id=1, source_target_pairs={{0,64},{64,0},{128,192},{192,128},{256,320},{320,256},{384,448},{4... | collective-permute-start | bytes 786440 | tf_op jit(solution)/shard_map/ppermute | solution.py:270
  145.0 25.5 %collective-permute-done.4.refs_1_ = f32[64,1024]{1,0:T(8,128)S(1)} collective-permute-done((f32[64,1024]{1,0:T(8,128)S(1)}, f32[64,1024]{1,0:T(8,128)S(1)}, u32[]{:S(2)}, u32[]{:S(2)}) %collective-permute-start.4) | collective-permute-done | bytes 262176 | tf_op jit(solution)/shard_map/ppermute | solution.py:270
  170.5 1.1 shard_map.89
  171.6 10.2 %all_to_all.44.parts_ref = f32[8,72,128]{2,1,0:T(8,128)S(1)} all-to-all(f32[8,72,128]{2,1,0:T(8,128)S(1)} %bitcast.26), channel_id=1, replica_groups={{0,1,16,17,32,33,48,49},{2,3,18,19,34,35,50,51},{4,5,20,21,36,37,52,53}..., dimensions={0} | all-to-all | bytes 589824 | tf_op jit(solution)/shard_map/all_to_all | solution.py:38
  181.9 19.0 %all_to_all.45.parts_ref = f32[8,72,128]{2,1,0:T(8,128)S(1)} all-to-all(f32[8,72,128]{2,1,0:T(8,128)S(1)} %shard_map.90), channel_id=1, replica_groups={{0,2,4,6,8,10,12,14},{1,3,5,7,9,11,13,15},{16,18,20,22,24,26,28,30},{17..., dimensions={0} | all-to-all | bytes 589824 | tf_op jit(solution)/shard_map/all_to_all | solution.py:38
  200.9 0.7 shard_map.91
  201.7 6.8 %all-to-all-start.7 = ((f32[8,72,128]{2,1,0:T(8,128)}), f32[8,72,128]{2,1,0:T(8,128)S(1)}, u32[]{:S(2)}, u32[]{:S(2)}) async-start(f32[8,72,128]{2,1,0:T(8,128)} %shard_map.91), calls=%async_computation.7 | async-start | bytes 589824 | tf_op jit(solution)/shard_map/all_to_all | solution.py:38
  208.5 5.9 %shard_map.92 = f32[1024,128]{1,0:T(8,128)} custom-call(f32[64,1024]{1,0:T(8,128)S(1)} %get-tuple-element.16.refs_0_, bf16[1024,128]{1,0:T(8,128)(2,1)S(1)} %copy-done.1, bf16[2,576,128]{2,1,0:T(8,128)(2,1)S(1)} %pad_maximum_fusion.refs_2_, bf16[2,576,128]{2,1,0:T(8,128)(2,1)} %collective-permute-done.1.refs_3_, ...), custom_call_target="tpu_custom_call" | custom-call | flops 2147483648 | bytes 3145728 | tf_op jit(solution)/shard_map/pallas_call | solution.py:289
  214.3 1.0 all-to-all-done.7
  215.3 0.6 slice_bitcast_fusion.1
  215.9 0.7 slice_bitcast_fusion
  (27 shorter events, 0.5 us)
Async XLA Ops:
  26.1 7.8 %copy-start.4 = (f32[64,8]{0,1:T(8,128)S(1)}, f32[64,8]{0,1:T(8,128)}, u32[]{:S(2)}) copy-start(f32[64,8]{0,1:T(8,128)} %param.10) | copy-start | bytes 6148
  26.1 8.0 %copy-start.3 = (bf16[64,8,128]{2,1,0:T(8,128)(2,1)S(1)}, bf16[64,8,128]{2,1,0:T(8,128)(2,1)}, u32[]{:S(2)}) copy-start(bf16[64,8,128]{2,1,0:T(8,128)(2,1)} %param.8) | copy-start | bytes 393220
  26.1 55.9 %all-to-all-start.1 = ((bf16[8,8,16,576]{3,2,1,0:T(8,128)(2,1)}), bf16[8,8,16,576]{3,2,1,0:T(8,128)(2,1)S(1)}, u32[]{:S(2)}, u32[]{:S(2)}) async-start(bf16[8,8,16,576]{3,2,1,0:T(8,128)(2,1)} %broadcast_in_dim.10), calls=%async_computation.1 | async-start | bytes 2621440 | tf_op jit(solution)/shard_map/all_to_all | solution.py:38
  33.9 33.0 %copy-start.5 = (s32[64]{0:T(128)S(1)}, s32[64]{0:T(128)}, u32[]{:S(2)}) copy-start(s32[64]{0:T(128)} %param.11) | copy-start | bytes 772
  33.9 43.4 %copy-start.1 = (bf16[1024,128]{1,0:T(8,128)(2,1)S(1)}, bf16[1024,128]{1,0:T(8,128)(2,1)}, u32[]{:S(2)}) copy-start(bf16[1024,128]{1,0:T(8,128)(2,1)} %refs_1_.3) | copy-start | bytes 786436
  34.1 23.8 %collective-permute-start = (bf16[576,128]{1,0:T(8,128)(2,1)S(1)}, bf16[576,128]{1,0:T(8,128)(2,1)S(1)}, u32[]{:S(2)}, u32[]{:S(2)}) collective-permute-start(bf16[576,128]{1,0:T(8,128)(2,1)S(1)} %get-tuple-element.18.refs_4_), channel_id=1, source_target_pairs={{0,64},{64,0},{128,192},{192,128},{256,320},{320,256},{384,448},{4... | collective-permute-start | bytes 442376 | tf_op jit(solution)/shard_map/ppermute | solution.py:218
  57.9 15.9 %collective-permute-start.3 = (bf16[2,576,128]{2,1,0:T(8,128)(2,1)S(1)}, bf16[2,576,128]{2,1,0:T(8,128)(2,1)}, u32[]{:S(2)}, u32[]{:S(2)}) collective-permute-start(bf16[2,576,128]{2,1,0:T(8,128)(2,1)S(1)} %pad_maximum_fusion.refs_2_), channel_id=1, source_target_pairs={{0,384},{64,448},{128,256},{192,320},{256,128},{320,192},{384,0},{... | collective-permute-start | bytes 884744 | tf_op jit(solution)/shard_map/ppermute | solution.py:219
  62.3 11.5 %collective-permute-start.2 = (bf16[2,576,128]{2,1,0:T(8,128)(2,1)S(1)}, bf16[2,576,128]{2,1,0:T(8,128)(2,1)}, u32[]{:S(2)}, u32[]{:S(2)}) collective-permute-start(bf16[2,576,128]{2,1,0:T(8,128)(2,1)S(1)} %pad_maximum_fusion.refs_2_), channel_id=1, source_target_pairs={{0,256},{64,320},{128,384},{192,448},{256,0},{320,64},{384,128},{4... | collective-permute-start | bytes 884744 | tf_op jit(solution)/shard_map/ppermute | solution.py:219
  64.8 12.6 %collective-permute-start.1 = (bf16[2,576,128]{2,1,0:T(8,128)(2,1)S(1)}, bf16[2,576,128]{2,1,0:T(8,128)(2,1)}, u32[]{:S(2)}, u32[]{:S(2)}) collective-permute-start(bf16[2,576,128]{2,1,0:T(8,128)(2,1)S(1)} %pad_maximum_fusion.refs_2_), channel_id=1, source_target_pairs={{0,128},{64,192},{128,0},{192,64},{256,384},{320,448},{384,256},{4... | collective-permute-start | bytes 884744 | tf_op jit(solution)/shard_map/ppermute | solution.py:219
  67.3 14.7 %copy-start.2 = (bf16[1024,576]{0,1:T(8,128)(2,1)S(1)}, bf16[1024,576]{0,1:T(8,128)(2,1)}, u32[]{:S(2)}) copy-start(bf16[1024,576]{0,1:T(8,128)(2,1)} %param.7) | copy-start | bytes 3538948
  114.7 2.2 %copy-start = (f32[1024,1024]{1,0:T(8,128)S(1)}, f32[1024,1024]{1,0:T(8,128)}, u32[]{:S(2)}) copy-start(f32[1024,1024]{1,0:T(8,128)} %get-tuple-element.13.e_ref) | copy-start | bytes 12582916
  136.6 33.9 %collective-permute-start.4 = (f32[64,1024]{1,0:T(8,128)S(1)}, f32[64,1024]{1,0:T(8,128)S(1)}, u32[]{:S(2)}, u32[]{:S(2)}) collective-permute-start(f32[64,1024]{1,0:T(8,128)S(1)} %reduce_sum.9.refs_0_), channel_id=1, source_target_pairs={{0,64},{64,0},{128,192},{192,128},{256,320},{320,256},{384,448},{4... | collective-permute-start | bytes 786440 | tf_op jit(solution)/shard_map/ppermute | solution.py:270
  201.7 13.7 %all-to-all-start.7 = ((f32[8,72,128]{2,1,0:T(8,128)}), f32[8,72,128]{2,1,0:T(8,128)S(1)}, u32[]{:S(2)}, u32[]{:S(2)}) async-start(f32[8,72,128]{2,1,0:T(8,128)} %shard_map.91), calls=%async_computation.7 | async-start | bytes 589824 | tf_op jit(solution)/shard_map/all_to_all | solution.py:38

commit v3 on v2

v3 whole, which is shorter than its diff:
```python
import jax
import jax.numpy as jnp
from jax import lax
from jax.experimental import pallas as pl
from jax.experimental.pallas import tpu as pltpu
from jax.sharding import PartitionSpec as P

H = 128
NX, NZH = 4, 2
NY, NZ, NC = 4, 8, 2
NYC = NY * NC
GRAD_SCALE = 8192.0
VMEM = 32 << 20

softmax_scale = 192.0 ** (-0.5)
masked_value = -1e30
f32, bf16 = jnp.float32, jnp.bfloat16


def token_at(y, z, c):
    return (y * NZ + z) * NC + c


def head_at(x, z):
    return x * NZH + z


all_y, all_z, all_c = range(NY), range(NZ), range(NC)
groups_z = [[token_at(y, z, c) for z in all_z] for y in all_y for c in all_c]
groups_z4 = [
    [token_at(y, half + z, c) for z in range(4)] for half in (0, 4) for y in all_y for c in all_c
]
groups_y = [[token_at(y, z, c) for y in all_y] for z in all_z for c in all_c]
groups_yc = [[token_at(y, z, c) for c in all_c for y in all_y] for z in all_z]
pairs_c = [(token_at(y, z, c), token_at(y, z, 1 - c)) for y in all_y for z in all_z for c in all_c]
pairs_z4 = [(token_at(y, z, c), token_at(y, z ^ 4, c)) for y in all_y for z in all_z for c in all_c]
groups_x = [[head_at(x, z) for x in range(NX)] for z in range(NZH)]
pairs_zh = [(head_at(x, z), head_at(x, 1 - z)) for x in range(NX) for z in range(NZH)]


def pairs_x(flip):
    return [(head_at(x, z), head_at(x ^ flip, z)) for x in range(NX) for z in range(NZH)]


def exchanged(parts, axis, groups):
    return lax.all_to_all(parts, axis, 0, 0, tiled=True, axis_index_groups=groups)


def gathered(value, axis, groups):
    copies = jnp.broadcast_to(value[None], (len(groups[0]), *value.shape))
    return exchanged(copies, axis, groups)


def diagonal(rows, lanes):
    return lax.broadcasted_iota(jnp.int32, (rows, lanes), 0) == lax.broadcasted_iota(
        jnp.int32, (rows, lanes), 1
    )


def as_row(column, lanes=128):
    return jnp.sum(jnp.where(diagonal(column.shape[0], lanes), column, 0.0), axis=0, keepdims=True)


def as_column(row, rows):
    return jnp.sum(jnp.where(diagonal(rows, row.shape[1]), row, 0.0), axis=1, keepdims=True)


def call(kernel, out_shape, flops=0, moved=0):
    return pl.pallas_call(
        kernel,
        out_shape=out_shape,
        compiler_params=pltpu.CompilerParams(vmem_limit_bytes=VMEM),
        cost_estimate=pl.CostEstimate(flops=flops, bytes_accessed=moved, transcendentals=0),
    )


def score_kernel(heads, limit_ref, q_ref, k_ref, e_ref, m_ref, l_ref):
    rows, keys = e_ref.shape
    block = rows // NY
    key = lax.broadcasted_iota(jnp.int32, (1, keys), 1)
    k = k_ref[...]
    for y in range(NY):
        lines = slice(y * block, (y + 1) * block)
        s = jnp.dot(q_ref[lines], k, preferred_element_type=f32) * softmax_scale
        s = jnp.where(key <= limit_ref[lines], s, masked_value)
        m = jnp.max(s, axis=1, keepdims=True)
        e = jnp.exp(s - m)
        e_ref[lines] = e
        m_ref[y : y + 1] = as_row(m)
        l_ref[y : y + 1] = as_row(jnp.sum(e, axis=1, keepdims=True))


def message_parts(ref, tokens, heads):
    block = ref[tokens * heads :, :].astype(f32)
    w = block[:, :heads] + block[:, heads : 2 * heads] + block[:, 2 * heads : 3 * heads]
    return ref[: tokens * heads, :], w


def index_dot(iq, ik):
    return lax.dot_general(iq, ik, (((1,), (1,)), ((), ())), preferred_element_type=f32)


def logits_kernel(heads, scale, message_ref, ik_ref, out_ref):
    tokens = out_ref.shape[0]
    iq, w = message_parts(message_ref, tokens, heads)
    active = index_dot(iq, ik_ref[...])
    logits = jnp.zeros(out_ref.shape, f32)
    for j in range(heads):
        here = active[j * tokens : (j + 1) * tokens] * scale
        logits = logits + w[:, j : j + 1] * jnp.maximum(here, 0.0)
    out_ref[...] = logits


def index_stats_kernel(limit_ref, one_ref, two_ref, logits_ref, stat_ref):
    key = lax.broadcasted_iota(jnp.int32, (1, logits_ref.shape[1]), 1)
    logits = jnp.where(key <= limit_ref[...], one_ref[...] + two_ref[...], masked_value)
    m = jnp.max(logits, axis=1, keepdims=True)
    l = jnp.sum(jnp.exp(logits - m), axis=1, keepdims=True)
    logits_ref[...] = logits
    stat_ref[...] = jnp.concatenate([as_row(m), as_row(l), jnp.zeros((6, 128), f32)], axis=0)


def joined(stats):
    def one(m, l):
        top = jnp.max(m, axis=0)
        return top, jnp.sum(l * jnp.exp(m - top), axis=0)

    return (*one(stats[:, 0:8], stats[:, 8:16]), *one(stats[:, 16:17], stats[:, 17:18]))


def join_kernel(stats_ref, out_ref):
    lines = jnp.concatenate([*joined(stats_ref[...]), jnp.zeros((6, 128), f32)], axis=0)
    out_ref[...] = jnp.broadcast_to(lines[None], out_ref.shape)


def target_kernel(core_ref, stats_ref, m_ref, own_ref, other_ref, out_ref):
    stats = stats_ref[...]
    top, total, _, _ = joined(stats)
    weights = jnp.exp(m_ref[...] - top) / total
    keys = out_ref.shape[1]
    half = out_ref.shape[0] // NC
    block = own_ref.shape[0] // NY
    own = core_ref[0]
    for y in range(NY):
        for core, e_ref in ((own, own_ref), (1 - own, other_ref)):
            row = jnp.where(core == 0, weights[y : y + 1], weights[NY + y : NY + y + 1])
            e = e_ref[y * block : (y + 1) * block] * as_column(row, block)
            part = jnp.sum(e.reshape(NZ, block // NZ, keys), axis=1)
            out_ref[pl.ds(pl.multiple_of(core * half + y * NZ, NZ), NZ), :] = part


def dlogit_kernel(one_ref, two_ref, logits_ref, stats_ref, out_ref):
    rows = logits_ref.shape[0]
    _, _, top, total = joined(stats_ref[...])
    probs = jnp.exp(logits_ref[...] - as_column(top, rows)) / as_column(total, rows)
    dlogit = GRAD_SCALE * (probs - (one_ref[...] + two_ref[...]) / H)
    out_ref[...] = jnp.broadcast_to(dlogit[None], out_ref.shape)


def grad_kernel(heads, scale, d_ref, message_ref, ik_ref, out_ref):
    dlogit = d_ref[...]
    tokens = dlogit.shape[0]
    iq, w = message_parts(message_ref, tokens, heads)
    ik = ik_ref[...]
    active = index_dot(iq, ik)
    row = lax.broadcasted_iota(jnp.int32, (tokens, 128), 0)
    place = row // NZ % NY * (NC * NZ) + row % NZ * NC + row // (NY * NZ)
    places = place == lax.broadcasted_iota(jnp.int32, (tokens, 128), 1)
    out_ref[tokens * heads :, :] = jnp.zeros((out_ref.shape[0] - tokens * heads, 128), f32)
    for j in range(heads):
        here = active[j * tokens : (j + 1) * tokens]
        gate = jnp.where(here > 0.0, dlogit * w[:, j : j + 1], 0.0).astype(bf16)
        grad = jnp.dot(gate, ik, preferred_element_type=f32) * scale
        for b in range(NYC):
            first = b % NY * (NZ * NC) + b // NY
            lines = pl.ds(first * heads + j, NZ, stride=NC * heads)
            out_ref[lines, :] = grad[b * NZ : (b + 1) * NZ]
        weight_grad = jnp.sum(dlogit * jnp.maximum(here * scale, 0.0), axis=1, keepdims=True)
        out_ref[tokens * heads + j : tokens * heads + j + 1, :] = jnp.sum(
            jnp.where(places, weight_grad, 0.0), axis=0, keepdims=True
        )


def key_kernel(heads, scale, d_ref, ik_ref, *refs):
    messages, out_ref = refs[:-1], refs[-1]
    dlogit, ik = d_ref[...], ik_ref[...]
    tokens, keys = dlogit.shape
    total = jnp.zeros((ik.shape[1], keys), f32)
    for message in messages:
        for part in range(message.shape[0]):
            iq, w = message_parts(message.at[part], tokens, heads)
            active = index_dot(iq, ik)
            gates = []
            for j in range(heads):
                here = active[j * tokens : (j + 1) * tokens]
                gates.append(jnp.where(here > 0.0, dlogit * w[:, j : j + 1], 0.0).astype(bf16))
            gate = jnp.concatenate(gates, axis=0)
            total = total + jnp.dot(iq.T, gate, preferred_element_type=f32)
    out_ref[...] = total.T * scale


def sum_kernel(parts_ref, out_ref):
    out_ref[...] = jnp.broadcast_to(jnp.sum(parts_ref[...], axis=0)[None], out_ref.shape)


def pair_kernel(one_ref, two_ref, out_ref):
    out_ref[...] = jnp.broadcast_to((one_ref[...] + two_ref[...])[None], out_ref.shape)


def in_order(value):
    return jnp.moveaxis(value.reshape(NY, NZ, NC, *value.shape[1:]), 2, 0).reshape(value.shape)


def x_scatter_sum(parts, x):
    total = lax.dynamic_index_in_dim(parts, x, 0, keepdims=False)
    for flip in range(1, NX):
        piece = lax.dynamic_index_in_dim(parts, x ^ flip, 0, keepdims=False)
        total = total + lax.ppermute(piece, "heads", pairs_x(flip))
    return total


def local(queries, latent_keys, index_queries, index_keys, index_weights, positions):
    heads_here, width = queries.shape[0], queries.shape[2]
    key_count = latent_keys.shape[0]
    query_count, index_heads, index_width = index_queries.shape
    index_scale = index_width ** (-0.5)
    share_rows = query_count // NX
    shape = jax.ShapeDtypeStruct
    x = lax.axis_index("heads") // NZH
    core = lax.axis_index("tokens") % NC
    limit = in_order(positions - lax.axis_index("tokens") * key_count)

    along_z = gathered(queries.reshape(heads_here, width), "tokens", groups_z)

    high = lax.reduce_precision(index_weights, 8, 7)
    middle = lax.reduce_precision(index_weights - high, 8, 7)
    low = index_weights - high - middle
    lines = in_order(jnp.concatenate([high, middle, low], axis=1))
    lines = jnp.pad(lines, ((0, 0), (0, 128 - 3 * index_heads)))
    by_head = in_order(index_queries).transpose(1, 0, 2)
    by_head = by_head.reshape(index_heads * query_count, index_width)
    mine = jnp.concatenate([by_head, lines.astype(bf16)])

    index_flops = 2 * query_count * index_heads * key_count * index_width
    partial = call(
        lambda *refs: logits_kernel(index_heads, index_scale, *refs),
        shape((query_count, key_count), f32),
        flops=index_flops,
        moved=1 << 20,
    )(mine, index_keys)
    along_z, partial = lax.optimization_barrier((along_z, partial))
    over_x = x_scatter_sum(partial.reshape(NX, share_rows, key_count), x)
    other = lax.ppermute(over_x, "heads", pairs_zh)
    share_limit = lax.dynamic_slice_in_dim(limit, x * share_rows, share_rows, 0)
    logits, index_stats = call(
        index_stats_kernel,
        (shape((share_rows, key_count), f32), shape((8, 128), f32)),
    )(share_limit[:, None], over_x, other)

    own_rows = gathered(along_z, "tokens", groups_y)
    other_rows = lax.ppermute(own_rows, "tokens", pairs_c)
    row_limit = jnp.repeat(limit.reshape(NC, -1), heads_here, axis=1)[:, :, None]
    row_count = row_limit.shape[1]
    score = call(
        lambda *refs: score_kernel(heads_here, *refs),
        (
            shape((row_count, key_count), f32),
            shape((NY, row_count // NY), f32),
            shape((NY, row_count // NY), f32),
        ),
        flops=2 * row_count * key_count * width,
        moved=4 << 20,
    )
    keys_t = latent_keys.T
    first_limit = jnp.where(core == 0, row_limit[0], row_limit[1])
    second_limit = jnp.where(core == 0, row_limit[1], row_limit[0])
    own_e, own_max, own_total = score(first_limit, own_rows.reshape(-1, width), keys_t)
    other_e, other_max, other_total = score(second_limit, other_rows.reshape(-1, width), keys_t)

    def by_core(own, other):
        return jnp.where(core == 0, jnp.concatenate([own, other]), jnp.concatenate([other, own]))

    local_max = by_core(own_max, other_max)
    stats = jnp.concatenate([local_max, by_core(own_total, other_total), index_stats])
    stats, mine = lax.optimization_barrier((stats, mine))
    pair = jnp.stack([mine, lax.ppermute(mine, "heads", pairs_zh)])
    stats = gathered(stats, "tokens", groups_z)
    stats = call(join_kernel, shape((NYC, *stats.shape[1:]), f32))(stats)
    stats = exchanged(stats, "tokens", groups_yc)

    partial = call(target_kernel, shape((query_count, key_count), f32), moved=5 << 20)(
        core.reshape(1), stats, local_max, own_e, other_e
    )
    partial, pair = lax.optimization_barrier((partial, pair))
    messages = [pair] + [lax.ppermute(pair, "heads", pairs_x(flip)) for flip in range(1, NX)]
    over_x = exchanged(partial.reshape(NX, share_rows, key_count), "heads", groups_x).sum(axis=0)
    other = lax.ppermute(over_x, "heads", pairs_zh)
    dlogit = call(dlogit_kernel, shape((NX, share_rows, key_count), f32))(
        over_x, other, logits, stats
    )
    dlogit = exchanged(dlogit, "heads", groups_x).reshape(query_count, key_count)

    query_lines = query_count * index_heads
    piece_rows = -(-(query_lines + index_heads) // (NYC * 8)) * 8
    both = call(
        lambda *refs: grad_kernel(index_heads, index_scale, *refs),
        shape((piece_rows * NYC, 128), f32),
        flops=2 * index_flops,
        moved=2 << 20,
    )(dlogit, mine, index_keys)

    piece = exchanged(both.reshape(NYC, piece_rows, 128), "tokens", groups_yc)
    piece = call(sum_kernel, shape((NZ // 2, piece_rows, 128), f32))(piece)
    piece = exchanged(piece, "tokens", groups_z4).sum(axis=0)
    other = lax.ppermute(piece, "tokens", pairs_z4)
    piece = call(pair_kernel, shape((NYC, piece_rows, 128), f32))(piece, other)
    both = exchanged(piece, "tokens", groups_yc).reshape(-1, 128)
    query_grad = both[:query_lines].reshape(query_count, index_heads, index_width)
    weight_grad = both[query_lines : query_lines + index_heads, :query_count].T

    key_grad = call(
        lambda *refs: key_kernel(index_heads, index_scale, *refs),
        shape((key_count, index_width), f32),
        flops=2 * index_flops * NX * NZH,
        moved=3 << 20,
    )(dlogit, index_keys, *messages)
    return (query_grad, weight_grad, key_grad)


def solution(mesh):
    placed = (
        P("heads", "tokens", None),
        P("tokens", None),
        P(None, "heads", None),
        P("tokens", None),
        P(None, "heads"),
        P(),
    )
    return jax.shard_map(
        local,
        mesh=mesh,
        in_specs=placed,
        out_specs=(P(None, "heads", None), P(None, "heads"), P("tokens", None)),
        check_vma=False,
    )
```

time: 217 us -> 202 us (0.931)
  blocking collectives: 96.8 us -> 29.9 us
  starting transfers between devices: 40 us -> 103 us
  waiting for transfers between devices: 52.3 us -> 39.7 us
  Pallas kernels: 20.6 us -> 13.2 us
  local copies, waits for them, and re-layouts: 5.96 us -> 12.8 us
    all_to_all x6 -> x3, blocking collectives: 96.8 us -> 29.9 us  [exchanged(): lax.all_to_all(parts, axis, 0, 0, tiled=True, axis_index_groups=groups)]
    all_to_all x2 -> x6, starting transfers between devices: 14.6 us -> 44.7 us  [exchanged(): lax.all_to_all(parts, axis, 0, 0, tiled=True, axis_index_groups=groups)]
    ppermute x0 -> x5, starting transfers between devices: none -> 22.7 us  [the longest x3 9.4 us: x_scatter_sum(): total = total + lax.ppermute(piece, 'heads', pairs_x(flip))]
    all_to_all x2 -> x6, waiting for transfers between devices: 0.98 us -> 21.9 us  [exchanged(): lax.all_to_all(parts, axis, 0, 0, tiled=True, axis_index_groups=groups)]
    ppermute x1, waiting for transfers between devices: 15.8 us -> 0.01 us  [local(): pair = jnp.stack([mine, lax.ppermute(mine, 'heads', pairs_zh)])]
    ppermute x1 -> x2, waiting for transfers between devices: 25.5 us -> 12.5 us  [local(): other = lax.ppermute(over_x, 'heads', pairs_zh)]
    ppermute x3, waiting for transfers between devices: 9.99 us -> 0.01 us  [local(): lax.ppermute(pair, 'heads', pairs_x(flip))]
    pallas_call x6 -> x9, Pallas kernels: 14.7 us -> 7.78 us  [the longest x1 2.42 us: local(): score(second_limit, other_rows.reshape(-1, width), keys_t)]
  transfers between devices with their start and end apart: 7 -> 17, of which waited for: 5 -> 8; matrix products, arithmetic and copies ran while one was open for 0% -> 2% of each run, Pallas kernels for 5% -> 4%
where the time goes in v3:
time: 202 us; the launch traced here: 201 us
  starting transfers between devices  103 us (51%)
  waiting for transfers between devices  39.7 us (20%)
  blocking collectives  29.9 us (15%)
  Pallas kernels  13.2 us (7%)
  local copies, waits for them, and re-layouts  12.8 us (6%)
    all_to_all x6, starting transfers between devices, exchanged(): lax.all_to_all(parts, axis, 0, 0, tiled=True, axis_index_groups=groups)  44.7 us
    all_to_all x3, blocking collectives, exchanged(): lax.all_to_all(parts, axis, 0, 0, tiled=True, axis_index_groups=groups)  29.9 us
    all_to_all x6, waiting for transfers between devices, exchanged(): lax.all_to_all(parts, axis, 0, 0, tiled=True, axis_index_groups=groups)  21.9 us
    ppermute x2, starting transfers between devices, local(): other = lax.ppermute(over_x, 'heads', pairs_zh)  14.5 us
    ppermute x2, waiting for transfers between devices, local(): other = lax.ppermute(over_x, 'heads', pairs_zh)  12.5 us
    ppermute x1, starting transfers between devices, local(): pair = jnp.stack([mine, lax.ppermute(mine, 'heads', pairs_zh)])  12.1 us
    ppermute x3, starting transfers between devices, x_scatter_sum(): total = total + lax.ppermute(piece, 'heads', pairs_x(flip))  9.4 us
    ppermute x3, starting transfers between devices, local(): lax.ppermute(pair, 'heads', pairs_x(flip))  8.97 us
  transfers between devices with their start and end apart: 17, of which 8 were waited for; matrix products, arithmetic and copies ran while one was open for 2% of the time, Pallas kernels for 4%

profile of v3, /device:TPU:1, one launch (start us, length us, event | category | flops | bytes accessed | tf_op | source)
XLA Modules:
  0.0 200.6 jit_solution(262087255331269218)
XLA Ops:
  0.6 1.4 broadcast_in_dim.29
  2.1 13.1 %all-to-all-start = ((bf16[8,16,576]{2,1,0:T(8,128)(2,1)}), bf16[8,16,576]{2,1,0:T(8,128)(2,1)S(1)}, u32[]{:S(2)}, u32[]{:S(2)}) async-start(bf16[8,16,576]{2,1,0:T(8,128)(2,1)} %broadcast_in_dim.29), calls=%async_computation | async-start | bytes 327680 | tf_op jit(solution)/shard_map/all_to_all | solution.py:46
  18.3 7.5 %all-to-all-done = bf16[8,16,576]{2,1,0:T(8,128)(2,1)S(1)} async-done(((bf16[8,16,576]{2,1,0:T(8,128)(2,1)}), bf16[8,16,576]{2,1,0:T(8,128)(2,1)S(1)}, u32[]{:S(2)}, u32[]{:S(2)}) %all-to-all-start) | async-done | bytes 147488 | tf_op jit(solution)/shard_map/all_to_all | solution.py:46
  26.7 4.2 %all-to-all-start.1 = ((bf16[4,8,16,576]{3,2,1,0:T(8,128)(2,1)}), bf16[4,8,16,576]{3,2,1,0:T(8,128)(2,1)S(1)}, u32[]{:S(2)}, u32[]{:S(2)}) async-start(bf16[4,8,16,576]{3,2,1,0:T(8,128)(2,1)} %broadcast_in_dim.30), calls=%async_computation.1 | async-start | bytes 1310720 | tf_op jit(solution)/shard_map/all_to_all | solution.py:46
  31.2 7.3 %all-to-all-done.1 = bf16[4,8,16,576]{3,2,1,0:T(8,128)(2,1)S(1)} async-done(((bf16[4,8,16,576]{3,2,1,0:T(8,128)(2,1)}), bf16[4,8,16,576]{3,2,1,0:T(8,128)(2,1)S(1)}, u32[]{:S(2)}, u32[]{:S(2)}) %all-to-all-start.1) | async-done | bytes 589856 | tf_op jit(solution)/shard_map/all_to_all | solution.py:46
  38.5 6.5 %collective-permute-start = (bf16[4,8,16,576]{3,2,1,0:T(8,128)(2,1)S(1)}, bf16[4,8,16,576]{3,2,1,0:T(8,128)(2,1)}, u32[]{:S(2)}, u32[]{:S(2)}) collective-permute-start(bf16[4,8,16,576]{3,2,1,0:T(8,128)(2,1)S(1)} %all-to-all-done.1), channel_id=1, source_target_pairs={{0,1},{1,0},{2,3},{3,2},{4,5},{5,4},{6,7},{7,6},{8,9},{9,8},{10,11... | collective-permute-start | bytes 1769480 | tf_op jit(solution)/shard_map/ppermute | solution.py:261
  45.1 3.1 %collective-permute-start.1 = (f32[16,1024]{1,0:T(8,128)S(1)}, f32[16,1024]{1,0:T(8,128)S(1)}, u32[]{:S(2)}, u32[]{:S(2)}) collective-permute-start(f32[16,1024]{1,0:T(8,128)S(1)} %get-tuple-element.33), channel_id=1, source_target_pairs={{0,128},{64,192},{128,0},{192,64},{256,384},{320,448},{384,256},{4... | collective-permute-start | bytes 196616 | tf_op jit(solution)/shard_map/ppermute | solution.py:218
  48.2 3.7 %collective-permute-start.3 = (f32[16,1024]{1,0:T(8,128)S(1)}, f32[16,1024]{1,0:T(8,128)S(1)}, u32[]{:S(2)}, u32[]{:S(2)}) collective-permute-start(f32[16,1024]{1,0:T(8,128)S(1)} %get-tuple-element.34), channel_id=1, source_target_pairs={{0,384},{64,448},{128,256},{192,320},{256,128},{320,192},{384,0},{... | collective-permute-start | bytes 196616 | tf_op jit(solution)/shard_map/ppermute | solution.py:218
  51.9 2.6 %collective-permute-start.2 = (f32[16,1024]{1,0:T(8,128)S(1)}, f32[16,1024]{1,0:T(8,128)S(1)}, u32[]{:S(2)}, u32[]{:S(2)}) collective-permute-start(f32[16,1024]{1,0:T(8,128)S(1)} %get-tuple-element.35), channel_id=1, source_target_pairs={{0,256},{64,320},{128,384},{192,448},{256,0},{320,64},{384,128},{4... | collective-permute-start | bytes 196616 | tf_op jit(solution)/shard_map/ppermute | solution.py:218
  55.0 3.5 %collective-permute-done.2 = f32[16,1024]{1,0:T(8,128)S(1)} collective-permute-done((f32[16,1024]{1,0:T(8,128)S(1)}, f32[16,1024]{1,0:T(8,128)S(1)}, u32[]{:S(2)}, u32[]{:S(2)}) %collective-permute-start.2) | collective-permute-done | bytes 65568 | tf_op jit(solution)/shard_map/ppermute | solution.py:218
  58.5 7.9 %collective-permute-start.4 = (f32[16,1024]{1,0:T(8,128)S(1)}, f32[16,1024]{1,0:T(8,128)S(1)}, u32[]{:S(2)}, u32[]{:S(2)}) collective-permute-start(f32[16,1024]{1,0:T(8,128)S(1)} %fusion.3.one_ref), channel_id=1, source_target_pairs={{0,64},{64,0},{128,192},{192,128},{256,320},{320,256},{384,448},{4... | collective-permute-start | bytes 196616 | tf_op jit(solution)/shard_map/ppermute | solution.py:253
  67.0 5.2 %collective-permute-done.4.two_ref = f32[16,1024]{1,0:T(8,128)S(1)} collective-permute-done((f32[16,1024]{1,0:T(8,128)S(1)}, f32[16,1024]{1,0:T(8,128)S(1)}, u32[]{:S(2)}, u32[]{:S(2)}) %collective-permute-start.4) | collective-permute-done | bytes 65568 | tf_op jit(solution)/shard_map/ppermute | solution.py:253
  76.4 2.4 %shard_map.87 = (f32[512,1024]{1,0:T(8,128)S(1)}, f32[4,128]{1,0:T(4,128)S(1)}, f32[4,128]{1,0:T(4,128)S(1)}) custom-call(s32[512,1]{1,0:T(8,128)S(1)} %select_n.77.refs_0_, bf16[512,576]{1,0:T(8,128)(2,1)} %bitcast.13.refs_1_, bf16[576,1024]{1,0:T(8,128)(2,1)S(1)} %bitcast.52), custom_call_target="tpu_custom_call" | custom-call | flops 603979776 | bytes 4194304 | tf_op jit(solution)/shard_map/pallas_call | solution.py:278
  80.8 6.5 %all-to-all-start.2 = ((f32[8,24,128]{2,1,0:T(8,128)}), f32[8,24,128]{2,1,0:T(8,128)S(1)}, u32[]{:S(2)}, u32[]{:S(2)}) async-start(f32[8,24,128]{2,1,0:T(8,128)} %broadcast_in_dim.33), calls=%async_computation.2 | async-start | bytes 196608 | tf_op jit(solution)/shard_map/all_to_all | solution.py:46
  87.3 12.1 %collective-permute-start.5 = (bf16[576,128]{1,0:T(8,128)(2,1)S(1)}, bf16[576,128]{1,0:T(8,128)(2,1)S(1)}, u32[]{:S(2)}, u32[]{:S(2)}) collective-permute-start(bf16[576,128]{1,0:T(8,128)(2,1)S(1)} %fusion.1.refs_0_.refs_1_), channel_id=1, source_target_pairs={{0,64},{64,0},{128,192},{192,128},{256,320},{320,256},{384,448},{4... | collective-permute-start | bytes 442376 | tf_op jit(solution)/shard_map/ppermute | solution.py:286
  100.1 10.5 %all-to-all-start.3 = ((f32[8,24,128]{2,1,0:T(8,128)}), f32[8,24,128]{2,1,0:T(8,128)S(1)}, u32[]{:S(2)}, u32[]{:S(2)}) async-start(f32[8,24,128]{2,1,0:T(8,128)} %shard_map.89), calls=%async_computation.3 | async-start | bytes 196608 | tf_op jit(solution)/shard_map/all_to_all | solution.py:46
  110.6 5.0 %all-to-all-done.3.stats_ref = f32[8,24,128]{2,1,0:T(8,128)S(1)} async-done(((f32[8,24,128]{2,1,0:T(8,128)}), f32[8,24,128]{2,1,0:T(8,128)S(1)}, u32[]{:S(2)}, u32[]{:S(2)}) %all-to-all-start.3) | async-done | bytes 98336 | tf_op jit(solution)/shard_map/all_to_all | solution.py:46
  115.6 1.6 copy-done.1
  118.0 8.8 %all_to_all.45 = f32[4,16,1024]{2,1,0:T(8,128)S(1)} all-to-all(f32[4,16,1024]{2,1,0:T(8,128)S(1)} %bitcast.44), channel_id=1, replica_groups={{0,128,256,384},{64,192,320,448},{1,129,257,385},{65,193,321,449},{2,13..., dimensions={0} | all-to-all | bytes 524288 | tf_op jit(solution)/shard_map/all_to_all | solution.py:46
  126.8 6.5 %collective-permute-start.6 = (f32[16,1024]{1,0:T(8,128)S(1)}, f32[16,1024]{1,0:T(8,128)S(1)}, u32[]{:S(2)}, u32[]{:S(2)}) collective-permute-start(f32[16,1024]{1,0:T(8,128)S(1)} %reduce_sum.18.one_ref), channel_id=1, source_target_pairs={{0,64},{64,0},{128,192},{192,128},{256,320},{320,256},{384,448},{4... | collective-permute-start | bytes 196616 | tf_op jit(solution)/shard_map/ppermute | solution.py:297
  133.3 7.2 %collective-permute-done.6.two_ref = f32[16,1024]{1,0:T(8,128)S(1)} collective-permute-done((f32[16,1024]{1,0:T(8,128)S(1)}, f32[16,1024]{1,0:T(8,128)S(1)}, u32[]{:S(2)}, u32[]{:S(2)}) %collective-permute-start.6) | collective-permute-done | bytes 65568 | tf_op jit(solution)/shard_map/ppermute | solution.py:297
  140.7 7.9 %all_to_all.46 = f32[4,16,1024]{2,1,0:T(8,128)S(1)} all-to-all(f32[4,16,1024]{2,1,0:T(8,128)S(1)} %shard_map.91), channel_id=1, replica_groups={{0,128,256,384},{64,192,320,448},{1,129,257,385},{65,193,321,449},{2,13..., dimensions={0} | all-to-all | bytes 524288 | tf_op jit(solution)/shard_map/all_to_all | solution.py:46
  149.7 13.2 %all_to_all.47.parts_ref = f32[8,72,128]{2,1,0:T(8,128)S(1)} all-to-all(f32[8,72,128]{2,1,0:T(8,128)S(1)} %bitcast.48), channel_id=1, replica_groups={{0,16,32,48,1,17,33,49},{2,18,34,50,3,19,35,51},{4,20,36,52,5,21,37,53}..., dimensions={0} | all-to-all | bytes 589824 | tf_op jit(solution)/shard_map/all_to_all | solution.py:46
  163.5 3.8 %all-to-all-start.7 = ((f32[4,72,128]{2,1,0:T(8,128)}), f32[4,72,128]{2,1,0:T(8,128)S(1)}, u32[]{:S(2)}, u32[]{:S(2)}) async-start(f32[4,72,128]{2,1,0:T(8,128)} %shard_map.93), calls=%async_computation.7 | async-start | bytes 294912 | tf_op jit(solution)/shard_map/all_to_all | solution.py:46
  167.4 2.8 %collective-permute-start.10 = (bf16[2,576,128]{2,1,0:T(8,128)(2,1)S(1)}, bf16[2,576,128]{2,1,0:T(8,128)(2,1)S(1)}, u32[]{:S(2)}, u32[]{:S(2)}) collective-permute-start(bf16[2,576,128]{2,1,0:T(8,128)(2,1)S(1)} %pad_maximum_fusion.refs_2_), channel_id=1, source_target_pairs={{0,384},{64,448},{128,256},{192,320},{256,128},{320,192},{384,0},{... | collective-permute-start | bytes 884744 | tf_op jit(solution)/shard_map/ppermute | solution.py:295
  170.2 3.1 %collective-permute-start.9 = (bf16[2,576,128]{2,1,0:T(8,128)(2,1)S(1)}, bf16[2,576,128]{2,1,0:T(8,128)(2,1)S(1)}, u32[]{:S(2)}, u32[]{:S(2)}) collective-permute-start(bf16[2,576,128]{2,1,0:T(8,128)(2,1)S(1)} %pad_maximum_fusion.refs_2_), channel_id=1, source_target_pairs={{0,256},{64,320},{128,384},{192,448},{256,0},{320,64},{384,128},{4... | collective-permute-start | bytes 884744 | tf_op jit(solution)/shard_map/ppermute | solution.py:295
  173.3 3.1 %collective-permute-start.8 = (bf16[2,576,128]{2,1,0:T(8,128)(2,1)S(1)}, bf16[2,576,128]{2,1,0:T(8,128)(2,1)S(1)}, u32[]{:S(2)}, u32[]{:S(2)}) collective-permute-start(bf16[2,576,128]{2,1,0:T(8,128)(2,1)S(1)} %pad_maximum_fusion.refs_2_), channel_id=1, source_target_pairs={{0,128},{64,192},{128,0},{192,64},{256,384},{320,448},{384,256},{4... | collective-permute-start | bytes 884744 | tf_op jit(solution)/shard_map/ppermute | solution.py:295
  176.4 6.8 %collective-permute-start.7 = (f32[72,128]{1,0:T(8,128)S(1)}, f32[72,128]{1,0:T(8,128)S(1)}, u32[]{:S(2)}, u32[]{:S(2)}) collective-permute-start(f32[72,128]{1,0:T(8,128)S(1)} %reduce_sum.19.one_ref), channel_id=1, source_target_pairs={{0,8},{1,9},{2,10},{3,11},{4,12},{5,13},{6,14},{7,15},{8,0},{9,1},... | collective-permute-start | bytes 110600 | tf_op jit(solution)/shard_map/ppermute | solution.py:315
  183.2 1.8 collective-permute-done.7.two_ref
  185.7 6.6 %all-to-all-start.8 = ((f32[8,72,128]{2,1,0:T(8,128)}), f32[8,72,128]{2,1,0:T(8,128)S(1)}, u32[]{:S(2)}, u32[]{:S(2)}) async-start(f32[8,72,128]{2,1,0:T(8,128)} %shard_map.94), calls=%async_computation.8 | async-start | bytes 589824 | tf_op jit(solution)/shard_map/all_to_all | solution.py:46
  192.4 4.7 %shard_map.95 = f32[1024,128]{1,0:T(8,128)} custom-call(f32[64,1024]{1,0:T(8,128)S(1)} %bitcast.50, bf16[1024,128]{1,0:T(8,128)(2,1)S(1)} %copy-done.3, bf16[2,576,128]{2,1,0:T(8,128)(2,1)S(1)} %pad_maximum_fusion.refs_2_, bf16[2,576,128]{2,1,0:T(8,128)(2,1)S(1)} %collective-permute-done.8.refs_3_, bf16[2,576,128]{2,1,0:T(8,128)(2,1)S(1)} %collective-permute-done.9.refs_4_, ...), custom_call_target="tpu_custom_call" | custom-call | flops 2147483648 | bytes 3145728 | tf_op jit(solution)/shard_map/pallas_call | solution.py:321
  197.1 2.2 %all-to-all-done.8 = f32[8,72,128]{2,1,0:T(8,128)S(1)} async-done(((f32[8,72,128]{2,1,0:T(8,128)}), f32[8,72,128]{2,1,0:T(8,128)S(1)}, u32[]{:S(2)}, u32[]{:S(2)}) %all-to-all-start.8) | async-done | bytes 294944 | tf_op jit(solution)/shard_map/all_to_all | solution.py:46
  (61 shorter events, 17.0 us)
Async XLA Ops:
  0.6 30.2 %copy-start.6 = (s32[64]{0:T(128)S(1)}, s32[64]{0:T(128)}, u32[]{:S(2)}) copy-start(s32[64]{0:T(128)} %param.11) | copy-start | bytes 772
  2.1 23.7 %all-to-all-start = ((bf16[8,16,576]{2,1,0:T(8,128)(2,1)}), bf16[8,16,576]{2,1,0:T(8,128)(2,1)S(1)}, u32[]{:S(2)}, u32[]{:S(2)}) async-start(bf16[8,16,576]{2,1,0:T(8,128)(2,1)} %broadcast_in_dim.29), calls=%async_computation | async-start | bytes 327680 | tf_op jit(solution)/shard_map/all_to_all | solution.py:46
  16.9 1.0 copy-start.2
  26.7 11.8 %all-to-all-start.1 = ((bf16[4,8,16,576]{3,2,1,0:T(8,128)(2,1)}), bf16[4,8,16,576]{3,2,1,0:T(8,128)(2,1)S(1)}, u32[]{:S(2)}, u32[]{:S(2)}) async-start(bf16[4,8,16,576]{3,2,1,0:T(8,128)(2,1)} %broadcast_in_dim.30), calls=%async_computation.1 | async-start | bytes 1310720 | tf_op jit(solution)/shard_map/all_to_all | solution.py:46
  38.5 36.6 %collective-permute-start = (bf16[4,8,16,576]{3,2,1,0:T(8,128)(2,1)S(1)}, bf16[4,8,16,576]{3,2,1,0:T(8,128)(2,1)}, u32[]{:S(2)}, u32[]{:S(2)}) collective-permute-start(bf16[4,8,16,576]{3,2,1,0:T(8,128)(2,1)S(1)} %all-to-all-done.1), channel_id=1, source_target_pairs={{0,1},{1,0},{2,3},{3,2},{4,5},{5,4},{6,7},{7,6},{8,9},{9,8},{10,11... | collective-permute-start | bytes 1769480 | tf_op jit(solution)/shard_map/ppermute | solution.py:261
  45.1 9.9 %collective-permute-start.1 = (f32[16,1024]{1,0:T(8,128)S(1)}, f32[16,1024]{1,0:T(8,128)S(1)}, u32[]{:S(2)}, u32[]{:S(2)}) collective-permute-start(f32[16,1024]{1,0:T(8,128)S(1)} %get-tuple-element.33), channel_id=1, source_target_pairs={{0,128},{64,192},{128,0},{192,64},{256,384},{320,448},{384,256},{4... | collective-permute-start | bytes 196616 | tf_op jit(solution)/shard_map/ppermute | solution.py:218
  48.2 6.8 %collective-permute-start.3 = (f32[16,1024]{1,0:T(8,128)S(1)}, f32[16,1024]{1,0:T(8,128)S(1)}, u32[]{:S(2)}, u32[]{:S(2)}) collective-permute-start(f32[16,1024]{1,0:T(8,128)S(1)} %get-tuple-element.34), channel_id=1, source_target_pairs={{0,384},{64,448},{128,256},{192,320},{256,128},{320,192},{384,0},{... | collective-permute-start | bytes 196616 | tf_op jit(solution)/shard_map/ppermute | solution.py:218
  51.9 6.5 %collective-permute-start.2 = (f32[16,1024]{1,0:T(8,128)S(1)}, f32[16,1024]{1,0:T(8,128)S(1)}, u32[]{:S(2)}, u32[]{:S(2)}) collective-permute-start(f32[16,1024]{1,0:T(8,128)S(1)} %get-tuple-element.35), channel_id=1, source_target_pairs={{0,256},{64,320},{128,384},{192,448},{256,0},{320,64},{384,128},{4... | collective-permute-start | bytes 196616 | tf_op jit(solution)/shard_map/ppermute | solution.py:218
  58.5 13.8 %collective-permute-start.4 = (f32[16,1024]{1,0:T(8,128)S(1)}, f32[16,1024]{1,0:T(8,128)S(1)}, u32[]{:S(2)}, u32[]{:S(2)}) collective-permute-start(f32[16,1024]{1,0:T(8,128)S(1)} %fusion.3.one_ref), channel_id=1, source_target_pairs={{0,64},{64,0},{128,192},{192,128},{256,320},{320,256},{384,448},{4... | collective-permute-start | bytes 196616 | tf_op jit(solution)/shard_map/ppermute | solution.py:253
  72.5 1.3 copy-start.4
  75.1 1.3 copy-start.5
  78.8 1.3 copy-start
  80.8 18.6 %all-to-all-start.2 = ((f32[8,24,128]{2,1,0:T(8,128)}), f32[8,24,128]{2,1,0:T(8,128)S(1)}, u32[]{:S(2)}, u32[]{:S(2)}) async-start(f32[8,24,128]{2,1,0:T(8,128)} %broadcast_in_dim.33), calls=%async_computation.2 | async-start | bytes 196608 | tf_op jit(solution)/shard_map/all_to_all | solution.py:46
  87.3 23.3 %collective-permute-start.5 = (bf16[576,128]{1,0:T(8,128)(2,1)S(1)}, bf16[576,128]{1,0:T(8,128)(2,1)S(1)}, u32[]{:S(2)}, u32[]{:S(2)}) collective-permute-start(bf16[576,128]{1,0:T(8,128)(2,1)S(1)} %fusion.1.refs_0_.refs_1_), channel_id=1, source_target_pairs={{0,64},{64,0},{128,192},{192,128},{256,320},{320,256},{384,448},{4... | collective-permute-start | bytes 442376 | tf_op jit(solution)/shard_map/ppermute | solution.py:286
  100.1 15.5 %all-to-all-start.3 = ((f32[8,24,128]{2,1,0:T(8,128)}), f32[8,24,128]{2,1,0:T(8,128)S(1)}, u32[]{:S(2)}, u32[]{:S(2)}) async-start(f32[8,24,128]{2,1,0:T(8,128)} %shard_map.89), calls=%async_computation.3 | async-start | bytes 196608 | tf_op jit(solution)/shard_map/all_to_all | solution.py:46
  115.6 1.6 copy-start.1
  117.2 31.4 %copy-start.3 = (bf16[1024,128]{1,0:T(8,128)(2,1)S(1)}, bf16[1024,128]{1,0:T(8,128)(2,1)}, u32[]{:S(2)}) copy-start(bf16[1024,128]{1,0:T(8,128)(2,1)} %refs_1_.3) | copy-start | bytes 786436
  126.8 13.8 %collective-permute-start.6 = (f32[16,1024]{1,0:T(8,128)S(1)}, f32[16,1024]{1,0:T(8,128)S(1)}, u32[]{:S(2)}, u32[]{:S(2)}) collective-permute-start(f32[16,1024]{1,0:T(8,128)S(1)} %reduce_sum.18.one_ref), channel_id=1, source_target_pairs={{0,64},{64,0},{128,192},{192,128},{256,320},{320,256},{384,448},{4... | collective-permute-start | bytes 196616 | tf_op jit(solution)/shard_map/ppermute | solution.py:297
  163.5 12.8 %all-to-all-start.7 = ((f32[4,72,128]{2,1,0:T(8,128)}), f32[4,72,128]{2,1,0:T(8,128)S(1)}, u32[]{:S(2)}, u32[]{:S(2)}) async-start(f32[4,72,128]{2,1,0:T(8,128)} %shard_map.93), calls=%async_computation.7 | async-start | bytes 294912 | tf_op jit(solution)/shard_map/all_to_all | solution.py:46
  167.4 25.0 %collective-permute-start.10 = (bf16[2,576,128]{2,1,0:T(8,128)(2,1)S(1)}, bf16[2,576,128]{2,1,0:T(8,128)(2,1)S(1)}, u32[]{:S(2)}, u32[]{:S(2)}) collective-permute-start(bf16[2,576,128]{2,1,0:T(8,128)(2,1)S(1)} %pad_maximum_fusion.refs_2_), channel_id=1, source_target_pairs={{0,384},{64,448},{128,256},{192,320},{256,128},{320,192},{384,0},{... | collective-permute-start | bytes 884744 | tf_op jit(solution)/shard_map/ppermute | solution.py:295
  170.2 22.2 %collective-permute-start.9 = (bf16[2,576,128]{2,1,0:T(8,128)(2,1)S(1)}, bf16[2,576,128]{2,1,0:T(8,128)(2,1)S(1)}, u32[]{:S(2)}, u32[]{:S(2)}) collective-permute-start(bf16[2,576,128]{2,1,0:T(8,128)(2,1)S(1)} %pad_maximum_fusion.refs_2_), channel_id=1, source_target_pairs={{0,256},{64,320},{128,384},{192,448},{256,0},{320,64},{384,128},{4... | collective-permute-start | bytes 884744 | tf_op jit(solution)/shard_map/ppermute | solution.py:295
  173.3 19.1 %collective-permute-start.8 = (bf16[2,576,128]{2,1,0:T(8,128)(2,1)S(1)}, bf16[2,576,128]{2,1,0:T(8,128)(2,1)S(1)}, u32[]{:S(2)}, u32[]{:S(2)}) collective-permute-start(bf16[2,576,128]{2,1,0:T(8,128)(2,1)S(1)} %pad_maximum_fusion.refs_2_), channel_id=1, source_target_pairs={{0,128},{64,192},{128,0},{192,64},{256,384},{320,448},{384,256},{4... | collective-permute-start | bytes 884744 | tf_op jit(solution)/shard_map/ppermute | solution.py:295
  176.4 8.6 %collective-permute-start.7 = (f32[72,128]{1,0:T(8,128)S(1)}, f32[72,128]{1,0:T(8,128)S(1)}, u32[]{:S(2)}, u32[]{:S(2)}) collective-permute-start(f32[72,128]{1,0:T(8,128)S(1)} %reduce_sum.19.one_ref), channel_id=1, source_target_pairs={{0,8},{1,9},{2,10},{3,11},{4,12},{5,13},{6,14},{7,15},{8,0},{9,1},... | collective-permute-start | bytes 110600 | tf_op jit(solution)/shard_map/ppermute | solution.py:315
  185.7 13.5 %all-to-all-start.8 = ((f32[8,72,128]{2,1,0:T(8,128)}), f32[8,72,128]{2,1,0:T(8,128)S(1)}, u32[]{:S(2)}, u32[]{:S(2)}) async-start(f32[8,72,128]{2,1,0:T(8,128)} %shard_map.94), calls=%async_computation.8 | async-start | bytes 589824 | tf_op jit(solution)/shard_map/all_to_all | solution.py:46

commit v4 on v3

--- a/solution.py
+++ b/solution.py
@@ -10,7 +10,7 @@
 NY, NZ, NC = 4, 8, 2
 NYC = NY * NC
 GRAD_SCALE = 8192.0
-VMEM = 32 << 20
+VMEM = 12 << 20
 
 softmax_scale = 192.0 ** (-0.5)
 masked_value = -1e30
@@ -30,9 +30,7 @@
 groups_z4 = [
     [token_at(y, half + z, c) for z in range(4)] for half in (0, 4) for y in all_y for c in all_c
 ]
-groups_y = [[token_at(y, z, c) for y in all_y] for z in all_z for c in all_c]
 groups_yc = [[token_at(y, z, c) for c in all_c for y in all_y] for z in all_z]
-pairs_c = [(token_at(y, z, c), token_at(y, z, 1 - c)) for y in all_y for z in all_z for c in all_c]
 pairs_z4 = [(token_at(y, z, c), token_at(y, z ^ 4, c)) for y in all_y for z in all_z for c in all_c]
 groups_x = [[head_at(x, z) for x in range(NX)] for z in range(NZH)]
 pairs_zh = [(head_at(x, z), head_at(x, 1 - z)) for x in range(NX) for z in range(NZH)]
@@ -74,20 +72,20 @@
     )
 
 
-def score_kernel(heads, limit_ref, q_ref, k_ref, e_ref, m_ref, l_ref):
+def score_kernel(limit_ref, q_ref, k_ref, e_ref, m_ref, l_ref):
     rows, keys = e_ref.shape
-    block = rows // NY
+    block = rows // NYC
     key = lax.broadcasted_iota(jnp.int32, (1, keys), 1)
     k = k_ref[...]
-    for y in range(NY):
-        lines = slice(y * block, (y + 1) * block)
+    for b in range(NYC):
+        lines = slice(b * block, (b + 1) * block)
         s = jnp.dot(q_ref[lines], k, preferred_element_type=f32) * softmax_scale
         s = jnp.where(key <= limit_ref[lines], s, masked_value)
         m = jnp.max(s, axis=1, keepdims=True)
         e = jnp.exp(s - m)
         e_ref[lines] = e
-        m_ref[y : y + 1] = as_row(m)
-        l_ref[y : y + 1] = as_row(jnp.sum(e, axis=1, keepdims=True))
+        m_ref[b : b + 1] = as_row(m)
+        l_ref[b : b + 1] = as_row(jnp.sum(e, axis=1, keepdims=True))
 
 
 def message_parts(ref, tokens, heads):
@@ -133,20 +131,14 @@
     out_ref[...] = jnp.broadcast_to(lines[None], out_ref.shape)
 
 
-def target_kernel(core_ref, stats_ref, m_ref, own_ref, other_ref, out_ref):
-    stats = stats_ref[...]
-    top, total, _, _ = joined(stats)
+def target_kernel(stats_ref, m_ref, e_ref, out_ref):
+    top, total, _, _ = joined(stats_ref[...])
     weights = jnp.exp(m_ref[...] - top) / total
     keys = out_ref.shape[1]
-    half = out_ref.shape[0] // NC
-    block = own_ref.shape[0] // NY
-    own = core_ref[0]
-    for y in range(NY):
-        for core, e_ref in ((own, own_ref), (1 - own, other_ref)):
-            row = jnp.where(core == 0, weights[y : y + 1], weights[NY + y : NY + y + 1])
-            e = e_ref[y * block : (y + 1) * block] * as_column(row, block)
-            part = jnp.sum(e.reshape(NZ, block // NZ, keys), axis=1)
-            out_ref[pl.ds(pl.multiple_of(core * half + y * NZ, NZ), NZ), :] = part
+    block = e_ref.shape[0] // NYC
+    for b in range(NYC):
+        e = e_ref[b * block : (b + 1) * block] * as_column(weights[b : b + 1], block)
+        out_ref[b * NZ : (b + 1) * NZ] = jnp.sum(e.reshape(NZ, block // NZ, keys), axis=1)
 
 
 def dlogit_kernel(one_ref, two_ref, logits_ref, stats_ref, out_ref):
@@ -227,7 +219,6 @@
     share_rows = query_count // NX
     shape = jax.ShapeDtypeStruct
     x = lax.axis_index("heads") // NZH
-    core = lax.axis_index("tokens") % NC
     limit = in_order(positions - lax.axis_index("tokens") * key_count)
 
     along_z = gathered(queries.reshape(heads_here, width), "tokens", groups_z)
@@ -248,57 +239,46 @@
         flops=index_flops,
         moved=1 << 20,
     )(mine, index_keys)
-    along_z, partial = lax.optimization_barrier((along_z, partial))
     over_x = x_scatter_sum(partial.reshape(NX, share_rows, key_count), x)
+    along_z, over_x = lax.optimization_barrier((along_z, over_x))
     other = lax.ppermute(over_x, "heads", pairs_zh)
+    rows = gathered(along_z, "tokens", groups_yc).reshape(-1, width)
+    rows, other = lax.optimization_barrier((rows, other))
     share_limit = lax.dynamic_slice_in_dim(limit, x * share_rows, share_rows, 0)
     logits, index_stats = call(
         index_stats_kernel,
         (shape((share_rows, key_count), f32), shape((8, 128), f32)),
     )(share_limit[:, None], over_x, other)
 
-    own_rows = gathered(along_z, "tokens", groups_y)
-    other_rows = lax.ppermute(own_rows, "tokens", pairs_c)
-    row_limit = jnp.repeat(limit.reshape(NC, -1), heads_here, axis=1)[:, :, None]
-    row_count = row_limit.shape[1]
-    score = call(
-        lambda *refs: score_kernel(heads_here, *refs),
-        (
-            shape((row_count, key_count), f32),
-            shape((NY, row_count // NY), f32),
-            shape((NY, row_count // NY), f32),
-        ),
+    row_count = rows.shape[0]
+    lines_shape = shape((NYC, row_count // NYC), f32)
+    exponent, local_max, local_total = call(
+        score_kernel,
+        (shape((row_count, key_count), f32), lines_shape, lines_shape),
         flops=2 * row_count * key_count * width,
         moved=4 << 20,
-    )
-    keys_t = latent_keys.T
-    first_limit = jnp.where(core == 0, row_limit[0], row_limit[1])
-    second_limit = jnp.where(core == 0, row_limit[1], row_limit[0])
-    own_e, own_max, own_total = score(first_limit, own_rows.reshape(-1, width), keys_t)
-    other_e, other_max, other_total = score(second_limit, other_rows.reshape(-1, width), keys_t)
-
-    def by_core(own, other):
-        return jnp.where(core == 0, jnp.concatenate([own, other]), jnp.concatenate([other, own]))
-
-    local_max = by_core(own_max, other_max)
-    stats = jnp.concatenate([local_max, by_core(own_total, other_total), index_stats])
-    stats, mine = lax.optimization_barrier((stats, mine))
-    pair = jnp.stack([mine, lax.ppermute(mine, "heads", pairs_zh)])
+    )(jnp.repeat(limit, heads_here)[:, None], rows, latent_keys.T)
+
+    stats = jnp.concatenate([local_max, local_total, index_stats])
     stats = gathered(stats, "tokens", groups_z)
     stats = call(join_kernel, shape((NYC, *stats.shape[1:]), f32))(stats)
+    stats, sent = lax.optimization_barrier((stats, mine))
+    swapped = lax.ppermute(sent, "heads", pairs_zh)
     stats = exchanged(stats, "tokens", groups_yc)
 
     partial = call(target_kernel, shape((query_count, key_count), f32), moved=5 << 20)(
-        core.reshape(1), stats, local_max, own_e, other_e
-    )
-    partial, pair = lax.optimization_barrier((partial, pair))
-    messages = [pair] + [lax.ppermute(pair, "heads", pairs_x(flip)) for flip in range(1, NX)]
+        stats, local_max, exponent
+    )
     over_x = exchanged(partial.reshape(NX, share_rows, key_count), "heads", groups_x).sum(axis=0)
     other = lax.ppermute(over_x, "heads", pairs_zh)
+    other, swapped = lax.optimization_barrier((other, swapped))
+    pair = jnp.stack([mine, swapped])
+    messages = [pair] + [lax.ppermute(pair, "heads", pairs_x(flip)) for flip in range(1, NX)]
     dlogit = call(dlogit_kernel, shape((NX, share_rows, key_count), f32))(
         over_x, other, logits, stats
     )
     dlogit = exchanged(dlogit, "heads", groups_x).reshape(query_count, key_count)
+    dlogit, messages[1] = lax.optimization_barrier((dlogit, messages[1]))
 
     query_lines = query_count * index_heads
     piece_rows = -(-(query_lines + index_heads) // (NYC * 8)) * 8
@@ -310,6 +290,7 @@
     )(dlogit, mine, index_keys)
 
     piece = exchanged(both.reshape(NYC, piece_rows, 128), "tokens", groups_yc)
+    piece, messages[2] = lax.optimization_barrier((piece, messages[2]))
     piece = call(sum_kernel, shape((NZ // 2, piece_rows, 128), f32))(piece)
     piece = exchanged(piece, "tokens", groups_z4).sum(axis=0)
     other = lax.ppermute(piece, "tokens", pairs_z4)

time: 202 us -> 192 us (0.950)
  starting transfers between devices: 103 us -> 90 us
  waiting for transfers between devices: 39.7 us -> 47.7 us
  local copies, waits for them, and re-layouts: 12.8 us -> 7.12 us
    ppermute x2 -> x1, waiting for transfers between devices: 0.01 us -> 11.9 us  [local(): swapped = lax.ppermute(sent, 'heads', pairs_zh)]
    ppermute x2 -> x1, starting transfers between devices: 18.6 us -> 7.94 us  [local(): swapped = lax.ppermute(sent, 'heads', pairs_zh)]
    unnamed x14 -> x6, local copies, waits for them, and re-layouts: 6.41 us -> 1.28 us
    ppermute x1, waiting for transfers between devices: 1.81 us -> 6.68 us  [local(): other = lax.ppermute(piece, 'tokens', pairs_z4)]
    ppermute x1, starting transfers between devices: 6.8 us -> 1.92 us  [local(): other = lax.ppermute(piece, 'tokens', pairs_z4)]
    ppermute x2, waiting for transfers between devices: 12.5 us -> 7.83 us  [local(): other = lax.ppermute(over_x, 'heads', pairs_zh)]
    all_to_all x6 -> x7, waiting for transfers between devices: 21.9 us -> 17.4 us  [exchanged(): lax.all_to_all(parts, axis, 0, 0, tiled=True, axis_index_groups=groups)]
    all_to_all x6 -> x7, starting transfers between devices: 44.7 us -> 46.6 us  [exchanged(): lax.all_to_all(parts, axis, 0, 0, tiled=True, axis_index_groups=groups)]
  transfers between devices with their start and end apart: 17 -> 17, of which waited for: 8 -> 11; matrix products, arithmetic and copies ran while one was open for 2% -> 1% of each run, Pallas kernels for 4% -> 4%
where the time goes in v4:
time: 192 us; the launch traced here: 190 us
  starting transfers between devices  90 us (47%)
  waiting for transfers between devices  47.7 us (25%)
  blocking collectives  30.7 us (16%)
  Pallas kernels  13.2 us (7%)
  local copies, waits for them, and re-layouts  7.12 us (4%)
    all_to_all x7, starting transfers between devices, exchanged(): lax.all_to_all(parts, axis, 0, 0, tiled=True, axis_index_groups=groups)  46.6 us
    all_to_all x2, blocking collectives, exchanged(): lax.all_to_all(parts, axis, 0, 0, tiled=True, axis_index_groups=groups)  30.7 us
    all_to_all x7, waiting for transfers between devices, exchanged(): lax.all_to_all(parts, axis, 0, 0, tiled=True, axis_index_groups=groups)  17.4 us
    ppermute x2, starting transfers between devices, local(): other = lax.ppermute(over_x, 'heads', pairs_zh)  14 us
    ppermute x1, waiting for transfers between devices, local(): swapped = lax.ppermute(sent, 'heads', pairs_zh)  11.9 us
    ppermute x3, starting transfers between devices, local(): lax.ppermute(pair, 'heads', pairs_x(flip))  10.1 us
    ppermute x3, starting transfers between devices, x_scatter_sum(): total = total + lax.ppermute(piece, 'heads', pairs_x(flip))  9.4 us
    ppermute x1, starting transfers between devices, local(): swapped = lax.ppermute(sent, 'heads', pairs_zh)  7.94 us
  transfers between devices with their start and end apart: 17, of which 11 were waited for; matrix products, arithmetic and copies ran while one was open for 1% of the time, Pallas kernels for 4%

profile of v4, /device:TPU:1, one launch (start us, length us, event | category | flops | bytes accessed | tf_op | source)
XLA Modules:
  0.0 190.4 jit_solution(15610269648932744228)
XLA Ops:
  2.1 13.1 %all-to-all-start = ((bf16[8,16,576]{2,1,0:T(8,128)(2,1)}), bf16[8,16,576]{2,1,0:T(8,128)(2,1)S(1)}, u32[]{:S(2)}, u32[]{:S(2)}) async-start(bf16[8,16,576]{2,1,0:T(8,128)(2,1)} %broadcast_in_dim.27), calls=%async_computation | async-start | bytes 327680 | tf_op jit(solution)/shard_map/all_to_all | solution.py:44
  17.5 3.1 %collective-permute-start = (f32[16,1024]{1,0:T(8,128)S(1)}, f32[16,1024]{1,0:T(8,128)S(1)}, u32[]{:S(2)}, u32[]{:S(2)}) collective-permute-start(f32[16,1024]{1,0:T(8,128)S(1)} %get-tuple-element.37), channel_id=1, source_target_pairs={{0,128},{64,192},{128,0},{192,64},{256,384},{320,448},{384,256},{4... | collective-permute-start | bytes 196616 | tf_op jit(solution)/shard_map/ppermute | solution.py:210
  20.6 3.7 %collective-permute-start.2 = (f32[16,1024]{1,0:T(8,128)S(1)}, f32[16,1024]{1,0:T(8,128)S(1)}, u32[]{:S(2)}, u32[]{:S(2)}) collective-permute-start(f32[16,1024]{1,0:T(8,128)S(1)} %get-tuple-element.38), channel_id=1, source_target_pairs={{0,384},{64,448},{128,256},{192,320},{256,128},{320,192},{384,0},{... | collective-permute-start | bytes 196616 | tf_op jit(solution)/shard_map/ppermute | solution.py:210
  24.3 2.6 %collective-permute-start.1 = (f32[16,1024]{1,0:T(8,128)S(1)}, f32[16,1024]{1,0:T(8,128)S(1)}, u32[]{:S(2)}, u32[]{:S(2)}) collective-permute-start(f32[16,1024]{1,0:T(8,128)S(1)} %get-tuple-element.39), channel_id=1, source_target_pairs={{0,256},{64,320},{128,384},{192,448},{256,0},{320,64},{384,128},{4... | collective-permute-start | bytes 196616 | tf_op jit(solution)/shard_map/ppermute | solution.py:210
  27.1 3.7 %collective-permute-done.1 = f32[16,1024]{1,0:T(8,128)S(1)} collective-permute-done((f32[16,1024]{1,0:T(8,128)S(1)}, f32[16,1024]{1,0:T(8,128)S(1)}, u32[]{:S(2)}, u32[]{:S(2)}) %collective-permute-start.1) | collective-permute-done | bytes 65568 | tf_op jit(solution)/shard_map/ppermute | solution.py:210
  32.1 7.3 %all-to-all-start.1 = ((bf16[8,8,16,576]{3,2,1,0:T(8,128)(2,1)}), bf16[8,8,16,576]{3,2,1,0:T(8,128)(2,1)S(1)}, u32[]{:S(2)}, u32[]{:S(2)}) async-start(bf16[8,8,16,576]{3,2,1,0:T(8,128)(2,1)} %broadcast_in_dim.28), calls=%async_computation.1 | async-start | bytes 2621440 | tf_op jit(solution)/shard_map/all_to_all | solution.py:44
  39.6 7.9 %collective-permute-start.3 = (f32[16,1024]{1,0:T(8,128)S(1)}, f32[16,1024]{1,0:T(8,128)S(1)}, u32[]{:S(2)}, u32[]{:S(2)}) collective-permute-start(f32[16,1024]{1,0:T(8,128)S(1)} %fusion.3.one_ref), channel_id=1, source_target_pairs={{0,64},{64,0},{128,192},{192,128},{256,320},{320,256},{384,448},{4... | collective-permute-start | bytes 196616 | tf_op jit(solution)/shard_map/ppermute | solution.py:244
  48.1 5.8 %collective-permute-done.3.two_ref = f32[16,1024]{1,0:T(8,128)S(1)} collective-permute-done((f32[16,1024]{1,0:T(8,128)S(1)}, f32[16,1024]{1,0:T(8,128)S(1)}, u32[]{:S(2)}, u32[]{:S(2)}) %collective-permute-start.3) | collective-permute-done | bytes 65568 | tf_op jit(solution)/shard_map/ppermute | solution.py:244
  53.9 3.2 %all-to-all-done.1 = bf16[8,8,16,576]{3,2,1,0:T(8,128)(2,1)S(1)} async-done(((bf16[8,8,16,576]{3,2,1,0:T(8,128)(2,1)}), bf16[8,8,16,576]{3,2,1,0:T(8,128)(2,1)S(1)}, u32[]{:S(2)}, u32[]{:S(2)}) %all-to-all-start.1) | async-done | bytes 1179680 | tf_op jit(solution)/shard_map/all_to_all | solution.py:44
  58.6 2.3 %shard_map.86 = (f32[1024,1024]{1,0:T(8,128)S(1)}, f32[8,128]{1,0:T(8,128)S(1)}, f32[8,128]{1,0:T(8,128)S(1)}) custom-call(s32[1024,1]{1,0:T(8,128)S(1)} %broadcast_in_dim_reshape.5.limit_ref, bf16[1024,576]{1,0:T(8,128)(2,1)S(1)} %bitcast.42, bf16[576,1024]{1,0:T(8,128)(2,1)S(1)} %bitcast.47), custom_call_target="tpu_custom_call" | custom-call | flops 1207959552 | bytes 4194304 | tf_op jit(solution)/shard_map/pallas_call | solution.py:255
  61.0 19.5 %all_to_all.45.stats_ref = f32[8,24,128]{2,1,0:T(8,128)S(1)} all-to-all(f32[8,24,128]{2,1,0:T(8,128)S(1)} %broadcast_in_dim.30), channel_id=1, replica_groups={{0,2,4,6,8,10,12,14},{1,3,5,7,9,11,13,15},{16,18,20,22,24,26,28,30},{17..., dimensions={0} | all-to-all | bytes 196608 | tf_op jit(solution)/shard_map/all_to_all | solution.py:44
  80.5 11.2 %all_to_all.46.stats_ref = f32[8,24,128]{2,1,0:T(8,128)S(1)} all-to-all(f32[8,24,128]{2,1,0:T(8,128)S(1)} %shard_map.88), channel_id=1, replica_groups={{0,16,32,48,1,17,33,49},{2,18,34,50,3,19,35,51},{4,20,36,52,5,21,37,53}..., dimensions={0} | all-to-all | bytes 196608 | tf_op jit(solution)/shard_map/all_to_all | solution.py:44
  93.2 3.4 %all-to-all-start.4 = ((f32[4,16,1024]{2,1,0:T(8,128)}), f32[4,16,1024]{2,1,0:T(8,128)S(1)}, u32[]{:S(2)}, u32[]{:S(2)}) async-start(f32[4,16,1024]{2,1,0:T(8,128)} %bitcast.18), calls=%async_computation.4 | async-start | bytes 524288 | tf_op jit(solution)/shard_map/all_to_all | solution.py:44
  96.6 7.9 %collective-permute-start.5 = (bf16[576,128]{1,0:T(8,128)(2,1)S(1)}, bf16[576,128]{1,0:T(8,128)(2,1)S(1)}, u32[]{:S(2)}, u32[]{:S(2)}) collective-permute-start(bf16[576,128]{1,0:T(8,128)(2,1)S(1)} %get-tuple-element.29.refs_0_.refs_1_), channel_id=1, source_target_pairs={{0,64},{64,0},{128,192},{192,128},{256,320},{320,256},{384,448},{4... | collective-permute-start | bytes 442376 | tf_op jit(solution)/shard_map/ppermute | solution.py:266
  104.6 6.1 %collective-permute-start.4 = (f32[16,1024]{1,0:T(8,128)S(1)}, f32[16,1024]{1,0:T(8,128)S(1)}, u32[]{:S(2)}, u32[]{:S(2)}) collective-permute-start(f32[16,1024]{1,0:T(8,128)S(1)} %reduce_sum.18.one_ref), channel_id=1, source_target_pairs={{0,64},{64,0},{128,192},{192,128},{256,320},{320,256},{384,448},{4... | collective-permute-start | bytes 196616 | tf_op jit(solution)/shard_map/ppermute | solution.py:273
  110.7 11.9 %collective-permute-done.5 = bf16[576,128]{1,0:T(8,128)(2,1)S(1)} collective-permute-done((bf16[576,128]{1,0:T(8,128)(2,1)S(1)}, bf16[576,128]{1,0:T(8,128)(2,1)S(1)}, u32[]{:S(2)}, u32[]{:S(2)}) %collective-permute-start.5) | collective-permute-done | bytes 147488 | tf_op jit(solution)/shard_map/ppermute | solution.py:266
  122.6 2.0 %collective-permute-done.4.two_ref = f32[16,1024]{1,0:T(8,128)S(1)} collective-permute-done((f32[16,1024]{1,0:T(8,128)S(1)}, f32[16,1024]{1,0:T(8,128)S(1)}, u32[]{:S(2)}, u32[]{:S(2)}) %collective-permute-start.4) | collective-permute-done | bytes 65568 | tf_op jit(solution)/shard_map/ppermute | solution.py:273
  124.6 3.3 %collective-permute-start.6 = (bf16[2,576,128]{2,1,0:T(8,128)(2,1)S(1)}, bf16[2,576,128]{2,1,0:T(8,128)(2,1)S(1)}, u32[]{:S(2)}, u32[]{:S(2)}) collective-permute-start(bf16[2,576,128]{2,1,0:T(8,128)(2,1)S(1)} %pad_maximum_fusion.refs_2_), channel_id=1, source_target_pairs={{0,128},{64,192},{128,0},{192,64},{256,384},{320,448},{384,256},{4... | collective-permute-start | bytes 884744 | tf_op jit(solution)/shard_map/ppermute | solution.py:276
  128.8 3.7 %all-to-all-start.5 = ((f32[4,16,1024]{2,1,0:T(8,128)}), f32[4,16,1024]{2,1,0:T(8,128)S(1)}, u32[]{:S(2)}, u32[]{:S(2)}) async-start(f32[4,16,1024]{2,1,0:T(8,128)} %shard_map.90), calls=%async_computation.5 | async-start | bytes 524288 | tf_op jit(solution)/shard_map/all_to_all | solution.py:44
  132.5 4.9 %collective-permute-start.7 = (bf16[2,576,128]{2,1,0:T(8,128)(2,1)S(1)}, bf16[2,576,128]{2,1,0:T(8,128)(2,1)S(1)}, u32[]{:S(2)}, u32[]{:S(2)}) collective-permute-start(bf16[2,576,128]{2,1,0:T(8,128)(2,1)S(1)} %pad_maximum_fusion.refs_2_), channel_id=1, source_target_pairs={{0,256},{64,320},{128,384},{192,448},{256,0},{320,64},{384,128},{4... | collective-permute-start | bytes 884744 | tf_op jit(solution)/shard_map/ppermute | solution.py:276
  137.3 2.1 %all-to-all-done.5 = f32[4,16,1024]{2,1,0:T(8,128)S(1)} async-done(((f32[4,16,1024]{2,1,0:T(8,128)}), f32[4,16,1024]{2,1,0:T(8,128)S(1)}, u32[]{:S(2)}, u32[]{:S(2)}) %all-to-all-start.5) | async-done | bytes 262176 | tf_op jit(solution)/shard_map/all_to_all | solution.py:44
  139.5 1.8 shard_map.91
  141.2 6.0 %all-to-all-start.6 = ((f32[8,72,128]{2,1,0:T(8,128)}), f32[8,72,128]{2,1,0:T(8,128)S(1)}, u32[]{:S(2)}, u32[]{:S(2)}) async-start(f32[8,72,128]{2,1,0:T(8,128)} %bitcast.22), calls=%async_computation.6 | async-start | bytes 589824 | tf_op jit(solution)/shard_map/all_to_all | solution.py:44
  147.2 6.9 %all-to-all-done.6.parts_ref = f32[8,72,128]{2,1,0:T(8,128)S(1)} async-done(((f32[8,72,128]{2,1,0:T(8,128)}), f32[8,72,128]{2,1,0:T(8,128)S(1)}, u32[]{:S(2)}, u32[]{:S(2)}) %all-to-all-start.6) | async-done | bytes 294944 | tf_op jit(solution)/shard_map/all_to_all | solution.py:44
  154.8 4.9 %all-to-all-start.7 = ((f32[4,72,128]{2,1,0:T(8,128)}), f32[4,72,128]{2,1,0:T(8,128)S(1)}, u32[]{:S(2)}, u32[]{:S(2)}) async-start(f32[4,72,128]{2,1,0:T(8,128)} %shard_map.92), calls=%async_computation.7 | async-start | bytes 294912 | tf_op jit(solution)/shard_map/all_to_all | solution.py:44
  159.7 1.9 %collective-permute-start.9 = (bf16[2,576,128]{2,1,0:T(8,128)(2,1)S(1)}, bf16[2,576,128]{2,1,0:T(8,128)(2,1)S(1)}, u32[]{:S(2)}, u32[]{:S(2)}) collective-permute-start(bf16[2,576,128]{2,1,0:T(8,128)(2,1)S(1)} %pad_maximum_fusion.refs_2_), channel_id=1, source_target_pairs={{0,384},{64,448},{128,256},{192,320},{256,128},{320,192},{384,0},{... | collective-permute-start | bytes 884744 | tf_op jit(solution)/shard_map/ppermute | solution.py:276
  161.6 2.9 %all-to-all-done.7 = f32[4,72,128]{2,1,0:T(8,128)S(1)} async-done(((f32[4,72,128]{2,1,0:T(8,128)}), f32[4,72,128]{2,1,0:T(8,128)S(1)}, u32[]{:S(2)}, u32[]{:S(2)}) %all-to-all-start.7) | async-done | bytes 147488 | tf_op jit(solution)/shard_map/all_to_all | solution.py:44
  164.6 1.9 %collective-permute-start.8 = (f32[72,128]{1,0:T(8,128)S(1)}, f32[72,128]{1,0:T(8,128)S(1)}, u32[]{:S(2)}, u32[]{:S(2)}) collective-permute-start(f32[72,128]{1,0:T(8,128)S(1)} %reduce_sum.19.one_ref), channel_id=1, source_target_pairs={{0,8},{1,9},{2,10},{3,11},{4,12},{5,13},{6,14},{7,15},{8,0},{9,1},... | collective-permute-start | bytes 110600 | tf_op jit(solution)/shard_map/ppermute | solution.py:296
  166.5 6.7 %collective-permute-done.8.two_ref = f32[72,128]{1,0:T(8,128)S(1)} collective-permute-done((f32[72,128]{1,0:T(8,128)S(1)}, f32[72,128]{1,0:T(8,128)S(1)}, u32[]{:S(2)}, u32[]{:S(2)}) %collective-permute-start.8) | collective-permute-done | bytes 36896 | tf_op jit(solution)/shard_map/ppermute | solution.py:296
  173.9 8.3 %all-to-all-start.8 = ((f32[8,72,128]{2,1,0:T(8,128)}), f32[8,72,128]{2,1,0:T(8,128)S(1)}, u32[]{:S(2)}, u32[]{:S(2)}) async-start(f32[8,72,128]{2,1,0:T(8,128)} %shard_map.93), calls=%async_computation.8 | async-start | bytes 589824 | tf_op jit(solution)/shard_map/all_to_all | solution.py:44
  182.2 4.7 %shard_map.94 = f32[1024,128]{1,0:T(8,128)} custom-call(f32[64,1024]{1,0:T(8,128)S(1)} %bitcast.46, bf16[1024,128]{1,0:T(8,128)(2,1)S(1)} %copy-done, bf16[2,576,128]{2,1,0:T(8,128)(2,1)S(1)} %pad_maximum_fusion.refs_2_, bf16[2,576,128]{2,1,0:T(8,128)(2,1)S(1)} %collective-permute-done.6.refs_3_, bf16[2,576,128]{2,1,0:T(8,128)(2,1)S(1)} %collective-permute-done.7.refs_4_, ...), custom_call_target="tpu_custom_call" | custom-call | flops 2147483648 | bytes 3145728 | tf_op jit(solution)/shard_map/pallas_call | solution.py:302
  186.9 2.2 %all-to-all-done.8 = f32[8,72,128]{2,1,0:T(8,128)S(1)} async-done(((f32[8,72,128]{2,1,0:T(8,128)}), f32[8,72,128]{2,1,0:T(8,128)S(1)}, u32[]{:S(2)}, u32[]{:S(2)}) %all-to-all-start.8) | async-done | bytes 294944 | tf_op jit(solution)/shard_map/all_to_all | solution.py:44
  (45 shorter events, 12.6 us)
Async XLA Ops:
  0.6 16.3 %copy-start = (bf16[1024,128]{1,0:T(8,128)(2,1)S(1)}, bf16[1024,128]{1,0:T(8,128)(2,1)}, u32[]{:S(2)}) copy-start(bf16[1024,128]{1,0:T(8,128)(2,1)} %refs_1_.3) | copy-start | bytes 786436
  2.1 28.8 %all-to-all-start = ((bf16[8,16,576]{2,1,0:T(8,128)(2,1)}), bf16[8,16,576]{2,1,0:T(8,128)(2,1)S(1)}, u32[]{:S(2)}, u32[]{:S(2)}) async-start(bf16[8,16,576]{2,1,0:T(8,128)(2,1)} %broadcast_in_dim.27), calls=%async_computation | async-start | bytes 327680 | tf_op jit(solution)/shard_map/all_to_all | solution.py:44
  17.5 9.4 %collective-permute-start = (f32[16,1024]{1,0:T(8,128)S(1)}, f32[16,1024]{1,0:T(8,128)S(1)}, u32[]{:S(2)}, u32[]{:S(2)}) collective-permute-start(f32[16,1024]{1,0:T(8,128)S(1)} %get-tuple-element.37), channel_id=1, source_target_pairs={{0,128},{64,192},{128,0},{192,64},{256,384},{320,448},{384,256},{4... | collective-permute-start | bytes 196616 | tf_op jit(solution)/shard_map/ppermute | solution.py:210
  20.6 6.5 %collective-permute-start.2 = (f32[16,1024]{1,0:T(8,128)S(1)}, f32[16,1024]{1,0:T(8,128)S(1)}, u32[]{:S(2)}, u32[]{:S(2)}) collective-permute-start(f32[16,1024]{1,0:T(8,128)S(1)} %get-tuple-element.38), channel_id=1, source_target_pairs={{0,384},{64,448},{128,256},{192,320},{256,128},{320,192},{384,0},{... | collective-permute-start | bytes 196616 | tf_op jit(solution)/shard_map/ppermute | solution.py:210
  24.3 6.5 %collective-permute-start.1 = (f32[16,1024]{1,0:T(8,128)S(1)}, f32[16,1024]{1,0:T(8,128)S(1)}, u32[]{:S(2)}, u32[]{:S(2)}) collective-permute-start(f32[16,1024]{1,0:T(8,128)S(1)} %get-tuple-element.39), channel_id=1, source_target_pairs={{0,256},{64,320},{128,384},{192,448},{256,0},{320,64},{384,128},{4... | collective-permute-start | bytes 196616 | tf_op jit(solution)/shard_map/ppermute | solution.py:210
  32.0 7.3 %copy-start.2 = (s32[64]{0:T(128)S(1)}, s32[64]{0:T(128)}, u32[]{:S(2)}) copy-start(s32[64]{0:T(128)} %param.11) | copy-start | bytes 772
  32.1 25.1 %all-to-all-start.1 = ((bf16[8,8,16,576]{3,2,1,0:T(8,128)(2,1)}), bf16[8,8,16,576]{3,2,1,0:T(8,128)(2,1)S(1)}, u32[]{:S(2)}, u32[]{:S(2)}) async-start(bf16[8,8,16,576]{3,2,1,0:T(8,128)(2,1)} %broadcast_in_dim.28), calls=%async_computation.1 | async-start | bytes 2621440 | tf_op jit(solution)/shard_map/all_to_all | solution.py:44
  39.6 14.3 %collective-permute-start.3 = (f32[16,1024]{1,0:T(8,128)S(1)}, f32[16,1024]{1,0:T(8,128)S(1)}, u32[]{:S(2)}, u32[]{:S(2)}) collective-permute-start(f32[16,1024]{1,0:T(8,128)S(1)} %fusion.3.one_ref), channel_id=1, source_target_pairs={{0,64},{64,0},{128,192},{192,128},{256,320},{320,256},{384,448},{4... | collective-permute-start | bytes 196616 | tf_op jit(solution)/shard_map/ppermute | solution.py:244
  57.4 1.3 copy-start.1
  93.2 11.4 %all-to-all-start.4 = ((f32[4,16,1024]{2,1,0:T(8,128)}), f32[4,16,1024]{2,1,0:T(8,128)S(1)}, u32[]{:S(2)}, u32[]{:S(2)}) async-start(f32[4,16,1024]{2,1,0:T(8,128)} %bitcast.18), calls=%async_computation.4 | async-start | bytes 524288 | tf_op jit(solution)/shard_map/all_to_all | solution.py:44
  96.6 26.0 %collective-permute-start.5 = (bf16[576,128]{1,0:T(8,128)(2,1)S(1)}, bf16[576,128]{1,0:T(8,128)(2,1)S(1)}, u32[]{:S(2)}, u32[]{:S(2)}) collective-permute-start(bf16[576,128]{1,0:T(8,128)(2,1)S(1)} %get-tuple-element.29.refs_0_.refs_1_), channel_id=1, source_target_pairs={{0,64},{64,0},{128,192},{192,128},{256,320},{320,256},{384,448},{4... | collective-permute-start | bytes 442376 | tf_op jit(solution)/shard_map/ppermute | solution.py:266
  104.6 20.0 %collective-permute-start.4 = (f32[16,1024]{1,0:T(8,128)S(1)}, f32[16,1024]{1,0:T(8,128)S(1)}, u32[]{:S(2)}, u32[]{:S(2)}) collective-permute-start(f32[16,1024]{1,0:T(8,128)S(1)} %reduce_sum.18.one_ref), channel_id=1, source_target_pairs={{0,64},{64,0},{128,192},{192,128},{256,320},{320,256},{384,448},{4... | collective-permute-start | bytes 196616 | tf_op jit(solution)/shard_map/ppermute | solution.py:273
  124.6 14.8 %collective-permute-start.6 = (bf16[2,576,128]{2,1,0:T(8,128)(2,1)S(1)}, bf16[2,576,128]{2,1,0:T(8,128)(2,1)S(1)}, u32[]{:S(2)}, u32[]{:S(2)}) collective-permute-start(bf16[2,576,128]{2,1,0:T(8,128)(2,1)S(1)} %pad_maximum_fusion.refs_2_), channel_id=1, source_target_pairs={{0,128},{64,192},{128,0},{192,64},{256,384},{320,448},{384,256},{4... | collective-permute-start | bytes 884744 | tf_op jit(solution)/shard_map/ppermute | solution.py:276
  128.8 10.7 %all-to-all-start.5 = ((f32[4,16,1024]{2,1,0:T(8,128)}), f32[4,16,1024]{2,1,0:T(8,128)S(1)}, u32[]{:S(2)}, u32[]{:S(2)}) async-start(f32[4,16,1024]{2,1,0:T(8,128)} %shard_map.90), calls=%async_computation.5 | async-start | bytes 524288 | tf_op jit(solution)/shard_map/all_to_all | solution.py:44
  132.5 14.7 %collective-permute-start.7 = (bf16[2,576,128]{2,1,0:T(8,128)(2,1)S(1)}, bf16[2,576,128]{2,1,0:T(8,128)(2,1)S(1)}, u32[]{:S(2)}, u32[]{:S(2)}) collective-permute-start(bf16[2,576,128]{2,1,0:T(8,128)(2,1)S(1)} %pad_maximum_fusion.refs_2_), channel_id=1, source_target_pairs={{0,256},{64,320},{128,384},{192,448},{256,0},{320,64},{384,128},{4... | collective-permute-start | bytes 884744 | tf_op jit(solution)/shard_map/ppermute | solution.py:276
  141.2 12.9 %all-to-all-start.6 = ((f32[8,72,128]{2,1,0:T(8,128)}), f32[8,72,128]{2,1,0:T(8,128)S(1)}, u32[]{:S(2)}, u32[]{:S(2)}) async-start(f32[8,72,128]{2,1,0:T(8,128)} %bitcast.22), calls=%async_computation.6 | async-start | bytes 589824 | tf_op jit(solution)/shard_map/all_to_all | solution.py:44
  154.8 9.8 %all-to-all-start.7 = ((f32[4,72,128]{2,1,0:T(8,128)}), f32[4,72,128]{2,1,0:T(8,128)S(1)}, u32[]{:S(2)}, u32[]{:S(2)}) async-start(f32[4,72,128]{2,1,0:T(8,128)} %shard_map.92), calls=%async_computation.7 | async-start | bytes 294912 | tf_op jit(solution)/shard_map/all_to_all | solution.py:44
  159.7 22.5 %collective-permute-start.9 = (bf16[2,576,128]{2,1,0:T(8,128)(2,1)S(1)}, bf16[2,576,128]{2,1,0:T(8,128)(2,1)S(1)}, u32[]{:S(2)}, u32[]{:S(2)}) collective-permute-start(bf16[2,576,128]{2,1,0:T(8,128)(2,1)S(1)} %pad_maximum_fusion.refs_2_), channel_id=1, source_target_pairs={{0,384},{64,448},{128,256},{192,320},{256,128},{320,192},{384,0},{... | collective-permute-start | bytes 884744 | tf_op jit(solution)/shard_map/ppermute | solution.py:276
  164.6 8.6 %collective-permute-start.8 = (f32[72,128]{1,0:T(8,128)S(1)}, f32[72,128]{1,0:T(8,128)S(1)}, u32[]{:S(2)}, u32[]{:S(2)}) collective-permute-start(f32[72,128]{1,0:T(8,128)S(1)} %reduce_sum.19.one_ref), channel_id=1, source_target_pairs={{0,8},{1,9},{2,10},{3,11},{4,12},{5,13},{6,14},{7,15},{8,0},{9,1},... | collective-permute-start | bytes 110600 | tf_op jit(solution)/shard_map/ppermute | solution.py:296
  173.9 15.2 %all-to-all-start.8 = ((f32[8,72,128]{2,1,0:T(8,128)}), f32[8,72,128]{2,1,0:T(8,128)S(1)}, u32[]{:S(2)}, u32[]{:S(2)}) async-start(f32[8,72,128]{2,1,0:T(8,128)} %shard_map.93), calls=%async_computation.8 | async-start | bytes 589824 | tf_op jit(solution)/shard_map/all_to_all | solution.py:44

commit v5 on v4

--- a/solution.py
+++ b/solution.py
@@ -30,6 +30,7 @@
 groups_z4 = [
     [token_at(y, half + z, c) for z in range(4)] for half in (0, 4) for y in all_y for c in all_c
 ]
+pairs_c = [(token_at(y, z, c), token_at(y, z, 1 - c)) for y in all_y for z in all_z for c in all_c]
 groups_yc = [[token_at(y, z, c) for c in all_c for y in all_y] for z in all_z]
 pairs_z4 = [(token_at(y, z, c), token_at(y, z ^ 4, c)) for y in all_y for z in all_z for c in all_c]
 groups_x = [[head_at(x, z) for x in range(NX)] for z in range(NZH)]
@@ -98,20 +99,24 @@
     return lax.dot_general(iq, ik, (((1,), (1,)), ((), ())), preferred_element_type=f32)
 
 
-def logits_kernel(heads, scale, message_ref, ik_ref, out_ref):
+def logits_kernel(heads, scale, message_ref, ik_ref, *refs):
+    before, out_ref = refs[:-1], refs[-1]
     tokens = out_ref.shape[0]
-    iq, w = message_parts(message_ref, tokens, heads)
-    active = index_dot(iq, ik_ref[...])
-    logits = jnp.zeros(out_ref.shape, f32)
-    for j in range(heads):
-        here = active[j * tokens : (j + 1) * tokens] * scale
-        logits = logits + w[:, j : j + 1] * jnp.maximum(here, 0.0)
+    ik = ik_ref[...]
+    logits = before[0][...] if before else jnp.zeros(out_ref.shape, f32)
+    for part in range(message_ref.shape[0]):
+        iq, w = message_parts(message_ref.at[part], tokens, heads)
+        active = index_dot(iq, ik)
+        for j in range(heads):
+            here = active[j * tokens : (j + 1) * tokens] * scale
+            logits = logits + w[:, j : j + 1] * jnp.maximum(here, 0.0)
     out_ref[...] = logits
 
 
-def index_stats_kernel(limit_ref, one_ref, two_ref, logits_ref, stat_ref):
+def index_stats_kernel(heads, scale, message_ref, ik_ref, before_ref, limit_ref, logits_ref, stat_ref):
+    logits_kernel(heads, scale, message_ref, ik_ref, before_ref, logits_ref)
     key = lax.broadcasted_iota(jnp.int32, (1, logits_ref.shape[1]), 1)
-    logits = jnp.where(key <= limit_ref[...], one_ref[...] + two_ref[...], masked_value)
+    logits = jnp.where(key <= limit_ref[...], logits_ref[...], masked_value)
     m = jnp.max(logits, axis=1, keepdims=True)
     l = jnp.sum(jnp.exp(logits - m), axis=1, keepdims=True)
     logits_ref[...] = logits
@@ -141,10 +146,15 @@
         out_ref[b * NZ : (b + 1) * NZ] = jnp.sum(e.reshape(NZ, block // NZ, keys), axis=1)
 
 
-def dlogit_kernel(one_ref, two_ref, logits_ref, stats_ref, out_ref):
-    rows = logits_ref.shape[0]
+def dlogit_kernel(x_ref, one_ref, two_ref, logits_ref, stats_ref, out_ref):
+    rows = one_ref.shape[0]
+    first = pl.multiple_of(x_ref[0] * rows, rows)
     _, _, top, total = joined(stats_ref[...])
-    probs = jnp.exp(logits_ref[...] - as_column(top, rows)) / as_column(total, rows)
+    lane = lax.broadcasted_iota(jnp.int32, (rows, 128), 1)
+    mine = lane == lax.broadcasted_iota(jnp.int32, (rows, 128), 0) + first
+    top = jnp.sum(jnp.where(mine, top, 0.0), axis=1, keepdims=True)
+    total = jnp.sum(jnp.where(mine, total, 0.0), axis=1, keepdims=True)
+    probs = jnp.exp(logits_ref[pl.ds(first, rows), :] - top) / total
     dlogit = GRAD_SCALE * (probs - (one_ref[...] + two_ref[...]) / H)
     out_ref[...] = jnp.broadcast_to(dlogit[None], out_ref.shape)
 
@@ -152,25 +162,29 @@
 def grad_kernel(heads, scale, d_ref, message_ref, ik_ref, out_ref):
     dlogit = d_ref[...]
     tokens = dlogit.shape[0]
-    iq, w = message_parts(message_ref, tokens, heads)
+    parts = message_ref.shape[0]
     ik = ik_ref[...]
-    active = index_dot(iq, ik)
     row = lax.broadcasted_iota(jnp.int32, (tokens, 128), 0)
     place = row // NZ % NY * (NC * NZ) + row % NZ * NC + row // (NY * NZ)
     places = place == lax.broadcasted_iota(jnp.int32, (tokens, 128), 1)
-    out_ref[tokens * heads :, :] = jnp.zeros((out_ref.shape[0] - tokens * heads, 128), f32)
-    for j in range(heads):
-        here = active[j * tokens : (j + 1) * tokens]
-        gate = jnp.where(here > 0.0, dlogit * w[:, j : j + 1], 0.0).astype(bf16)
-        grad = jnp.dot(gate, ik, preferred_element_type=f32) * scale
-        for b in range(NYC):
-            first = b % NY * (NZ * NC) + b // NY
-            lines = pl.ds(first * heads + j, NZ, stride=NC * heads)
-            out_ref[lines, :] = grad[b * NZ : (b + 1) * NZ]
-        weight_grad = jnp.sum(dlogit * jnp.maximum(here * scale, 0.0), axis=1, keepdims=True)
-        out_ref[tokens * heads + j : tokens * heads + j + 1, :] = jnp.sum(
-            jnp.where(places, weight_grad, 0.0), axis=0, keepdims=True
-        )
+    weights = tokens * heads * parts
+    out_ref[weights:, :] = jnp.zeros((out_ref.shape[0] - weights, 128), f32)
+    for part in range(parts):
+        iq, w = message_parts(message_ref.at[part], tokens, heads)
+        active = index_dot(iq, ik)
+        for j in range(heads):
+            here = active[j * tokens : (j + 1) * tokens]
+            gate = jnp.where(here > 0.0, dlogit * w[:, j : j + 1], 0.0).astype(bf16)
+            grad = jnp.dot(gate, ik, preferred_element_type=f32) * scale
+            head = part * heads + j
+            for b in range(NYC):
+                first = b % NY * (NZ * NC) + b // NY
+                lines = pl.ds(first * heads * parts + head, NZ, stride=NC * heads * parts)
+                out_ref[lines, :] = grad[b * NZ : (b + 1) * NZ]
+            weight_grad = jnp.sum(dlogit * jnp.maximum(here * scale, 0.0), axis=1, keepdims=True)
+            out_ref[weights + head : weights + head + 1, :] = jnp.sum(
+                jnp.where(places, weight_grad, 0.0), axis=0, keepdims=True
+            )
 
 
 def key_kernel(heads, scale, d_ref, ik_ref, *refs):
@@ -203,14 +217,6 @@
     return jnp.moveaxis(value.reshape(NY, NZ, NC, *value.shape[1:]), 2, 0).reshape(value.shape)
 
 
-def x_scatter_sum(parts, x):
-    total = lax.dynamic_index_in_dim(parts, x, 0, keepdims=False)
-    for flip in range(1, NX):
-        piece = lax.dynamic_index_in_dim(parts, x ^ flip, 0, keepdims=False)
-        total = total + lax.ppermute(piece, "heads", pairs_x(flip))
-    return total
-
-
 def local(queries, latent_keys, index_queries, index_keys, index_weights, positions):
     heads_here, width = queries.shape[0], queries.shape[2]
     key_count = latent_keys.shape[0]
@@ -219,6 +225,7 @@
     share_rows = query_count // NX
     shape = jax.ShapeDtypeStruct
     x = lax.axis_index("heads") // NZH
+    core = lax.axis_index("tokens") % NC
     limit = in_order(positions - lax.axis_index("tokens") * key_count)
 
     along_z = gathered(queries.reshape(heads_here, width), "tokens", groups_z)
@@ -226,29 +233,35 @@
     high = lax.reduce_precision(index_weights, 8, 7)
     middle = lax.reduce_precision(index_weights - high, 8, 7)
     low = index_weights - high - middle
-    lines = in_order(jnp.concatenate([high, middle, low], axis=1))
-    lines = jnp.pad(lines, ((0, 0), (0, 128 - 3 * index_heads)))
+    half = index_heads // NC
+    lines = jnp.stack([high, middle, low], axis=1).reshape(query_count, 3, NC, half)
+    lines = in_order(lines.transpose(0, 2, 1, 3).reshape(query_count, NC, 3 * half))
+    lines = jnp.pad(lines.transpose(1, 0, 2), ((0, 0), (0, 0), (0, 128 - 3 * half)))
     by_head = in_order(index_queries).transpose(1, 0, 2)
-    by_head = by_head.reshape(index_heads * query_count, index_width)
-    mine = jnp.concatenate([by_head, lines.astype(bf16)])
-
-    index_flops = 2 * query_count * index_heads * key_count * index_width
-    partial = call(
-        lambda *refs: logits_kernel(index_heads, index_scale, *refs),
-        shape((query_count, key_count), f32),
-        flops=index_flops,
+    by_head = by_head.reshape(NC, half * query_count, index_width)
+    mine = jnp.concatenate([by_head, lines.astype(bf16)], axis=1)
+
+    first = lax.ppermute(lax.dynamic_index_in_dim(mine, core, 0), "heads", pairs_zh)
+    second = lax.ppermute(first, "tokens", pairs_c)
+    four = jnp.concatenate([mine, first, second])
+    messages = [four] + [lax.ppermute(four, "heads", pairs_x(flip)) for flip in range(1, NX)]
+
+    index_flops = 2 * query_count * half * key_count * index_width
+    logits = None
+    for message in messages[:-1]:
+        logits = call(
+            lambda *refs: logits_kernel(half, index_scale, *refs),
+            shape((query_count, key_count), f32),
+            flops=4 * index_flops,
+            moved=1 << 20,
+        )(message, index_keys, *([] if logits is None else [logits]))
+    logits, index_stats = call(
+        lambda *refs: index_stats_kernel(half, index_scale, *refs),
+        (shape((query_count, key_count), f32), shape((8, 128), f32)),
+        flops=80 * index_flops,
         moved=1 << 20,
-    )(mine, index_keys)
-    over_x = x_scatter_sum(partial.reshape(NX, share_rows, key_count), x)
-    along_z, over_x = lax.optimization_barrier((along_z, over_x))
-    other = lax.ppermute(over_x, "heads", pairs_zh)
+    )(messages[-1], index_keys, logits, limit[:, None])
     rows = gathered(along_z, "tokens", groups_yc).reshape(-1, width)
-    rows, other = lax.optimization_barrier((rows, other))
-    share_limit = lax.dynamic_slice_in_dim(limit, x * share_rows, share_rows, 0)
-    logits, index_stats = call(
-        index_stats_kernel,
-        (shape((share_rows, key_count), f32), shape((8, 128), f32)),
-    )(share_limit[:, None], over_x, other)
 
     row_count = rows.shape[0]
     lines_shape = shape((NYC, row_count // NYC), f32)
@@ -262,8 +275,6 @@
     stats = jnp.concatenate([local_max, local_total, index_stats])
     stats = gathered(stats, "tokens", groups_z)
     stats = call(join_kernel, shape((NYC, *stats.shape[1:]), f32))(stats)
-    stats, sent = lax.optimization_barrier((stats, mine))
-    swapped = lax.ppermute(sent, "heads", pairs_zh)
     stats = exchanged(stats, "tokens", groups_yc)
 
     partial = call(target_kernel, shape((query_count, key_count), f32), moved=5 << 20)(
@@ -271,26 +282,21 @@
     )
     over_x = exchanged(partial.reshape(NX, share_rows, key_count), "heads", groups_x).sum(axis=0)
     other = lax.ppermute(over_x, "heads", pairs_zh)
-    other, swapped = lax.optimization_barrier((other, swapped))
-    pair = jnp.stack([mine, swapped])
-    messages = [pair] + [lax.ppermute(pair, "heads", pairs_x(flip)) for flip in range(1, NX)]
     dlogit = call(dlogit_kernel, shape((NX, share_rows, key_count), f32))(
-        over_x, other, logits, stats
+        x.reshape(1), over_x, other, logits, stats
     )
     dlogit = exchanged(dlogit, "heads", groups_x).reshape(query_count, key_count)
-    dlogit, messages[1] = lax.optimization_barrier((dlogit, messages[1]))
 
     query_lines = query_count * index_heads
     piece_rows = -(-(query_lines + index_heads) // (NYC * 8)) * 8
     both = call(
-        lambda *refs: grad_kernel(index_heads, index_scale, *refs),
+        lambda *refs: grad_kernel(half, index_scale, *refs),
         shape((piece_rows * NYC, 128), f32),
-        flops=2 * index_flops,
+        flops=4 * index_flops,
         moved=2 << 20,
     )(dlogit, mine, index_keys)
 
     piece = exchanged(both.reshape(NYC, piece_rows, 128), "tokens", groups_yc)
-    piece, messages[2] = lax.optimization_barrier((piece, messages[2]))
     piece = call(sum_kernel, shape((NZ // 2, piece_rows, 128), f32))(piece)
     piece = exchanged(piece, "tokens", groups_z4).sum(axis=0)
     other = lax.ppermute(piece, "tokens", pairs_z4)
@@ -300,9 +306,9 @@
     weight_grad = both[query_lines : query_lines + index_heads, :query_count].T
 
     key_grad = call(
-        lambda *refs: key_kernel(index_heads, index_scale, *refs),
+        lambda *refs: key_kernel(half, index_scale, *refs),
         shape((key_count, index_width), f32),
-        flops=2 * index_flops * NX * NZH,
+        flops=4 * index_flops * NX * NZH,
         moved=3 << 20,
     )(dlogit, index_keys, *messages)
     return (query_grad, weight_grad, key_grad)

time: 192 us -> 192 us (level)
  blocking collectives: 30.7 us -> 66.4 us
  starting transfers between devices: 90 us -> 60 us
  waiting for transfers between devices: 47.7 us -> 38.3 us
  Pallas kernels: 13.2 us -> 17.7 us
    all_to_all x2 -> x5, blocking collectives: 30.7 us -> 66.4 us  [exchanged(): lax.all_to_all(parts, axis, 0, 0, tiled=True, axis_index_groups=groups)]
    all_to_all x7 -> x4, starting transfers between devices: 46.6 us -> 28.4 us  [exchanged(): lax.all_to_all(parts, axis, 0, 0, tiled=True, axis_index_groups=groups)]
    all_to_all x7 -> x4, waiting for transfers between devices: 17.4 us -> 5.48 us  [exchanged(): lax.all_to_all(parts, axis, 0, 0, tiled=True, axis_index_groups=groups)]
    ppermute x2 -> x1, starting transfers between devices: 14 us -> 7.95 us  [local(): other = lax.ppermute(over_x, 'heads', pairs_zh)]
    pallas_call x4 -> x6, Pallas kernels: 7.16 us -> 13 us  [the longest x1 7.25 us: local(): call(lambda *refs: key_kernel(half, index_scale, *refs), shape((key_count...]
    ppermute x7 -> x5, starting transfers between devices: 27.5 us -> 21.7 us  [the longest x3 9.72 us: local(): lax.ppermute(four, 'heads', pairs_x(flip))]
    ppermute x7 -> x5, waiting for transfers between devices: 15.9 us -> 19.9 us  [the longest x3 13.8 us: local(): lax.ppermute(four, 'heads', pairs_x(flip))]
    ppermute x2 -> x1, waiting for transfers between devices: 7.83 us -> 5.77 us  [local(): other = lax.ppermute(over_x, 'heads', pairs_zh)]
  transfers between devices with their start and end apart: 17 -> 11, of which waited for: 11 -> 6; matrix products, arithmetic and copies ran while one was open for 1% -> 2% of each run, Pallas kernels for 4% -> 6%
where the time goes in v5:
time: 192 us; the launch traced here: 191 us
  blocking collectives  66.4 us (35%)
  starting transfers between devices  60 us (31%)
  waiting for transfers between devices  38.3 us (20%)
  Pallas kernels  17.7 us (9%)
  local copies, waits for them, and re-layouts  7.17 us (4%)
    all_to_all x5, blocking collectives, exchanged(): lax.all_to_all(parts, axis, 0, 0, tiled=True, axis_index_groups=groups)  66.4 us
    all_to_all x4, starting transfers between devices, exchanged(): lax.all_to_all(parts, axis, 0, 0, tiled=True, axis_index_groups=groups)  28.4 us
    ppermute x3, waiting for transfers between devices, local(): lax.ppermute(four, 'heads', pairs_x(flip))  13.8 us
    ppermute x3, starting transfers between devices, local(): lax.ppermute(four, 'heads', pairs_x(flip))  9.72 us
    ppermute x1, starting transfers between devices, local(): other = lax.ppermute(over_x, 'heads', pairs_zh)  7.95 us
    ppermute x1, starting transfers between devices, local(): lax.ppermute(lax.dynamic_index_in_dim(mine, core, 0), 'heads', pairs_zh)  7.94 us
    pallas_call x1, Pallas kernels, local(): call(lambda *refs: key_kernel(half, index_scale, *refs), shape((key_count...  7.25 us
    ppermute x1, waiting for transfers between devices, local(): other = lax.ppermute(piece, 'tokens', pairs_z4)  7.08 us
  transfers between devices with their start and end apart: 11, of which 6 were waited for; matrix products, arithmetic and copies ran while one was open for 2% of the time, Pallas kernels for 6%

profile of v5, /device:TPU:1, one launch (start us, length us, event | category | flops | bytes accessed | tf_op | source)
XLA Modules:
  0.0 191.2 jit_solution(13720805319155049464)
XLA Ops:
  0.6 1.4 broadcast_in_dim.24
  2.0 13.1 %all-to-all-start = ((bf16[8,16,576]{2,1,0:T(8,128)(2,1)}), bf16[8,16,576]{2,1,0:T(8,128)(2,1)S(1)}, u32[]{:S(2)}, u32[]{:S(2)}) async-start(bf16[8,16,576]{2,1,0:T(8,128)(2,1)} %broadcast_in_dim.24), calls=%async_computation | async-start | bytes 327680 | tf_op jit(solution)/shard_map/all_to_all | solution.py:45
  16.1 0.9 copy.24
  17.1 7.9 %collective-permute-start = (bf16[1,320,128]{2,1,0:T(8,128)(2,1)S(1)}, bf16[1,320,128]{2,1,0:T(8,128)(2,1)S(1)}, u32[]{:S(2)}, u32[]{:S(2)}) collective-permute-start(bf16[1,320,128]{2,1,0:T(8,128)(2,1)S(1)} %fusion), channel_id=1, source_target_pairs={{0,64},{64,0},{128,192},{192,128},{256,320},{320,256},{384,448},{4... | collective-permute-start | bytes 245768 | tf_op jit(solution)/shard_map/ppermute | solution.py:244
  25.1 6.2 %collective-permute-done = bf16[1,320,128]{2,1,0:T(8,128)(2,1)S(1)} collective-permute-done((bf16[1,320,128]{2,1,0:T(8,128)(2,1)S(1)}, bf16[1,320,128]{2,1,0:T(8,128)(2,1)S(1)}, u32[]{:S(2)}, u32[]{:S(2)}) %collective-permute-start) | collective-permute-done | bytes 81952 | tf_op jit(solution)/shard_map/ppermute | solution.py:244
  31.2 4.1 %collective-permute-start.1 = (bf16[1,320,128]{2,1,0:T(8,128)(2,1)S(1)}, bf16[1,320,128]{2,1,0:T(8,128)(2,1)S(1)}, u32[]{:S(2)}, u32[]{:S(2)}) collective-permute-start(bf16[1,320,128]{2,1,0:T(8,128)(2,1)S(1)} %collective-permute-done), channel_id=1, source_target_pairs={{0,1},{1,0},{2,3},{3,2},{4,5},{5,4},{6,7},{7,6},{8,9},{9,8},{10,11... | collective-permute-start | bytes 245768 | tf_op jit(solution)/shard_map/ppermute | solution.py:245
  35.3 1.2 broadcast_in_dim.25
  36.5 4.7 %all-to-all-start.1 = ((bf16[8,8,16,576]{3,2,1,0:T(8,128)(2,1)}), bf16[8,8,16,576]{3,2,1,0:T(8,128)(2,1)S(1)}, u32[]{:S(2)}, u32[]{:S(2)}) async-start(bf16[8,8,16,576]{3,2,1,0:T(8,128)(2,1)} %broadcast_in_dim.25), calls=%async_computation.1 | async-start | bytes 2621440 | tf_op jit(solution)/shard_map/all_to_all | solution.py:45
  41.3 3.3 %collective-permute-start.4 = (bf16[4,320,128]{2,1,0:T(8,128)(2,1)S(1)}, bf16[4,320,128]{2,1,0:T(8,128)(2,1)S(1)}, u32[]{:S(2)}, u32[]{:S(2)}) collective-permute-start(bf16[4,320,128]{2,1,0:T(8,128)(2,1)S(1)} %pad_maximum_fusion.refs_0_.refs_2_), channel_id=1, source_target_pairs={{0,128},{64,192},{128,0},{192,64},{256,384},{320,448},{384,256},{4... | collective-permute-start | bytes 983048 | tf_op jit(solution)/shard_map/ppermute | solution.py:247
  44.5 4.4 %collective-permute-start.3 = (bf16[4,320,128]{2,1,0:T(8,128)(2,1)S(1)}, bf16[4,320,128]{2,1,0:T(8,128)(2,1)S(1)}, u32[]{:S(2)}, u32[]{:S(2)}) collective-permute-start(bf16[4,320,128]{2,1,0:T(8,128)(2,1)S(1)} %pad_maximum_fusion.refs_0_.refs_2_), channel_id=1, source_target_pairs={{0,256},{64,320},{128,384},{192,448},{256,0},{320,64},{384,128},{4... | collective-permute-start | bytes 983048 | tf_op jit(solution)/shard_map/ppermute | solution.py:247
  48.9 2.1 %collective-permute-start.2 = (bf16[4,320,128]{2,1,0:T(8,128)(2,1)S(1)}, bf16[4,320,128]{2,1,0:T(8,128)(2,1)}, u32[]{:S(2)}, u32[]{:S(2)}) collective-permute-start(bf16[4,320,128]{2,1,0:T(8,128)(2,1)S(1)} %pad_maximum_fusion.refs_0_.refs_2_), channel_id=1, source_target_pairs={{0,384},{64,448},{128,256},{192,320},{256,128},{320,192},{384,0},{... | collective-permute-start | bytes 983048 | tf_op jit(solution)/shard_map/ppermute | solution.py:247
  52.7 0.9 shard_map.87.refs_2_
  53.6 8.3 %collective-permute-done.3.refs_0_.refs_4_ = bf16[4,320,128]{2,1,0:T(8,128)(2,1)S(1)} collective-permute-done((bf16[4,320,128]{2,1,0:T(8,128)(2,1)S(1)}, bf16[4,320,128]{2,1,0:T(8,128)(2,1)S(1)}, u32[]{:S(2)}, u32[]{:S(2)}) %collective-permute-start.3) | collective-permute-done | bytes 327712 | tf_op jit(solution)/shard_map/ppermute | solution.py:247
  61.9 0.9 shard_map.88.refs_2_
  62.8 5.5 %collective-permute-done.2.refs_0_.refs_5_ = bf16[4,320,128]{2,1,0:T(8,128)(2,1)} collective-permute-done((bf16[4,320,128]{2,1,0:T(8,128)(2,1)S(1)}, bf16[4,320,128]{2,1,0:T(8,128)(2,1)}, u32[]{:S(2)}, u32[]{:S(2)}) %collective-permute-start.2) | collective-permute-done | bytes 327712 | tf_op jit(solution)/shard_map/ppermute | solution.py:247
  68.3 2.0 %shard_map.89 = (f32[64,1024]{1,0:T(8,128)S(1)}, f32[8,128]{1,0:T(8,128)S(1)}) custom-call(bf16[4,320,128]{2,1,0:T(8,128)(2,1)} %collective-permute-done.2.refs_0_.refs_5_, bf16[1024,128]{1,0:T(8,128)(2,1)S(1)} %copy-done, f32[64,1024]{1,0:T(8,128)S(1)} %shard_map.88.refs_2_, s32[64,1]{1,0:T(8,128)S(1)} %broadcast_in_dim_reshape.10.refs_3_), custom_call_target="tpu_custom_call" | custom-call | flops 5368709120 | bytes 1048576 | tf_op jit(solution)/shard_map/pallas_call | solution.py:258
  70.3 1.3 copy-done.1
  71.5 2.3 %shard_map.85 = (f32[1024,1024]{1,0:T(8,128)S(1)}, f32[8,128]{1,0:T(8,128)S(1)}, f32[8,128]{1,0:T(8,128)S(1)}) custom-call(s32[1024,1]{1,0:T(8,128)S(1)} %broadcast_in_dim_reshape.9.limit_ref, bf16[1024,576]{1,0:T(8,128)(2,1)S(1)} %bitcast.30, bf16[576,1024]{1,0:T(8,128)(2,1)S(1)} %bitcast.35), custom_call_target="tpu_custom_call" | custom-call | flops 1207959552 | bytes 4194304 | tf_op jit(solution)/shard_map/pallas_call | solution.py:268
  73.9 22.4 %all_to_all.45.stats_ref = f32[8,24,128]{2,1,0:T(8,128)S(1)} all-to-all(f32[8,24,128]{2,1,0:T(8,128)S(1)} %broadcast_in_dim.26), channel_id=1, replica_groups={{0,2,4,6,8,10,12,14},{1,3,5,7,9,11,13,15},{16,18,20,22,24,26,28,30},{17..., dimensions={0} | all-to-all | bytes 196608 | tf_op jit(solution)/shard_map/all_to_all | solution.py:45
  96.3 11.5 %all_to_all.46.stats_ref = f32[8,24,128]{2,1,0:T(8,128)S(1)} all-to-all(f32[8,24,128]{2,1,0:T(8,128)S(1)} %shard_map.90), channel_id=1, replica_groups={{0,16,32,48,1,17,33,49},{2,18,34,50,3,19,35,51},{4,20,36,52,5,21,37,53}..., dimensions={0} | all-to-all | bytes 196608 | tf_op jit(solution)/shard_map/all_to_all | solution.py:45
  108.7 8.8 %all_to_all.47 = f32[4,16,1024]{2,1,0:T(8,128)S(1)} all-to-all(f32[4,16,1024]{2,1,0:T(8,128)S(1)} %bitcast.31), channel_id=1, replica_groups={{0,128,256,384},{64,192,320,448},{1,129,257,385},{65,193,321,449},{2,13..., dimensions={0} | all-to-all | bytes 524288 | tf_op jit(solution)/shard_map/all_to_all | solution.py:45
  117.5 7.9 %collective-permute-start.5 = (f32[16,1024]{1,0:T(8,128)S(1)}, f32[16,1024]{1,0:T(8,128)S(1)}, u32[]{:S(2)}, u32[]{:S(2)}) collective-permute-start(f32[16,1024]{1,0:T(8,128)S(1)} %reduce_sum.18.one_ref), channel_id=1, source_target_pairs={{0,64},{64,0},{128,192},{192,128},{256,320},{320,256},{384,448},{4... | collective-permute-start | bytes 196616 | tf_op jit(solution)/shard_map/ppermute | solution.py:284
  125.4 5.8 %collective-permute-done.5.two_ref = f32[16,1024]{1,0:T(8,128)S(1)} collective-permute-done((f32[16,1024]{1,0:T(8,128)S(1)}, f32[16,1024]{1,0:T(8,128)S(1)}, u32[]{:S(2)}, u32[]{:S(2)}) %collective-permute-start.5) | collective-permute-done | bytes 65568 | tf_op jit(solution)/shard_map/ppermute | solution.py:284
  132.0 3.4 %all-to-all-start.5 = ((f32[4,16,1024]{2,1,0:T(8,128)}), f32[4,16,1024]{2,1,0:T(8,128)S(1)}, u32[]{:S(2)}, u32[]{:S(2)}) async-start(f32[4,16,1024]{2,1,0:T(8,128)} %shard_map.92), calls=%async_computation.5 | async-start | bytes 524288 | tf_op jit(solution)/shard_map/all_to_all | solution.py:45
  135.5 5.5 %all-to-all-done.5 = f32[4,16,1024]{2,1,0:T(8,128)S(1)} async-done(((f32[4,16,1024]{2,1,0:T(8,128)}), f32[4,16,1024]{2,1,0:T(8,128)S(1)}, u32[]{:S(2)}, u32[]{:S(2)}) %all-to-all-start.5) | async-done | bytes 262176 | tf_op jit(solution)/shard_map/all_to_all | solution.py:45
  141.0 1.1 shard_map.93
  142.0 14.5 %all_to_all.48.parts_ref = f32[8,72,128]{2,1,0:T(8,128)S(1)} all-to-all(f32[8,72,128]{2,1,0:T(8,128)S(1)} %bitcast.32), channel_id=1, replica_groups={{0,16,32,48,1,17,33,49},{2,18,34,50,3,19,35,51},{4,20,36,52,5,21,37,53}..., dimensions={0} | all-to-all | bytes 589824 | tf_op jit(solution)/shard_map/all_to_all | solution.py:45
  156.5 9.2 %all_to_all.49 = f32[4,72,128]{2,1,0:T(8,128)S(1)} all-to-all(f32[4,72,128]{2,1,0:T(8,128)S(1)} %shard_map.94), channel_id=1, replica_groups={{0,2,4,6},{1,3,5,7},{16,18,20,22},{17,19,21,23},{32,34,36,38},{33,35,37..., dimensions={0} | all-to-all | bytes 294912 | tf_op jit(solution)/shard_map/all_to_all | solution.py:45
  165.7 1.9 %collective-permute-start.6 = (f32[72,128]{1,0:T(8,128)S(1)}, f32[72,128]{1,0:T(8,128)S(1)}, u32[]{:S(2)}, u32[]{:S(2)}) collective-permute-start(f32[72,128]{1,0:T(8,128)S(1)} %reduce_sum.19.one_ref), channel_id=1, source_target_pairs={{0,8},{1,9},{2,10},{3,11},{4,12},{5,13},{6,14},{7,15},{8,0},{9,1},... | collective-permute-start | bytes 110600 | tf_op jit(solution)/shard_map/ppermute | solution.py:302
  167.6 7.1 %collective-permute-done.6.two_ref = f32[72,128]{1,0:T(8,128)S(1)} collective-permute-done((f32[72,128]{1,0:T(8,128)S(1)}, f32[72,128]{1,0:T(8,128)S(1)}, u32[]{:S(2)}, u32[]{:S(2)}) %collective-permute-start.6) | collective-permute-done | bytes 36896 | tf_op jit(solution)/shard_map/ppermute | solution.py:302
  175.4 7.2 %all-to-all-start.8 = ((f32[8,72,128]{2,1,0:T(8,128)}), f32[8,72,128]{2,1,0:T(8,128)S(1)}, u32[]{:S(2)}, u32[]{:S(2)}) async-start(f32[8,72,128]{2,1,0:T(8,128)} %shard_map.95), calls=%async_computation.8 | async-start | bytes 589824 | tf_op jit(solution)/shard_map/all_to_all | solution.py:45
  182.6 7.2 %shard_map.96 = f32[1024,128]{1,0:T(8,128)} custom-call(f32[64,1024]{1,0:T(8,128)S(1)} %bitcast.34, bf16[1024,128]{1,0:T(8,128)(2,1)S(1)} %copy-done, bf16[4,320,128]{2,1,0:T(8,128)(2,1)S(1)} %pad_maximum_fusion.refs_0_.refs_2_, bf16[4,320,128]{2,1,0:T(8,128)(2,1)S(1)} %collective-permute-done.4.refs_0_.refs_3_, ...), custom_call_target="tpu_custom_call" | custom-call | flops 2147483648 | bytes 3145728 | tf_op jit(solution)/shard_map/pallas_call | solution.py:308
  (38 shorter events, 6.5 us)
Async XLA Ops:
  2.0 33.3 %all-to-all-start = ((bf16[8,16,576]{2,1,0:T(8,128)(2,1)}), bf16[8,16,576]{2,1,0:T(8,128)(2,1)S(1)}, u32[]{:S(2)}, u32[]{:S(2)}) async-start(bf16[8,16,576]{2,1,0:T(8,128)(2,1)} %broadcast_in_dim.24), calls=%async_computation | async-start | bytes 327680 | tf_op jit(solution)/shard_map/all_to_all | solution.py:45
  17.1 14.1 %collective-permute-start = (bf16[1,320,128]{2,1,0:T(8,128)(2,1)S(1)}, bf16[1,320,128]{2,1,0:T(8,128)(2,1)S(1)}, u32[]{:S(2)}, u32[]{:S(2)}) collective-permute-start(bf16[1,320,128]{2,1,0:T(8,128)(2,1)S(1)} %fusion), channel_id=1, source_target_pairs={{0,64},{64,0},{128,192},{192,128},{256,320},{320,256},{384,448},{4... | collective-permute-start | bytes 245768 | tf_op jit(solution)/shard_map/ppermute | solution.py:244
  31.2 10.0 %collective-permute-start.1 = (bf16[1,320,128]{2,1,0:T(8,128)(2,1)S(1)}, bf16[1,320,128]{2,1,0:T(8,128)(2,1)S(1)}, u32[]{:S(2)}, u32[]{:S(2)}) collective-permute-start(bf16[1,320,128]{2,1,0:T(8,128)(2,1)S(1)} %collective-permute-done), channel_id=1, source_target_pairs={{0,1},{1,0},{2,3},{3,2},{4,5},{5,4},{6,7},{7,6},{8,9},{9,8},{10,11... | collective-permute-start | bytes 245768 | tf_op jit(solution)/shard_map/ppermute | solution.py:245
  36.5 14.5 %copy-start.2 = (s32[64]{0:T(128)S(1)}, s32[64]{0:T(128)}, u32[]{:S(2)}) copy-start(s32[64]{0:T(128)} %param.11) | copy-start | bytes 772
  36.5 33.7 %all-to-all-start.1 = ((bf16[8,8,16,576]{3,2,1,0:T(8,128)(2,1)}), bf16[8,8,16,576]{3,2,1,0:T(8,128)(2,1)S(1)}, u32[]{:S(2)}, u32[]{:S(2)}) async-start(bf16[8,8,16,576]{3,2,1,0:T(8,128)(2,1)} %broadcast_in_dim.25), calls=%async_computation.1 | async-start | bytes 2621440 | tf_op jit(solution)/shard_map/all_to_all | solution.py:45
  41.2 10.6 %copy-start = (bf16[1024,128]{1,0:T(8,128)(2,1)S(1)}, bf16[1024,128]{1,0:T(8,128)(2,1)}, u32[]{:S(2)}) copy-start(bf16[1024,128]{1,0:T(8,128)(2,1)} %refs_1_.9) | copy-start | bytes 786436
  41.3 11.4 %collective-permute-start.4 = (bf16[4,320,128]{2,1,0:T(8,128)(2,1)S(1)}, bf16[4,320,128]{2,1,0:T(8,128)(2,1)S(1)}, u32[]{:S(2)}, u32[]{:S(2)}) collective-permute-start(bf16[4,320,128]{2,1,0:T(8,128)(2,1)S(1)} %pad_maximum_fusion.refs_0_.refs_2_), channel_id=1, source_target_pairs={{0,128},{64,192},{128,0},{192,64},{256,384},{320,448},{384,256},{4... | collective-permute-start | bytes 983048 | tf_op jit(solution)/shard_map/ppermute | solution.py:247
  44.5 17.4 %collective-permute-start.3 = (bf16[4,320,128]{2,1,0:T(8,128)(2,1)S(1)}, bf16[4,320,128]{2,1,0:T(8,128)(2,1)S(1)}, u32[]{:S(2)}, u32[]{:S(2)}) collective-permute-start(bf16[4,320,128]{2,1,0:T(8,128)(2,1)S(1)} %pad_maximum_fusion.refs_0_.refs_2_), channel_id=1, source_target_pairs={{0,256},{64,320},{128,384},{192,448},{256,0},{320,64},{384,128},{4... | collective-permute-start | bytes 983048 | tf_op jit(solution)/shard_map/ppermute | solution.py:247
  48.9 19.3 %collective-permute-start.2 = (bf16[4,320,128]{2,1,0:T(8,128)(2,1)S(1)}, bf16[4,320,128]{2,1,0:T(8,128)(2,1)}, u32[]{:S(2)}, u32[]{:S(2)}) collective-permute-start(bf16[4,320,128]{2,1,0:T(8,128)(2,1)S(1)} %pad_maximum_fusion.refs_0_.refs_2_), channel_id=1, source_target_pairs={{0,384},{64,448},{128,256},{192,320},{256,128},{320,192},{384,0},{... | collective-permute-start | bytes 983048 | tf_op jit(solution)/shard_map/ppermute | solution.py:247
  70.3 1.3 copy-start.1
  117.5 13.7 %collective-permute-start.5 = (f32[16,1024]{1,0:T(8,128)S(1)}, f32[16,1024]{1,0:T(8,128)S(1)}, u32[]{:S(2)}, u32[]{:S(2)}) collective-permute-start(f32[16,1024]{1,0:T(8,128)S(1)} %reduce_sum.18.one_ref), channel_id=1, source_target_pairs={{0,64},{64,0},{128,192},{192,128},{256,320},{320,256},{384,448},{4... | collective-permute-start | bytes 196616 | tf_op jit(solution)/shard_map/ppermute | solution.py:284
  132.0 8.9 %all-to-all-start.5 = ((f32[4,16,1024]{2,1,0:T(8,128)}), f32[4,16,1024]{2,1,0:T(8,128)S(1)}, u32[]{:S(2)}, u32[]{:S(2)}) async-start(f32[4,16,1024]{2,1,0:T(8,128)} %shard_map.92), calls=%async_computation.5 | async-start | bytes 524288 | tf_op jit(solution)/shard_map/all_to_all | solution.py:45
  165.7 9.0 %collective-permute-start.6 = (f32[72,128]{1,0:T(8,128)S(1)}, f32[72,128]{1,0:T(8,128)S(1)}, u32[]{:S(2)}, u32[]{:S(2)}) collective-permute-start(f32[72,128]{1,0:T(8,128)S(1)} %reduce_sum.19.one_ref), channel_id=1, source_target_pairs={{0,8},{1,9},{2,10},{3,11},{4,12},{5,13},{6,14},{7,15},{8,0},{9,1},... | collective-permute-start | bytes 110600 | tf_op jit(solution)/shard_map/ppermute | solution.py:302
  175.4 14.5 %all-to-all-start.8 = ((f32[8,72,128]{2,1,0:T(8,128)}), f32[8,72,128]{2,1,0:T(8,128)S(1)}, u32[]{:S(2)}, u32[]{:S(2)}) async-start(f32[8,72,128]{2,1,0:T(8,128)} %shard_map.95), calls=%async_computation.8 | async-start | bytes 589824 | tf_op jit(solution)/shard_map/all_to_all | solution.py:45

commit v6 on v4

--- a/solution.py
+++ b/solution.py
@@ -11,6 +11,7 @@
 NYC = NY * NC
 GRAD_SCALE = 8192.0
 VMEM = 12 << 20
+WEIGHT = 160
 
 softmax_scale = 192.0 ** (-0.5)
 masked_value = -1e30
@@ -30,6 +31,8 @@
 groups_z4 = [
     [token_at(y, half + z, c) for z in range(4)] for half in (0, 4) for y in all_y for c in all_c
 ]
+pairs_c = [(token_at(y, z, c), token_at(y, z, 1 - c)) for y in all_y for z in all_z for c in all_c]
+groups_y = [[token_at(y, z, c) for y in all_y] for z in all_z for c in all_c]
 groups_yc = [[token_at(y, z, c) for c in all_c for y in all_y] for z in all_z]
 pairs_z4 = [(token_at(y, z, c), token_at(y, z ^ 4, c)) for y in all_y for z in all_z for c in all_c]
 groups_x = [[head_at(x, z) for x in range(NX)] for z in range(NZH)]
@@ -63,29 +66,32 @@
     return jnp.sum(jnp.where(diagonal(rows, row.shape[1]), row, 0.0), axis=1, keepdims=True)
 
 
-def call(kernel, out_shape, flops=0, moved=0):
+def call(kernel, out_shape, flops=0, moved=0, aliases={}):
     return pl.pallas_call(
         kernel,
         out_shape=out_shape,
+        input_output_aliases=aliases,
         compiler_params=pltpu.CompilerParams(vmem_limit_bytes=VMEM),
         cost_estimate=pl.CostEstimate(flops=flops, bytes_accessed=moved, transcendentals=0),
     )
 
 
-def score_kernel(limit_ref, q_ref, k_ref, e_ref, m_ref, l_ref):
-    rows, keys = e_ref.shape
-    block = rows // NYC
-    key = lax.broadcasted_iota(jnp.int32, (1, keys), 1)
+def score_kernel(core_ref, limit_ref, q_ref, k_ref, *refs):
+    e_ref, m_ref, l_ref = refs[-3:]
+    block = e_ref.shape[0] // NYC
+    key = lax.broadcasted_iota(jnp.int32, (1, e_ref.shape[1]), 1)
     k = k_ref[...]
-    for b in range(NYC):
-        lines = slice(b * block, (b + 1) * block)
-        s = jnp.dot(q_ref[lines], k, preferred_element_type=f32) * softmax_scale
-        s = jnp.where(key <= limit_ref[lines], s, masked_value)
+    core = core_ref[0]
+    for y in range(NY):
+        line = core * NY + y
+        lines = pl.ds(pl.multiple_of(line * block, block), block)
+        s = jnp.dot(q_ref[y * block : (y + 1) * block], k, preferred_element_type=f32)
+        s = jnp.where(key <= limit_ref[lines], s * softmax_scale, masked_value)
         m = jnp.max(s, axis=1, keepdims=True)
         e = jnp.exp(s - m)
         e_ref[lines] = e
-        m_ref[b : b + 1] = as_row(m)
-        l_ref[b : b + 1] = as_row(jnp.sum(e, axis=1, keepdims=True))
+        m_ref[pl.ds(line, 1)] = as_row(m)
+        l_ref[pl.ds(line, 1)] = as_row(jnp.sum(e, axis=1, keepdims=True))
 
 
 def message_parts(ref, tokens, heads):
@@ -219,6 +225,7 @@
     share_rows = query_count // NX
     shape = jax.ShapeDtypeStruct
     x = lax.axis_index("heads") // NZH
+    core = lax.axis_index("tokens") % NC
     limit = in_order(positions - lax.axis_index("tokens") * key_count)
 
     along_z = gathered(queries.reshape(heads_here, width), "tokens", groups_z)
@@ -240,45 +247,61 @@
         moved=1 << 20,
     )(mine, index_keys)
     over_x = x_scatter_sum(partial.reshape(NX, share_rows, key_count), x)
-    along_z, over_x = lax.optimization_barrier((along_z, over_x))
     other = lax.ppermute(over_x, "heads", pairs_zh)
-    rows = gathered(along_z, "tokens", groups_yc).reshape(-1, width)
-    rows, other = lax.optimization_barrier((rows, other))
     share_limit = lax.dynamic_slice_in_dim(limit, x * share_rows, share_rows, 0)
     logits, index_stats = call(
         index_stats_kernel,
         (shape((share_rows, key_count), f32), shape((8, 128), f32)),
+        flops=WEIGHT * index_flops,
+        moved=1 << 20,
     )(share_limit[:, None], over_x, other)
 
-    row_count = rows.shape[0]
+    rows = gathered(along_z, "tokens", groups_y)
+    other_rows = lax.ppermute(rows, "tokens", pairs_c)
+    row_count = NC * rows.size // width
+    row_limit = jnp.repeat(limit, heads_here)[:, None]
     lines_shape = shape((NYC, row_count // NYC), f32)
-    exponent, local_max, local_total = call(
-        score_kernel,
-        (shape((row_count, key_count), f32), lines_shape, lines_shape),
-        flops=2 * row_count * key_count * width,
-        moved=4 << 20,
-    )(jnp.repeat(limit, heads_here)[:, None], rows, latent_keys.T)
+    scored = ()
+    for where, part in ((core, rows), (1 - core, other_rows)):
+        scored = call(
+            score_kernel,
+            (shape((row_count, key_count), f32), lines_shape, lines_shape),
+            flops=row_count * key_count * width,
+            moved=4 << 20,
+            aliases={4 + i: i for i in range(len(scored))},
+        )(where.reshape(1), row_limit, part.reshape(-1, width), latent_keys.T, *scored)
+    exponent, local_max, local_total = scored
 
     stats = jnp.concatenate([local_max, local_total, index_stats])
+
     stats = gathered(stats, "tokens", groups_z)
     stats = call(join_kernel, shape((NYC, *stats.shape[1:]), f32))(stats)
-    stats, sent = lax.optimization_barrier((stats, mine))
-    swapped = lax.ppermute(sent, "heads", pairs_zh)
     stats = exchanged(stats, "tokens", groups_yc)
 
     partial = call(target_kernel, shape((query_count, key_count), f32), moved=5 << 20)(
         stats, local_max, exponent
     )
+
+    mine_rows = mine.shape[0] // NC
+    partial, late = lax.optimization_barrier((partial, mine))
+    sent = lax.dynamic_slice_in_dim(late, core * mine_rows, mine_rows, 0)
+    swapped = lax.ppermute(sent, "heads", pairs_zh)
     over_x = exchanged(partial.reshape(NX, share_rows, key_count), "heads", groups_x).sum(axis=0)
     other = lax.ppermute(over_x, "heads", pairs_zh)
     other, swapped = lax.optimization_barrier((other, swapped))
-    pair = jnp.stack([mine, swapped])
-    messages = [pair] + [lax.ppermute(pair, "heads", pairs_x(flip)) for flip in range(1, NX)]
+    swapped_other = lax.ppermute(swapped, "tokens", pairs_c)
     dlogit = call(dlogit_kernel, shape((NX, share_rows, key_count), f32))(
         over_x, other, logits, stats
     )
     dlogit = exchanged(dlogit, "heads", groups_x).reshape(query_count, key_count)
-    dlogit, messages[1] = lax.optimization_barrier((dlogit, messages[1]))
+    dlogit, swapped_other = lax.optimization_barrier((dlogit, swapped_other))
+    halves = jnp.where(
+        core == 0,
+        jnp.concatenate([swapped, swapped_other]),
+        jnp.concatenate([swapped_other, swapped]),
+    )
+    pair = jnp.stack([mine, halves])
+    messages = [pair] + [lax.ppermute(pair, "heads", pairs_x(flip)) for flip in range(1, NX)]
 
     query_lines = query_count * index_heads
     piece_rows = -(-(query_lines + index_heads) // (NYC * 8)) * 8
@@ -290,7 +313,6 @@
     )(dlogit, mine, index_keys)
 
     piece = exchanged(both.reshape(NYC, piece_rows, 128), "tokens", groups_yc)
-    piece, messages[2] = lax.optimization_barrier((piece, messages[2]))
     piece = call(sum_kernel, shape((NZ // 2, piece_rows, 128), f32))(piece)
     piece = exchanged(piece, "tokens", groups_z4).sum(axis=0)
     other = lax.ppermute(piece, "tokens", pairs_z4)

time: 192 us -> 176 us (0.917)
  waiting for transfers between devices: 47.7 us -> 16.8 us
  blocking collectives: 30.7 us -> 47.9 us
    all_to_all x2 -> x3, blocking collectives: 30.7 us -> 47.9 us  [exchanged(): lax.all_to_all(parts, axis, 0, 0, tiled=True, axis_index_groups=groups)]
    all_to_all x7 -> x6, waiting for transfers between devices: 17.4 us -> 2.17 us  [exchanged(): lax.all_to_all(parts, axis, 0, 0, tiled=True, axis_index_groups=groups)]
    all_to_all x7 -> x6, starting transfers between devices: 46.6 us -> 34 us  [exchanged(): lax.all_to_all(parts, axis, 0, 0, tiled=True, axis_index_groups=groups)]
    ppermute x0 -> x2, starting transfers between devices: none -> 11.1 us  [the longest x1 6.28 us: local(): swapped_other = lax.ppermute(swapped, 'tokens', pairs_c)]
    ppermute x1, waiting for transfers between devices: 11.9 us -> 3 us  [local(): swapped = lax.ppermute(sent, 'heads', pairs_zh)]
    ppermute x3, waiting for transfers between devices: 3.93 us -> 0.01 us  [x_scatter_sum(): total = total + lax.ppermute(piece, 'heads', pairs_x(flip))]
    ppermute x1, waiting for transfers between devices: 6.68 us -> 4.43 us  [local(): other = lax.ppermute(piece, 'tokens', pairs_z4)]
    ppermute x1, starting transfers between devices: 1.92 us -> 4.17 us  [local(): other = lax.ppermute(piece, 'tokens', pairs_z4)]
  transfers between devices with their start and end apart: 17 -> 18, of which waited for: 11 -> 6; matrix products, arithmetic and copies ran while one was open for 1% -> 2% of each run, Pallas kernels for 4% -> 4%
where the time goes in v6:
time: 176 us; the launch traced here: 175 us
  starting transfers between devices  89.3 us (51%)
  blocking collectives  47.9 us (27%)
  waiting for transfers between devices  16.8 us (10%)
  Pallas kernels  12.9 us (7%)
  local copies, waits for them, and re-layouts  6.5 us (4%)
    all_to_all x3, blocking collectives, exchanged(): lax.all_to_all(parts, axis, 0, 0, tiled=True, axis_index_groups=groups)  47.9 us
    all_to_all x6, starting transfers between devices, exchanged(): lax.all_to_all(parts, axis, 0, 0, tiled=True, axis_index_groups=groups)  34 us
    ppermute x2, starting transfers between devices, local(): other = lax.ppermute(over_x, 'heads', pairs_zh)  14 us
    ppermute x3, starting transfers between devices, x_scatter_sum(): total = total + lax.ppermute(piece, 'heads', pairs_x(flip))  9.58 us
    ppermute x3, starting transfers between devices, local(): lax.ppermute(pair, 'heads', pairs_x(flip))  8.41 us
    ppermute x1, starting transfers between devices, local(): swapped = lax.ppermute(sent, 'heads', pairs_zh)  7.94 us
    ppermute x1, starting transfers between devices, local(): swapped_other = lax.ppermute(swapped, 'tokens', pairs_c)  6.28 us
    ppermute x2, waiting for transfers between devices, local(): other = lax.ppermute(over_x, 'heads', pairs_zh)  6.24 us
  transfers between devices with their start and end apart: 18, of which 6 were waited for; matrix products, arithmetic and copies ran while one was open for 2% of the time, Pallas kernels for 4%

profile of v6, /device:TPU:1, one launch (start us, length us, event | category | flops | bytes accessed | tf_op | source)
XLA Modules:
  0.0 175.2 jit_solution(2769800448060692559)
XLA Ops:
  0.6 1.4 broadcast_in_dim.27
  2.1 13.1 %all-to-all-start = ((bf16[8,16,576]{2,1,0:T(8,128)(2,1)}), bf16[8,16,576]{2,1,0:T(8,128)(2,1)S(1)}, u32[]{:S(2)}, u32[]{:S(2)}) async-start(bf16[8,16,576]{2,1,0:T(8,128)(2,1)} %broadcast_in_dim.27), calls=%async_computation | async-start | bytes 327680 | tf_op jit(solution)/shard_map/all_to_all | solution.py:47
  15.9 0.9 copy.27
  18.4 3.1 %collective-permute-start.1 = (f32[16,1024]{1,0:T(8,128)S(1)}, f32[16,1024]{1,0:T(8,128)S(1)}, u32[]{:S(2)}, u32[]{:S(2)}) collective-permute-start(f32[16,1024]{1,0:T(8,128)S(1)} %get-tuple-element.31), channel_id=1, source_target_pairs={{0,128},{64,192},{128,0},{192,64},{256,384},{320,448},{384,256},{4... | collective-permute-start | bytes 196616 | tf_op jit(solution)/shard_map/ppermute | solution.py:216
  21.5 4.4 %collective-permute-start.2 = (f32[16,1024]{1,0:T(8,128)S(1)}, f32[16,1024]{1,0:T(8,128)S(1)}, u32[]{:S(2)}, u32[]{:S(2)}) collective-permute-start(f32[16,1024]{1,0:T(8,128)S(1)} %get-tuple-element.33), channel_id=1, source_target_pairs={{0,256},{64,320},{128,384},{192,448},{256,0},{320,64},{384,128},{4... | collective-permute-start | bytes 196616 | tf_op jit(solution)/shard_map/ppermute | solution.py:216
  25.9 2.1 %collective-permute-start.3 = (f32[16,1024]{1,0:T(8,128)S(1)}, f32[16,1024]{1,0:T(8,128)S(1)}, u32[]{:S(2)}, u32[]{:S(2)}) collective-permute-start(f32[16,1024]{1,0:T(8,128)S(1)} %get-tuple-element.32), channel_id=1, source_target_pairs={{0,384},{64,448},{128,256},{192,320},{256,128},{320,192},{384,0},{... | collective-permute-start | bytes 196616 | tf_op jit(solution)/shard_map/ppermute | solution.py:216
  28.9 4.2 %all-to-all-start.1 = ((bf16[4,8,16,576]{3,2,1,0:T(8,128)(2,1)}), bf16[4,8,16,576]{3,2,1,0:T(8,128)(2,1)S(1)}, u32[]{:S(2)}, u32[]{:S(2)}) async-start(bf16[4,8,16,576]{3,2,1,0:T(8,128)(2,1)} %broadcast_in_dim.28), calls=%async_computation.1 | async-start | bytes 1310720 | tf_op jit(solution)/shard_map/all_to_all | solution.py:47
  33.8 7.9 %collective-permute-start.4 = (f32[16,1024]{1,0:T(8,128)S(1)}, f32[16,1024]{1,0:T(8,128)S(1)}, u32[]{:S(2)}, u32[]{:S(2)}) collective-permute-start(f32[16,1024]{1,0:T(8,128)S(1)} %fusion.3.one_ref), channel_id=1, source_target_pairs={{0,64},{64,0},{128,192},{192,128},{256,320},{320,256},{384,448},{4... | collective-permute-start | bytes 196616 | tf_op jit(solution)/shard_map/ppermute | solution.py:250
  42.0 4.8 %collective-permute-start = (bf16[4,8,16,576]{3,2,1,0:T(8,128)(2,1)S(1)}, bf16[4,8,16,576]{3,2,1,0:T(8,128)(2,1)S(1)}, u32[]{:S(2)}, u32[]{:S(2)}) collective-permute-start(bf16[4,8,16,576]{3,2,1,0:T(8,128)(2,1)S(1)} %all-to-all-done.1), channel_id=1, source_target_pairs={{0,1},{1,0},{2,3},{3,2},{4,5},{5,4},{6,7},{7,6},{8,9},{9,8},{10,11... | collective-permute-start | bytes 1769480 | tf_op jit(solution)/shard_map/ppermute | solution.py:260
  48.0 1.3 shard_map.85
  49.3 1.3 shard_map.86
  50.7 22.7 %all_to_all.45.stats_ref = f32[8,24,128]{2,1,0:T(8,128)S(1)} all-to-all(f32[8,24,128]{2,1,0:T(8,128)S(1)} %broadcast_in_dim.30), channel_id=1, replica_groups={{0,2,4,6,8,10,12,14},{1,3,5,7,9,11,13,15},{16,18,20,22,24,26,28,30},{17..., dimensions={0} | all-to-all | bytes 196608 | tf_op jit(solution)/shard_map/all_to_all | solution.py:47
  73.4 11.7 %all_to_all.46.stats_ref = f32[8,24,128]{2,1,0:T(8,128)S(1)} all-to-all(f32[8,24,128]{2,1,0:T(8,128)S(1)} %shard_map.89), channel_id=1, replica_groups={{0,16,32,48,1,17,33,49},{2,18,34,50,3,19,35,51},{4,20,36,52,5,21,37,53}..., dimensions={0} | all-to-all | bytes 196608 | tf_op jit(solution)/shard_map/all_to_all | solution.py:47
  85.1 1.5 shard_map.90
  86.5 3.7 %all-to-all-start.4 = ((f32[4,16,1024]{2,1,0:T(8,128)}), f32[4,16,1024]{2,1,0:T(8,128)S(1)}, u32[]{:S(2)}, u32[]{:S(2)}) async-start(f32[4,16,1024]{2,1,0:T(8,128)} %bitcast.21), calls=%async_computation.4 | async-start | bytes 524288 | tf_op jit(solution)/shard_map/all_to_all | solution.py:47
  90.3 7.9 %collective-permute-start.6 = (bf16[288,128]{1,0:T(8,128)(2,1)S(1)}, bf16[288,128]{1,0:T(8,128)(2,1)S(1)}, u32[]{:S(2)}, u32[]{:S(2)}) collective-permute-start(bf16[288,128]{1,0:T(8,128)(2,1)S(1)} %constant_dynamic-slice_fusion), channel_id=1, source_target_pairs={{0,64},{64,0},{128,192},{192,128},{256,320},{320,256},{384,448},{4... | collective-permute-start | bytes 221192 | tf_op jit(solution)/shard_map/ppermute | solution.py:288
  98.3 6.1 %collective-permute-start.5 = (f32[16,1024]{1,0:T(8,128)S(1)}, f32[16,1024]{1,0:T(8,128)S(1)}, u32[]{:S(2)}, u32[]{:S(2)}) collective-permute-start(f32[16,1024]{1,0:T(8,128)S(1)} %reduce_sum.18.one_ref), channel_id=1, source_target_pairs={{0,64},{64,0},{128,192},{192,128},{256,320},{320,256},{384,448},{4... | collective-permute-start | bytes 196616 | tf_op jit(solution)/shard_map/ppermute | solution.py:290
  104.3 3.0 %collective-permute-done.6 = bf16[288,128]{1,0:T(8,128)(2,1)S(1)} collective-permute-done((bf16[288,128]{1,0:T(8,128)(2,1)S(1)}, bf16[288,128]{1,0:T(8,128)(2,1)S(1)}, u32[]{:S(2)}, u32[]{:S(2)}) %collective-permute-start.6) | collective-permute-done | bytes 73760 | tf_op jit(solution)/shard_map/ppermute | solution.py:288
  107.4 5.3 %collective-permute-done.5.two_ref = f32[16,1024]{1,0:T(8,128)S(1)} collective-permute-done((f32[16,1024]{1,0:T(8,128)S(1)}, f32[16,1024]{1,0:T(8,128)S(1)}, u32[]{:S(2)}, u32[]{:S(2)}) %collective-permute-start.5) | collective-permute-done | bytes 65568 | tf_op jit(solution)/shard_map/ppermute | solution.py:290
  113.5 4.0 %all-to-all-start.5 = ((f32[4,16,1024]{2,1,0:T(8,128)}), f32[4,16,1024]{2,1,0:T(8,128)S(1)}, u32[]{:S(2)}, u32[]{:S(2)}) async-start(f32[4,16,1024]{2,1,0:T(8,128)} %shard_map.91), calls=%async_computation.5 | async-start | bytes 524288 | tf_op jit(solution)/shard_map/all_to_all | solution.py:47
  117.5 6.3 %collective-permute-start.7 = (bf16[288,128]{1,0:T(8,128)(2,1)S(1)}, bf16[288,128]{1,0:T(8,128)(2,1)S(1)}, u32[]{:S(2)}, u32[]{:S(2)}) collective-permute-start(bf16[288,128]{1,0:T(8,128)(2,1)S(1)} %collective-permute-done.6), channel_id=1, source_target_pairs={{0,1},{1,0},{2,3},{3,2},{4,5},{5,4},{6,7},{7,6},{8,9},{9,8},{10,11... | collective-permute-start | bytes 221192 | tf_op jit(solution)/shard_map/ppermute | solution.py:292
  124.7 1.0 shard_map.92
  125.7 13.6 %all_to_all.47.parts_ref = f32[8,72,128]{2,1,0:T(8,128)S(1)} all-to-all(f32[8,72,128]{2,1,0:T(8,128)S(1)} %bitcast.52), channel_id=1, replica_groups={{0,16,32,48,1,17,33,49},{2,18,34,50,3,19,35,51},{4,20,36,52,5,21,37,53}..., dimensions={0} | all-to-all | bytes 589824 | tf_op jit(solution)/shard_map/all_to_all | solution.py:47
  140.0 3.3 %all-to-all-start.7 = ((f32[4,72,128]{2,1,0:T(8,128)}), f32[4,72,128]{2,1,0:T(8,128)S(1)}, u32[]{:S(2)}, u32[]{:S(2)}) async-start(f32[4,72,128]{2,1,0:T(8,128)} %shard_map.93), calls=%async_computation.7 | async-start | bytes 294912 | tf_op jit(solution)/shard_map/all_to_all | solution.py:47
  143.5 2.2 %collective-permute-start.10 = (bf16[2,576,128]{2,1,0:T(8,128)(2,1)S(1)}, bf16[2,576,128]{2,1,0:T(8,128)(2,1)S(1)}, u32[]{:S(2)}, u32[]{:S(2)}) collective-permute-start(bf16[2,576,128]{2,1,0:T(8,128)(2,1)S(1)} %pad_maximum_fusion.refs_2_), channel_id=1, source_target_pairs={{0,256},{64,320},{128,384},{192,448},{256,0},{320,64},{384,128},{4... | collective-permute-start | bytes 884744 | tf_op jit(solution)/shard_map/ppermute | solution.py:304
  145.7 4.3 %collective-permute-start.11 = (bf16[2,576,128]{2,1,0:T(8,128)(2,1)S(1)}, bf16[2,576,128]{2,1,0:T(8,128)(2,1)S(1)}, u32[]{:S(2)}, u32[]{:S(2)}) collective-permute-start(bf16[2,576,128]{2,1,0:T(8,128)(2,1)S(1)} %pad_maximum_fusion.refs_2_), channel_id=1, source_target_pairs={{0,384},{64,448},{128,256},{192,320},{256,128},{320,192},{384,0},{... | collective-permute-start | bytes 884744 | tf_op jit(solution)/shard_map/ppermute | solution.py:304
  150.0 1.9 %collective-permute-start.9 = (bf16[2,576,128]{2,1,0:T(8,128)(2,1)S(1)}, bf16[2,576,128]{2,1,0:T(8,128)(2,1)S(1)}, u32[]{:S(2)}, u32[]{:S(2)}) collective-permute-start(bf16[2,576,128]{2,1,0:T(8,128)(2,1)S(1)} %pad_maximum_fusion.refs_2_), channel_id=1, source_target_pairs={{0,128},{64,192},{128,0},{192,64},{256,384},{320,448},{384,256},{4... | collective-permute-start | bytes 884744 | tf_op jit(solution)/shard_map/ppermute | solution.py:304
  151.9 4.2 %collective-permute-start.8 = (f32[72,128]{1,0:T(8,128)S(1)}, f32[72,128]{1,0:T(8,128)S(1)}, u32[]{:S(2)}, u32[]{:S(2)}) collective-permute-start(f32[72,128]{1,0:T(8,128)S(1)} %reduce_sum.19.one_ref), channel_id=1, source_target_pairs={{0,8},{1,9},{2,10},{3,11},{4,12},{5,13},{6,14},{7,15},{8,0},{9,1},... | collective-permute-start | bytes 110600 | tf_op jit(solution)/shard_map/ppermute | solution.py:318
  156.1 4.4 %collective-permute-done.8.two_ref = f32[72,128]{1,0:T(8,128)S(1)} collective-permute-done((f32[72,128]{1,0:T(8,128)S(1)}, f32[72,128]{1,0:T(8,128)S(1)}, u32[]{:S(2)}, u32[]{:S(2)}) %collective-permute-start.8) | collective-permute-done | bytes 36896 | tf_op jit(solution)/shard_map/ppermute | solution.py:318
  161.3 5.7 %all-to-all-start.8 = ((f32[8,72,128]{2,1,0:T(8,128)}), f32[8,72,128]{2,1,0:T(8,128)S(1)}, u32[]{:S(2)}, u32[]{:S(2)}) async-start(f32[8,72,128]{2,1,0:T(8,128)} %shard_map.94), calls=%async_computation.8 | async-start | bytes 589824 | tf_op jit(solution)/shard_map/all_to_all | solution.py:47
  167.0 4.7 %shard_map.95 = f32[1024,128]{1,0:T(8,128)} custom-call(f32[64,1024]{1,0:T(8,128)S(1)} %bitcast.54, bf16[1024,128]{1,0:T(8,128)(2,1)S(1)} %copy-done.2, bf16[2,576,128]{2,1,0:T(8,128)(2,1)S(1)} %pad_maximum_fusion.refs_2_, bf16[2,576,128]{2,1,0:T(8,128)(2,1)S(1)} %collective-permute-done.9.refs_3_, bf16[2,576,128]{2,1,0:T(8,128)(2,1)S(1)} %collective-permute-done.10.refs_4_, ...), custom_call_target="tpu_custom_call" | custom-call | flops 2147483648 | bytes 3145728 | tf_op jit(solution)/shard_map/pallas_call | solution.py:324
  171.7 2.2 %all-to-all-done.8 = f32[8,72,128]{2,1,0:T(8,128)S(1)} async-done(((f32[8,72,128]{2,1,0:T(8,128)}), f32[8,72,128]{2,1,0:T(8,128)S(1)}, u32[]{:S(2)}, u32[]{:S(2)}) %all-to-all-start.8) | async-done | bytes 294944 | tf_op jit(solution)/shard_map/all_to_all | solution.py:47
  (53 shorter events, 9.8 us)
Async XLA Ops:
  0.6 32.4 %copy-start.3 = (s32[64]{0:T(128)S(1)}, s32[64]{0:T(128)}, u32[]{:S(2)}) copy-start(s32[64]{0:T(128)} %param.11) | copy-start | bytes 772
  2.1 25.9 %all-to-all-start = ((bf16[8,16,576]{2,1,0:T(8,128)(2,1)}), bf16[8,16,576]{2,1,0:T(8,128)(2,1)S(1)}, u32[]{:S(2)}, u32[]{:S(2)}) async-start(bf16[8,16,576]{2,1,0:T(8,128)(2,1)} %broadcast_in_dim.27), calls=%async_computation | async-start | bytes 327680 | tf_op jit(solution)/shard_map/all_to_all | solution.py:47
  16.9 1.0 copy-start.1
  18.4 15.4 %collective-permute-start.1 = (f32[16,1024]{1,0:T(8,128)S(1)}, f32[16,1024]{1,0:T(8,128)S(1)}, u32[]{:S(2)}, u32[]{:S(2)}) collective-permute-start(f32[16,1024]{1,0:T(8,128)S(1)} %get-tuple-element.31), channel_id=1, source_target_pairs={{0,128},{64,192},{128,0},{192,64},{256,384},{320,448},{384,256},{4... | collective-permute-start | bytes 196616 | tf_op jit(solution)/shard_map/ppermute | solution.py:216
  21.5 12.3 %collective-permute-start.2 = (f32[16,1024]{1,0:T(8,128)S(1)}, f32[16,1024]{1,0:T(8,128)S(1)}, u32[]{:S(2)}, u32[]{:S(2)}) collective-permute-start(f32[16,1024]{1,0:T(8,128)S(1)} %get-tuple-element.33), channel_id=1, source_target_pairs={{0,256},{64,320},{128,384},{192,448},{256,0},{320,64},{384,128},{4... | collective-permute-start | bytes 196616 | tf_op jit(solution)/shard_map/ppermute | solution.py:216
  25.9 7.9 %collective-permute-start.3 = (f32[16,1024]{1,0:T(8,128)S(1)}, f32[16,1024]{1,0:T(8,128)S(1)}, u32[]{:S(2)}, u32[]{:S(2)}) collective-permute-start(f32[16,1024]{1,0:T(8,128)S(1)} %get-tuple-element.32), channel_id=1, source_target_pairs={{0,384},{64,448},{128,256},{192,320},{256,128},{320,192},{384,0},{... | collective-permute-start | bytes 196616 | tf_op jit(solution)/shard_map/ppermute | solution.py:216
  28.9 13.1 %all-to-all-start.1 = ((bf16[4,8,16,576]{3,2,1,0:T(8,128)(2,1)}), bf16[4,8,16,576]{3,2,1,0:T(8,128)(2,1)S(1)}, u32[]{:S(2)}, u32[]{:S(2)}) async-start(bf16[4,8,16,576]{3,2,1,0:T(8,128)(2,1)} %broadcast_in_dim.28), calls=%async_computation.1 | async-start | bytes 1310720 | tf_op jit(solution)/shard_map/all_to_all | solution.py:47
  33.8 13.9 %collective-permute-start.4 = (f32[16,1024]{1,0:T(8,128)S(1)}, f32[16,1024]{1,0:T(8,128)S(1)}, u32[]{:S(2)}, u32[]{:S(2)}) collective-permute-start(f32[16,1024]{1,0:T(8,128)S(1)} %fusion.3.one_ref), channel_id=1, source_target_pairs={{0,64},{64,0},{128,192},{192,128},{256,320},{320,256},{384,448},{4... | collective-permute-start | bytes 196616 | tf_op jit(solution)/shard_map/ppermute | solution.py:250
  42.0 6.0 %copy-start = (bf16[1024,576]{0,1:T(8,128)(2,1)S(1)}, bf16[1024,576]{0,1:T(8,128)(2,1)}, u32[]{:S(2)}) copy-start(bf16[1024,576]{0,1:T(8,128)(2,1)} %param.7) | copy-start | bytes 3538948
  42.0 7.3 %collective-permute-start = (bf16[4,8,16,576]{3,2,1,0:T(8,128)(2,1)S(1)}, bf16[4,8,16,576]{3,2,1,0:T(8,128)(2,1)S(1)}, u32[]{:S(2)}, u32[]{:S(2)}) collective-permute-start(bf16[4,8,16,576]{3,2,1,0:T(8,128)(2,1)S(1)} %all-to-all-done.1), channel_id=1, source_target_pairs={{0,1},{1,0},{2,3},{3,2},{4,5},{5,4},{6,7},{7,6},{8,9},{9,8},{10,11... | collective-permute-start | bytes 1769480 | tf_op jit(solution)/shard_map/ppermute | solution.py:260
  50.7 74.0 %copy-start.2 = (bf16[1024,128]{1,0:T(8,128)(2,1)S(1)}, bf16[1024,128]{1,0:T(8,128)(2,1)}, u32[]{:S(2)}) copy-start(bf16[1024,128]{1,0:T(8,128)(2,1)} %refs_1_.3) | copy-start | bytes 786436
  86.5 11.7 %all-to-all-start.4 = ((f32[4,16,1024]{2,1,0:T(8,128)}), f32[4,16,1024]{2,1,0:T(8,128)S(1)}, u32[]{:S(2)}, u32[]{:S(2)}) async-start(f32[4,16,1024]{2,1,0:T(8,128)} %bitcast.21), calls=%async_computation.4 | async-start | bytes 524288 | tf_op jit(solution)/shard_map/all_to_all | solution.py:47
  90.3 17.1 %collective-permute-start.6 = (bf16[288,128]{1,0:T(8,128)(2,1)S(1)}, bf16[288,128]{1,0:T(8,128)(2,1)S(1)}, u32[]{:S(2)}, u32[]{:S(2)}) collective-permute-start(bf16[288,128]{1,0:T(8,128)(2,1)S(1)} %constant_dynamic-slice_fusion), channel_id=1, source_target_pairs={{0,64},{64,0},{128,192},{192,128},{256,320},{320,256},{384,448},{4... | collective-permute-start | bytes 221192 | tf_op jit(solution)/shard_map/ppermute | solution.py:288
  98.3 14.4 %collective-permute-start.5 = (f32[16,1024]{1,0:T(8,128)S(1)}, f32[16,1024]{1,0:T(8,128)S(1)}, u32[]{:S(2)}, u32[]{:S(2)}) collective-permute-start(f32[16,1024]{1,0:T(8,128)S(1)} %reduce_sum.18.one_ref), channel_id=1, source_target_pairs={{0,64},{64,0},{128,192},{192,128},{256,320},{320,256},{384,448},{4... | collective-permute-start | bytes 196616 | tf_op jit(solution)/shard_map/ppermute | solution.py:290
  113.5 11.2 %all-to-all-start.5 = ((f32[4,16,1024]{2,1,0:T(8,128)}), f32[4,16,1024]{2,1,0:T(8,128)S(1)}, u32[]{:S(2)}, u32[]{:S(2)}) async-start(f32[4,16,1024]{2,1,0:T(8,128)} %shard_map.91), calls=%async_computation.5 | async-start | bytes 524288 | tf_op jit(solution)/shard_map/all_to_all | solution.py:47
  117.5 7.2 %collective-permute-start.7 = (bf16[288,128]{1,0:T(8,128)(2,1)S(1)}, bf16[288,128]{1,0:T(8,128)(2,1)S(1)}, u32[]{:S(2)}, u32[]{:S(2)}) collective-permute-start(bf16[288,128]{1,0:T(8,128)(2,1)S(1)} %collective-permute-done.6), channel_id=1, source_target_pairs={{0,1},{1,0},{2,3},{3,2},{4,5},{5,4},{6,7},{7,6},{8,9},{9,8},{10,11... | collective-permute-start | bytes 221192 | tf_op jit(solution)/shard_map/ppermute | solution.py:292
  140.0 11.9 %all-to-all-start.7 = ((f32[4,72,128]{2,1,0:T(8,128)}), f32[4,72,128]{2,1,0:T(8,128)S(1)}, u32[]{:S(2)}, u32[]{:S(2)}) async-start(f32[4,72,128]{2,1,0:T(8,128)} %shard_map.93), calls=%async_computation.7 | async-start | bytes 294912 | tf_op jit(solution)/shard_map/all_to_all | solution.py:47
  143.5 23.5 %collective-permute-start.10 = (bf16[2,576,128]{2,1,0:T(8,128)(2,1)S(1)}, bf16[2,576,128]{2,1,0:T(8,128)(2,1)S(1)}, u32[]{:S(2)}, u32[]{:S(2)}) collective-permute-start(bf16[2,576,128]{2,1,0:T(8,128)(2,1)S(1)} %pad_maximum_fusion.refs_2_), channel_id=1, source_target_pairs={{0,256},{64,320},{128,384},{192,448},{256,0},{320,64},{384,128},{4... | collective-permute-start | bytes 884744 | tf_op jit(solution)/shard_map/ppermute | solution.py:304
  145.7 21.3 %collective-permute-start.11 = (bf16[2,576,128]{2,1,0:T(8,128)(2,1)S(1)}, bf16[2,576,128]{2,1,0:T(8,128)(2,1)S(1)}, u32[]{:S(2)}, u32[]{:S(2)}) collective-permute-start(bf16[2,576,128]{2,1,0:T(8,128)(2,1)S(1)} %pad_maximum_fusion.refs_2_), channel_id=1, source_target_pairs={{0,384},{64,448},{128,256},{192,320},{256,128},{320,192},{384,0},{... | collective-permute-start | bytes 884744 | tf_op jit(solution)/shard_map/ppermute | solution.py:304
  150.0 17.0 %collective-permute-start.9 = (bf16[2,576,128]{2,1,0:T(8,128)(2,1)S(1)}, bf16[2,576,128]{2,1,0:T(8,128)(2,1)S(1)}, u32[]{:S(2)}, u32[]{:S(2)}) collective-permute-start(bf16[2,576,128]{2,1,0:T(8,128)(2,1)S(1)} %pad_maximum_fusion.refs_2_), channel_id=1, source_target_pairs={{0,128},{64,192},{128,0},{192,64},{256,384},{320,448},{384,256},{4... | collective-permute-start | bytes 884744 | tf_op jit(solution)/shard_map/ppermute | solution.py:304
  151.9 8.6 %collective-permute-start.8 = (f32[72,128]{1,0:T(8,128)S(1)}, f32[72,128]{1,0:T(8,128)S(1)}, u32[]{:S(2)}, u32[]{:S(2)}) collective-permute-start(f32[72,128]{1,0:T(8,128)S(1)} %reduce_sum.19.one_ref), channel_id=1, source_target_pairs={{0,8},{1,9},{2,10},{3,11},{4,12},{5,13},{6,14},{7,15},{8,0},{9,1},... | collective-permute-start | bytes 110600 | tf_op jit(solution)/shard_map/ppermute | solution.py:318
  161.3 12.6 %all-to-all-start.8 = ((f32[8,72,128]{2,1,0:T(8,128)}), f32[8,72,128]{2,1,0:T(8,128)S(1)}, u32[]{:S(2)}, u32[]{:S(2)}) async-start(f32[8,72,128]{2,1,0:T(8,128)} %shard_map.94), calls=%async_computation.8 | async-start | bytes 589824 | tf_op jit(solution)/shard_map/all_to_all | solution.py:47

commit v7 on v6

--- a/solution.py
+++ b/solution.py
@@ -66,22 +66,26 @@
     return jnp.sum(jnp.where(diagonal(rows, row.shape[1]), row, 0.0), axis=1, keepdims=True)
 
 
-def call(kernel, out_shape, flops=0, moved=0, aliases={}):
+def call(kernel, out_shape, flops=0, moved=0, aliases={}, vmem=VMEM, **specs):
     return pl.pallas_call(
         kernel,
+        **specs,
         out_shape=out_shape,
         input_output_aliases=aliases,
-        compiler_params=pltpu.CompilerParams(vmem_limit_bytes=VMEM),
+        compiler_params=pltpu.CompilerParams(vmem_limit_bytes=vmem),
         cost_estimate=pl.CostEstimate(flops=flops, bytes_accessed=moved, transcendentals=0),
     )
 
 
 def score_kernel(core_ref, limit_ref, q_ref, k_ref, *refs):
-    e_ref, m_ref, l_ref = refs[-3:]
-    block = e_ref.shape[0] // NYC
-    key = lax.broadcasted_iota(jnp.int32, (1, e_ref.shape[1]), 1)
+    e_ref, m_ref, l_ref, held, sems = refs[-5:]
+    for before, after in zip(refs[1:-5], (m_ref, l_ref)):
+        after[...] = before[...]
+    block = held.shape[1]
+    key = lax.broadcasted_iota(jnp.int32, (1, held.shape[2]), 1)
     k = k_ref[...]
     core = core_ref[0]
+    copies = []
     for y in range(NY):
         line = core * NY + y
         lines = pl.ds(pl.multiple_of(line * block, block), block)
@@ -89,9 +93,13 @@
         s = jnp.where(key <= limit_ref[lines], s * softmax_scale, masked_value)
         m = jnp.max(s, axis=1, keepdims=True)
         e = jnp.exp(s - m)
-        e_ref[lines] = e
+        held[y] = e
+        copies.append(pltpu.make_async_copy(held.at[y], e_ref.at[lines], sems.at[y]))
+        copies[-1].start()
         m_ref[pl.ds(line, 1)] = as_row(m)
         l_ref[pl.ds(line, 1)] = as_row(jnp.sum(e, axis=1, keepdims=True))
+    for copy in copies:
+        copy.wait()
 
 
 def message_parts(ref, tokens, heads):
@@ -137,13 +145,20 @@
     out_ref[...] = jnp.broadcast_to(lines[None], out_ref.shape)
 
 
-def target_kernel(stats_ref, m_ref, e_ref, out_ref):
+def target_kernel(stats_ref, m_ref, e_ref, out_ref, held, sems):
+    block = held.shape[1]
+    copies = []
+    for b in range(NYC):
+        lines = e_ref.at[b * block : (b + 1) * block]
+        copies.append(pltpu.make_async_copy(lines, held.at[b], sems.at[b]))
+        copies[-1].start()
     top, total, _, _ = joined(stats_ref[...])
     weights = jnp.exp(m_ref[...] - top) / total
     keys = out_ref.shape[1]
-    block = e_ref.shape[0] // NYC
     for b in range(NYC):
-        e = e_ref[b * block : (b + 1) * block] * as_column(weights[b : b + 1], block)
+        weight = as_column(weights[b : b + 1], block)
+        copies[b].wait()
+        e = held[b] * weight
         out_ref[b * NZ : (b + 1) * NZ] = jnp.sum(e.reshape(NZ, block // NZ, keys), axis=1)
 
 
@@ -261,6 +276,7 @@
     row_count = NC * rows.size // width
     row_limit = jnp.repeat(limit, heads_here)[:, None]
     lines_shape = shape((NYC, row_count // NYC), f32)
+    hbm, vmem, smem = (pl.BlockSpec(memory_space=m) for m in (pltpu.HBM, pltpu.VMEM, pltpu.SMEM))
     scored = ()
     for where, part in ((core, rows), (1 - core, other_rows)):
         scored = call(
@@ -268,40 +284,56 @@
             (shape((row_count, key_count), f32), lines_shape, lines_shape),
             flops=row_count * key_count * width,
             moved=4 << 20,
-            aliases={4 + i: i for i in range(len(scored))},
+            aliases={4: 0} if scored else {},
+            in_specs=[smem, vmem, vmem, vmem, *[hbm, vmem, vmem][: len(scored)]],
+            out_specs=(hbm, vmem, vmem),
+            vmem=48 << 20,
+            scratch_shapes=[
+                pltpu.VMEM((NY, row_count // NYC, key_count), f32),
+                pltpu.SemaphoreType.DMA((NY,)),
+            ],
         )(where.reshape(1), row_limit, part.reshape(-1, width), latent_keys.T, *scored)
     exponent, local_max, local_total = scored
 
     stats = jnp.concatenate([local_max, local_total, index_stats])
 
+    mine_rows = mine.shape[0] // NC
+    sent = lax.dynamic_slice_in_dim(mine, core * mine_rows, mine_rows, 0)
+    stats, sent = lax.optimization_barrier((stats, sent))
+    swapped = lax.ppermute(sent, "heads", pairs_zh)
     stats = gathered(stats, "tokens", groups_z)
     stats = call(join_kernel, shape((NYC, *stats.shape[1:]), f32))(stats)
     stats = exchanged(stats, "tokens", groups_yc)
-
-    partial = call(target_kernel, shape((query_count, key_count), f32), moved=5 << 20)(
-        stats, local_max, exponent
-    )
-
-    mine_rows = mine.shape[0] // NC
-    partial, late = lax.optimization_barrier((partial, mine))
-    sent = lax.dynamic_slice_in_dim(late, core * mine_rows, mine_rows, 0)
-    swapped = lax.ppermute(sent, "heads", pairs_zh)
-    over_x = exchanged(partial.reshape(NX, share_rows, key_count), "heads", groups_x).sum(axis=0)
-    other = lax.ppermute(over_x, "heads", pairs_zh)
-    other, swapped = lax.optimization_barrier((other, swapped))
     swapped_other = lax.ppermute(swapped, "tokens", pairs_c)
-    dlogit = call(dlogit_kernel, shape((NX, share_rows, key_count), f32))(
-        over_x, other, logits, stats
-    )
-    dlogit = exchanged(dlogit, "heads", groups_x).reshape(query_count, key_count)
-    dlogit, swapped_other = lax.optimization_barrier((dlogit, swapped_other))
+
+    partial = call(
+        target_kernel,
+        shape((query_count, key_count), f32),
+        moved=5 << 20,
+        in_specs=[vmem, vmem, hbm],
+        out_specs=vmem,
+        vmem=52 << 20,
+        scratch_shapes=[
+            pltpu.VMEM((NYC, row_count // NYC, key_count), f32),
+            pltpu.SemaphoreType.DMA((NYC,)),
+        ],
+    )(stats, local_max, exponent)
+    partial, swapped_other = lax.optimization_barrier((partial, swapped_other))
     halves = jnp.where(
         core == 0,
         jnp.concatenate([swapped, swapped_other]),
         jnp.concatenate([swapped_other, swapped]),
     )
     pair = jnp.stack([mine, halves])
-    messages = [pair] + [lax.ppermute(pair, "heads", pairs_x(flip)) for flip in range(1, NX)]
+    messages = [pair] + [lax.ppermute(pair, "heads", pairs_x(flip)) for flip in (1, 3, 2)]
+    over_x = exchanged(partial.reshape(NX, share_rows, key_count), "heads", groups_x).sum(axis=0)
+    over_x, pair = lax.optimization_barrier((over_x, pair))
+    other = lax.ppermute(over_x, "heads", pairs_zh)
+    dlogit = call(dlogit_kernel, shape((NX, share_rows, key_count), f32))(
+        over_x, other, logits, stats
+    )
+    dlogit = exchanged(dlogit, "heads", groups_x).reshape(query_count, key_count)
+    dlogit, messages[1], messages[2] = lax.optimization_barrier((dlogit, messages[1], messages[2]))
 
     query_lines = query_count * index_heads
     piece_rows = -(-(query_lines + index_heads) // (NYC * 8)) * 8

time: 176 us -> 178 us (1.011)
  blocking collectives: 47.9 us -> 13.5 us
  starting transfers between devices: 89.3 us -> 114 us
  waiting for transfers between devices: 16.8 us -> 23.6 us
  Pallas kernels: 12.9 us -> 16.5 us
    all_to_all x3 -> x1, blocking collectives: 47.9 us -> 13.5 us  [exchanged(): lax.all_to_all(parts, axis, 0, 0, tiled=True, axis_index_groups=groups)]
    all_to_all x6 -> x8, starting transfers between devices: 34 us -> 55.9 us  [exchanged(): lax.all_to_all(parts, axis, 0, 0, tiled=True, axis_index_groups=groups)]
    all_to_all x6 -> x8, waiting for transfers between devices: 2.17 us -> 15.8 us  [exchanged(): lax.all_to_all(parts, axis, 0, 0, tiled=True, axis_index_groups=groups)]
    ppermute x1, starting transfers between devices: 6.28 us -> 1.91 us  [local(): swapped_other = lax.ppermute(swapped, 'tokens', pairs_c)]
    ppermute x1, starting transfers between devices: 4.17 us -> 8.09 us  [local(): other = lax.ppermute(piece, 'tokens', pairs_z4)]
    ppermute x1, waiting for transfers between devices: 4.43 us -> 1.33 us  [local(): other = lax.ppermute(piece, 'tokens', pairs_z4)]
    ppermute x1, waiting for transfers between devices: 3 us -> 0.01 us  [local(): swapped = lax.ppermute(sent, 'heads', pairs_zh)]
    ppermute x2, starting transfers between devices: 14 us -> 15.9 us  [local(): other = lax.ppermute(over_x, 'heads', pairs_zh)]
  transfers between devices with their start and end apart: 18 -> 20, of which waited for: 6 -> 9; matrix products, arithmetic and copies ran while one was open for 2% -> 2% of each run, Pallas kernels for 4% -> 7%
where the time goes in v7:
time: 178 us; the launch traced here: 177 us
  starting transfers between devices  114 us (64%)
  waiting for transfers between devices  23.6 us (13%)
  Pallas kernels  16.5 us (9%)
  blocking collectives  13.5 us (8%)
  local copies, waits for them, and re-layouts  7.12 us (4%)
    all_to_all x8, starting transfers between devices, exchanged(): lax.all_to_all(parts, axis, 0, 0, tiled=True, axis_index_groups=groups)  55.9 us
    ppermute x2, starting transfers between devices, local(): other = lax.ppermute(over_x, 'heads', pairs_zh)  15.9 us
    all_to_all x8, waiting for transfers between devices, exchanged(): lax.all_to_all(parts, axis, 0, 0, tiled=True, axis_index_groups=groups)  15.8 us
    all_to_all x1, blocking collectives, exchanged(): lax.all_to_all(parts, axis, 0, 0, tiled=True, axis_index_groups=groups)  13.5 us
    ppermute x3, starting transfers between devices, x_scatter_sum(): total = total + lax.ppermute(piece, 'heads', pairs_x(flip))  9.58 us
    ppermute x3, starting transfers between devices, local(): lax.ppermute(pair, 'heads', pairs_x(flip))  9.24 us
    ppermute x1, starting transfers between devices, local(): other = lax.ppermute(piece, 'tokens', pairs_z4)  8.09 us
    ppermute x1, starting transfers between devices, local(): swapped = lax.ppermute(sent, 'heads', pairs_zh)  7.95 us
  transfers between devices with their start and end apart: 20, of which 9 were waited for; matrix products, arithmetic and copies ran while one was open for 2% of the time, Pallas kernels for 7%

profile of v7, /device:TPU:1, one launch (start us, length us, event | category | flops | bytes accessed | tf_op | source)
XLA Modules:
  0.0 177.0 jit_solution(9241703155250984924)
XLA Ops:
  0.6 1.4 broadcast_in_dim.27
  2.0 13.1 %all-to-all-start = ((bf16[8,16,576]{2,1,0:T(8,128)(2,1)}), bf16[8,16,576]{2,1,0:T(8,128)(2,1)S(1)}, u32[]{:S(2)}, u32[]{:S(2)}) async-start(bf16[8,16,576]{2,1,0:T(8,128)(2,1)} %broadcast_in_dim.27), calls=%async_computation | async-start | bytes 327680 | tf_op jit(solution)/shard_map/all_to_all | solution.py:47
  18.4 3.1 %collective-permute-start.1 = (f32[16,1024]{1,0:T(8,128)S(1)}, f32[16,1024]{1,0:T(8,128)S(1)}, u32[]{:S(2)}, u32[]{:S(2)}) collective-permute-start(f32[16,1024]{1,0:T(8,128)S(1)} %get-tuple-element.35), channel_id=1, source_target_pairs={{0,128},{64,192},{128,0},{192,64},{256,384},{320,448},{384,256},{4... | collective-permute-start | bytes 196616 | tf_op jit(solution)/shard_map/ppermute | solution.py:231
  21.5 4.4 %collective-permute-start.2 = (f32[16,1024]{1,0:T(8,128)S(1)}, f32[16,1024]{1,0:T(8,128)S(1)}, u32[]{:S(2)}, u32[]{:S(2)}) collective-permute-start(f32[16,1024]{1,0:T(8,128)S(1)} %get-tuple-element.37), channel_id=1, source_target_pairs={{0,256},{64,320},{128,384},{192,448},{256,0},{320,64},{384,128},{4... | collective-permute-start | bytes 196616 | tf_op jit(solution)/shard_map/ppermute | solution.py:231
  25.9 2.1 %collective-permute-start.3 = (f32[16,1024]{1,0:T(8,128)S(1)}, f32[16,1024]{1,0:T(8,128)S(1)}, u32[]{:S(2)}, u32[]{:S(2)}) collective-permute-start(f32[16,1024]{1,0:T(8,128)S(1)} %get-tuple-element.36), channel_id=1, source_target_pairs={{0,384},{64,448},{128,256},{192,320},{256,128},{320,192},{384,0},{... | collective-permute-start | bytes 196616 | tf_op jit(solution)/shard_map/ppermute | solution.py:231
  30.2 4.2 %all-to-all-start.1 = ((bf16[4,8,16,576]{3,2,1,0:T(8,128)(2,1)}), bf16[4,8,16,576]{3,2,1,0:T(8,128)(2,1)S(1)}, u32[]{:S(2)}, u32[]{:S(2)}) async-start(bf16[4,8,16,576]{3,2,1,0:T(8,128)(2,1)} %broadcast_in_dim.28), calls=%async_computation.1 | async-start | bytes 1310720 | tf_op jit(solution)/shard_map/all_to_all | solution.py:47
  34.6 7.9 %collective-permute-start.4 = (f32[16,1024]{1,0:T(8,128)S(1)}, f32[16,1024]{1,0:T(8,128)S(1)}, u32[]{:S(2)}, u32[]{:S(2)}) collective-permute-start(f32[16,1024]{1,0:T(8,128)S(1)} %fusion.3.one_ref), channel_id=1, source_target_pairs={{0,64},{64,0},{128,192},{192,128},{256,320},{320,256},{384,448},{4... | collective-permute-start | bytes 196616 | tf_op jit(solution)/shard_map/ppermute | solution.py:265
  43.0 5.2 %collective-permute-start = (bf16[4,8,16,576]{3,2,1,0:T(8,128)(2,1)S(1)}, bf16[4,8,16,576]{3,2,1,0:T(8,128)(2,1)S(1)}, u32[]{:S(2)}, u32[]{:S(2)}) collective-permute-start(bf16[4,8,16,576]{3,2,1,0:T(8,128)(2,1)S(1)} %all-to-all-done.1), channel_id=1, source_target_pairs={{0,1},{1,0},{2,3},{3,2},{4,5},{5,4},{6,7},{7,6},{8,9},{9,8},{10,11... | collective-permute-start | bytes 1769480 | tf_op jit(solution)/shard_map/ppermute | solution.py:275
  48.8 2.1 %shard_map.85 = (f32[1024,1024]{1,0:T(8,128)}, f32[8,128]{1,0:T(8,128)S(1)}, f32[8,128]{1,0:T(8,128)S(1)}) custom-call(s32[1]{0:T(128)} %bitcast.5.core_ref, s32[1024,1]{1,0:T(8,128)S(1)} %broadcast_in_dim_reshape.5.limit_ref, bf16[512,576]{1,0:T(8,128)(2,1)S(1)} %bitcast.48, bf16[576,1024]{1,0:T(8,128)(2,1)S(1)} %bitcast.46), custom_call_target="tpu_custom_call" | custom-call | flops 603979776 | bytes 4194304 | tf_op jit(solution)/shard_map/pallas_call | solution.py:282
  50.9 2.1 %shard_map.86 = (f32[1024,1024]{1,0:T(8,128)}, f32[8,128]{1,0:T(8,128)S(1)}, f32[8,128]{1,0:T(8,128)S(1)}) custom-call(s32[1]{0:T(128)} %bitcast.core_ref, s32[1024,1]{1,0:T(8,128)S(1)} %broadcast_in_dim_reshape.5.limit_ref, bf16[512,576]{1,0:T(8,128)(2,1)S(1)} %bitcast.51, bf16[576,1024]{1,0:T(8,128)(2,1)S(1)} %bitcast.47, ...), custom_call_target="tpu_custom_call", output_to_operand_aliasing={{0}: (4, {})} | custom-call | flops 603979776 | bytes 4194304 | tf_op jit(solution)/shard_map/pallas_call | solution.py:282
  53.7 12.7 %all-to-all-start.2 = ((f32[8,24,128]{2,1,0:T(8,128)}), f32[8,24,128]{2,1,0:T(8,128)S(1)}, u32[]{:S(2)}, u32[]{:S(2)}) async-start(f32[8,24,128]{2,1,0:T(8,128)} %broadcast_in_dim.30), calls=%async_computation.2 | async-start | bytes 196608 | tf_op jit(solution)/shard_map/all_to_all | solution.py:47
  66.4 8.0 %collective-permute-start.5 = (bf16[288,128]{1,0:T(8,128)(2,1)S(1)}, bf16[288,128]{1,0:T(8,128)(2,1)S(1)}, u32[]{:S(2)}, u32[]{:S(2)}) collective-permute-start(bf16[288,128]{1,0:T(8,128)(2,1)S(1)} %constant_dynamic-slice_fusion), channel_id=1, source_target_pairs={{0,64},{64,0},{128,192},{192,128},{256,320},{320,256},{384,448},{4... | collective-permute-start | bytes 221192 | tf_op jit(solution)/shard_map/ppermute | solution.py:303
  74.3 2.1 %all-to-all-done.2.stats_ref = f32[8,24,128]{2,1,0:T(8,128)S(1)} async-done(((f32[8,24,128]{2,1,0:T(8,128)}), f32[8,24,128]{2,1,0:T(8,128)S(1)}, u32[]{:S(2)}, u32[]{:S(2)}) %all-to-all-start.2) | async-done | bytes 98336 | tf_op jit(solution)/shard_map/all_to_all | solution.py:47
  77.1 6.8 %all-to-all-start.3 = ((f32[8,24,128]{2,1,0:T(8,128)}), f32[8,24,128]{2,1,0:T(8,128)S(1)}, u32[]{:S(2)}, u32[]{:S(2)}) async-start(f32[8,24,128]{2,1,0:T(8,128)} %shard_map.89), calls=%async_computation.3 | async-start | bytes 196608 | tf_op jit(solution)/shard_map/all_to_all | solution.py:47
  83.9 1.9 %collective-permute-start.6 = (bf16[288,128]{1,0:T(8,128)(2,1)S(1)}, bf16[288,128]{1,0:T(8,128)(2,1)S(1)}, u32[]{:S(2)}, u32[]{:S(2)}) collective-permute-start(bf16[288,128]{1,0:T(8,128)(2,1)S(1)} %collective-permute-done.5), channel_id=1, source_target_pairs={{0,1},{1,0},{2,3},{3,2},{4,5},{5,4},{6,7},{7,6},{8,9},{9,8},{10,11... | collective-permute-start | bytes 221192 | tf_op jit(solution)/shard_map/ppermute | solution.py:307
  85.9 3.1 %all-to-all-done.3.stats_ref = f32[8,24,128]{2,1,0:T(8,128)S(1)} async-done(((f32[8,24,128]{2,1,0:T(8,128)}), f32[8,24,128]{2,1,0:T(8,128)S(1)}, u32[]{:S(2)}, u32[]{:S(2)}) %all-to-all-start.3) | async-done | bytes 98336 | tf_op jit(solution)/shard_map/all_to_all | solution.py:47
  88.9 3.0 %shard_map.90 = f32[64,1024]{1,0:T(8,128)} custom-call(f32[8,24,128]{2,1,0:T(8,128)S(1)} %all-to-all-done.3.stats_ref, f32[8,128]{1,0:T(8,128)S(1)} %get-tuple-element.22.m_ref, f32[1024,1024]{1,0:T(8,128)} %get-tuple-element.26.e_ref), custom_call_target="tpu_custom_call" | custom-call | bytes 5242880 | tf_op jit(solution)/shard_map/pallas_call | solution.py:309
  92.0 3.8 %all-to-all-start.4 = ((f32[4,16,1024]{2,1,0:T(8,128)}), f32[4,16,1024]{2,1,0:T(8,128)S(1)}, u32[]{:S(2)}, u32[]{:S(2)}) async-start(f32[4,16,1024]{2,1,0:T(8,128)} %bitcast.21), calls=%async_computation.4 | async-start | bytes 524288 | tf_op jit(solution)/shard_map/all_to_all | solution.py:47
  95.8 3.4 %collective-permute-start.8 = (bf16[2,576,128]{2,1,0:T(8,128)(2,1)S(1)}, bf16[2,576,128]{2,1,0:T(8,128)(2,1)S(1)}, u32[]{:S(2)}, u32[]{:S(2)}) collective-permute-start(bf16[2,576,128]{2,1,0:T(8,128)(2,1)S(1)} %pad_maximum_fusion.refs_2_), channel_id=1, source_target_pairs={{0,128},{64,192},{128,0},{192,64},{256,384},{320,448},{384,256},{4... | collective-permute-start | bytes 884744 | tf_op jit(solution)/shard_map/ppermute | solution.py:328
  99.2 3.7 %collective-permute-start.9 = (bf16[2,576,128]{2,1,0:T(8,128)(2,1)S(1)}, bf16[2,576,128]{2,1,0:T(8,128)(2,1)S(1)}, u32[]{:S(2)}, u32[]{:S(2)}) collective-permute-start(bf16[2,576,128]{2,1,0:T(8,128)(2,1)S(1)} %pad_maximum_fusion.refs_2_), channel_id=1, source_target_pairs={{0,384},{64,448},{128,256},{192,320},{256,128},{320,192},{384,0},{... | collective-permute-start | bytes 884744 | tf_op jit(solution)/shard_map/ppermute | solution.py:328
  102.9 8.0 %collective-permute-start.7 = (f32[16,1024]{1,0:T(8,128)S(1)}, f32[16,1024]{1,0:T(8,128)S(1)}, u32[]{:S(2)}, u32[]{:S(2)}) collective-permute-start(f32[16,1024]{1,0:T(8,128)S(1)} %reduce_sum.18.one_ref), channel_id=1, source_target_pairs={{0,64},{64,0},{128,192},{192,128},{256,320},{320,256},{384,448},{4... | collective-permute-start | bytes 196616 | tf_op jit(solution)/shard_map/ppermute | solution.py:331
  110.9 6.1 %collective-permute-done.7.two_ref = f32[16,1024]{1,0:T(8,128)S(1)} collective-permute-done((f32[16,1024]{1,0:T(8,128)S(1)}, f32[16,1024]{1,0:T(8,128)S(1)}, u32[]{:S(2)}, u32[]{:S(2)}) %collective-permute-start.7) | collective-permute-done | bytes 65568 | tf_op jit(solution)/shard_map/ppermute | solution.py:331
  117.8 3.4 %all-to-all-start.5 = ((f32[4,16,1024]{2,1,0:T(8,128)}), f32[4,16,1024]{2,1,0:T(8,128)S(1)}, u32[]{:S(2)}, u32[]{:S(2)}) async-start(f32[4,16,1024]{2,1,0:T(8,128)} %shard_map.91), calls=%async_computation.5 | async-start | bytes 524288 | tf_op jit(solution)/shard_map/all_to_all | solution.py:47
  121.2 5.5 %all-to-all-done.5 = f32[4,16,1024]{2,1,0:T(8,128)S(1)} async-done(((f32[4,16,1024]{2,1,0:T(8,128)}), f32[4,16,1024]{2,1,0:T(8,128)S(1)}, u32[]{:S(2)}, u32[]{:S(2)}) %all-to-all-start.5) | async-done | bytes 262176 | tf_op jit(solution)/shard_map/all_to_all | solution.py:47
  127.7 13.5 %all_to_all.45.parts_ref = f32[8,72,128]{2,1,0:T(8,128)S(1)} all-to-all(f32[8,72,128]{2,1,0:T(8,128)S(1)} %bitcast.52), channel_id=1, replica_groups={{0,16,32,48,1,17,33,49},{2,18,34,50,3,19,35,51},{4,20,36,52,5,21,37,53}..., dimensions={0} | all-to-all | bytes 589824 | tf_op jit(solution)/shard_map/all_to_all | solution.py:47
  141.9 3.8 %all-to-all-start.7 = ((f32[4,72,128]{2,1,0:T(8,128)}), f32[4,72,128]{2,1,0:T(8,128)S(1)}, u32[]{:S(2)}, u32[]{:S(2)}) async-start(f32[4,72,128]{2,1,0:T(8,128)} %shard_map.93), calls=%async_computation.7 | async-start | bytes 294912 | tf_op jit(solution)/shard_map/all_to_all | solution.py:47
  145.8 2.2 %collective-permute-start.11 = (bf16[2,576,128]{2,1,0:T(8,128)(2,1)S(1)}, bf16[2,576,128]{2,1,0:T(8,128)(2,1)S(1)}, u32[]{:S(2)}, u32[]{:S(2)}) collective-permute-start(bf16[2,576,128]{2,1,0:T(8,128)(2,1)S(1)} %pad_maximum_fusion.refs_2_), channel_id=1, source_target_pairs={{0,256},{64,320},{128,384},{192,448},{256,0},{320,64},{384,128},{4... | collective-permute-start | bytes 884744 | tf_op jit(solution)/shard_map/ppermute | solution.py:328
  147.9 2.7 %all-to-all-done.7 = f32[4,72,128]{2,1,0:T(8,128)S(1)} async-done(((f32[4,72,128]{2,1,0:T(8,128)}), f32[4,72,128]{2,1,0:T(8,128)S(1)}, u32[]{:S(2)}, u32[]{:S(2)}) %all-to-all-start.7) | async-done | bytes 147488 | tf_op jit(solution)/shard_map/all_to_all | solution.py:47
  150.6 8.1 %collective-permute-start.10 = (f32[72,128]{1,0:T(8,128)S(1)}, f32[72,128]{1,0:T(8,128)S(1)}, u32[]{:S(2)}, u32[]{:S(2)}) collective-permute-start(f32[72,128]{1,0:T(8,128)S(1)} %reduce_sum.19.one_ref), channel_id=1, source_target_pairs={{0,8},{1,9},{2,10},{3,11},{4,12},{5,13},{6,14},{7,15},{8,0},{9,1},... | collective-permute-start | bytes 110600 | tf_op jit(solution)/shard_map/ppermute | solution.py:350
  160.8 8.0 %all-to-all-start.8 = ((f32[8,72,128]{2,1,0:T(8,128)}), f32[8,72,128]{2,1,0:T(8,128)S(1)}, u32[]{:S(2)}, u32[]{:S(2)}) async-start(f32[8,72,128]{2,1,0:T(8,128)} %shard_map.94), calls=%async_computation.8 | async-start | bytes 589824 | tf_op jit(solution)/shard_map/all_to_all | solution.py:47
  168.8 4.7 %shard_map.95 = f32[1024,128]{1,0:T(8,128)} custom-call(f32[64,1024]{1,0:T(8,128)S(1)} %bitcast.54, bf16[1024,128]{1,0:T(8,128)(2,1)S(1)} %copy-done.2, bf16[2,576,128]{2,1,0:T(8,128)(2,1)S(1)} %pad_maximum_fusion.refs_2_, bf16[2,576,128]{2,1,0:T(8,128)(2,1)S(1)} %collective-permute-done.8.refs_3_, bf16[2,576,128]{2,1,0:T(8,128)(2,1)S(1)} %collective-permute-done.9.refs_4_, ...), custom_call_target="tpu_custom_call" | custom-call | flops 2147483648 | bytes 3145728 | tf_op jit(solution)/shard_map/pallas_call | solution.py:356
  173.5 2.2 %all-to-all-done.8 = f32[8,72,128]{2,1,0:T(8,128)S(1)} async-done(((f32[8,72,128]{2,1,0:T(8,128)}), f32[8,72,128]{2,1,0:T(8,128)S(1)}, u32[]{:S(2)}, u32[]{:S(2)}) %all-to-all-start.8) | async-done | bytes 294944 | tf_op jit(solution)/shard_map/all_to_all | solution.py:47
  (53 shorter events, 13.9 us)
Async XLA Ops:
  2.0 27.3 %all-to-all-start = ((bf16[8,16,576]{2,1,0:T(8,128)(2,1)}), bf16[8,16,576]{2,1,0:T(8,128)(2,1)S(1)}, u32[]{:S(2)}, u32[]{:S(2)}) async-start(bf16[8,16,576]{2,1,0:T(8,128)(2,1)} %broadcast_in_dim.27), calls=%async_computation | async-start | bytes 327680 | tf_op jit(solution)/shard_map/all_to_all | solution.py:47
  16.9 1.0 copy-start.1
  18.4 16.2 %collective-permute-start.1 = (f32[16,1024]{1,0:T(8,128)S(1)}, f32[16,1024]{1,0:T(8,128)S(1)}, u32[]{:S(2)}, u32[]{:S(2)}) collective-permute-start(f32[16,1024]{1,0:T(8,128)S(1)} %get-tuple-element.35), channel_id=1, source_target_pairs={{0,128},{64,192},{128,0},{192,64},{256,384},{320,448},{384,256},{4... | collective-permute-start | bytes 196616 | tf_op jit(solution)/shard_map/ppermute | solution.py:231
  21.5 13.1 %collective-permute-start.2 = (f32[16,1024]{1,0:T(8,128)S(1)}, f32[16,1024]{1,0:T(8,128)S(1)}, u32[]{:S(2)}, u32[]{:S(2)}) collective-permute-start(f32[16,1024]{1,0:T(8,128)S(1)} %get-tuple-element.37), channel_id=1, source_target_pairs={{0,256},{64,320},{128,384},{192,448},{256,0},{320,64},{384,128},{4... | collective-permute-start | bytes 196616 | tf_op jit(solution)/shard_map/ppermute | solution.py:231
  25.9 8.7 %collective-permute-start.3 = (f32[16,1024]{1,0:T(8,128)S(1)}, f32[16,1024]{1,0:T(8,128)S(1)}, u32[]{:S(2)}, u32[]{:S(2)}) collective-permute-start(f32[16,1024]{1,0:T(8,128)S(1)} %get-tuple-element.36), channel_id=1, source_target_pairs={{0,384},{64,448},{128,256},{192,320},{256,128},{320,192},{384,0},{... | collective-permute-start | bytes 196616 | tf_op jit(solution)/shard_map/ppermute | solution.py:231
  30.2 12.7 %all-to-all-start.1 = ((bf16[4,8,16,576]{3,2,1,0:T(8,128)(2,1)}), bf16[4,8,16,576]{3,2,1,0:T(8,128)(2,1)S(1)}, u32[]{:S(2)}, u32[]{:S(2)}) async-start(bf16[4,8,16,576]{3,2,1,0:T(8,128)(2,1)} %broadcast_in_dim.28), calls=%async_computation.1 | async-start | bytes 1310720 | tf_op jit(solution)/shard_map/all_to_all | solution.py:47
  34.6 13.9 %collective-permute-start.4 = (f32[16,1024]{1,0:T(8,128)S(1)}, f32[16,1024]{1,0:T(8,128)S(1)}, u32[]{:S(2)}, u32[]{:S(2)}) collective-permute-start(f32[16,1024]{1,0:T(8,128)S(1)} %fusion.3.one_ref), channel_id=1, source_target_pairs={{0,64},{64,0},{128,192},{192,128},{256,320},{320,256},{384,448},{4... | collective-permute-start | bytes 196616 | tf_op jit(solution)/shard_map/ppermute | solution.py:265
  42.6 6.2 %copy-start = (bf16[1024,576]{0,1:T(8,128)(2,1)S(1)}, bf16[1024,576]{0,1:T(8,128)(2,1)}, u32[]{:S(2)}) copy-start(bf16[1024,576]{0,1:T(8,128)(2,1)} %param.7) | copy-start | bytes 3538948
  43.0 7.9 %collective-permute-start = (bf16[4,8,16,576]{3,2,1,0:T(8,128)(2,1)S(1)}, bf16[4,8,16,576]{3,2,1,0:T(8,128)(2,1)S(1)}, u32[]{:S(2)}, u32[]{:S(2)}) collective-permute-start(bf16[4,8,16,576]{3,2,1,0:T(8,128)(2,1)S(1)} %all-to-all-done.1), channel_id=1, source_target_pairs={{0,1},{1,0},{2,3},{3,2},{4,5},{5,4},{6,7},{7,6},{8,9},{9,8},{10,11... | collective-permute-start | bytes 1769480 | tf_op jit(solution)/shard_map/ppermute | solution.py:275
  53.0 73.7 %copy-start.2 = (bf16[1024,128]{1,0:T(8,128)(2,1)S(1)}, bf16[1024,128]{1,0:T(8,128)(2,1)}, u32[]{:S(2)}) copy-start(bf16[1024,128]{1,0:T(8,128)(2,1)} %refs_1_.3) | copy-start | bytes 786436
  53.7 22.7 %all-to-all-start.2 = ((f32[8,24,128]{2,1,0:T(8,128)}), f32[8,24,128]{2,1,0:T(8,128)S(1)}, u32[]{:S(2)}, u32[]{:S(2)}) async-start(f32[8,24,128]{2,1,0:T(8,128)} %broadcast_in_dim.30), calls=%async_computation.2 | async-start | bytes 196608 | tf_op jit(solution)/shard_map/all_to_all | solution.py:47
  66.4 17.5 %collective-permute-start.5 = (bf16[288,128]{1,0:T(8,128)(2,1)S(1)}, bf16[288,128]{1,0:T(8,128)(2,1)S(1)}, u32[]{:S(2)}, u32[]{:S(2)}) collective-permute-start(bf16[288,128]{1,0:T(8,128)(2,1)S(1)} %constant_dynamic-slice_fusion), channel_id=1, source_target_pairs={{0,64},{64,0},{128,192},{192,128},{256,320},{320,256},{384,448},{4... | collective-permute-start | bytes 221192 | tf_op jit(solution)/shard_map/ppermute | solution.py:303
  77.1 11.9 %all-to-all-start.3 = ((f32[8,24,128]{2,1,0:T(8,128)}), f32[8,24,128]{2,1,0:T(8,128)S(1)}, u32[]{:S(2)}, u32[]{:S(2)}) async-start(f32[8,24,128]{2,1,0:T(8,128)} %shard_map.89), calls=%async_computation.3 | async-start | bytes 196608 | tf_op jit(solution)/shard_map/all_to_all | solution.py:47
  83.9 8.0 %collective-permute-start.6 = (bf16[288,128]{1,0:T(8,128)(2,1)S(1)}, bf16[288,128]{1,0:T(8,128)(2,1)S(1)}, u32[]{:S(2)}, u32[]{:S(2)}) collective-permute-start(bf16[288,128]{1,0:T(8,128)(2,1)S(1)} %collective-permute-done.5), channel_id=1, source_target_pairs={{0,1},{1,0},{2,3},{3,2},{4,5},{5,4},{6,7},{7,6},{8,9},{9,8},{10,11... | collective-permute-start | bytes 221192 | tf_op jit(solution)/shard_map/ppermute | solution.py:307
  92.0 10.9 %all-to-all-start.4 = ((f32[4,16,1024]{2,1,0:T(8,128)}), f32[4,16,1024]{2,1,0:T(8,128)S(1)}, u32[]{:S(2)}, u32[]{:S(2)}) async-start(f32[4,16,1024]{2,1,0:T(8,128)} %bitcast.21), calls=%async_computation.4 | async-start | bytes 524288 | tf_op jit(solution)/shard_map/all_to_all | solution.py:47
  95.8 25.4 %collective-permute-start.8 = (bf16[2,576,128]{2,1,0:T(8,128)(2,1)S(1)}, bf16[2,576,128]{2,1,0:T(8,128)(2,1)S(1)}, u32[]{:S(2)}, u32[]{:S(2)}) collective-permute-start(bf16[2,576,128]{2,1,0:T(8,128)(2,1)S(1)} %pad_maximum_fusion.refs_2_), channel_id=1, source_target_pairs={{0,128},{64,192},{128,0},{192,64},{256,384},{320,448},{384,256},{4... | collective-permute-start | bytes 884744 | tf_op jit(solution)/shard_map/ppermute | solution.py:328
  99.2 22.0 %collective-permute-start.9 = (bf16[2,576,128]{2,1,0:T(8,128)(2,1)S(1)}, bf16[2,576,128]{2,1,0:T(8,128)(2,1)S(1)}, u32[]{:S(2)}, u32[]{:S(2)}) collective-permute-start(bf16[2,576,128]{2,1,0:T(8,128)(2,1)S(1)} %pad_maximum_fusion.refs_2_), channel_id=1, source_target_pairs={{0,384},{64,448},{128,256},{192,320},{256,128},{320,192},{384,0},{... | collective-permute-start | bytes 884744 | tf_op jit(solution)/shard_map/ppermute | solution.py:328
  102.9 14.0 %collective-permute-start.7 = (f32[16,1024]{1,0:T(8,128)S(1)}, f32[16,1024]{1,0:T(8,128)S(1)}, u32[]{:S(2)}, u32[]{:S(2)}) collective-permute-start(f32[16,1024]{1,0:T(8,128)S(1)} %reduce_sum.18.one_ref), channel_id=1, source_target_pairs={{0,64},{64,0},{128,192},{192,128},{256,320},{320,256},{384,448},{4... | collective-permute-start | bytes 196616 | tf_op jit(solution)/shard_map/ppermute | solution.py:331
  117.8 8.9 %all-to-all-start.5 = ((f32[4,16,1024]{2,1,0:T(8,128)}), f32[4,16,1024]{2,1,0:T(8,128)S(1)}, u32[]{:S(2)}, u32[]{:S(2)}) async-start(f32[4,16,1024]{2,1,0:T(8,128)} %shard_map.91), calls=%async_computation.5 | async-start | bytes 524288 | tf_op jit(solution)/shard_map/all_to_all | solution.py:47
  141.9 8.7 %all-to-all-start.7 = ((f32[4,72,128]{2,1,0:T(8,128)}), f32[4,72,128]{2,1,0:T(8,128)S(1)}, u32[]{:S(2)}, u32[]{:S(2)}) async-start(f32[4,72,128]{2,1,0:T(8,128)} %shard_map.93), calls=%async_computation.7 | async-start | bytes 294912 | tf_op jit(solution)/shard_map/all_to_all | solution.py:47
  145.8 23.1 %collective-permute-start.11 = (bf16[2,576,128]{2,1,0:T(8,128)(2,1)S(1)}, bf16[2,576,128]{2,1,0:T(8,128)(2,1)S(1)}, u32[]{:S(2)}, u32[]{:S(2)}) collective-permute-start(bf16[2,576,128]{2,1,0:T(8,128)(2,1)S(1)} %pad_maximum_fusion.refs_2_), channel_id=1, source_target_pairs={{0,256},{64,320},{128,384},{192,448},{256,0},{320,64},{384,128},{4... | collective-permute-start | bytes 884744 | tf_op jit(solution)/shard_map/ppermute | solution.py:328
  150.6 9.4 %collective-permute-start.10 = (f32[72,128]{1,0:T(8,128)S(1)}, f32[72,128]{1,0:T(8,128)S(1)}, u32[]{:S(2)}, u32[]{:S(2)}) collective-permute-start(f32[72,128]{1,0:T(8,128)S(1)} %reduce_sum.19.one_ref), channel_id=1, source_target_pairs={{0,8},{1,9},{2,10},{3,11},{4,12},{5,13},{6,14},{7,15},{8,0},{9,1},... | collective-permute-start | bytes 110600 | tf_op jit(solution)/shard_map/ppermute | solution.py:350
  160.8 14.9 %all-to-all-start.8 = ((f32[8,72,128]{2,1,0:T(8,128)}), f32[8,72,128]{2,1,0:T(8,128)S(1)}, u32[]{:S(2)}, u32[]{:S(2)}) async-start(f32[8,72,128]{2,1,0:T(8,128)} %shard_map.94), calls=%async_computation.8 | async-start | bytes 589824 | tf_op jit(solution)/shard_map/all_to_all | solution.py:47

commit v8 on v6

--- a/solution.py
+++ b/solution.py
@@ -289,19 +289,20 @@
     over_x = exchanged(partial.reshape(NX, share_rows, key_count), "heads", groups_x).sum(axis=0)
     other = lax.ppermute(over_x, "heads", pairs_zh)
     other, swapped = lax.optimization_barrier((other, swapped))
-    swapped_other = lax.ppermute(swapped, "tokens", pairs_c)
     dlogit = call(dlogit_kernel, shape((NX, share_rows, key_count), f32))(
         over_x, other, logits, stats
     )
+    dlogit, swapped = lax.optimization_barrier((dlogit, swapped))
+    swapped_other = lax.ppermute(swapped, "tokens", pairs_c)
     dlogit = exchanged(dlogit, "heads", groups_x).reshape(query_count, key_count)
-    dlogit, swapped_other = lax.optimization_barrier((dlogit, swapped_other))
     halves = jnp.where(
         core == 0,
         jnp.concatenate([swapped, swapped_other]),
         jnp.concatenate([swapped_other, swapped]),
     )
     pair = jnp.stack([mine, halves])
-    messages = [pair] + [lax.ppermute(pair, "heads", pairs_x(flip)) for flip in range(1, NX)]
+    nearer = jnp.concatenate([pair, lax.ppermute(pair, "heads", pairs_x(1))])
+    messages = [nearer, lax.ppermute(nearer, "heads", pairs_x(2))]
 
     query_lines = query_count * index_heads
     piece_rows = -(-(query_lines + index_heads) // (NYC * 8)) * 8

time: 176 us -> 178 us (1.011)
  waiting for transfers between devices: 16.8 us -> 25 us
  blocking collectives: 47.9 us -> 43.1 us
  starting transfers between devices: 89.3 us -> 87.3 us
    all_to_all x6, waiting for transfers between devices: 2.17 us -> 9.13 us  [exchanged(): lax.all_to_all(parts, axis, 0, 0, tiled=True, axis_index_groups=groups)]
    all_to_all x3, blocking collectives: 47.9 us -> 43.1 us  [exchanged(): lax.all_to_all(parts, axis, 0, 0, tiled=True, axis_index_groups=groups)]
    ppermute x1, waiting for transfers between devices: 4.43 us -> 6.66 us  [local(): other = lax.ppermute(piece, 'tokens', pairs_z4)]
    ppermute x3 -> x2, starting transfers between devices: 8.41 us -> 6.33 us  [the longest x1 3.37 us: local(): nearer = jnp.concatenate([pair, lax.ppermute(pair, 'heads', pairs_x(1))])]
  transfers between devices with their start and end apart: 18 -> 17, of which waited for: 6 -> 7; matrix products, arithmetic and copies ran while one was open for 2% -> 2% of each run, Pallas kernels for 4% -> 5%
where the time goes in v8:
time: 178 us; the launch traced here: 177 us
  starting transfers between devices  87.3 us (49%)
  blocking collectives  43.1 us (24%)
  waiting for transfers between devices  25 us (14%)
  Pallas kernels  12.9 us (7%)
  local copies, waits for them, and re-layouts  6.51 us (4%)
    all_to_all x3, blocking collectives, exchanged(): lax.all_to_all(parts, axis, 0, 0, tiled=True, axis_index_groups=groups)  43.1 us
    all_to_all x6, starting transfers between devices, exchanged(): lax.all_to_all(parts, axis, 0, 0, tiled=True, axis_index_groups=groups)  34.1 us
    ppermute x2, starting transfers between devices, local(): other = lax.ppermute(over_x, 'heads', pairs_zh)  14 us
    ppermute x3, starting transfers between devices, x_scatter_sum(): total = total + lax.ppermute(piece, 'heads', pairs_x(flip))  9.58 us
    all_to_all x6, waiting for transfers between devices, exchanged(): lax.all_to_all(parts, axis, 0, 0, tiled=True, axis_index_groups=groups)  9.13 us
    ppermute x1, starting transfers between devices, local(): swapped = lax.ppermute(sent, 'heads', pairs_zh)  7.95 us
    ppermute x1, waiting for transfers between devices, local(): other = lax.ppermute(piece, 'tokens', pairs_z4)  6.66 us
    ppermute x2, waiting for transfers between devices, local(): other = lax.ppermute(over_x, 'heads', pairs_zh)  6.23 us
  transfers between devices with their start and end apart: 17, of which 7 were waited for; matrix products, arithmetic and copies ran while one was open for 2% of the time, Pallas kernels for 5%

profile of v8, /device:TPU:1, one launch (start us, length us, event | category | flops | bytes accessed | tf_op | source)
XLA Modules:
  0.0 176.8 jit_solution(12830733688311574672)
XLA Ops:
  0.6 1.4 broadcast_in_dim.27
  2.1 13.1 %all-to-all-start = ((bf16[8,16,576]{2,1,0:T(8,128)(2,1)}), bf16[8,16,576]{2,1,0:T(8,128)(2,1)S(1)}, u32[]{:S(2)}, u32[]{:S(2)}) async-start(bf16[8,16,576]{2,1,0:T(8,128)(2,1)} %broadcast_in_dim.27), calls=%async_computation | async-start | bytes 327680 | tf_op jit(solution)/shard_map/all_to_all | solution.py:47
  18.4 3.1 %collective-permute-start.1 = (f32[16,1024]{1,0:T(8,128)S(1)}, f32[16,1024]{1,0:T(8,128)S(1)}, u32[]{:S(2)}, u32[]{:S(2)}) collective-permute-start(f32[16,1024]{1,0:T(8,128)S(1)} %get-tuple-element.31), channel_id=1, source_target_pairs={{0,128},{64,192},{128,0},{192,64},{256,384},{320,448},{384,256},{4... | collective-permute-start | bytes 196616 | tf_op jit(solution)/shard_map/ppermute | solution.py:216
  21.5 4.4 %collective-permute-start.2 = (f32[16,1024]{1,0:T(8,128)S(1)}, f32[16,1024]{1,0:T(8,128)S(1)}, u32[]{:S(2)}, u32[]{:S(2)}) collective-permute-start(f32[16,1024]{1,0:T(8,128)S(1)} %get-tuple-element.33), channel_id=1, source_target_pairs={{0,256},{64,320},{128,384},{192,448},{256,0},{320,64},{384,128},{4... | collective-permute-start | bytes 196616 | tf_op jit(solution)/shard_map/ppermute | solution.py:216
  25.9 2.1 %collective-permute-start.3 = (f32[16,1024]{1,0:T(8,128)S(1)}, f32[16,1024]{1,0:T(8,128)S(1)}, u32[]{:S(2)}, u32[]{:S(2)}) collective-permute-start(f32[16,1024]{1,0:T(8,128)S(1)} %get-tuple-element.32), channel_id=1, source_target_pairs={{0,384},{64,448},{128,256},{192,320},{256,128},{320,192},{384,0},{... | collective-permute-start | bytes 196616 | tf_op jit(solution)/shard_map/ppermute | solution.py:216
  28.9 4.2 %all-to-all-start.1 = ((bf16[4,8,16,576]{3,2,1,0:T(8,128)(2,1)}), bf16[4,8,16,576]{3,2,1,0:T(8,128)(2,1)S(1)}, u32[]{:S(2)}, u32[]{:S(2)}) async-start(bf16[4,8,16,576]{3,2,1,0:T(8,128)(2,1)} %broadcast_in_dim.28), calls=%async_computation.1 | async-start | bytes 1310720 | tf_op jit(solution)/shard_map/all_to_all | solution.py:47
  33.8 7.9 %collective-permute-start.4 = (f32[16,1024]{1,0:T(8,128)S(1)}, f32[16,1024]{1,0:T(8,128)S(1)}, u32[]{:S(2)}, u32[]{:S(2)}) collective-permute-start(f32[16,1024]{1,0:T(8,128)S(1)} %fusion.3.one_ref), channel_id=1, source_target_pairs={{0,64},{64,0},{128,192},{192,128},{256,320},{320,256},{384,448},{4... | collective-permute-start | bytes 196616 | tf_op jit(solution)/shard_map/ppermute | solution.py:250
  42.0 4.8 %collective-permute-start = (bf16[4,8,16,576]{3,2,1,0:T(8,128)(2,1)S(1)}, bf16[4,8,16,576]{3,2,1,0:T(8,128)(2,1)S(1)}, u32[]{:S(2)}, u32[]{:S(2)}) collective-permute-start(bf16[4,8,16,576]{3,2,1,0:T(8,128)(2,1)S(1)} %all-to-all-done.1), channel_id=1, source_target_pairs={{0,1},{1,0},{2,3},{3,2},{4,5},{5,4},{6,7},{7,6},{8,9},{9,8},{10,11... | collective-permute-start | bytes 1769480 | tf_op jit(solution)/shard_map/ppermute | solution.py:260
  48.0 1.3 shard_map.85
  49.3 1.4 shard_map.86
  50.7 22.7 %all_to_all.45.stats_ref = f32[8,24,128]{2,1,0:T(8,128)S(1)} all-to-all(f32[8,24,128]{2,1,0:T(8,128)S(1)} %broadcast_in_dim.30), channel_id=1, replica_groups={{0,2,4,6,8,10,12,14},{1,3,5,7,9,11,13,15},{16,18,20,22,24,26,28,30},{17..., dimensions={0} | all-to-all | bytes 196608 | tf_op jit(solution)/shard_map/all_to_all | solution.py:47
  73.4 11.6 %all_to_all.46.stats_ref = f32[8,24,128]{2,1,0:T(8,128)S(1)} all-to-all(f32[8,24,128]{2,1,0:T(8,128)S(1)} %shard_map.89), channel_id=1, replica_groups={{0,16,32,48,1,17,33,49},{2,18,34,50,3,19,35,51},{4,20,36,52,5,21,37,53}..., dimensions={0} | all-to-all | bytes 196608 | tf_op jit(solution)/shard_map/all_to_all | solution.py:47
  85.0 1.5 shard_map.90
  86.5 3.7 %all-to-all-start.4 = ((f32[4,16,1024]{2,1,0:T(8,128)}), f32[4,16,1024]{2,1,0:T(8,128)S(1)}, u32[]{:S(2)}, u32[]{:S(2)}) async-start(f32[4,16,1024]{2,1,0:T(8,128)} %bitcast.21), calls=%async_computation.4 | async-start | bytes 524288 | tf_op jit(solution)/shard_map/all_to_all | solution.py:47
  90.3 8.0 %collective-permute-start.6 = (bf16[288,128]{1,0:T(8,128)(2,1)S(1)}, bf16[288,128]{1,0:T(8,128)(2,1)S(1)}, u32[]{:S(2)}, u32[]{:S(2)}) collective-permute-start(bf16[288,128]{1,0:T(8,128)(2,1)S(1)} %constant_dynamic-slice_fusion), channel_id=1, source_target_pairs={{0,64},{64,0},{128,192},{192,128},{256,320},{320,256},{384,448},{4... | collective-permute-start | bytes 221192 | tf_op jit(solution)/shard_map/ppermute | solution.py:288
  98.3 6.0 %collective-permute-start.5 = (f32[16,1024]{1,0:T(8,128)S(1)}, f32[16,1024]{1,0:T(8,128)S(1)}, u32[]{:S(2)}, u32[]{:S(2)}) collective-permute-start(f32[16,1024]{1,0:T(8,128)S(1)} %reduce_sum.18.one_ref), channel_id=1, source_target_pairs={{0,64},{64,0},{128,192},{192,128},{256,320},{320,256},{384,448},{4... | collective-permute-start | bytes 196616 | tf_op jit(solution)/shard_map/ppermute | solution.py:290
  104.3 3.0 %collective-permute-done.6 = bf16[288,128]{1,0:T(8,128)(2,1)S(1)} collective-permute-done((bf16[288,128]{1,0:T(8,128)(2,1)S(1)}, bf16[288,128]{1,0:T(8,128)(2,1)S(1)}, u32[]{:S(2)}, u32[]{:S(2)}) %collective-permute-start.6) | collective-permute-done | bytes 73760 | tf_op jit(solution)/shard_map/ppermute | solution.py:288
  107.3 5.3 %collective-permute-done.5.two_ref = f32[16,1024]{1,0:T(8,128)S(1)} collective-permute-done((f32[16,1024]{1,0:T(8,128)S(1)}, f32[16,1024]{1,0:T(8,128)S(1)}, u32[]{:S(2)}, u32[]{:S(2)}) %collective-permute-start.5) | collective-permute-done | bytes 65568 | tf_op jit(solution)/shard_map/ppermute | solution.py:290
  113.5 5.9 %collective-permute-start.8 = (bf16[288,128]{1,0:T(8,128)(2,1)S(1)}, bf16[288,128]{1,0:T(8,128)(2,1)S(1)}, u32[]{:S(2)}, u32[]{:S(2)}) collective-permute-start(bf16[288,128]{1,0:T(8,128)(2,1)S(1)} %collective-permute-done.6), channel_id=1, source_target_pairs={{0,1},{1,0},{2,3},{3,2},{4,5},{5,4},{6,7},{7,6},{8,9},{9,8},{10,11... | collective-permute-start | bytes 221192 | tf_op jit(solution)/shard_map/ppermute | solution.py:296
  119.4 4.1 %all-to-all-start.5 = ((f32[4,16,1024]{2,1,0:T(8,128)}), f32[4,16,1024]{2,1,0:T(8,128)S(1)}, u32[]{:S(2)}, u32[]{:S(2)}) async-start(f32[4,16,1024]{2,1,0:T(8,128)} %shard_map.91), calls=%async_computation.5 | async-start | bytes 524288 | tf_op jit(solution)/shard_map/all_to_all | solution.py:47
  123.6 3.4 %collective-permute-start.9 = (bf16[2,576,128]{2,1,0:T(8,128)(2,1)S(1)}, bf16[2,576,128]{2,1,0:T(8,128)(2,1)S(1)}, u32[]{:S(2)}, u32[]{:S(2)}) collective-permute-start(bf16[2,576,128]{2,1,0:T(8,128)(2,1)S(1)} %pad_maximum_fusion.1), channel_id=1, source_target_pairs={{0,128},{64,192},{128,0},{192,64},{256,384},{320,448},{384,256},{4... | collective-permute-start | bytes 884744 | tf_op jit(solution)/shard_map/ppermute | solution.py:304
  127.0 2.8 %all-to-all-done.5 = f32[4,16,1024]{2,1,0:T(8,128)S(1)} async-done(((f32[4,16,1024]{2,1,0:T(8,128)}), f32[4,16,1024]{2,1,0:T(8,128)S(1)}, u32[]{:S(2)}, u32[]{:S(2)}) %all-to-all-start.5) | async-done | bytes 262176 | tf_op jit(solution)/shard_map/all_to_all | solution.py:47
  129.7 1.8 shard_map.92
  131.5 4.8 %all-to-all-start.6 = ((f32[8,72,128]{2,1,0:T(8,128)}), f32[8,72,128]{2,1,0:T(8,128)S(1)}, u32[]{:S(2)}, u32[]{:S(2)}) async-start(f32[8,72,128]{2,1,0:T(8,128)} %bitcast.23), calls=%async_computation.6 | async-start | bytes 589824 | tf_op jit(solution)/shard_map/all_to_all | solution.py:47
  136.4 3.0 %collective-permute-start.10 = (bf16[4,576,128]{2,1,0:T(8,128)(2,1)S(1)}, bf16[4,576,128]{2,1,0:T(8,128)(2,1)S(1)}, u32[]{:S(2)}, u32[]{:S(2)}) collective-permute-start(bf16[4,576,128]{2,1,0:T(8,128)(2,1)S(1)} %pad_maximum_fusion.refs_2_), channel_id=1, source_target_pairs={{0,256},{64,320},{128,384},{192,448},{256,0},{320,64},{384,128},{4... | collective-permute-start | bytes 1769480 | tf_op jit(solution)/shard_map/ppermute | solution.py:305
  139.4 4.2 %all-to-all-done.6.parts_ref = f32[8,72,128]{2,1,0:T(8,128)S(1)} async-done(((f32[8,72,128]{2,1,0:T(8,128)}), f32[8,72,128]{2,1,0:T(8,128)S(1)}, u32[]{:S(2)}, u32[]{:S(2)}) %all-to-all-start.6) | async-done | bytes 294944 | tf_op jit(solution)/shard_map/all_to_all | solution.py:47
  143.6 8.8 %all_to_all.47 = f32[4,72,128]{2,1,0:T(8,128)S(1)} all-to-all(f32[4,72,128]{2,1,0:T(8,128)S(1)} %shard_map.93), channel_id=1, replica_groups={{0,2,4,6},{1,3,5,7},{16,18,20,22},{17,19,21,23},{32,34,36,38},{33,35,37..., dimensions={0} | all-to-all | bytes 294912 | tf_op jit(solution)/shard_map/all_to_all | solution.py:47
  152.4 4.7 %collective-permute-start.7 = (f32[72,128]{1,0:T(8,128)S(1)}, f32[72,128]{1,0:T(8,128)S(1)}, u32[]{:S(2)}, u32[]{:S(2)}) collective-permute-start(f32[72,128]{1,0:T(8,128)S(1)} %reduce_sum.19.one_ref), channel_id=1, source_target_pairs={{0,8},{1,9},{2,10},{3,11},{4,12},{5,13},{6,14},{7,15},{8,0},{9,1},... | collective-permute-start | bytes 110600 | tf_op jit(solution)/shard_map/ppermute | solution.py:319
  157.1 6.7 %collective-permute-done.7.two_ref = f32[72,128]{1,0:T(8,128)S(1)} collective-permute-done((f32[72,128]{1,0:T(8,128)S(1)}, f32[72,128]{1,0:T(8,128)S(1)}, u32[]{:S(2)}, u32[]{:S(2)}) %collective-permute-start.7) | collective-permute-done | bytes 36896 | tf_op jit(solution)/shard_map/ppermute | solution.py:319
  164.4 4.1 %all-to-all-start.8 = ((f32[8,72,128]{2,1,0:T(8,128)}), f32[8,72,128]{2,1,0:T(8,128)S(1)}, u32[]{:S(2)}, u32[]{:S(2)}) async-start(f32[8,72,128]{2,1,0:T(8,128)} %shard_map.94), calls=%async_computation.8 | async-start | bytes 589824 | tf_op jit(solution)/shard_map/all_to_all | solution.py:47
  168.5 4.7 %shard_map.95 = f32[1024,128]{1,0:T(8,128)} custom-call(f32[64,1024]{1,0:T(8,128)S(1)} %bitcast.53, bf16[1024,128]{1,0:T(8,128)(2,1)S(1)} %copy-done.2, bf16[4,576,128]{2,1,0:T(8,128)(2,1)S(1)} %pad_maximum_fusion.refs_2_, bf16[4,576,128]{2,1,0:T(8,128)(2,1)S(1)} %collective-permute-done.10.refs_3_), custom_call_target="tpu_custom_call" | custom-call | flops 2147483648 | bytes 3145728 | tf_op jit(solution)/shard_map/pallas_call | solution.py:325
  173.2 2.2 %all-to-all-done.8 = f32[8,72,128]{2,1,0:T(8,128)S(1)} async-done(((f32[8,72,128]{2,1,0:T(8,128)}), f32[8,72,128]{2,1,0:T(8,128)S(1)}, u32[]{:S(2)}, u32[]{:S(2)}) %all-to-all-start.8) | async-done | bytes 294944 | tf_op jit(solution)/shard_map/all_to_all | solution.py:47
  (52 shorter events, 9.2 us)
Async XLA Ops:
  0.6 32.4 %copy-start.3 = (s32[64]{0:T(128)S(1)}, s32[64]{0:T(128)}, u32[]{:S(2)}) copy-start(s32[64]{0:T(128)} %param.11) | copy-start | bytes 772
  2.1 25.9 %all-to-all-start = ((bf16[8,16,576]{2,1,0:T(8,128)(2,1)}), bf16[8,16,576]{2,1,0:T(8,128)(2,1)S(1)}, u32[]{:S(2)}, u32[]{:S(2)}) async-start(bf16[8,16,576]{2,1,0:T(8,128)(2,1)} %broadcast_in_dim.27), calls=%async_computation | async-start | bytes 327680 | tf_op jit(solution)/shard_map/all_to_all | solution.py:47
  16.9 1.0 copy-start.1
  18.4 15.4 %collective-permute-start.1 = (f32[16,1024]{1,0:T(8,128)S(1)}, f32[16,1024]{1,0:T(8,128)S(1)}, u32[]{:S(2)}, u32[]{:S(2)}) collective-permute-start(f32[16,1024]{1,0:T(8,128)S(1)} %get-tuple-element.31), channel_id=1, source_target_pairs={{0,128},{64,192},{128,0},{192,64},{256,384},{320,448},{384,256},{4... | collective-permute-start | bytes 196616 | tf_op jit(solution)/shard_map/ppermute | solution.py:216
  21.5 12.3 %collective-permute-start.2 = (f32[16,1024]{1,0:T(8,128)S(1)}, f32[16,1024]{1,0:T(8,128)S(1)}, u32[]{:S(2)}, u32[]{:S(2)}) collective-permute-start(f32[16,1024]{1,0:T(8,128)S(1)} %get-tuple-element.33), channel_id=1, source_target_pairs={{0,256},{64,320},{128,384},{192,448},{256,0},{320,64},{384,128},{4... | collective-permute-start | bytes 196616 | tf_op jit(solution)/shard_map/ppermute | solution.py:216
  25.9 7.9 %collective-permute-start.3 = (f32[16,1024]{1,0:T(8,128)S(1)}, f32[16,1024]{1,0:T(8,128)S(1)}, u32[]{:S(2)}, u32[]{:S(2)}) collective-permute-start(f32[16,1024]{1,0:T(8,128)S(1)} %get-tuple-element.32), channel_id=1, source_target_pairs={{0,384},{64,448},{128,256},{192,320},{256,128},{320,192},{384,0},{... | collective-permute-start | bytes 196616 | tf_op jit(solution)/shard_map/ppermute | solution.py:216
  28.9 13.1 %all-to-all-start.1 = ((bf16[4,8,16,576]{3,2,1,0:T(8,128)(2,1)}), bf16[4,8,16,576]{3,2,1,0:T(8,128)(2,1)S(1)}, u32[]{:S(2)}, u32[]{:S(2)}) async-start(bf16[4,8,16,576]{3,2,1,0:T(8,128)(2,1)} %broadcast_in_dim.28), calls=%async_computation.1 | async-start | bytes 1310720 | tf_op jit(solution)/shard_map/all_to_all | solution.py:47
  33.8 13.9 %collective-permute-start.4 = (f32[16,1024]{1,0:T(8,128)S(1)}, f32[16,1024]{1,0:T(8,128)S(1)}, u32[]{:S(2)}, u32[]{:S(2)}) collective-permute-start(f32[16,1024]{1,0:T(8,128)S(1)} %fusion.3.one_ref), channel_id=1, source_target_pairs={{0,64},{64,0},{128,192},{192,128},{256,320},{320,256},{384,448},{4... | collective-permute-start | bytes 196616 | tf_op jit(solution)/shard_map/ppermute | solution.py:250
  42.0 6.0 %copy-start = (bf16[1024,576]{0,1:T(8,128)(2,1)S(1)}, bf16[1024,576]{0,1:T(8,128)(2,1)}, u32[]{:S(2)}) copy-start(bf16[1024,576]{0,1:T(8,128)(2,1)} %param.7) | copy-start | bytes 3538948
  42.0 7.3 %collective-permute-start = (bf16[4,8,16,576]{3,2,1,0:T(8,128)(2,1)S(1)}, bf16[4,8,16,576]{3,2,1,0:T(8,128)(2,1)S(1)}, u32[]{:S(2)}, u32[]{:S(2)}) collective-permute-start(bf16[4,8,16,576]{3,2,1,0:T(8,128)(2,1)S(1)} %all-to-all-done.1), channel_id=1, source_target_pairs={{0,1},{1,0},{2,3},{3,2},{4,5},{5,4},{6,7},{7,6},{8,9},{9,8},{10,11... | collective-permute-start | bytes 1769480 | tf_op jit(solution)/shard_map/ppermute | solution.py:260
  50.6 79.1 %copy-start.2 = (bf16[1024,128]{1,0:T(8,128)(2,1)S(1)}, bf16[1024,128]{1,0:T(8,128)(2,1)}, u32[]{:S(2)}) copy-start(bf16[1024,128]{1,0:T(8,128)(2,1)} %refs_1_.3) | copy-start | bytes 786436
  86.5 11.7 %all-to-all-start.4 = ((f32[4,16,1024]{2,1,0:T(8,128)}), f32[4,16,1024]{2,1,0:T(8,128)S(1)}, u32[]{:S(2)}, u32[]{:S(2)}) async-start(f32[4,16,1024]{2,1,0:T(8,128)} %bitcast.21), calls=%async_computation.4 | async-start | bytes 524288 | tf_op jit(solution)/shard_map/all_to_all | solution.py:47
  90.3 17.0 %collective-permute-start.6 = (bf16[288,128]{1,0:T(8,128)(2,1)S(1)}, bf16[288,128]{1,0:T(8,128)(2,1)S(1)}, u32[]{:S(2)}, u32[]{:S(2)}) collective-permute-start(bf16[288,128]{1,0:T(8,128)(2,1)S(1)} %constant_dynamic-slice_fusion), channel_id=1, source_target_pairs={{0,64},{64,0},{128,192},{192,128},{256,320},{320,256},{384,448},{4... | collective-permute-start | bytes 221192 | tf_op jit(solution)/shard_map/ppermute | solution.py:288
  98.3 14.4 %collective-permute-start.5 = (f32[16,1024]{1,0:T(8,128)S(1)}, f32[16,1024]{1,0:T(8,128)S(1)}, u32[]{:S(2)}, u32[]{:S(2)}) collective-permute-start(f32[16,1024]{1,0:T(8,128)S(1)} %reduce_sum.18.one_ref), channel_id=1, source_target_pairs={{0,64},{64,0},{128,192},{192,128},{256,320},{320,256},{384,448},{4... | collective-permute-start | bytes 196616 | tf_op jit(solution)/shard_map/ppermute | solution.py:290
  113.5 10.0 %collective-permute-start.8 = (bf16[288,128]{1,0:T(8,128)(2,1)S(1)}, bf16[288,128]{1,0:T(8,128)(2,1)S(1)}, u32[]{:S(2)}, u32[]{:S(2)}) collective-permute-start(bf16[288,128]{1,0:T(8,128)(2,1)S(1)} %collective-permute-done.6), channel_id=1, source_target_pairs={{0,1},{1,0},{2,3},{3,2},{4,5},{5,4},{6,7},{7,6},{8,9},{9,8},{10,11... | collective-permute-start | bytes 221192 | tf_op jit(solution)/shard_map/ppermute | solution.py:296
  119.4 10.4 %all-to-all-start.5 = ((f32[4,16,1024]{2,1,0:T(8,128)}), f32[4,16,1024]{2,1,0:T(8,128)S(1)}, u32[]{:S(2)}, u32[]{:S(2)}) async-start(f32[4,16,1024]{2,1,0:T(8,128)} %shard_map.91), calls=%async_computation.5 | async-start | bytes 524288 | tf_op jit(solution)/shard_map/all_to_all | solution.py:47
  123.6 12.7 %collective-permute-start.9 = (bf16[2,576,128]{2,1,0:T(8,128)(2,1)S(1)}, bf16[2,576,128]{2,1,0:T(8,128)(2,1)S(1)}, u32[]{:S(2)}, u32[]{:S(2)}) collective-permute-start(bf16[2,576,128]{2,1,0:T(8,128)(2,1)S(1)} %pad_maximum_fusion.1), channel_id=1, source_target_pairs={{0,128},{64,192},{128,0},{192,64},{256,384},{320,448},{384,256},{4... | collective-permute-start | bytes 884744 | tf_op jit(solution)/shard_map/ppermute | solution.py:304
  131.5 12.0 %all-to-all-start.6 = ((f32[8,72,128]{2,1,0:T(8,128)}), f32[8,72,128]{2,1,0:T(8,128)S(1)}, u32[]{:S(2)}, u32[]{:S(2)}) async-start(f32[8,72,128]{2,1,0:T(8,128)} %bitcast.23), calls=%async_computation.6 | async-start | bytes 589824 | tf_op jit(solution)/shard_map/all_to_all | solution.py:47
  136.4 32.1 %collective-permute-start.10 = (bf16[4,576,128]{2,1,0:T(8,128)(2,1)S(1)}, bf16[4,576,128]{2,1,0:T(8,128)(2,1)S(1)}, u32[]{:S(2)}, u32[]{:S(2)}) collective-permute-start(bf16[4,576,128]{2,1,0:T(8,128)(2,1)S(1)} %pad_maximum_fusion.refs_2_), channel_id=1, source_target_pairs={{0,256},{64,320},{128,384},{192,448},{256,0},{320,64},{384,128},{4... | collective-permute-start | bytes 1769480 | tf_op jit(solution)/shard_map/ppermute | solution.py:305
  152.4 11.3 %collective-permute-start.7 = (f32[72,128]{1,0:T(8,128)S(1)}, f32[72,128]{1,0:T(8,128)S(1)}, u32[]{:S(2)}, u32[]{:S(2)}) collective-permute-start(f32[72,128]{1,0:T(8,128)S(1)} %reduce_sum.19.one_ref), channel_id=1, source_target_pairs={{0,8},{1,9},{2,10},{3,11},{4,12},{5,13},{6,14},{7,15},{8,0},{9,1},... | collective-permute-start | bytes 110600 | tf_op jit(solution)/shard_map/ppermute | solution.py:319
  164.4 11.0 %all-to-all-start.8 = ((f32[8,72,128]{2,1,0:T(8,128)}), f32[8,72,128]{2,1,0:T(8,128)S(1)}, u32[]{:S(2)}, u32[]{:S(2)}) async-start(f32[8,72,128]{2,1,0:T(8,128)} %shard_map.94), calls=%async_computation.8 | async-start | bytes 589824 | tf_op jit(solution)/shard_map/all_to_all | solution.py:47

commit v9 on v4

--- a/solution.py
+++ b/solution.py
@@ -11,6 +11,7 @@
 NYC = NY * NC
 GRAD_SCALE = 8192.0
 VMEM = 12 << 20
+WEIGHT = 20
 
 softmax_scale = 192.0 ** (-0.5)
 masked_value = -1e30
@@ -30,6 +31,7 @@
 groups_z4 = [
     [token_at(y, half + z, c) for z in range(4)] for half in (0, 4) for y in all_y for c in all_c
 ]
+pairs_c = [(token_at(y, z, c), token_at(y, z, 1 - c)) for y in all_y for z in all_z for c in all_c]
 groups_yc = [[token_at(y, z, c) for c in all_c for y in all_y] for z in all_z]
 pairs_z4 = [(token_at(y, z, c), token_at(y, z ^ 4, c)) for y in all_y for z in all_z for c in all_c]
 groups_x = [[head_at(x, z) for x in range(NX)] for z in range(NZH)]
@@ -73,9 +75,8 @@
 
 
 def score_kernel(limit_ref, q_ref, k_ref, e_ref, m_ref, l_ref):
-    rows, keys = e_ref.shape
-    block = rows // NYC
-    key = lax.broadcasted_iota(jnp.int32, (1, keys), 1)
+    block = e_ref.shape[0] // NYC
+    key = lax.broadcasted_iota(jnp.int32, (1, e_ref.shape[1]), 1)
     k = k_ref[...]
     for b in range(NYC):
         lines = slice(b * block, (b + 1) * block)
@@ -88,30 +89,37 @@
         l_ref[b : b + 1] = as_row(jnp.sum(e, axis=1, keepdims=True))
 
 
-def message_parts(ref, tokens, heads):
-    block = ref[tokens * heads :, :].astype(f32)
-    w = block[:, :heads] + block[:, heads : 2 * heads] + block[:, 2 * heads : 3 * heads]
-    return ref[: tokens * heads, :], w
+def message_parts(one_ref, two_ref, tokens, heads):
+    rows = tokens * heads
+
+    def weights(ref):
+        block = ref[rows:, :].astype(f32)
+        return block[:, :heads] + block[:, heads : 2 * heads] + block[:, 2 * heads : 3 * heads]
+
+    iq = jnp.concatenate([one_ref[:rows, :], two_ref[:rows, :]])
+    return iq, [w[:, j : j + 1] for w in (weights(one_ref), weights(two_ref)) for j in range(heads)]
 
 
 def index_dot(iq, ik):
     return lax.dot_general(iq, ik, (((1,), (1,)), ((), ())), preferred_element_type=f32)
 
 
-def logits_kernel(heads, scale, message_ref, ik_ref, out_ref):
+def logits_kernel(heads, scale, mine_ref, one_ref, two_ref, ik_ref, out_ref):
     tokens = out_ref.shape[0]
-    iq, w = message_parts(message_ref, tokens, heads)
-    active = index_dot(iq, ik_ref[...])
+    ik = ik_ref[...]
     logits = jnp.zeros(out_ref.shape, f32)
-    for j in range(heads):
-        here = active[j * tokens : (j + 1) * tokens] * scale
-        logits = logits + w[:, j : j + 1] * jnp.maximum(here, 0.0)
+    for pair in ((mine_ref.at[0], mine_ref.at[1]), (one_ref.at[0], two_ref.at[0])):
+        iq, weights = message_parts(*pair, tokens, heads)
+        active = index_dot(iq, ik)
+        for j, w in enumerate(weights):
+            here = active[j * tokens : (j + 1) * tokens] * scale
+            logits = logits + w * jnp.maximum(here, 0.0)
     out_ref[...] = logits
 
 
-def index_stats_kernel(limit_ref, one_ref, two_ref, logits_ref, stat_ref):
+def index_stats_kernel(limit_ref, sum_ref, logits_ref, stat_ref):
     key = lax.broadcasted_iota(jnp.int32, (1, logits_ref.shape[1]), 1)
-    logits = jnp.where(key <= limit_ref[...], one_ref[...] + two_ref[...], masked_value)
+    logits = jnp.where(key <= limit_ref[...], sum_ref[...], masked_value)
     m = jnp.max(logits, axis=1, keepdims=True)
     l = jnp.sum(jnp.exp(logits - m), axis=1, keepdims=True)
     logits_ref[...] = logits
@@ -152,16 +160,17 @@
 def grad_kernel(heads, scale, d_ref, message_ref, ik_ref, out_ref):
     dlogit = d_ref[...]
     tokens = dlogit.shape[0]
-    iq, w = message_parts(message_ref, tokens, heads)
+    iq, weights = message_parts(message_ref.at[0], message_ref.at[1], tokens, heads)
     ik = ik_ref[...]
     active = index_dot(iq, ik)
+    heads = len(weights)
     row = lax.broadcasted_iota(jnp.int32, (tokens, 128), 0)
     place = row // NZ % NY * (NC * NZ) + row % NZ * NC + row // (NY * NZ)
     places = place == lax.broadcasted_iota(jnp.int32, (tokens, 128), 1)
     out_ref[tokens * heads :, :] = jnp.zeros((out_ref.shape[0] - tokens * heads, 128), f32)
-    for j in range(heads):
+    for j, w in enumerate(weights):
         here = active[j * tokens : (j + 1) * tokens]
-        gate = jnp.where(here > 0.0, dlogit * w[:, j : j + 1], 0.0).astype(bf16)
+        gate = jnp.where(here > 0.0, dlogit * w, 0.0).astype(bf16)
         grad = jnp.dot(gate, ik, preferred_element_type=f32) * scale
         for b in range(NYC):
             first = b % NY * (NZ * NC) + b // NY
@@ -179,13 +188,13 @@
     tokens, keys = dlogit.shape
     total = jnp.zeros((ik.shape[1], keys), f32)
     for message in messages:
-        for part in range(message.shape[0]):
-            iq, w = message_parts(message.at[part], tokens, heads)
+        for part in range(0, message.shape[0], 2):
+            iq, weights = message_parts(message.at[part], message.at[part + 1], tokens, heads)
             active = index_dot(iq, ik)
             gates = []
-            for j in range(heads):
+            for j, w in enumerate(weights):
                 here = active[j * tokens : (j + 1) * tokens]
-                gates.append(jnp.where(here > 0.0, dlogit * w[:, j : j + 1], 0.0).astype(bf16))
+                gates.append(jnp.where(here > 0.0, dlogit * w, 0.0).astype(bf16))
             gate = jnp.concatenate(gates, axis=0)
             total = total + jnp.dot(iq.T, gate, preferred_element_type=f32)
     out_ref[...] = total.T * scale
@@ -219,6 +228,7 @@
     share_rows = query_count // NX
     shape = jax.ShapeDtypeStruct
     x = lax.axis_index("heads") // NZH
+    core = lax.axis_index("tokens") % NC
     limit = in_order(positions - lax.axis_index("tokens") * key_count)
 
     along_z = gathered(queries.reshape(heads_here, width), "tokens", groups_z)
@@ -226,30 +236,34 @@
     high = lax.reduce_precision(index_weights, 8, 7)
     middle = lax.reduce_precision(index_weights - high, 8, 7)
     low = index_weights - high - middle
-    lines = in_order(jnp.concatenate([high, middle, low], axis=1))
-    lines = jnp.pad(lines, ((0, 0), (0, 128 - 3 * index_heads)))
+    half = index_heads // NC
+    lines = jnp.stack([high, middle, low], axis=1).reshape(query_count, 3, NC, half)
+    lines = in_order(lines.transpose(0, 2, 1, 3).reshape(query_count, NC, 3 * half))
+    lines = jnp.pad(lines.transpose(1, 0, 2), ((0, 0), (0, 0), (0, 128 - 3 * half)))
     by_head = in_order(index_queries).transpose(1, 0, 2)
-    by_head = by_head.reshape(index_heads * query_count, index_width)
-    mine = jnp.concatenate([by_head, lines.astype(bf16)])
+    by_head = by_head.reshape(NC, half * query_count, index_width)
+    mine = jnp.concatenate([by_head, lines.astype(bf16)], axis=1)
+
+    first = lax.ppermute(lax.dynamic_index_in_dim(mine, core, 0), "heads", pairs_zh)
+    second = lax.ppermute(first, "tokens", pairs_c)
 
     index_flops = 2 * query_count * index_heads * key_count * index_width
     partial = call(
-        lambda *refs: logits_kernel(index_heads, index_scale, *refs),
+        lambda *refs: logits_kernel(half, index_scale, *refs),
         shape((query_count, key_count), f32),
-        flops=index_flops,
+        flops=2 * index_flops,
         moved=1 << 20,
-    )(mine, index_keys)
+    )(mine, first, second, index_keys)
     over_x = x_scatter_sum(partial.reshape(NX, share_rows, key_count), x)
-    along_z, over_x = lax.optimization_barrier((along_z, over_x))
-    other = lax.ppermute(over_x, "heads", pairs_zh)
-    rows = gathered(along_z, "tokens", groups_yc).reshape(-1, width)
-    rows, other = lax.optimization_barrier((rows, other))
     share_limit = lax.dynamic_slice_in_dim(limit, x * share_rows, share_rows, 0)
     logits, index_stats = call(
         index_stats_kernel,
         (shape((share_rows, key_count), f32), shape((8, 128), f32)),
-    )(share_limit[:, None], over_x, other)
-
+        flops=WEIGHT * index_flops,
+        moved=1 << 20,
+    )(share_limit[:, None], over_x)
+
+    rows = gathered(along_z, "tokens", groups_yc).reshape(-1, width)
     row_count = rows.shape[0]
     lines_shape = shape((NYC, row_count // NYC), f32)
     exponent, local_max, local_total = call(
@@ -260,37 +274,35 @@
     )(jnp.repeat(limit, heads_here)[:, None], rows, latent_keys.T)
 
     stats = jnp.concatenate([local_max, local_total, index_stats])
+
     stats = gathered(stats, "tokens", groups_z)
     stats = call(join_kernel, shape((NYC, *stats.shape[1:]), f32))(stats)
-    stats, sent = lax.optimization_barrier((stats, mine))
-    swapped = lax.ppermute(sent, "heads", pairs_zh)
     stats = exchanged(stats, "tokens", groups_yc)
 
     partial = call(target_kernel, shape((query_count, key_count), f32), moved=5 << 20)(
         stats, local_max, exponent
     )
+
     over_x = exchanged(partial.reshape(NX, share_rows, key_count), "heads", groups_x).sum(axis=0)
     other = lax.ppermute(over_x, "heads", pairs_zh)
-    other, swapped = lax.optimization_barrier((other, swapped))
-    pair = jnp.stack([mine, swapped])
-    messages = [pair] + [lax.ppermute(pair, "heads", pairs_x(flip)) for flip in range(1, NX)]
     dlogit = call(dlogit_kernel, shape((NX, share_rows, key_count), f32))(
         over_x, other, logits, stats
     )
     dlogit = exchanged(dlogit, "heads", groups_x).reshape(query_count, key_count)
-    dlogit, messages[1] = lax.optimization_barrier((dlogit, messages[1]))
+    four = jnp.concatenate([mine, first, second])
+    nearer = jnp.concatenate([four, lax.ppermute(four, "heads", pairs_x(1))])
+    messages = [nearer, lax.ppermute(nearer, "heads", pairs_x(2))]
 
     query_lines = query_count * index_heads
     piece_rows = -(-(query_lines + index_heads) // (NYC * 8)) * 8
     both = call(
-        lambda *refs: grad_kernel(index_heads, index_scale, *refs),
+        lambda *refs: grad_kernel(half, index_scale, *refs),
         shape((piece_rows * NYC, 128), f32),
         flops=2 * index_flops,
         moved=2 << 20,
     )(dlogit, mine, index_keys)
 
     piece = exchanged(both.reshape(NYC, piece_rows, 128), "tokens", groups_yc)
-    piece, messages[2] = lax.optimization_barrier((piece, messages[2]))
     piece = call(sum_kernel, shape((NZ // 2, piece_rows, 128), f32))(piece)
     piece = exchanged(piece, "tokens", groups_z4).sum(axis=0)
     other = lax.ppermute(piece, "tokens", pairs_z4)
@@ -300,7 +312,7 @@
     weight_grad = both[query_lines : query_lines + index_heads, :query_count].T
 
     key_grad = call(
-        lambda *refs: key_kernel(index_heads, index_scale, *refs),
+        lambda *refs: key_kernel(half, index_scale, *refs),
         shape((key_count, index_width), f32),
         flops=2 * index_flops * NX * NZH,
         moved=3 << 20,

time: 192 us -> 175 us (0.911)
  waiting for transfers between devices: 47.7 us -> 28.4 us
  blocking collectives: 30.7 us -> 50 us
  starting transfers between devices: 90 us -> 74.2 us
    all_to_all x2 -> x4, blocking collectives: 30.7 us -> 50 us  [exchanged(): lax.all_to_all(parts, axis, 0, 0, tiled=True, axis_index_groups=groups)]
    ppermute x4, waiting for transfers between devices: 11.9 us -> 1.23 us  [the longest x1 1.22 us: local(): second = lax.ppermute(first, 'tokens', pairs_c)]
    all_to_all x7 -> x5, starting transfers between devices: 46.6 us -> 39.1 us  [exchanged(): lax.all_to_all(parts, axis, 0, 0, tiled=True, axis_index_groups=groups)]
    all_to_all x7 -> x5, waiting for transfers between devices: 17.4 us -> 10.3 us  [exchanged(): lax.all_to_all(parts, axis, 0, 0, tiled=True, axis_index_groups=groups)]
    ppermute x2 -> x1, starting transfers between devices: 14 us -> 7.95 us  [local(): other = lax.ppermute(over_x, 'heads', pairs_zh)]
    ppermute x4, starting transfers between devices: 18.1 us -> 15.6 us  [the longest x1 7.94 us: local(): lax.ppermute(lax.dynamic_index_in_dim(mine, core, 0), 'heads', pairs_zh)]
    ppermute x2 -> x1, waiting for transfers between devices: 7.83 us -> 5.87 us  [local(): other = lax.ppermute(over_x, 'heads', pairs_zh)]
  transfers between devices with their start and end apart: 17 -> 14, of which waited for: 11 -> 8; matrix products, arithmetic and copies ran while one was open for 1% -> 2% of each run, Pallas kernels for 4% -> 5%
where the time goes in v9:
time: 175 us; the launch traced here: 174 us
  starting transfers between devices  74.2 us (42%)
  blocking collectives  50 us (29%)
  waiting for transfers between devices  28.4 us (16%)
  Pallas kernels  12.2 us (7%)
  local copies, waits for them, and re-layouts  7.27 us (4%)
    all_to_all x4, blocking collectives, exchanged(): lax.all_to_all(parts, axis, 0, 0, tiled=True, axis_index_groups=groups)  50 us
    all_to_all x5, starting transfers between devices, exchanged(): lax.all_to_all(parts, axis, 0, 0, tiled=True, axis_index_groups=groups)  39.1 us
    all_to_all x5, waiting for transfers between devices, exchanged(): lax.all_to_all(parts, axis, 0, 0, tiled=True, axis_index_groups=groups)  10.3 us
    ppermute x3, starting transfers between devices, x_scatter_sum(): total = total + lax.ppermute(piece, 'heads', pairs_x(flip))  9.58 us
    ppermute x1, starting transfers between devices, local(): other = lax.ppermute(over_x, 'heads', pairs_zh)  7.95 us
    ppermute x1, starting transfers between devices, local(): lax.ppermute(lax.dynamic_index_in_dim(mine, core, 0), 'heads', pairs_zh)  7.94 us
    ppermute x1, waiting for transfers between devices, local(): other = lax.ppermute(piece, 'tokens', pairs_z4)  7.47 us
    ppermute x1, waiting for transfers between devices, local(): other = lax.ppermute(over_x, 'heads', pairs_zh)  5.87 us
  transfers between devices with their start and end apart: 14, of which 8 were waited for; matrix products, arithmetic and copies ran while one was open for 2% of the time, Pallas kernels for 5%

profile of v9, /device:TPU:1, one launch (start us, length us, event | category | flops | bytes accessed | tf_op | source)
XLA Modules:
  0.0 173.8 jit_solution(15952257791008368311)
XLA Ops:
  0.6 1.4 broadcast_in_dim.27
  2.0 13.1 %all-to-all-start = ((bf16[8,16,576]{2,1,0:T(8,128)(2,1)}), bf16[8,16,576]{2,1,0:T(8,128)(2,1)S(1)}, u32[]{:S(2)}, u32[]{:S(2)}) async-start(bf16[8,16,576]{2,1,0:T(8,128)(2,1)} %broadcast_in_dim.27), calls=%async_computation | async-start | bytes 327680 | tf_op jit(solution)/shard_map/all_to_all | solution.py:46
  17.1 7.9 %collective-permute-start = (bf16[1,320,128]{2,1,0:T(8,128)(2,1)S(1)}, bf16[1,320,128]{2,1,0:T(8,128)(2,1)S(1)}, u32[]{:S(2)}, u32[]{:S(2)}) collective-permute-start(bf16[1,320,128]{2,1,0:T(8,128)(2,1)S(1)} %fusion), channel_id=1, source_target_pairs={{0,64},{64,0},{128,192},{192,128},{256,320},{320,256},{384,448},{4... | collective-permute-start | bytes 245768 | tf_op jit(solution)/shard_map/ppermute | solution.py:247
  25.8 1.2 broadcast_in_dim.28
  26.9 7.9 %all-to-all-start.1 = ((bf16[8,8,16,576]{3,2,1,0:T(8,128)(2,1)}), bf16[8,8,16,576]{3,2,1,0:T(8,128)(2,1)S(1)}, u32[]{:S(2)}, u32[]{:S(2)}) async-start(bf16[8,8,16,576]{3,2,1,0:T(8,128)(2,1)} %broadcast_in_dim.28), calls=%async_computation.1 | async-start | bytes 2621440 | tf_op jit(solution)/shard_map/all_to_all | solution.py:46
  35.2 1.9 %collective-permute-start.1 = (bf16[1,320,128]{2,1,0:T(8,128)(2,1)S(1)}, bf16[1,320,128]{2,1,0:T(8,128)(2,1)S(1)}, u32[]{:S(2)}, u32[]{:S(2)}) collective-permute-start(bf16[1,320,128]{2,1,0:T(8,128)(2,1)S(1)} %collective-permute-done.refs_1_), channel_id=1, source_target_pairs={{0,1},{1,0},{2,3},{3,2},{4,5},{5,4},{6,7},{7,6},{8,9},{9,8},{10,11... | collective-permute-start | bytes 245768 | tf_op jit(solution)/shard_map/ppermute | solution.py:248
  37.1 1.2 collective-permute-done.1.refs_2_
  39.2 3.1 %collective-permute-start.2 = (f32[16,1024]{1,0:T(8,128)S(1)}, f32[16,1024]{1,0:T(8,128)S(1)}, u32[]{:S(2)}, u32[]{:S(2)}) collective-permute-start(f32[16,1024]{1,0:T(8,128)S(1)} %get-tuple-element.13), channel_id=1, source_target_pairs={{0,128},{64,192},{128,0},{192,64},{256,384},{320,448},{384,256},{4... | collective-permute-start | bytes 196616 | tf_op jit(solution)/shard_map/ppermute | solution.py:219
  42.3 4.4 %collective-permute-start.3 = (f32[16,1024]{1,0:T(8,128)S(1)}, f32[16,1024]{1,0:T(8,128)S(1)}, u32[]{:S(2)}, u32[]{:S(2)}) collective-permute-start(f32[16,1024]{1,0:T(8,128)S(1)} %get-tuple-element.15), channel_id=1, source_target_pairs={{0,256},{64,320},{128,384},{192,448},{256,0},{320,64},{384,128},{4... | collective-permute-start | bytes 196616 | tf_op jit(solution)/shard_map/ppermute | solution.py:219
  46.7 2.1 %collective-permute-start.4 = (f32[16,1024]{1,0:T(8,128)S(1)}, f32[16,1024]{1,0:T(8,128)S(1)}, u32[]{:S(2)}, u32[]{:S(2)}) collective-permute-start(f32[16,1024]{1,0:T(8,128)S(1)} %get-tuple-element.14), channel_id=1, source_target_pairs={{0,384},{64,448},{128,256},{192,320},{256,128},{320,192},{384,0},{... | collective-permute-start | bytes 196616 | tf_op jit(solution)/shard_map/ppermute | solution.py:219
  49.4 3.5 %collective-permute-done.4 = f32[16,1024]{1,0:T(8,128)S(1)} collective-permute-done((f32[16,1024]{1,0:T(8,128)S(1)}, f32[16,1024]{1,0:T(8,128)S(1)}, u32[]{:S(2)}, u32[]{:S(2)}) %collective-permute-start.4) | collective-permute-done | bytes 65568 | tf_op jit(solution)/shard_map/ppermute | solution.py:219
  53.2 1.3 copy-done
  54.5 2.3 %shard_map.85 = (f32[1024,1024]{1,0:T(8,128)S(1)}, f32[8,128]{1,0:T(8,128)S(1)}, f32[8,128]{1,0:T(8,128)S(1)}) custom-call(s32[1024,1]{1,0:T(8,128)S(1)} %broadcast_in_dim_reshape.5.limit_ref, bf16[1024,576]{1,0:T(8,128)(2,1)S(1)} %bitcast.44, bf16[576,1024]{1,0:T(8,128)(2,1)S(1)} %bitcast.49), custom_call_target="tpu_custom_call" | custom-call | flops 1207959552 | bytes 4194304 | tf_op jit(solution)/shard_map/pallas_call | solution.py:269
  56.8 20.3 %all_to_all.45.stats_ref = f32[8,24,128]{2,1,0:T(8,128)S(1)} all-to-all(f32[8,24,128]{2,1,0:T(8,128)S(1)} %broadcast_in_dim.30), channel_id=1, replica_groups={{0,2,4,6,8,10,12,14},{1,3,5,7,9,11,13,15},{16,18,20,22,24,26,28,30},{17..., dimensions={0} | all-to-all | bytes 196608 | tf_op jit(solution)/shard_map/all_to_all | solution.py:46
  77.1 12.8 %all_to_all.46.stats_ref = f32[8,24,128]{2,1,0:T(8,128)S(1)} all-to-all(f32[8,24,128]{2,1,0:T(8,128)S(1)} %shard_map.88), channel_id=1, replica_groups={{0,16,32,48,1,17,33,49},{2,18,34,50,3,19,35,51},{4,20,36,52,5,21,37,53}..., dimensions={0} | all-to-all | bytes 196608 | tf_op jit(solution)/shard_map/all_to_all | solution.py:46
  89.9 1.5 shard_map.89
  91.4 3.4 %all-to-all-start.4 = ((f32[4,16,1024]{2,1,0:T(8,128)}), f32[4,16,1024]{2,1,0:T(8,128)S(1)}, u32[]{:S(2)}, u32[]{:S(2)}) async-start(f32[4,16,1024]{2,1,0:T(8,128)} %bitcast.22), calls=%async_computation.4 | async-start | bytes 524288 | tf_op jit(solution)/shard_map/all_to_all | solution.py:46
  94.8 3.3 %collective-permute-start.7 = (bf16[4,320,128]{2,1,0:T(8,128)(2,1)S(1)}, bf16[4,320,128]{2,1,0:T(8,128)(2,1)S(1)}, u32[]{:S(2)}, u32[]{:S(2)}) collective-permute-start(bf16[4,320,128]{2,1,0:T(8,128)(2,1)S(1)} %pad_maximum_fusion.1), channel_id=1, source_target_pairs={{0,128},{64,192},{128,0},{192,64},{256,384},{320,448},{384,256},{4... | collective-permute-start | bytes 983048 | tf_op jit(solution)/shard_map/ppermute | solution.py:293
  98.1 2.7 %all-to-all-done.4 = f32[4,16,1024]{2,1,0:T(8,128)S(1)} async-done(((f32[4,16,1024]{2,1,0:T(8,128)}), f32[4,16,1024]{2,1,0:T(8,128)S(1)}, u32[]{:S(2)}, u32[]{:S(2)}) %all-to-all-start.4) | async-done | bytes 262176 | tf_op jit(solution)/shard_map/all_to_all | solution.py:46
  100.9 7.9 %collective-permute-start.5 = (f32[16,1024]{1,0:T(8,128)S(1)}, f32[16,1024]{1,0:T(8,128)S(1)}, u32[]{:S(2)}, u32[]{:S(2)}) collective-permute-start(f32[16,1024]{1,0:T(8,128)S(1)} %reduce_sum.18.one_ref), channel_id=1, source_target_pairs={{0,64},{64,0},{128,192},{192,128},{256,320},{320,256},{384,448},{4... | collective-permute-start | bytes 196616 | tf_op jit(solution)/shard_map/ppermute | solution.py:287
  108.8 5.9 %collective-permute-done.5.two_ref = f32[16,1024]{1,0:T(8,128)S(1)} collective-permute-done((f32[16,1024]{1,0:T(8,128)S(1)}, f32[16,1024]{1,0:T(8,128)S(1)}, u32[]{:S(2)}, u32[]{:S(2)}) %collective-permute-start.5) | collective-permute-done | bytes 65568 | tf_op jit(solution)/shard_map/ppermute | solution.py:287
  114.8 7.9 %all_to_all.47 = f32[4,16,1024]{2,1,0:T(8,128)S(1)} all-to-all(f32[4,16,1024]{2,1,0:T(8,128)S(1)} %shard_map.90), channel_id=1, replica_groups={{0,128,256,384},{64,192,320,448},{1,129,257,385},{65,193,321,449},{2,13..., dimensions={0} | all-to-all | bytes 524288 | tf_op jit(solution)/shard_map/all_to_all | solution.py:46
  122.7 1.8 %shard_map.91 = f32[576,128]{1,0:T(8,128)} custom-call(f32[64,1024]{1,0:T(8,128)S(1)} %bitcast.47, bf16[2,320,128]{2,1,0:T(8,128)(2,1)S(1)} %pad_maximum_fusion.2.refs_0_.refs_1_, bf16[1024,128]{1,0:T(8,128)(2,1)S(1)} %copy-done.1), custom_call_target="tpu_custom_call" | custom-call | flops 268435456 | bytes 2097152 | tf_op jit(solution)/shard_map/pallas_call | solution.py:298
  124.5 8.5 %all-to-all-start.6 = ((f32[8,72,128]{2,1,0:T(8,128)}), f32[8,72,128]{2,1,0:T(8,128)S(1)}, u32[]{:S(2)}, u32[]{:S(2)}) async-start(f32[8,72,128]{2,1,0:T(8,128)} %bitcast.24), calls=%async_computation.6 | async-start | bytes 589824 | tf_op jit(solution)/shard_map/all_to_all | solution.py:46
  133.0 2.4 %collective-permute-start.8 = (bf16[8,320,128]{2,1,0:T(8,128)(2,1)S(1)}, bf16[8,320,128]{2,1,0:T(8,128)(2,1)S(1)}, u32[]{:S(2)}, u32[]{:S(2)}) collective-permute-start(bf16[8,320,128]{2,1,0:T(8,128)(2,1)S(1)} %pad_maximum_fusion.refs_2_), channel_id=1, source_target_pairs={{0,256},{64,320},{128,384},{192,448},{256,0},{320,64},{384,128},{4... | collective-permute-start | bytes 1966088 | tf_op jit(solution)/shard_map/ppermute | solution.py:294
  135.5 4.7 %all-to-all-done.6.parts_ref = f32[8,72,128]{2,1,0:T(8,128)S(1)} async-done(((f32[8,72,128]{2,1,0:T(8,128)}), f32[8,72,128]{2,1,0:T(8,128)S(1)}, u32[]{:S(2)}, u32[]{:S(2)}) %all-to-all-start.6) | async-done | bytes 294944 | tf_op jit(solution)/shard_map/all_to_all | solution.py:46
  140.2 9.0 %all_to_all.48 = f32[4,72,128]{2,1,0:T(8,128)S(1)} all-to-all(f32[4,72,128]{2,1,0:T(8,128)S(1)} %shard_map.92), channel_id=1, replica_groups={{0,2,4,6},{1,3,5,7},{16,18,20,22},{17,19,21,23},{32,34,36,38},{33,35,37..., dimensions={0} | all-to-all | bytes 294912 | tf_op jit(solution)/shard_map/all_to_all | solution.py:46
  149.3 1.9 %collective-permute-start.6 = (f32[72,128]{1,0:T(8,128)S(1)}, f32[72,128]{1,0:T(8,128)S(1)}, u32[]{:S(2)}, u32[]{:S(2)}) collective-permute-start(f32[72,128]{1,0:T(8,128)S(1)} %reduce_sum.19.one_ref), channel_id=1, source_target_pairs={{0,8},{1,9},{2,10},{3,11},{4,12},{5,13},{6,14},{7,15},{8,0},{9,1},... | collective-permute-start | bytes 110600 | tf_op jit(solution)/shard_map/ppermute | solution.py:308
  151.2 7.5 %collective-permute-done.6.two_ref = f32[72,128]{1,0:T(8,128)S(1)} collective-permute-done((f32[72,128]{1,0:T(8,128)S(1)}, f32[72,128]{1,0:T(8,128)S(1)}, u32[]{:S(2)}, u32[]{:S(2)}) %collective-permute-start.6) | collective-permute-done | bytes 36896 | tf_op jit(solution)/shard_map/ppermute | solution.py:308
  159.4 6.2 %all-to-all-start.8 = ((f32[8,72,128]{2,1,0:T(8,128)}), f32[8,72,128]{2,1,0:T(8,128)S(1)}, u32[]{:S(2)}, u32[]{:S(2)}) async-start(f32[8,72,128]{2,1,0:T(8,128)} %shard_map.93), calls=%async_computation.8 | async-start | bytes 589824 | tf_op jit(solution)/shard_map/all_to_all | solution.py:46
  165.6 4.7 %shard_map.94 = f32[1024,128]{1,0:T(8,128)} custom-call(f32[64,1024]{1,0:T(8,128)S(1)} %bitcast.48, bf16[1024,128]{1,0:T(8,128)(2,1)S(1)} %copy-done.1, bf16[8,320,128]{2,1,0:T(8,128)(2,1)S(1)} %pad_maximum_fusion.refs_2_, bf16[8,320,128]{2,1,0:T(8,128)(2,1)S(1)} %collective-permute-done.8.refs_3_), custom_call_target="tpu_custom_call" | custom-call | flops 2147483648 | bytes 3145728 | tf_op jit(solution)/shard_map/pallas_call | solution.py:314
  170.4 2.2 %all-to-all-done.8 = f32[8,72,128]{2,1,0:T(8,128)S(1)} async-done(((f32[8,72,128]{2,1,0:T(8,128)}), f32[8,72,128]{2,1,0:T(8,128)S(1)}, u32[]{:S(2)}, u32[]{:S(2)}) %all-to-all-start.8) | async-done | bytes 294944 | tf_op jit(solution)/shard_map/all_to_all | solution.py:46
  (45 shorter events, 6.9 us)
Async XLA Ops:
  2.0 23.7 %all-to-all-start = ((bf16[8,16,576]{2,1,0:T(8,128)(2,1)}), bf16[8,16,576]{2,1,0:T(8,128)(2,1)S(1)}, u32[]{:S(2)}, u32[]{:S(2)}) async-start(bf16[8,16,576]{2,1,0:T(8,128)(2,1)} %broadcast_in_dim.27), calls=%async_computation | async-start | bytes 327680 | tf_op jit(solution)/shard_map/all_to_all | solution.py:46
  17.1 18.1 %collective-permute-start = (bf16[1,320,128]{2,1,0:T(8,128)(2,1)S(1)}, bf16[1,320,128]{2,1,0:T(8,128)(2,1)S(1)}, u32[]{:S(2)}, u32[]{:S(2)}) collective-permute-start(bf16[1,320,128]{2,1,0:T(8,128)(2,1)S(1)} %fusion), channel_id=1, source_target_pairs={{0,64},{64,0},{128,192},{192,128},{256,320},{320,256},{384,448},{4... | collective-permute-start | bytes 245768 | tf_op jit(solution)/shard_map/ppermute | solution.py:247
  26.9 7.9 %copy-start.2 = (s32[64]{0:T(128)S(1)}, s32[64]{0:T(128)}, u32[]{:S(2)}) copy-start(s32[64]{0:T(128)} %param.11) | copy-start | bytes 772
  26.9 11.4 %copy-start.1 = (bf16[1024,128]{1,0:T(8,128)(2,1)S(1)}, bf16[1024,128]{1,0:T(8,128)(2,1)}, u32[]{:S(2)}) copy-start(bf16[1024,128]{1,0:T(8,128)(2,1)} %refs_1_.1) | copy-start | bytes 786436
  26.9 26.2 %all-to-all-start.1 = ((bf16[8,8,16,576]{3,2,1,0:T(8,128)(2,1)}), bf16[8,8,16,576]{3,2,1,0:T(8,128)(2,1)S(1)}, u32[]{:S(2)}, u32[]{:S(2)}) async-start(bf16[8,8,16,576]{3,2,1,0:T(8,128)(2,1)} %broadcast_in_dim.28), calls=%async_computation.1 | async-start | bytes 2621440 | tf_op jit(solution)/shard_map/all_to_all | solution.py:46
  35.2 3.2 %collective-permute-start.1 = (bf16[1,320,128]{2,1,0:T(8,128)(2,1)S(1)}, bf16[1,320,128]{2,1,0:T(8,128)(2,1)S(1)}, u32[]{:S(2)}, u32[]{:S(2)}) collective-permute-start(bf16[1,320,128]{2,1,0:T(8,128)(2,1)S(1)} %collective-permute-done.refs_1_), channel_id=1, source_target_pairs={{0,1},{1,0},{2,3},{3,2},{4,5},{5,4},{6,7},{7,6},{8,9},{9,8},{10,11... | collective-permute-start | bytes 245768 | tf_op jit(solution)/shard_map/ppermute | solution.py:248
  39.2 10.2 %collective-permute-start.2 = (f32[16,1024]{1,0:T(8,128)S(1)}, f32[16,1024]{1,0:T(8,128)S(1)}, u32[]{:S(2)}, u32[]{:S(2)}) collective-permute-start(f32[16,1024]{1,0:T(8,128)S(1)} %get-tuple-element.13), channel_id=1, source_target_pairs={{0,128},{64,192},{128,0},{192,64},{256,384},{320,448},{384,256},{4... | collective-permute-start | bytes 196616 | tf_op jit(solution)/shard_map/ppermute | solution.py:219
  42.3 7.0 %collective-permute-start.3 = (f32[16,1024]{1,0:T(8,128)S(1)}, f32[16,1024]{1,0:T(8,128)S(1)}, u32[]{:S(2)}, u32[]{:S(2)}) collective-permute-start(f32[16,1024]{1,0:T(8,128)S(1)} %get-tuple-element.15), channel_id=1, source_target_pairs={{0,256},{64,320},{128,384},{192,448},{256,0},{320,64},{384,128},{4... | collective-permute-start | bytes 196616 | tf_op jit(solution)/shard_map/ppermute | solution.py:219
  46.7 6.2 %collective-permute-start.4 = (f32[16,1024]{1,0:T(8,128)S(1)}, f32[16,1024]{1,0:T(8,128)S(1)}, u32[]{:S(2)}, u32[]{:S(2)}) collective-permute-start(f32[16,1024]{1,0:T(8,128)S(1)} %get-tuple-element.14), channel_id=1, source_target_pairs={{0,384},{64,448},{128,256},{192,320},{256,128},{320,192},{384,0},{... | collective-permute-start | bytes 196616 | tf_op jit(solution)/shard_map/ppermute | solution.py:219
  53.2 1.3 copy-start
  91.4 9.5 %all-to-all-start.4 = ((f32[4,16,1024]{2,1,0:T(8,128)}), f32[4,16,1024]{2,1,0:T(8,128)S(1)}, u32[]{:S(2)}, u32[]{:S(2)}) async-start(f32[4,16,1024]{2,1,0:T(8,128)} %bitcast.22), calls=%async_computation.4 | async-start | bytes 524288 | tf_op jit(solution)/shard_map/all_to_all | solution.py:46
  94.8 38.2 %collective-permute-start.7 = (bf16[4,320,128]{2,1,0:T(8,128)(2,1)S(1)}, bf16[4,320,128]{2,1,0:T(8,128)(2,1)S(1)}, u32[]{:S(2)}, u32[]{:S(2)}) collective-permute-start(bf16[4,320,128]{2,1,0:T(8,128)(2,1)S(1)} %pad_maximum_fusion.1), channel_id=1, source_target_pairs={{0,128},{64,192},{128,0},{192,64},{256,384},{320,448},{384,256},{4... | collective-permute-start | bytes 983048 | tf_op jit(solution)/shard_map/ppermute | solution.py:293
  100.9 13.8 %collective-permute-start.5 = (f32[16,1024]{1,0:T(8,128)S(1)}, f32[16,1024]{1,0:T(8,128)S(1)}, u32[]{:S(2)}, u32[]{:S(2)}) collective-permute-start(f32[16,1024]{1,0:T(8,128)S(1)} %reduce_sum.18.one_ref), channel_id=1, source_target_pairs={{0,64},{64,0},{128,192},{192,128},{256,320},{320,256},{384,448},{4... | collective-permute-start | bytes 196616 | tf_op jit(solution)/shard_map/ppermute | solution.py:287
  124.5 15.7 %all-to-all-start.6 = ((f32[8,72,128]{2,1,0:T(8,128)}), f32[8,72,128]{2,1,0:T(8,128)S(1)}, u32[]{:S(2)}, u32[]{:S(2)}) async-start(f32[8,72,128]{2,1,0:T(8,128)} %bitcast.24), calls=%async_computation.6 | async-start | bytes 589824 | tf_op jit(solution)/shard_map/all_to_all | solution.py:46
  133.0 32.6 %collective-permute-start.8 = (bf16[8,320,128]{2,1,0:T(8,128)(2,1)S(1)}, bf16[8,320,128]{2,1,0:T(8,128)(2,1)S(1)}, u32[]{:S(2)}, u32[]{:S(2)}) collective-permute-start(bf16[8,320,128]{2,1,0:T(8,128)(2,1)S(1)} %pad_maximum_fusion.refs_2_), channel_id=1, source_target_pairs={{0,256},{64,320},{128,384},{192,448},{256,0},{320,64},{384,128},{4... | collective-permute-start | bytes 1966088 | tf_op jit(solution)/shard_map/ppermute | solution.py:294
  149.3 9.4 %collective-permute-start.6 = (f32[72,128]{1,0:T(8,128)S(1)}, f32[72,128]{1,0:T(8,128)S(1)}, u32[]{:S(2)}, u32[]{:S(2)}) collective-permute-start(f32[72,128]{1,0:T(8,128)S(1)} %reduce_sum.19.one_ref), channel_id=1, source_target_pairs={{0,8},{1,9},{2,10},{3,11},{4,12},{5,13},{6,14},{7,15},{8,0},{9,1},... | collective-permute-start | bytes 110600 | tf_op jit(solution)/shard_map/ppermute | solution.py:308
  159.4 13.1 %all-to-all-start.8 = ((f32[8,72,128]{2,1,0:T(8,128)}), f32[8,72,128]{2,1,0:T(8,128)S(1)}, u32[]{:S(2)}, u32[]{:S(2)}) async-start(f32[8,72,128]{2,1,0:T(8,128)} %shard_map.93), calls=%async_computation.8 | async-start | bytes 589824 | tf_op jit(solution)/shard_map/all_to_all | solution.py:46

commit v10 on v9

--- a/solution.py
+++ b/solution.py
@@ -182,22 +182,22 @@
         )
 
 
-def key_kernel(heads, scale, d_ref, ik_ref, *refs):
-    messages, out_ref = refs[:-1], refs[-1]
+def key_kernel(heads, scale, d_ref, ik_ref, message, *refs):
+    before, out_ref = refs[:-1], refs[-1]
     dlogit, ik = d_ref[...], ik_ref[...]
     tokens, keys = dlogit.shape
     total = jnp.zeros((ik.shape[1], keys), f32)
-    for message in messages:
-        for part in range(0, message.shape[0], 2):
-            iq, weights = message_parts(message.at[part], message.at[part + 1], tokens, heads)
-            active = index_dot(iq, ik)
-            gates = []
-            for j, w in enumerate(weights):
-                here = active[j * tokens : (j + 1) * tokens]
-                gates.append(jnp.where(here > 0.0, dlogit * w, 0.0).astype(bf16))
-            gate = jnp.concatenate(gates, axis=0)
-            total = total + jnp.dot(iq.T, gate, preferred_element_type=f32)
-    out_ref[...] = total.T * scale
+    for part in range(0, message.shape[0], 2):
+        iq, weights = message_parts(message.at[part], message.at[part + 1], tokens, heads)
+        active = index_dot(iq, ik)
+        gates = []
+        for j, w in enumerate(weights):
+            here = active[j * tokens : (j + 1) * tokens]
+            gates.append(jnp.where(here > 0.0, dlogit * w, 0.0).astype(bf16))
+        gate = jnp.concatenate(gates, axis=0)
+        total = total + jnp.dot(iq.T, gate, preferred_element_type=f32)
+    grad = total.T * scale
+    out_ref[...] = before[0][...] + grad if before else grad
 
 
 def sum_kernel(parts_ref, out_ref):
@@ -288,11 +288,10 @@
     dlogit = call(dlogit_kernel, shape((NX, share_rows, key_count), f32))(
         over_x, other, logits, stats
     )
+    dlogit, *three = lax.optimization_barrier((dlogit, mine, first, second))
+    four = jnp.concatenate(three)
+    near = lax.ppermute(four, "heads", pairs_x(1))
     dlogit = exchanged(dlogit, "heads", groups_x).reshape(query_count, key_count)
-    four = jnp.concatenate([mine, first, second])
-    nearer = jnp.concatenate([four, lax.ppermute(four, "heads", pairs_x(1))])
-    messages = [nearer, lax.ppermute(nearer, "heads", pairs_x(2))]
-
     query_lines = query_count * index_heads
     piece_rows = -(-(query_lines + index_heads) // (NYC * 8)) * 8
     both = call(
@@ -303,6 +302,8 @@
     )(dlogit, mine, index_keys)
 
     piece = exchanged(both.reshape(NYC, piece_rows, 128), "tokens", groups_yc)
+    eight = jnp.concatenate([four, near])
+    far = lax.ppermute(eight, "heads", pairs_x(2))
     piece = call(sum_kernel, shape((NZ // 2, piece_rows, 128), f32))(piece)
     piece = exchanged(piece, "tokens", groups_z4).sum(axis=0)
     other = lax.ppermute(piece, "tokens", pairs_z4)
@@ -311,13 +312,16 @@
     query_grad = both[:query_lines].reshape(query_count, index_heads, index_width)
     weight_grad = both[query_lines : query_lines + index_heads, :query_count].T
 
-    key_grad = call(
-        lambda *refs: key_kernel(half, index_scale, *refs),
-        shape((key_count, index_width), f32),
-        flops=2 * index_flops * NX * NZH,
-        moved=3 << 20,
-    )(dlogit, index_keys, *messages)
-    return (query_grad, weight_grad, key_grad)
+    key_flops = index_flops * NX * NZH
+    key_grad = ()
+    for message in (eight, far):
+        key_grad = call(
+            lambda *refs: key_kernel(half, index_scale, *refs),
+            shape((key_count, index_width), f32),
+            flops=key_flops,
+            moved=2 << 20,
+        )(dlogit, index_keys, message, *key_grad),
+    return (query_grad, weight_grad, *key_grad)
 
 
 def solution(mesh):

time: 175 us -> 175 us (level)
    pallas_call x1 -> x2, Pallas kernels: 4.73 us -> 4.92 us  [local(): call(lambda *refs: key_kernel(half, index_scale, *refs), shape((key_count...]
  transfers between devices with their start and end apart: 14 -> 14, of which waited for: 8 -> 9; matrix products, arithmetic and copies ran while one was open for 2% -> 2% of each run, Pallas kernels for 5% -> 5%
where the time goes in v10:
time: 175 us; the launch traced here: 174 us
  starting transfers between devices  74.1 us (42%)
  blocking collectives  50.6 us (29%)
  waiting for transfers between devices  27.6 us (16%)
  Pallas kernels  12.4 us (7%)
  local copies, waits for them, and re-layouts  7.37 us (4%)
    all_to_all x4, blocking collectives, exchanged(): lax.all_to_all(parts, axis, 0, 0, tiled=True, axis_index_groups=groups)  50.6 us
    all_to_all x5, starting transfers between devices, exchanged(): lax.all_to_all(parts, axis, 0, 0, tiled=True, axis_index_groups=groups)  39.8 us
    all_to_all x5, waiting for transfers between devices, exchanged(): lax.all_to_all(parts, axis, 0, 0, tiled=True, axis_index_groups=groups)  10.1 us
    ppermute x3, starting transfers between devices, x_scatter_sum(): total = total + lax.ppermute(piece, 'heads', pairs_x(flip))  9.4 us
    ppermute x1, starting transfers between devices, local(): other = lax.ppermute(over_x, 'heads', pairs_zh)  7.95 us
    ppermute x1, starting transfers between devices, local(): lax.ppermute(lax.dynamic_index_in_dim(mine, core, 0), 'heads', pairs_zh)  7.94 us
    ppermute x1, waiting for transfers between devices, local(): other = lax.ppermute(piece, 'tokens', pairs_z4)  7.47 us
    ppermute x1, waiting for transfers between devices, local(): other = lax.ppermute(over_x, 'heads', pairs_zh)  5.77 us
  transfers between devices with their start and end apart: 14, of which 9 were waited for; matrix products, arithmetic and copies ran while one was open for 2% of the time, Pallas kernels for 5%

profile of v10, /device:TPU:1, one launch (start us, length us, event | category | flops | bytes accessed | tf_op | source)
XLA Modules:
  0.0 173.9 jit_solution(816530813427875904)
XLA Ops:
  0.6 1.4 broadcast_in_dim.27
  2.0 13.1 %all-to-all-start = ((bf16[8,16,576]{2,1,0:T(8,128)(2,1)}), bf16[8,16,576]{2,1,0:T(8,128)(2,1)S(1)}, u32[]{:S(2)}, u32[]{:S(2)}) async-start(bf16[8,16,576]{2,1,0:T(8,128)(2,1)} %broadcast_in_dim.27), calls=%async_computation | async-start | bytes 327680 | tf_op jit(solution)/shard_map/all_to_all | solution.py:46
  16.1 0.9 copy.22
  17.1 7.9 %collective-permute-start = (bf16[1,320,128]{2,1,0:T(8,128)(2,1)S(1)}, bf16[1,320,128]{2,1,0:T(8,128)(2,1)S(1)}, u32[]{:S(2)}, u32[]{:S(2)}) collective-permute-start(bf16[1,320,128]{2,1,0:T(8,128)(2,1)S(1)} %constant_dynamic-slice_fusion), channel_id=1, source_target_pairs={{0,64},{64,0},{128,192},{192,128},{256,320},{320,256},{384,448},{4... | collective-permute-start | bytes 245768 | tf_op jit(solution)/shard_map/ppermute | solution.py:247
  25.8 1.2 broadcast_in_dim.28
  26.9 7.9 %all-to-all-start.1 = ((bf16[8,8,16,576]{3,2,1,0:T(8,128)(2,1)}), bf16[8,8,16,576]{3,2,1,0:T(8,128)(2,1)S(1)}, u32[]{:S(2)}, u32[]{:S(2)}) async-start(bf16[8,8,16,576]{3,2,1,0:T(8,128)(2,1)} %broadcast_in_dim.28), calls=%async_computation.1 | async-start | bytes 2621440 | tf_op jit(solution)/shard_map/all_to_all | solution.py:46
  34.9 1.9 %collective-permute-start.1 = (bf16[1,320,128]{2,1,0:T(8,128)(2,1)S(1)}, bf16[1,320,128]{2,1,0:T(8,128)(2,1)S(1)}, u32[]{:S(2)}, u32[]{:S(2)}) collective-permute-start(bf16[1,320,128]{2,1,0:T(8,128)(2,1)S(1)} %collective-permute-done.refs_1_), channel_id=1, source_target_pairs={{0,1},{1,0},{2,3},{3,2},{4,5},{5,4},{6,7},{7,6},{8,9},{9,8},{10,11... | collective-permute-start | bytes 245768 | tf_op jit(solution)/shard_map/ppermute | solution.py:248
  38.9 3.1 %collective-permute-start.2 = (f32[16,1024]{1,0:T(8,128)S(1)}, f32[16,1024]{1,0:T(8,128)S(1)}, u32[]{:S(2)}, u32[]{:S(2)}) collective-permute-start(f32[16,1024]{1,0:T(8,128)S(1)} %get-tuple-element.21), channel_id=1, source_target_pairs={{0,128},{64,192},{128,0},{192,64},{256,384},{320,448},{384,256},{4... | collective-permute-start | bytes 196616 | tf_op jit(solution)/shard_map/ppermute | solution.py:219
  42.0 3.7 %collective-permute-start.4 = (f32[16,1024]{1,0:T(8,128)S(1)}, f32[16,1024]{1,0:T(8,128)S(1)}, u32[]{:S(2)}, u32[]{:S(2)}) collective-permute-start(f32[16,1024]{1,0:T(8,128)S(1)} %get-tuple-element.22), channel_id=1, source_target_pairs={{0,384},{64,448},{128,256},{192,320},{256,128},{320,192},{384,0},{... | collective-permute-start | bytes 196616 | tf_op jit(solution)/shard_map/ppermute | solution.py:219
  45.7 2.6 %collective-permute-start.3 = (f32[16,1024]{1,0:T(8,128)S(1)}, f32[16,1024]{1,0:T(8,128)S(1)}, u32[]{:S(2)}, u32[]{:S(2)}) collective-permute-start(f32[16,1024]{1,0:T(8,128)S(1)} %get-tuple-element.23), channel_id=1, source_target_pairs={{0,256},{64,320},{128,384},{192,448},{256,0},{320,64},{384,128},{4... | collective-permute-start | bytes 196616 | tf_op jit(solution)/shard_map/ppermute | solution.py:219
  48.8 3.4 %collective-permute-done.3 = f32[16,1024]{1,0:T(8,128)S(1)} collective-permute-done((f32[16,1024]{1,0:T(8,128)S(1)}, f32[16,1024]{1,0:T(8,128)S(1)}, u32[]{:S(2)}, u32[]{:S(2)}) %collective-permute-start.3) | collective-permute-done | bytes 65568 | tf_op jit(solution)/shard_map/ppermute | solution.py:219
  52.6 1.3 copy-done
  53.9 2.3 %shard_map.85 = (f32[1024,1024]{1,0:T(8,128)S(1)}, f32[8,128]{1,0:T(8,128)S(1)}, f32[8,128]{1,0:T(8,128)S(1)}) custom-call(s32[1024,1]{1,0:T(8,128)S(1)} %broadcast_in_dim_reshape.5.limit_ref, bf16[1024,576]{1,0:T(8,128)(2,1)S(1)} %bitcast.44, bf16[576,1024]{1,0:T(8,128)(2,1)S(1)} %bitcast.51), custom_call_target="tpu_custom_call" | custom-call | flops 1207959552 | bytes 4194304 | tf_op jit(solution)/shard_map/pallas_call | solution.py:269
  56.2 20.5 %all_to_all.45.stats_ref = f32[8,24,128]{2,1,0:T(8,128)S(1)} all-to-all(f32[8,24,128]{2,1,0:T(8,128)S(1)} %broadcast_in_dim.30), channel_id=1, replica_groups={{0,2,4,6,8,10,12,14},{1,3,5,7,9,11,13,15},{16,18,20,22,24,26,28,30},{17..., dimensions={0} | all-to-all | bytes 196608 | tf_op jit(solution)/shard_map/all_to_all | solution.py:46
  76.8 12.8 %all_to_all.46.stats_ref = f32[8,24,128]{2,1,0:T(8,128)S(1)} all-to-all(f32[8,24,128]{2,1,0:T(8,128)S(1)} %shard_map.88), channel_id=1, replica_groups={{0,16,32,48,1,17,33,49},{2,18,34,50,3,19,35,51},{4,20,36,52,5,21,37,53}..., dimensions={0} | all-to-all | bytes 196608 | tf_op jit(solution)/shard_map/all_to_all | solution.py:46
  90.3 8.8 %all_to_all.47 = f32[4,16,1024]{2,1,0:T(8,128)S(1)} all-to-all(f32[4,16,1024]{2,1,0:T(8,128)S(1)} %bitcast.45), channel_id=1, replica_groups={{0,128,256,384},{64,192,320,448},{1,129,257,385},{65,193,321,449},{2,13..., dimensions={0} | all-to-all | bytes 524288 | tf_op jit(solution)/shard_map/all_to_all | solution.py:46
  99.1 7.9 %collective-permute-start.5 = (f32[16,1024]{1,0:T(8,128)S(1)}, f32[16,1024]{1,0:T(8,128)S(1)}, u32[]{:S(2)}, u32[]{:S(2)}) collective-permute-start(f32[16,1024]{1,0:T(8,128)S(1)} %reduce_sum.18.one_ref), channel_id=1, source_target_pairs={{0,64},{64,0},{128,192},{192,128},{256,320},{320,256},{384,448},{4... | collective-permute-start | bytes 196616 | tf_op jit(solution)/shard_map/ppermute | solution.py:287
  107.1 5.8 %collective-permute-done.5.two_ref = f32[16,1024]{1,0:T(8,128)S(1)} collective-permute-done((f32[16,1024]{1,0:T(8,128)S(1)}, f32[16,1024]{1,0:T(8,128)S(1)}, u32[]{:S(2)}, u32[]{:S(2)}) %collective-permute-start.5) | collective-permute-done | bytes 65568 | tf_op jit(solution)/shard_map/ppermute | solution.py:287
  113.7 3.4 %all-to-all-start.5 = ((f32[4,16,1024]{2,1,0:T(8,128)}), f32[4,16,1024]{2,1,0:T(8,128)S(1)}, u32[]{:S(2)}, u32[]{:S(2)}) async-start(f32[4,16,1024]{2,1,0:T(8,128)} %shard_map.90), calls=%async_computation.5 | async-start | bytes 524288 | tf_op jit(solution)/shard_map/all_to_all | solution.py:46
  117.2 3.3 %collective-permute-start.7 = (bf16[4,320,128]{2,1,0:T(8,128)(2,1)S(1)}, bf16[4,320,128]{2,1,0:T(8,128)(2,1)S(1)}, u32[]{:S(2)}, u32[]{:S(2)}) collective-permute-start(bf16[4,320,128]{2,1,0:T(8,128)(2,1)S(1)} %pad_maximum_fusion), channel_id=1, source_target_pairs={{0,128},{64,192},{128,0},{192,64},{256,384},{320,448},{384,256},{4... | collective-permute-start | bytes 983048 | tf_op jit(solution)/shard_map/ppermute | solution.py:293
  120.5 2.1 %all-to-all-done.5 = f32[4,16,1024]{2,1,0:T(8,128)S(1)} async-done(((f32[4,16,1024]{2,1,0:T(8,128)}), f32[4,16,1024]{2,1,0:T(8,128)S(1)}, u32[]{:S(2)}, u32[]{:S(2)}) %all-to-all-start.5) | async-done | bytes 262176 | tf_op jit(solution)/shard_map/all_to_all | solution.py:46
  122.6 1.8 %shard_map.91 = f32[576,128]{1,0:T(8,128)} custom-call(f32[64,1024]{1,0:T(8,128)S(1)} %bitcast.48, bf16[2,320,128]{2,1,0:T(8,128)(2,1)S(1)} %fusion.1.refs_0_.refs_1_, bf16[1024,128]{1,0:T(8,128)(2,1)S(1)} %copy-done.1), custom_call_target="tpu_custom_call" | custom-call | flops 268435456 | bytes 2097152 | tf_op jit(solution)/shard_map/pallas_call | solution.py:297
  124.4 9.2 %all-to-all-start.6 = ((f32[8,72,128]{2,1,0:T(8,128)}), f32[8,72,128]{2,1,0:T(8,128)S(1)}, u32[]{:S(2)}, u32[]{:S(2)}) async-start(f32[8,72,128]{2,1,0:T(8,128)} %bitcast.24), calls=%async_computation.6 | async-start | bytes 589824 | tf_op jit(solution)/shard_map/all_to_all | solution.py:46
  133.6 1.9 %collective-permute-start.8 = (bf16[8,320,128]{2,1,0:T(8,128)(2,1)S(1)}, bf16[8,320,128]{2,1,0:T(8,128)(2,1)S(1)}, u32[]{:S(2)}, u32[]{:S(2)}) collective-permute-start(bf16[8,320,128]{2,1,0:T(8,128)(2,1)S(1)} %constant_dynamic-update-slice_fusion.refs_2_), channel_id=1, source_target_pairs={{0,256},{64,320},{128,384},{192,448},{256,0},{320,64},{384,128},{4... | collective-permute-start | bytes 1966088 | tf_op jit(solution)/shard_map/ppermute | solution.py:306
  135.6 5.2 %all-to-all-done.6.parts_ref = f32[8,72,128]{2,1,0:T(8,128)S(1)} async-done(((f32[8,72,128]{2,1,0:T(8,128)}), f32[8,72,128]{2,1,0:T(8,128)S(1)}, u32[]{:S(2)}, u32[]{:S(2)}) %all-to-all-start.6) | async-done | bytes 294944 | tf_op jit(solution)/shard_map/all_to_all | solution.py:46
  140.8 8.6 %all_to_all.48 = f32[4,72,128]{2,1,0:T(8,128)S(1)} all-to-all(f32[4,72,128]{2,1,0:T(8,128)S(1)} %shard_map.92), channel_id=1, replica_groups={{0,2,4,6},{1,3,5,7},{16,18,20,22},{17,19,21,23},{32,34,36,38},{33,35,37..., dimensions={0} | all-to-all | bytes 294912 | tf_op jit(solution)/shard_map/all_to_all | solution.py:46
  149.4 1.9 %collective-permute-start.6 = (f32[72,128]{1,0:T(8,128)S(1)}, f32[72,128]{1,0:T(8,128)S(1)}, u32[]{:S(2)}, u32[]{:S(2)}) collective-permute-start(f32[72,128]{1,0:T(8,128)S(1)} %reduce_sum.19.one_ref), channel_id=1, source_target_pairs={{0,8},{1,9},{2,10},{3,11},{4,12},{5,13},{6,14},{7,15},{8,0},{9,1},... | collective-permute-start | bytes 110600 | tf_op jit(solution)/shard_map/ppermute | solution.py:309
  151.3 7.5 %collective-permute-done.6.two_ref = f32[72,128]{1,0:T(8,128)S(1)} collective-permute-done((f32[72,128]{1,0:T(8,128)S(1)}, f32[72,128]{1,0:T(8,128)S(1)}, u32[]{:S(2)}, u32[]{:S(2)}) %collective-permute-start.6) | collective-permute-done | bytes 36896 | tf_op jit(solution)/shard_map/ppermute | solution.py:309
  159.5 6.2 %all-to-all-start.8 = ((f32[8,72,128]{2,1,0:T(8,128)}), f32[8,72,128]{2,1,0:T(8,128)S(1)}, u32[]{:S(2)}, u32[]{:S(2)}) async-start(f32[8,72,128]{2,1,0:T(8,128)} %shard_map.93), calls=%async_computation.8 | async-start | bytes 589824 | tf_op jit(solution)/shard_map/all_to_all | solution.py:46
  165.7 2.1 %shard_map.94.refs_3_ = f32[1024,128]{1,0:T(8,128)S(1)} custom-call(f32[64,1024]{1,0:T(8,128)S(1)} %bitcast.49, bf16[1024,128]{1,0:T(8,128)(2,1)S(1)} %copy-done.1, bf16[8,320,128]{2,1,0:T(8,128)(2,1)S(1)} %constant_dynamic-update-slice_fusion.refs_2_), custom_call_target="tpu_custom_call" | custom-call | flops 1073741824 | bytes 2097152 | tf_op jit(solution)/shard_map/pallas_call | solution.py:318
  167.8 2.9 %shard_map.95 = f32[1024,128]{1,0:T(8,128)} custom-call(f32[64,1024]{1,0:T(8,128)S(1)} %bitcast.50, bf16[1024,128]{1,0:T(8,128)(2,1)S(1)} %copy-done.1, bf16[8,320,128]{2,1,0:T(8,128)(2,1)S(1)} %collective-permute-done.8.refs_2_, f32[1024,128]{1,0:T(8,128)S(1)} %shard_map.94.refs_3_), custom_call_target="tpu_custom_call" | custom-call | flops 1073741824 | bytes 2097152 | tf_op jit(solution)/shard_map/pallas_call | solution.py:318
  170.6 2.0 %all-to-all-done.8 = f32[8,72,128]{2,1,0:T(8,128)S(1)} async-done(((f32[8,72,128]{2,1,0:T(8,128)}), f32[8,72,128]{2,1,0:T(8,128)S(1)}, u32[]{:S(2)}, u32[]{:S(2)}) %all-to-all-start.8) | async-done | bytes 294944 | tf_op jit(solution)/shard_map/all_to_all | solution.py:46
  (48 shorter events, 8.6 us)
Async XLA Ops:
  2.0 23.7 %all-to-all-start = ((bf16[8,16,576]{2,1,0:T(8,128)(2,1)}), bf16[8,16,576]{2,1,0:T(8,128)(2,1)S(1)}, u32[]{:S(2)}, u32[]{:S(2)}) async-start(bf16[8,16,576]{2,1,0:T(8,128)(2,1)} %broadcast_in_dim.27), calls=%async_computation | async-start | bytes 327680 | tf_op jit(solution)/shard_map/all_to_all | solution.py:46
  17.1 17.7 %collective-permute-start = (bf16[1,320,128]{2,1,0:T(8,128)(2,1)S(1)}, bf16[1,320,128]{2,1,0:T(8,128)(2,1)S(1)}, u32[]{:S(2)}, u32[]{:S(2)}) collective-permute-start(bf16[1,320,128]{2,1,0:T(8,128)(2,1)S(1)} %constant_dynamic-slice_fusion), channel_id=1, source_target_pairs={{0,64},{64,0},{128,192},{192,128},{256,320},{320,256},{384,448},{4... | collective-permute-start | bytes 245768 | tf_op jit(solution)/shard_map/ppermute | solution.py:247
  26.9 9.8 %copy-start.2 = (s32[64]{0:T(128)S(1)}, s32[64]{0:T(128)}, u32[]{:S(2)}) copy-start(s32[64]{0:T(128)} %param.11) | copy-start | bytes 772
  26.9 11.1 %copy-start.1 = (bf16[1024,128]{1,0:T(8,128)(2,1)S(1)}, bf16[1024,128]{1,0:T(8,128)(2,1)}, u32[]{:S(2)}) copy-start(bf16[1024,128]{1,0:T(8,128)(2,1)} %refs_1_.3) | copy-start | bytes 786436
  26.9 25.7 %all-to-all-start.1 = ((bf16[8,8,16,576]{3,2,1,0:T(8,128)(2,1)}), bf16[8,8,16,576]{3,2,1,0:T(8,128)(2,1)S(1)}, u32[]{:S(2)}, u32[]{:S(2)}) async-start(bf16[8,8,16,576]{3,2,1,0:T(8,128)(2,1)} %broadcast_in_dim.28), calls=%async_computation.1 | async-start | bytes 2621440 | tf_op jit(solution)/shard_map/all_to_all | solution.py:46
  34.9 3.2 %collective-permute-start.1 = (bf16[1,320,128]{2,1,0:T(8,128)(2,1)S(1)}, bf16[1,320,128]{2,1,0:T(8,128)(2,1)S(1)}, u32[]{:S(2)}, u32[]{:S(2)}) collective-permute-start(bf16[1,320,128]{2,1,0:T(8,128)(2,1)S(1)} %collective-permute-done.refs_1_), channel_id=1, source_target_pairs={{0,1},{1,0},{2,3},{3,2},{4,5},{5,4},{6,7},{7,6},{8,9},{9,8},{10,11... | collective-permute-start | bytes 245768 | tf_op jit(solution)/shard_map/ppermute | solution.py:248
  38.9 10.0 %collective-permute-start.2 = (f32[16,1024]{1,0:T(8,128)S(1)}, f32[16,1024]{1,0:T(8,128)S(1)}, u32[]{:S(2)}, u32[]{:S(2)}) collective-permute-start(f32[16,1024]{1,0:T(8,128)S(1)} %get-tuple-element.21), channel_id=1, source_target_pairs={{0,128},{64,192},{128,0},{192,64},{256,384},{320,448},{384,256},{4... | collective-permute-start | bytes 196616 | tf_op jit(solution)/shard_map/ppermute | solution.py:219
  42.0 6.9 %collective-permute-start.4 = (f32[16,1024]{1,0:T(8,128)S(1)}, f32[16,1024]{1,0:T(8,128)S(1)}, u32[]{:S(2)}, u32[]{:S(2)}) collective-permute-start(f32[16,1024]{1,0:T(8,128)S(1)} %get-tuple-element.22), channel_id=1, source_target_pairs={{0,384},{64,448},{128,256},{192,320},{256,128},{320,192},{384,0},{... | collective-permute-start | bytes 196616 | tf_op jit(solution)/shard_map/ppermute | solution.py:219
  45.7 6.5 %collective-permute-start.3 = (f32[16,1024]{1,0:T(8,128)S(1)}, f32[16,1024]{1,0:T(8,128)S(1)}, u32[]{:S(2)}, u32[]{:S(2)}) collective-permute-start(f32[16,1024]{1,0:T(8,128)S(1)} %get-tuple-element.23), channel_id=1, source_target_pairs={{0,256},{64,320},{128,384},{192,448},{256,0},{320,64},{384,128},{4... | collective-permute-start | bytes 196616 | tf_op jit(solution)/shard_map/ppermute | solution.py:219
  52.6 1.3 copy-start
  99.1 13.7 %collective-permute-start.5 = (f32[16,1024]{1,0:T(8,128)S(1)}, f32[16,1024]{1,0:T(8,128)S(1)}, u32[]{:S(2)}, u32[]{:S(2)}) collective-permute-start(f32[16,1024]{1,0:T(8,128)S(1)} %reduce_sum.18.one_ref), channel_id=1, source_target_pairs={{0,64},{64,0},{128,192},{192,128},{256,320},{320,256},{384,448},{4... | collective-permute-start | bytes 196616 | tf_op jit(solution)/shard_map/ppermute | solution.py:287
  113.7 8.9 %all-to-all-start.5 = ((f32[4,16,1024]{2,1,0:T(8,128)}), f32[4,16,1024]{2,1,0:T(8,128)S(1)}, u32[]{:S(2)}, u32[]{:S(2)}) async-start(f32[4,16,1024]{2,1,0:T(8,128)} %shard_map.90), calls=%async_computation.5 | async-start | bytes 524288 | tf_op jit(solution)/shard_map/all_to_all | solution.py:46
  117.2 16.4 %collective-permute-start.7 = (bf16[4,320,128]{2,1,0:T(8,128)(2,1)S(1)}, bf16[4,320,128]{2,1,0:T(8,128)(2,1)S(1)}, u32[]{:S(2)}, u32[]{:S(2)}) collective-permute-start(bf16[4,320,128]{2,1,0:T(8,128)(2,1)S(1)} %pad_maximum_fusion), channel_id=1, source_target_pairs={{0,128},{64,192},{128,0},{192,64},{256,384},{320,448},{384,256},{4... | collective-permute-start | bytes 983048 | tf_op jit(solution)/shard_map/ppermute | solution.py:293
  124.4 16.4 %all-to-all-start.6 = ((f32[8,72,128]{2,1,0:T(8,128)}), f32[8,72,128]{2,1,0:T(8,128)S(1)}, u32[]{:S(2)}, u32[]{:S(2)}) async-start(f32[8,72,128]{2,1,0:T(8,128)} %bitcast.24), calls=%async_computation.6 | async-start | bytes 589824 | tf_op jit(solution)/shard_map/all_to_all | solution.py:46
  133.6 34.1 %collective-permute-start.8 = (bf16[8,320,128]{2,1,0:T(8,128)(2,1)S(1)}, bf16[8,320,128]{2,1,0:T(8,128)(2,1)S(1)}, u32[]{:S(2)}, u32[]{:S(2)}) collective-permute-start(bf16[8,320,128]{2,1,0:T(8,128)(2,1)S(1)} %constant_dynamic-update-slice_fusion.refs_2_), channel_id=1, source_target_pairs={{0,256},{64,320},{128,384},{192,448},{256,0},{320,64},{384,128},{4... | collective-permute-start | bytes 1966088 | tf_op jit(solution)/shard_map/ppermute | solution.py:306
  149.4 9.4 %collective-permute-start.6 = (f32[72,128]{1,0:T(8,128)S(1)}, f32[72,128]{1,0:T(8,128)S(1)}, u32[]{:S(2)}, u32[]{:S(2)}) collective-permute-start(f32[72,128]{1,0:T(8,128)S(1)} %reduce_sum.19.one_ref), channel_id=1, source_target_pairs={{0,8},{1,9},{2,10},{3,11},{4,12},{5,13},{6,14},{7,15},{8,0},{9,1},... | collective-permute-start | bytes 110600 | tf_op jit(solution)/shard_map/ppermute | solution.py:309
  159.5 13.1 %all-to-all-start.8 = ((f32[8,72,128]{2,1,0:T(8,128)}), f32[8,72,128]{2,1,0:T(8,128)S(1)}, u32[]{:S(2)}, u32[]{:S(2)}) async-start(f32[8,72,128]{2,1,0:T(8,128)} %shard_map.93), calls=%async_computation.8 | async-start | bytes 589824 | tf_op jit(solution)/shard_map/all_to_all | solution.py:46

commit v11 on v10

--- a/solution.py
+++ b/solution.py
@@ -11,7 +11,7 @@
 NYC = NY * NC
 GRAD_SCALE = 8192.0
 VMEM = 12 << 20
-WEIGHT = 20
+WEIGHT = 48
 
 softmax_scale = 192.0 ** (-0.5)
 masked_value = -1e30
@@ -117,9 +117,11 @@
     out_ref[...] = logits
 
 
-def index_stats_kernel(limit_ref, sum_ref, logits_ref, stat_ref):
-    key = lax.broadcasted_iota(jnp.int32, (1, logits_ref.shape[1]), 1)
-    logits = jnp.where(key <= limit_ref[...], sum_ref[...], masked_value)
+def index_stats_kernel(limit_ref, *refs):
+    pieces, (logits_ref, stat_ref) = refs[:-2], refs[-2:]
+    logits = sum(piece[...] for piece in pieces)
+    key = lax.broadcasted_iota(jnp.int32, (1, logits.shape[1]), 1)
+    logits = jnp.where(key <= limit_ref[...], logits, masked_value)
     m = jnp.max(logits, axis=1, keepdims=True)
     l = jnp.sum(jnp.exp(logits - m), axis=1, keepdims=True)
     logits_ref[...] = logits
@@ -208,16 +210,21 @@
     out_ref[...] = jnp.broadcast_to((one_ref[...] + two_ref[...])[None], out_ref.shape)
 
 
+def cut_kernel(both_ref, query_ref, weight_ref):
+    lines, (rows, lanes) = query_ref.shape[0], weight_ref.shape
+    query_ref[...] = both_ref[:lines]
+    weight_ref[...] = both_ref[lines : lines + rows, :lanes]
+
+
 def in_order(value):
     return jnp.moveaxis(value.reshape(NY, NZ, NC, *value.shape[1:]), 2, 0).reshape(value.shape)
 
 
-def x_scatter_sum(parts, x):
-    total = lax.dynamic_index_in_dim(parts, x, 0, keepdims=False)
-    for flip in range(1, NX):
-        piece = lax.dynamic_index_in_dim(parts, x ^ flip, 0, keepdims=False)
-        total = total + lax.ppermute(piece, "heads", pairs_x(flip))
-    return total
+def x_scatter(parts, x):
+    pieces = [lax.dynamic_index_in_dim(parts, x ^ flip, 0, keepdims=False) for flip in range(NX)]
+    return pieces[:1] + [
+        lax.ppermute(pieces[flip], "heads", pairs_x(flip)) for flip in range(1, NX)
+    ]
 
 
 def local(queries, latent_keys, index_queries, index_keys, index_weights, positions):
@@ -251,18 +258,10 @@
     partial = call(
         lambda *refs: logits_kernel(half, index_scale, *refs),
         shape((query_count, key_count), f32),
-        flops=2 * index_flops,
+        flops=WEIGHT * index_flops,
         moved=1 << 20,
     )(mine, first, second, index_keys)
-    over_x = x_scatter_sum(partial.reshape(NX, share_rows, key_count), x)
-    share_limit = lax.dynamic_slice_in_dim(limit, x * share_rows, share_rows, 0)
-    logits, index_stats = call(
-        index_stats_kernel,
-        (shape((share_rows, key_count), f32), shape((8, 128), f32)),
-        flops=WEIGHT * index_flops,
-        moved=1 << 20,
-    )(share_limit[:, None], over_x)
-
+    pieces = x_scatter(partial.reshape(NX, share_rows, key_count), x)
     rows = gathered(along_z, "tokens", groups_yc).reshape(-1, width)
     row_count = rows.shape[0]
     lines_shape = shape((NYC, row_count // NYC), f32)
@@ -272,6 +271,15 @@
         flops=2 * row_count * key_count * width,
         moved=4 << 20,
     )(jnp.repeat(limit, heads_here)[:, None], rows, latent_keys.T)
+
+    local_max, *pieces = lax.optimization_barrier((local_max, *pieces))
+    share_limit = lax.dynamic_slice_in_dim(limit, x * share_rows, share_rows, 0)
+    logits, index_stats = call(
+        index_stats_kernel,
+        (shape((share_rows, key_count), f32), shape((8, 128), f32)),
+        flops=index_flops,
+        moved=1 << 20,
+    )(share_limit[:, None], *pieces)
 
     stats = jnp.concatenate([local_max, local_total, index_stats])
 
@@ -309,8 +317,11 @@
     other = lax.ppermute(piece, "tokens", pairs_z4)
     piece = call(pair_kernel, shape((NYC, piece_rows, 128), f32))(piece, other)
     both = exchanged(piece, "tokens", groups_yc).reshape(-1, 128)
-    query_grad = both[:query_lines].reshape(query_count, index_heads, index_width)
-    weight_grad = both[query_lines : query_lines + index_heads, :query_count].T
+    query_grad, weight_grad = call(
+        cut_kernel, (shape((query_lines, 128), f32), shape((index_heads, query_count), f32))
+    )(both)
+    query_grad = query_grad.reshape(query_count, index_heads, index_width)
+    weight_grad = weight_grad.T
 
     key_flops = index_flops * NX * NZH
     key_grad = ()

time: 175 us -> 174 us (level)
    ppermute x3, waiting for transfers between devices: 3.39 us -> 0.01 us  [x_scatter(): lax.ppermute(pieces[flip], 'heads', pairs_x(flip))]
    all_to_all x5, waiting for transfers between devices: 10.1 us -> 12.2 us  [exchanged(): lax.all_to_all(parts, axis, 0, 0, tiled=True, axis_index_groups=groups)]
  transfers between devices with their start and end apart: 14 -> 14, of which waited for: 9 -> 8; matrix products, arithmetic and copies ran while one was open for 2% -> 3% of each run, Pallas kernels for 5% -> 6%
where the time goes in v11:
time: 174 us; the launch traced here: 173 us
  starting transfers between devices  74.4 us (43%)
  blocking collectives  50.2 us (29%)
  waiting for transfers between devices  26.1 us (15%)
  Pallas kernels  14 us (8%)
  local copies, waits for them, and re-layouts  6.39 us (4%)
    all_to_all x4, blocking collectives, exchanged(): lax.all_to_all(parts, axis, 0, 0, tiled=True, axis_index_groups=groups)  50.2 us
    all_to_all x5, starting transfers between devices, exchanged(): lax.all_to_all(parts, axis, 0, 0, tiled=True, axis_index_groups=groups)  39.8 us
    all_to_all x5, waiting for transfers between devices, exchanged(): lax.all_to_all(parts, axis, 0, 0, tiled=True, axis_index_groups=groups)  12.2 us
    ppermute x3, starting transfers between devices, x_scatter(): lax.ppermute(pieces[flip], 'heads', pairs_x(flip))  9.57 us
    ppermute x1, starting transfers between devices, local(): other = lax.ppermute(over_x, 'heads', pairs_zh)  8.07 us
    ppermute x1, starting transfers between devices, local(): lax.ppermute(lax.dynamic_index_in_dim(mine, core, 0), 'heads', pairs_zh)  7.94 us
    ppermute x1, waiting for transfers between devices, local(): other = lax.ppermute(piece, 'tokens', pairs_z4)  7.47 us
    ppermute x1, waiting for transfers between devices, local(): other = lax.ppermute(over_x, 'heads', pairs_zh)  5.78 us
  transfers between devices with their start and end apart: 14, of which 8 were waited for; matrix products, arithmetic and copies ran while one was open for 3% of the time, Pallas kernels for 6%

profile of v11, /device:TPU:1, one launch (start us, length us, event | category | flops | bytes accessed | tf_op | source)
XLA Modules:
  0.0 173.0 jit_solution(1774782790671766905)
XLA Ops:
  0.6 1.4 broadcast_in_dim.27
  2.0 13.1 %all-to-all-start = ((bf16[8,16,576]{2,1,0:T(8,128)(2,1)}), bf16[8,16,576]{2,1,0:T(8,128)(2,1)S(1)}, u32[]{:S(2)}, u32[]{:S(2)}) async-start(bf16[8,16,576]{2,1,0:T(8,128)(2,1)} %broadcast_in_dim.27), calls=%async_computation | async-start | bytes 327680 | tf_op jit(solution)/shard_map/all_to_all | solution.py:46
  17.1 7.9 %collective-permute-start = (bf16[1,320,128]{2,1,0:T(8,128)(2,1)S(1)}, bf16[1,320,128]{2,1,0:T(8,128)(2,1)S(1)}, u32[]{:S(2)}, u32[]{:S(2)}) collective-permute-start(bf16[1,320,128]{2,1,0:T(8,128)(2,1)S(1)} %constant_dynamic-slice_fusion), channel_id=1, source_target_pairs={{0,64},{64,0},{128,192},{192,128},{256,320},{320,256},{384,448},{4... | collective-permute-start | bytes 245768 | tf_op jit(solution)/shard_map/ppermute | solution.py:254
  25.8 1.2 broadcast_in_dim.28
  26.9 7.9 %all-to-all-start.1 = ((bf16[8,8,16,576]{3,2,1,0:T(8,128)(2,1)}), bf16[8,8,16,576]{3,2,1,0:T(8,128)(2,1)S(1)}, u32[]{:S(2)}, u32[]{:S(2)}) async-start(bf16[8,8,16,576]{3,2,1,0:T(8,128)(2,1)} %broadcast_in_dim.28), calls=%async_computation.1 | async-start | bytes 2621440 | tf_op jit(solution)/shard_map/all_to_all | solution.py:46
  35.2 1.9 %collective-permute-start.1 = (bf16[1,320,128]{2,1,0:T(8,128)(2,1)S(1)}, bf16[1,320,128]{2,1,0:T(8,128)(2,1)S(1)}, u32[]{:S(2)}, u32[]{:S(2)}) collective-permute-start(bf16[1,320,128]{2,1,0:T(8,128)(2,1)S(1)} %collective-permute-done.refs_1_), channel_id=1, source_target_pairs={{0,1},{1,0},{2,3},{3,2},{4,5},{5,4},{6,7},{7,6},{8,9},{9,8},{10,11... | collective-permute-start | bytes 245768 | tf_op jit(solution)/shard_map/ppermute | solution.py:255
  38.4 0.9 copy-done.1
  40.8 3.1 %collective-permute-start.2 = (f32[16,1024]{1,0:T(8,128)}, f32[16,1024]{1,0:T(8,128)S(1)}, u32[]{:S(2)}, u32[]{:S(2)}) collective-permute-start(f32[16,1024]{1,0:T(8,128)} %get-tuple-element.37), channel_id=1, source_target_pairs={{0,128},{64,192},{128,0},{192,64},{256,384},{320,448},{384,256},{4... | collective-permute-start | bytes 196616 | tf_op jit(solution)/shard_map/ppermute | solution.py:226
  43.9 4.4 %collective-permute-start.3 = (f32[16,1024]{1,0:T(8,128)}, f32[16,1024]{1,0:T(8,128)S(1)}, u32[]{:S(2)}, u32[]{:S(2)}) collective-permute-start(f32[16,1024]{1,0:T(8,128)} %get-tuple-element.36), channel_id=1, source_target_pairs={{0,256},{64,320},{128,384},{192,448},{256,0},{320,64},{384,128},{4... | collective-permute-start | bytes 196616 | tf_op jit(solution)/shard_map/ppermute | solution.py:226
  48.3 2.1 %collective-permute-start.4 = (f32[16,1024]{1,0:T(8,128)}, f32[16,1024]{1,0:T(8,128)}, u32[]{:S(2)}, u32[]{:S(2)}) collective-permute-start(f32[16,1024]{1,0:T(8,128)} %get-tuple-element.35), channel_id=1, source_target_pairs={{0,384},{64,448},{128,256},{192,320},{256,128},{320,192},{384,0},{... | collective-permute-start | bytes 196616 | tf_op jit(solution)/shard_map/ppermute | solution.py:226
  50.4 2.3 %all-to-all-done.1 = bf16[8,8,16,576]{3,2,1,0:T(8,128)(2,1)S(1)} async-done(((bf16[8,8,16,576]{3,2,1,0:T(8,128)(2,1)}), bf16[8,8,16,576]{3,2,1,0:T(8,128)(2,1)S(1)}, u32[]{:S(2)}, u32[]{:S(2)}) %all-to-all-start.1) | async-done | bytes 1179680 | tf_op jit(solution)/shard_map/all_to_all | solution.py:46
  52.6 2.3 %shard_map.85 = (f32[1024,1024]{1,0:T(8,128)S(1)}, f32[8,128]{1,0:T(8,128)S(1)}, f32[8,128]{1,0:T(8,128)S(1)}) custom-call(s32[1024,1]{1,0:T(8,128)S(1)} %broadcast_in_dim_reshape.5.limit_ref, bf16[1024,576]{1,0:T(8,128)(2,1)S(1)} %bitcast.38, bf16[576,1024]{1,0:T(8,128)(2,1)S(1)} %bitcast.45), custom_call_target="tpu_custom_call" | custom-call | flops 1207959552 | bytes 4194304 | tf_op jit(solution)/shard_map/pallas_call | solution.py:268
  55.0 1.1 shard_map.87
  56.1 20.2 %all_to_all.45.stats_ref = f32[8,24,128]{2,1,0:T(8,128)S(1)} all-to-all(f32[8,24,128]{2,1,0:T(8,128)S(1)} %broadcast_in_dim.30), channel_id=1, replica_groups={{0,2,4,6,8,10,12,14},{1,3,5,7,9,11,13,15},{16,18,20,22,24,26,28,30},{17..., dimensions={0} | all-to-all | bytes 196608 | tf_op jit(solution)/shard_map/all_to_all | solution.py:46
  76.3 12.7 %all_to_all.46.stats_ref = f32[8,24,128]{2,1,0:T(8,128)S(1)} all-to-all(f32[8,24,128]{2,1,0:T(8,128)S(1)} %shard_map.88), channel_id=1, replica_groups={{0,16,32,48,1,17,33,49},{2,18,34,50,3,19,35,51},{4,20,36,52,5,21,37,53}..., dimensions={0} | all-to-all | bytes 196608 | tf_op jit(solution)/shard_map/all_to_all | solution.py:46
  89.8 8.8 %all_to_all.47 = f32[4,16,1024]{2,1,0:T(8,128)S(1)} all-to-all(f32[4,16,1024]{2,1,0:T(8,128)S(1)} %bitcast.40), channel_id=1, replica_groups={{0,128,256,384},{64,192,320,448},{1,129,257,385},{65,193,321,449},{2,13..., dimensions={0} | all-to-all | bytes 524288 | tf_op jit(solution)/shard_map/all_to_all | solution.py:46
  98.6 8.1 %collective-permute-start.5 = (f32[16,1024]{1,0:T(8,128)S(1)}, f32[16,1024]{1,0:T(8,128)S(1)}, u32[]{:S(2)}, u32[]{:S(2)}) collective-permute-start(f32[16,1024]{1,0:T(8,128)S(1)} %reduce_sum.18.one_ref), channel_id=1, source_target_pairs={{0,64},{64,0},{128,192},{192,128},{256,320},{320,256},{384,448},{4... | collective-permute-start | bytes 196616 | tf_op jit(solution)/shard_map/ppermute | solution.py:295
  106.7 5.8 %collective-permute-done.5.two_ref = f32[16,1024]{1,0:T(8,128)S(1)} collective-permute-done((f32[16,1024]{1,0:T(8,128)S(1)}, f32[16,1024]{1,0:T(8,128)S(1)}, u32[]{:S(2)}, u32[]{:S(2)}) %collective-permute-start.5) | collective-permute-done | bytes 65568 | tf_op jit(solution)/shard_map/ppermute | solution.py:295
  113.3 3.4 %all-to-all-start.5 = ((f32[4,16,1024]{2,1,0:T(8,128)}), f32[4,16,1024]{2,1,0:T(8,128)S(1)}, u32[]{:S(2)}, u32[]{:S(2)}) async-start(f32[4,16,1024]{2,1,0:T(8,128)} %shard_map.90), calls=%async_computation.5 | async-start | bytes 524288 | tf_op jit(solution)/shard_map/all_to_all | solution.py:46
  116.8 3.3 %collective-permute-start.7 = (bf16[4,320,128]{2,1,0:T(8,128)(2,1)S(1)}, bf16[4,320,128]{2,1,0:T(8,128)(2,1)S(1)}, u32[]{:S(2)}, u32[]{:S(2)}) collective-permute-start(bf16[4,320,128]{2,1,0:T(8,128)(2,1)S(1)} %pad_maximum_fusion), channel_id=1, source_target_pairs={{0,128},{64,192},{128,0},{192,64},{256,384},{320,448},{384,256},{4... | collective-permute-start | bytes 983048 | tf_op jit(solution)/shard_map/ppermute | solution.py:301
  120.1 2.1 %all-to-all-done.5 = f32[4,16,1024]{2,1,0:T(8,128)S(1)} async-done(((f32[4,16,1024]{2,1,0:T(8,128)}), f32[4,16,1024]{2,1,0:T(8,128)S(1)}, u32[]{:S(2)}, u32[]{:S(2)}) %all-to-all-start.5) | async-done | bytes 262176 | tf_op jit(solution)/shard_map/all_to_all | solution.py:46
  122.2 1.8 %shard_map.91 = f32[576,128]{1,0:T(8,128)} custom-call(f32[64,1024]{1,0:T(8,128)S(1)} %bitcast.41, bf16[2,320,128]{2,1,0:T(8,128)(2,1)S(1)} %fusion.1.refs_0_.refs_1_, bf16[1024,128]{1,0:T(8,128)(2,1)S(1)} %copy-done.2), custom_call_target="tpu_custom_call" | custom-call | flops 268435456 | bytes 2097152 | tf_op jit(solution)/shard_map/pallas_call | solution.py:305
  124.0 9.2 %all-to-all-start.6 = ((f32[8,72,128]{2,1,0:T(8,128)}), f32[8,72,128]{2,1,0:T(8,128)S(1)}, u32[]{:S(2)}, u32[]{:S(2)}) async-start(f32[8,72,128]{2,1,0:T(8,128)} %bitcast.24), calls=%async_computation.6 | async-start | bytes 589824 | tf_op jit(solution)/shard_map/all_to_all | solution.py:46
  133.3 1.9 %collective-permute-start.8 = (bf16[8,320,128]{2,1,0:T(8,128)(2,1)S(1)}, bf16[8,320,128]{2,1,0:T(8,128)(2,1)S(1)}, u32[]{:S(2)}, u32[]{:S(2)}) collective-permute-start(bf16[8,320,128]{2,1,0:T(8,128)(2,1)S(1)} %constant_dynamic-update-slice_fusion.refs_2_), channel_id=1, source_target_pairs={{0,256},{64,320},{128,384},{192,448},{256,0},{320,64},{384,128},{4... | collective-permute-start | bytes 1966088 | tf_op jit(solution)/shard_map/ppermute | solution.py:314
  135.2 5.2 %all-to-all-done.6.parts_ref = f32[8,72,128]{2,1,0:T(8,128)S(1)} async-done(((f32[8,72,128]{2,1,0:T(8,128)}), f32[8,72,128]{2,1,0:T(8,128)S(1)}, u32[]{:S(2)}, u32[]{:S(2)}) %all-to-all-start.6) | async-done | bytes 294944 | tf_op jit(solution)/shard_map/all_to_all | solution.py:46
  140.4 8.6 %all_to_all.48 = f32[4,72,128]{2,1,0:T(8,128)S(1)} all-to-all(f32[4,72,128]{2,1,0:T(8,128)S(1)} %shard_map.92), channel_id=1, replica_groups={{0,2,4,6},{1,3,5,7},{16,18,20,22},{17,19,21,23},{32,34,36,38},{33,35,37..., dimensions={0} | all-to-all | bytes 294912 | tf_op jit(solution)/shard_map/all_to_all | solution.py:46
  149.0 1.9 %collective-permute-start.6 = (f32[72,128]{1,0:T(8,128)S(1)}, f32[72,128]{1,0:T(8,128)S(1)}, u32[]{:S(2)}, u32[]{:S(2)}) collective-permute-start(f32[72,128]{1,0:T(8,128)S(1)} %reduce_sum.19.one_ref), channel_id=1, source_target_pairs={{0,8},{1,9},{2,10},{3,11},{4,12},{5,13},{6,14},{7,15},{8,0},{9,1},... | collective-permute-start | bytes 110600 | tf_op jit(solution)/shard_map/ppermute | solution.py:317
  150.9 7.5 %collective-permute-done.6.two_ref = f32[72,128]{1,0:T(8,128)S(1)} collective-permute-done((f32[72,128]{1,0:T(8,128)S(1)}, f32[72,128]{1,0:T(8,128)S(1)}, u32[]{:S(2)}, u32[]{:S(2)}) %collective-permute-start.6) | collective-permute-done | bytes 36896 | tf_op jit(solution)/shard_map/ppermute | solution.py:317
  159.1 6.2 %all-to-all-start.8 = ((f32[8,72,128]{2,1,0:T(8,128)}), f32[8,72,128]{2,1,0:T(8,128)S(1)}, u32[]{:S(2)}, u32[]{:S(2)}) async-start(f32[8,72,128]{2,1,0:T(8,128)} %shard_map.93), calls=%async_computation.8 | async-start | bytes 589824 | tf_op jit(solution)/shard_map/all_to_all | solution.py:46
  165.3 2.1 %shard_map.95.refs_3_ = f32[1024,128]{1,0:T(8,128)S(1)} custom-call(f32[64,1024]{1,0:T(8,128)S(1)} %bitcast.42, bf16[1024,128]{1,0:T(8,128)(2,1)S(1)} %copy-done.2, bf16[8,320,128]{2,1,0:T(8,128)(2,1)S(1)} %constant_dynamic-update-slice_fusion.refs_2_), custom_call_target="tpu_custom_call" | custom-call | flops 1073741824 | bytes 2097152 | tf_op jit(solution)/shard_map/pallas_call | solution.py:329
  167.4 2.9 %shard_map.96 = f32[1024,128]{1,0:T(8,128)} custom-call(f32[64,1024]{1,0:T(8,128)S(1)} %bitcast.43, bf16[1024,128]{1,0:T(8,128)(2,1)S(1)} %copy-done.2, bf16[8,320,128]{2,1,0:T(8,128)(2,1)S(1)} %collective-permute-done.8.refs_2_, f32[1024,128]{1,0:T(8,128)S(1)} %shard_map.95.refs_3_), custom_call_target="tpu_custom_call" | custom-call | flops 1073741824 | bytes 2097152 | tf_op jit(solution)/shard_map/pallas_call | solution.py:329
  170.3 2.0 %all-to-all-done.8 = f32[8,72,128]{2,1,0:T(8,128)S(1)} async-done(((f32[8,72,128]{2,1,0:T(8,128)}), f32[8,72,128]{2,1,0:T(8,128)S(1)}, u32[]{:S(2)}, u32[]{:S(2)}) %all-to-all-start.8) | async-done | bytes 294944 | tf_op jit(solution)/shard_map/all_to_all | solution.py:46
  (48 shorter events, 8.9 us)
Async XLA Ops:
  2.0 23.7 %all-to-all-start = ((bf16[8,16,576]{2,1,0:T(8,128)(2,1)}), bf16[8,16,576]{2,1,0:T(8,128)(2,1)S(1)}, u32[]{:S(2)}, u32[]{:S(2)}) async-start(bf16[8,16,576]{2,1,0:T(8,128)(2,1)} %broadcast_in_dim.27), calls=%async_computation | async-start | bytes 327680 | tf_op jit(solution)/shard_map/all_to_all | solution.py:46
  17.1 18.0 %collective-permute-start = (bf16[1,320,128]{2,1,0:T(8,128)(2,1)S(1)}, bf16[1,320,128]{2,1,0:T(8,128)(2,1)S(1)}, u32[]{:S(2)}, u32[]{:S(2)}) collective-permute-start(bf16[1,320,128]{2,1,0:T(8,128)(2,1)S(1)} %constant_dynamic-slice_fusion), channel_id=1, source_target_pairs={{0,64},{64,0},{128,192},{192,128},{256,320},{320,256},{384,448},{4... | collective-permute-start | bytes 245768 | tf_op jit(solution)/shard_map/ppermute | solution.py:254
  26.9 7.9 %copy-start.3 = (s32[64]{0:T(128)S(1)}, s32[64]{0:T(128)}, u32[]{:S(2)}) copy-start(s32[64]{0:T(128)} %param.11) | copy-start | bytes 772
  26.9 25.7 %all-to-all-start.1 = ((bf16[8,8,16,576]{3,2,1,0:T(8,128)(2,1)}), bf16[8,8,16,576]{3,2,1,0:T(8,128)(2,1)S(1)}, u32[]{:S(2)}, u32[]{:S(2)}) async-start(bf16[8,8,16,576]{3,2,1,0:T(8,128)(2,1)} %broadcast_in_dim.28), calls=%async_computation.1 | async-start | bytes 2621440 | tf_op jit(solution)/shard_map/all_to_all | solution.py:46
  35.2 3.2 %collective-permute-start.1 = (bf16[1,320,128]{2,1,0:T(8,128)(2,1)S(1)}, bf16[1,320,128]{2,1,0:T(8,128)(2,1)S(1)}, u32[]{:S(2)}, u32[]{:S(2)}) collective-permute-start(bf16[1,320,128]{2,1,0:T(8,128)(2,1)S(1)} %collective-permute-done.refs_1_), channel_id=1, source_target_pairs={{0,1},{1,0},{2,3},{3,2},{4,5},{5,4},{6,7},{7,6},{8,9},{9,8},{10,11... | collective-permute-start | bytes 245768 | tf_op jit(solution)/shard_map/ppermute | solution.py:255
  37.7 15.0 %copy-start = (bf16[1024,576]{0,1:T(8,128)(2,1)S(1)}, bf16[1024,576]{0,1:T(8,128)(2,1)}, u32[]{:S(2)}) copy-start(bf16[1024,576]{0,1:T(8,128)(2,1)} %param.7) | copy-start | bytes 3538948
  38.3 1.0 copy-start.1
  40.8 14.2 %collective-permute-start.2 = (f32[16,1024]{1,0:T(8,128)}, f32[16,1024]{1,0:T(8,128)S(1)}, u32[]{:S(2)}, u32[]{:S(2)}) collective-permute-start(f32[16,1024]{1,0:T(8,128)} %get-tuple-element.37), channel_id=1, source_target_pairs={{0,128},{64,192},{128,0},{192,64},{256,384},{320,448},{384,256},{4... | collective-permute-start | bytes 196616 | tf_op jit(solution)/shard_map/ppermute | solution.py:226
  43.9 11.1 %collective-permute-start.3 = (f32[16,1024]{1,0:T(8,128)}, f32[16,1024]{1,0:T(8,128)S(1)}, u32[]{:S(2)}, u32[]{:S(2)}) collective-permute-start(f32[16,1024]{1,0:T(8,128)} %get-tuple-element.36), channel_id=1, source_target_pairs={{0,256},{64,320},{128,384},{192,448},{256,0},{320,64},{384,128},{4... | collective-permute-start | bytes 196616 | tf_op jit(solution)/shard_map/ppermute | solution.py:226
  48.3 6.7 %collective-permute-start.4 = (f32[16,1024]{1,0:T(8,128)}, f32[16,1024]{1,0:T(8,128)}, u32[]{:S(2)}, u32[]{:S(2)}) collective-permute-start(f32[16,1024]{1,0:T(8,128)} %get-tuple-element.35), channel_id=1, source_target_pairs={{0,384},{64,448},{128,256},{192,320},{256,128},{320,192},{384,0},{... | collective-permute-start | bytes 196616 | tf_op jit(solution)/shard_map/ppermute | solution.py:226
  98.6 23.6 %copy-start.2 = (bf16[1024,128]{1,0:T(8,128)(2,1)S(1)}, bf16[1024,128]{1,0:T(8,128)(2,1)}, u32[]{:S(2)}) copy-start(bf16[1024,128]{1,0:T(8,128)(2,1)} %refs_1_.3) | copy-start | bytes 786436
  98.6 13.9 %collective-permute-start.5 = (f32[16,1024]{1,0:T(8,128)S(1)}, f32[16,1024]{1,0:T(8,128)S(1)}, u32[]{:S(2)}, u32[]{:S(2)}) collective-permute-start(f32[16,1024]{1,0:T(8,128)S(1)} %reduce_sum.18.one_ref), channel_id=1, source_target_pairs={{0,64},{64,0},{128,192},{192,128},{256,320},{320,256},{384,448},{4... | collective-permute-start | bytes 196616 | tf_op jit(solution)/shard_map/ppermute | solution.py:295
  113.3 8.9 %all-to-all-start.5 = ((f32[4,16,1024]{2,1,0:T(8,128)}), f32[4,16,1024]{2,1,0:T(8,128)S(1)}, u32[]{:S(2)}, u32[]{:S(2)}) async-start(f32[4,16,1024]{2,1,0:T(8,128)} %shard_map.90), calls=%async_computation.5 | async-start | bytes 524288 | tf_op jit(solution)/shard_map/all_to_all | solution.py:46
  116.8 16.4 %collective-permute-start.7 = (bf16[4,320,128]{2,1,0:T(8,128)(2,1)S(1)}, bf16[4,320,128]{2,1,0:T(8,128)(2,1)S(1)}, u32[]{:S(2)}, u32[]{:S(2)}) collective-permute-start(bf16[4,320,128]{2,1,0:T(8,128)(2,1)S(1)} %pad_maximum_fusion), channel_id=1, source_target_pairs={{0,128},{64,192},{128,0},{192,64},{256,384},{320,448},{384,256},{4... | collective-permute-start | bytes 983048 | tf_op jit(solution)/shard_map/ppermute | solution.py:301
  124.0 16.4 %all-to-all-start.6 = ((f32[8,72,128]{2,1,0:T(8,128)}), f32[8,72,128]{2,1,0:T(8,128)S(1)}, u32[]{:S(2)}, u32[]{:S(2)}) async-start(f32[8,72,128]{2,1,0:T(8,128)} %bitcast.24), calls=%async_computation.6 | async-start | bytes 589824 | tf_op jit(solution)/shard_map/all_to_all | solution.py:46
  133.3 34.1 %collective-permute-start.8 = (bf16[8,320,128]{2,1,0:T(8,128)(2,1)S(1)}, bf16[8,320,128]{2,1,0:T(8,128)(2,1)S(1)}, u32[]{:S(2)}, u32[]{:S(2)}) collective-permute-start(bf16[8,320,128]{2,1,0:T(8,128)(2,1)S(1)} %constant_dynamic-update-slice_fusion.refs_2_), channel_id=1, source_target_pairs={{0,256},{64,320},{128,384},{192,448},{256,0},{320,64},{384,128},{4... | collective-permute-start | bytes 1966088 | tf_op jit(solution)/shard_map/ppermute | solution.py:314
  149.0 9.4 %collective-permute-start.6 = (f32[72,128]{1,0:T(8,128)S(1)}, f32[72,128]{1,0:T(8,128)S(1)}, u32[]{:S(2)}, u32[]{:S(2)}) collective-permute-start(f32[72,128]{1,0:T(8,128)S(1)} %reduce_sum.19.one_ref), channel_id=1, source_target_pairs={{0,8},{1,9},{2,10},{3,11},{4,12},{5,13},{6,14},{7,15},{8,0},{9,1},... | collective-permute-start | bytes 110600 | tf_op jit(solution)/shard_map/ppermute | solution.py:317
  159.1 13.1 %all-to-all-start.8 = ((f32[8,72,128]{2,1,0:T(8,128)}), f32[8,72,128]{2,1,0:T(8,128)S(1)}, u32[]{:S(2)}, u32[]{:S(2)}) async-start(f32[8,72,128]{2,1,0:T(8,128)} %shard_map.93), calls=%async_computation.8 | async-start | bytes 589824 | tf_op jit(solution)/shard_map/all_to_all | solution.py:46

commit v12 on v11

--- a/solution.py
+++ b/solution.py
@@ -28,12 +28,8 @@
 
 all_y, all_z, all_c = range(NY), range(NZ), range(NC)
 groups_z = [[token_at(y, z, c) for z in all_z] for y in all_y for c in all_c]
-groups_z4 = [
-    [token_at(y, half + z, c) for z in range(4)] for half in (0, 4) for y in all_y for c in all_c
-]
 pairs_c = [(token_at(y, z, c), token_at(y, z, 1 - c)) for y in all_y for z in all_z for c in all_c]
 groups_yc = [[token_at(y, z, c) for c in all_c for y in all_y] for z in all_z]
-pairs_z4 = [(token_at(y, z, c), token_at(y, z ^ 4, c)) for y in all_y for z in all_z for c in all_c]
 groups_x = [[head_at(x, z) for x in range(NX)] for z in range(NZH)]
 pairs_zh = [(head_at(x, z), head_at(x, 1 - z)) for x in range(NX) for z in range(NZH)]
 
@@ -206,10 +202,6 @@
     out_ref[...] = jnp.broadcast_to(jnp.sum(parts_ref[...], axis=0)[None], out_ref.shape)
 
 
-def pair_kernel(one_ref, two_ref, out_ref):
-    out_ref[...] = jnp.broadcast_to((one_ref[...] + two_ref[...])[None], out_ref.shape)
-
-
 def cut_kernel(both_ref, query_ref, weight_ref):
     lines, (rows, lanes) = query_ref.shape[0], weight_ref.shape
     query_ref[...] = both_ref[:lines]
@@ -312,10 +304,9 @@
     piece = exchanged(both.reshape(NYC, piece_rows, 128), "tokens", groups_yc)
     eight = jnp.concatenate([four, near])
     far = lax.ppermute(eight, "heads", pairs_x(2))
-    piece = call(sum_kernel, shape((NZ // 2, piece_rows, 128), f32))(piece)
-    piece = exchanged(piece, "tokens", groups_z4).sum(axis=0)
-    other = lax.ppermute(piece, "tokens", pairs_z4)
-    piece = call(pair_kernel, shape((NYC, piece_rows, 128), f32))(piece, other)
+    piece = call(sum_kernel, shape((NZ, piece_rows, 128), f32))(piece)
+    piece = exchanged(piece, "tokens", groups_z)
+    piece = call(sum_kernel, shape((NYC, piece_rows, 128), f32))(piece)
     both = exchanged(piece, "tokens", groups_yc).reshape(-1, 128)
     query_grad, weight_grad = call(
         cut_kernel, (shape((query_lines, 128), f32), shape((index_heads, query_count), f32))

time: 174 us -> 175 us (level)
  blocking collectives: 50.2 us -> 63.9 us
  starting transfers between devices: 74.4 us -> 64.1 us
  waiting for transfers between devices: 26.1 us -> 23.2 us
    all_to_all x4 -> x5, blocking collectives: 50.2 us -> 63.9 us  [exchanged(): lax.all_to_all(parts, axis, 0, 0, tiled=True, axis_index_groups=groups)]
    ppermute x1, waiting for transfers between devices: 0.01 us -> 8.21 us  [local(): near = lax.ppermute(four, 'heads', pairs_x(1))]
    all_to_all x5 -> x4, starting transfers between devices: 39.8 us -> 31.9 us  [exchanged(): lax.all_to_all(parts, axis, 0, 0, tiled=True, axis_index_groups=groups)]
    ppermute x1 -> x0, waiting for transfers between devices: 7.47 us -> none  [local(): other = lax.ppermute(piece, 'tokens', pairs_z4)]
    all_to_all x5 -> x4, waiting for transfers between devices: 12.2 us -> 4.82 us  [exchanged(): lax.all_to_all(parts, axis, 0, 0, tiled=True, axis_index_groups=groups)]
    ppermute x1, waiting for transfers between devices: 0.01 us -> 3.74 us  [local(): far = lax.ppermute(eight, 'heads', pairs_x(2))]
    ppermute x1 -> x0, starting transfers between devices: 1.92 us -> none  [local(): other = lax.ppermute(piece, 'tokens', pairs_z4)]
  transfers between devices with their start and end apart: 14 -> 12, of which waited for: 8 -> 7; matrix products, arithmetic and copies ran while one was open for 3% -> 3% of each run, Pallas kernels for 6% -> 5%
where the time goes in v12:
time: 175 us; the launch traced here: 173 us
  starting transfers between devices  64.1 us (37%)
  blocking collectives  63.9 us (37%)
  waiting for transfers between devices  23.2 us (13%)
  Pallas kernels  13.3 us (8%)
  local copies, waits for them, and re-layouts  6.39 us (4%)
    all_to_all x5, blocking collectives, exchanged(): lax.all_to_all(parts, axis, 0, 0, tiled=True, axis_index_groups=groups)  63.9 us
    all_to_all x4, starting transfers between devices, exchanged(): lax.all_to_all(parts, axis, 0, 0, tiled=True, axis_index_groups=groups)  31.9 us
    ppermute x3, starting transfers between devices, x_scatter(): lax.ppermute(pieces[flip], 'heads', pairs_x(flip))  9.57 us
    ppermute x1, waiting for transfers between devices, local(): near = lax.ppermute(four, 'heads', pairs_x(1))  8.21 us
    ppermute x1, starting transfers between devices, local(): other = lax.ppermute(over_x, 'heads', pairs_zh)  7.94 us
    ppermute x1, starting transfers between devices, local(): lax.ppermute(lax.dynamic_index_in_dim(mine, core, 0), 'heads', pairs_zh)  7.94 us
    ppermute x1, waiting for transfers between devices, local(): other = lax.ppermute(over_x, 'heads', pairs_zh)  5.78 us
    pallas_call x2, Pallas kernels, local(): call(lambda *refs: key_kernel(half, index_scale, *refs), shape((key_count...  4.92 us
  transfers between devices with their start and end apart: 12, of which 7 were waited for; matrix products, arithmetic and copies ran while one was open for 3% of the time, Pallas kernels for 5%

profile of v12, /device:TPU:1, one launch (start us, length us, event | category | flops | bytes accessed | tf_op | source)
XLA Modules:
  0.0 172.6 jit_solution(15944522294391496702)
XLA Ops:
  0.6 1.4 broadcast_in_dim.27
  2.0 13.1 %all-to-all-start = ((bf16[8,16,576]{2,1,0:T(8,128)(2,1)}), bf16[8,16,576]{2,1,0:T(8,128)(2,1)S(1)}, u32[]{:S(2)}, u32[]{:S(2)}) async-start(bf16[8,16,576]{2,1,0:T(8,128)(2,1)} %broadcast_in_dim.27), calls=%async_computation | async-start | bytes 327680 | tf_op jit(solution)/shard_map/all_to_all | solution.py:42
  16.1 0.9 copy.22
  17.1 7.9 %collective-permute-start = (bf16[1,320,128]{2,1,0:T(8,128)(2,1)S(1)}, bf16[1,320,128]{2,1,0:T(8,128)(2,1)S(1)}, u32[]{:S(2)}, u32[]{:S(2)}) collective-permute-start(bf16[1,320,128]{2,1,0:T(8,128)(2,1)S(1)} %constant_dynamic-slice_fusion), channel_id=1, source_target_pairs={{0,64},{64,0},{128,192},{192,128},{256,320},{320,256},{384,448},{4... | collective-permute-start | bytes 245768 | tf_op jit(solution)/shard_map/ppermute | solution.py:246
  25.8 1.2 broadcast_in_dim.28
  26.9 7.9 %all-to-all-start.1 = ((bf16[8,8,16,576]{3,2,1,0:T(8,128)(2,1)}), bf16[8,8,16,576]{3,2,1,0:T(8,128)(2,1)S(1)}, u32[]{:S(2)}, u32[]{:S(2)}) async-start(bf16[8,8,16,576]{3,2,1,0:T(8,128)(2,1)} %broadcast_in_dim.28), calls=%async_computation.1 | async-start | bytes 2621440 | tf_op jit(solution)/shard_map/all_to_all | solution.py:42
  35.2 1.9 %collective-permute-start.1 = (bf16[1,320,128]{2,1,0:T(8,128)(2,1)S(1)}, bf16[1,320,128]{2,1,0:T(8,128)(2,1)S(1)}, u32[]{:S(2)}, u32[]{:S(2)}) collective-permute-start(bf16[1,320,128]{2,1,0:T(8,128)(2,1)S(1)} %collective-permute-done.refs_1_), channel_id=1, source_target_pairs={{0,1},{1,0},{2,3},{3,2},{4,5},{5,4},{6,7},{7,6},{8,9},{9,8},{10,11... | collective-permute-start | bytes 245768 | tf_op jit(solution)/shard_map/ppermute | solution.py:247
  38.4 0.9 copy-done.1
  39.3 0.8 shard_map.86
  40.8 3.1 %collective-permute-start.2 = (f32[16,1024]{1,0:T(8,128)}, f32[16,1024]{1,0:T(8,128)S(1)}, u32[]{:S(2)}, u32[]{:S(2)}) collective-permute-start(f32[16,1024]{1,0:T(8,128)} %get-tuple-element.37), channel_id=1, source_target_pairs={{0,128},{64,192},{128,0},{192,64},{256,384},{320,448},{384,256},{4... | collective-permute-start | bytes 196616 | tf_op jit(solution)/shard_map/ppermute | solution.py:218
  43.9 4.4 %collective-permute-start.3 = (f32[16,1024]{1,0:T(8,128)}, f32[16,1024]{1,0:T(8,128)S(1)}, u32[]{:S(2)}, u32[]{:S(2)}) collective-permute-start(f32[16,1024]{1,0:T(8,128)} %get-tuple-element.36), channel_id=1, source_target_pairs={{0,256},{64,320},{128,384},{192,448},{256,0},{320,64},{384,128},{4... | collective-permute-start | bytes 196616 | tf_op jit(solution)/shard_map/ppermute | solution.py:218
  48.3 2.1 %collective-permute-start.4 = (f32[16,1024]{1,0:T(8,128)}, f32[16,1024]{1,0:T(8,128)}, u32[]{:S(2)}, u32[]{:S(2)}) collective-permute-start(f32[16,1024]{1,0:T(8,128)} %get-tuple-element.35), channel_id=1, source_target_pairs={{0,384},{64,448},{128,256},{192,320},{256,128},{320,192},{384,0},{... | collective-permute-start | bytes 196616 | tf_op jit(solution)/shard_map/ppermute | solution.py:218
  50.4 2.3 %all-to-all-done.1 = bf16[8,8,16,576]{3,2,1,0:T(8,128)(2,1)S(1)} async-done(((bf16[8,8,16,576]{3,2,1,0:T(8,128)(2,1)}), bf16[8,8,16,576]{3,2,1,0:T(8,128)(2,1)S(1)}, u32[]{:S(2)}, u32[]{:S(2)}) %all-to-all-start.1) | async-done | bytes 1179680 | tf_op jit(solution)/shard_map/all_to_all | solution.py:42
  52.6 2.3 %shard_map.85 = (f32[1024,1024]{1,0:T(8,128)S(1)}, f32[8,128]{1,0:T(8,128)S(1)}, f32[8,128]{1,0:T(8,128)S(1)}) custom-call(s32[1024,1]{1,0:T(8,128)S(1)} %broadcast_in_dim_reshape.5.limit_ref, bf16[1024,576]{1,0:T(8,128)(2,1)S(1)} %bitcast.38, bf16[576,1024]{1,0:T(8,128)(2,1)S(1)} %bitcast.46), custom_call_target="tpu_custom_call" | custom-call | flops 1207959552 | bytes 4194304 | tf_op jit(solution)/shard_map/pallas_call | solution.py:260
  55.0 1.1 shard_map.87
  56.1 20.1 %all_to_all.45.stats_ref = f32[8,24,128]{2,1,0:T(8,128)S(1)} all-to-all(f32[8,24,128]{2,1,0:T(8,128)S(1)} %broadcast_in_dim.30), channel_id=1, replica_groups={{0,2,4,6,8,10,12,14},{1,3,5,7,9,11,13,15},{16,18,20,22,24,26,28,30},{17..., dimensions={0} | all-to-all | bytes 196608 | tf_op jit(solution)/shard_map/all_to_all | solution.py:42
  76.3 12.7 %all_to_all.46.stats_ref = f32[8,24,128]{2,1,0:T(8,128)S(1)} all-to-all(f32[8,24,128]{2,1,0:T(8,128)S(1)} %shard_map.88), channel_id=1, replica_groups={{0,16,32,48,1,17,33,49},{2,18,34,50,3,19,35,51},{4,20,36,52,5,21,37,53}..., dimensions={0} | all-to-all | bytes 196608 | tf_op jit(solution)/shard_map/all_to_all | solution.py:42
  89.8 8.9 %all_to_all.47 = f32[4,16,1024]{2,1,0:T(8,128)S(1)} all-to-all(f32[4,16,1024]{2,1,0:T(8,128)S(1)} %bitcast.40), channel_id=1, replica_groups={{0,128,256,384},{64,192,320,448},{1,129,257,385},{65,193,321,449},{2,13..., dimensions={0} | all-to-all | bytes 524288 | tf_op jit(solution)/shard_map/all_to_all | solution.py:42
  98.8 7.9 %collective-permute-start.5 = (f32[16,1024]{1,0:T(8,128)S(1)}, f32[16,1024]{1,0:T(8,128)S(1)}, u32[]{:S(2)}, u32[]{:S(2)}) collective-permute-start(f32[16,1024]{1,0:T(8,128)S(1)} %reduce_sum.9.one_ref), channel_id=1, source_target_pairs={{0,64},{64,0},{128,192},{192,128},{256,320},{320,256},{384,448},{4... | collective-permute-start | bytes 196616 | tf_op jit(solution)/shard_map/ppermute | solution.py:287
  106.7 5.8 %collective-permute-done.5.two_ref = f32[16,1024]{1,0:T(8,128)S(1)} collective-permute-done((f32[16,1024]{1,0:T(8,128)S(1)}, f32[16,1024]{1,0:T(8,128)S(1)}, u32[]{:S(2)}, u32[]{:S(2)}) %collective-permute-start.5) | collective-permute-done | bytes 65568 | tf_op jit(solution)/shard_map/ppermute | solution.py:287
  112.6 7.9 %all_to_all.48 = f32[4,16,1024]{2,1,0:T(8,128)S(1)} all-to-all(f32[4,16,1024]{2,1,0:T(8,128)S(1)} %shard_map.90), channel_id=1, replica_groups={{0,128,256,384},{64,192,320,448},{1,129,257,385},{65,193,321,449},{2,13..., dimensions={0} | all-to-all | bytes 524288 | tf_op jit(solution)/shard_map/all_to_all | solution.py:42
  120.5 1.0 shard_map.91
  121.6 14.2 %all_to_all.49.parts_ref = f32[8,72,128]{2,1,0:T(8,128)S(1)} all-to-all(f32[8,72,128]{2,1,0:T(8,128)S(1)} %bitcast.41), channel_id=1, replica_groups={{0,16,32,48,1,17,33,49},{2,18,34,50,3,19,35,51},{4,20,36,52,5,21,37,53}..., dimensions={0} | all-to-all | bytes 589824 | tf_op jit(solution)/shard_map/all_to_all | solution.py:42
  136.5 3.9 %all-to-all-start.7 = ((f32[8,72,128]{2,1,0:T(8,128)}), f32[8,72,128]{2,1,0:T(8,128)S(1)}, u32[]{:S(2)}, u32[]{:S(2)}) async-start(f32[8,72,128]{2,1,0:T(8,128)} %shard_map.92), calls=%async_computation.7 | async-start | bytes 589824 | tf_op jit(solution)/shard_map/all_to_all | solution.py:42
  140.5 2.2 %collective-permute-start.6 = (bf16[4,320,128]{2,1,0:T(8,128)(2,1)S(1)}, bf16[4,320,128]{2,1,0:T(8,128)(2,1)S(1)}, u32[]{:S(2)}, u32[]{:S(2)}) collective-permute-start(bf16[4,320,128]{2,1,0:T(8,128)(2,1)S(1)} %pad_maximum_fusion), channel_id=1, source_target_pairs={{0,128},{64,192},{128,0},{192,64},{256,384},{320,448},{384,256},{4... | collective-permute-start | bytes 983048 | tf_op jit(solution)/shard_map/ppermute | solution.py:293
  142.7 8.2 %collective-permute-done.6 = bf16[4,320,128]{2,1,0:T(8,128)(2,1)S(1)} collective-permute-done((bf16[4,320,128]{2,1,0:T(8,128)(2,1)S(1)}, bf16[4,320,128]{2,1,0:T(8,128)(2,1)S(1)}, u32[]{:S(2)}, u32[]{:S(2)}) %collective-permute-start.6) | collective-permute-done | bytes 327712 | tf_op jit(solution)/shard_map/ppermute | solution.py:293
  151.0 2.6 %collective-permute-start.7 = (bf16[8,320,128]{2,1,0:T(8,128)(2,1)S(1)}, bf16[8,320,128]{2,1,0:T(8,128)(2,1)S(1)}, u32[]{:S(2)}, u32[]{:S(2)}) collective-permute-start(bf16[8,320,128]{2,1,0:T(8,128)(2,1)S(1)} %constant_dynamic-update-slice_fusion.refs_2_), channel_id=1, source_target_pairs={{0,256},{64,320},{128,384},{192,448},{256,0},{320,64},{384,128},{4... | collective-permute-start | bytes 1966088 | tf_op jit(solution)/shard_map/ppermute | solution.py:306
  153.6 1.9 %all-to-all-done.7.parts_ref = f32[8,72,128]{2,1,0:T(8,128)S(1)} async-done(((f32[8,72,128]{2,1,0:T(8,128)}), f32[8,72,128]{2,1,0:T(8,128)S(1)}, u32[]{:S(2)}, u32[]{:S(2)}) %all-to-all-start.7) | async-done | bytes 294944 | tf_op jit(solution)/shard_map/all_to_all | solution.py:42
  156.2 7.0 %all-to-all-start.8 = ((f32[8,72,128]{2,1,0:T(8,128)}), f32[8,72,128]{2,1,0:T(8,128)S(1)}, u32[]{:S(2)}, u32[]{:S(2)}) async-start(f32[8,72,128]{2,1,0:T(8,128)} %shard_map.93), calls=%async_computation.8 | async-start | bytes 589824 | tf_op jit(solution)/shard_map/all_to_all | solution.py:42
  163.2 2.1 %shard_map.95.refs_3_ = f32[1024,128]{1,0:T(8,128)S(1)} custom-call(f32[64,1024]{1,0:T(8,128)S(1)} %bitcast.43, bf16[1024,128]{1,0:T(8,128)(2,1)S(1)} %copy-done.2, bf16[8,320,128]{2,1,0:T(8,128)(2,1)S(1)} %constant_dynamic-update-slice_fusion.refs_2_), custom_call_target="tpu_custom_call" | custom-call | flops 1073741824 | bytes 2097152 | tf_op jit(solution)/shard_map/pallas_call | solution.py:320
  165.3 3.7 %collective-permute-done.7.refs_2_ = bf16[8,320,128]{2,1,0:T(8,128)(2,1)S(1)} collective-permute-done((bf16[8,320,128]{2,1,0:T(8,128)(2,1)S(1)}, bf16[8,320,128]{2,1,0:T(8,128)(2,1)S(1)}, u32[]{:S(2)}, u32[]{:S(2)}) %collective-permute-start.7) | collective-permute-done | bytes 655392 | tf_op jit(solution)/shard_map/ppermute | solution.py:306
  169.1 2.9 %shard_map.96 = f32[1024,128]{1,0:T(8,128)} custom-call(f32[64,1024]{1,0:T(8,128)S(1)} %bitcast.44, bf16[1024,128]{1,0:T(8,128)(2,1)S(1)} %copy-done.2, bf16[8,320,128]{2,1,0:T(8,128)(2,1)S(1)} %collective-permute-done.7.refs_2_, f32[1024,128]{1,0:T(8,128)S(1)} %shard_map.95.refs_3_), custom_call_target="tpu_custom_call" | custom-call | flops 1073741824 | bytes 2097152 | tf_op jit(solution)/shard_map/pallas_call | solution.py:320
  (44 shorter events, 7.2 us)
Async XLA Ops:
  2.0 23.7 %all-to-all-start = ((bf16[8,16,576]{2,1,0:T(8,128)(2,1)}), bf16[8,16,576]{2,1,0:T(8,128)(2,1)S(1)}, u32[]{:S(2)}, u32[]{:S(2)}) async-start(bf16[8,16,576]{2,1,0:T(8,128)(2,1)} %broadcast_in_dim.27), calls=%async_computation | async-start | bytes 327680 | tf_op jit(solution)/shard_map/all_to_all | solution.py:42
  17.1 18.0 %collective-permute-start = (bf16[1,320,128]{2,1,0:T(8,128)(2,1)S(1)}, bf16[1,320,128]{2,1,0:T(8,128)(2,1)S(1)}, u32[]{:S(2)}, u32[]{:S(2)}) collective-permute-start(bf16[1,320,128]{2,1,0:T(8,128)(2,1)S(1)} %constant_dynamic-slice_fusion), channel_id=1, source_target_pairs={{0,64},{64,0},{128,192},{192,128},{256,320},{320,256},{384,448},{4... | collective-permute-start | bytes 245768 | tf_op jit(solution)/shard_map/ppermute | solution.py:246
  26.9 7.9 %copy-start.3 = (s32[64]{0:T(128)S(1)}, s32[64]{0:T(128)}, u32[]{:S(2)}) copy-start(s32[64]{0:T(128)} %param.11) | copy-start | bytes 772
  26.9 25.7 %all-to-all-start.1 = ((bf16[8,8,16,576]{3,2,1,0:T(8,128)(2,1)}), bf16[8,8,16,576]{3,2,1,0:T(8,128)(2,1)S(1)}, u32[]{:S(2)}, u32[]{:S(2)}) async-start(bf16[8,8,16,576]{3,2,1,0:T(8,128)(2,1)} %broadcast_in_dim.28), calls=%async_computation.1 | async-start | bytes 2621440 | tf_op jit(solution)/shard_map/all_to_all | solution.py:42
  35.2 3.2 %collective-permute-start.1 = (bf16[1,320,128]{2,1,0:T(8,128)(2,1)S(1)}, bf16[1,320,128]{2,1,0:T(8,128)(2,1)S(1)}, u32[]{:S(2)}, u32[]{:S(2)}) collective-permute-start(bf16[1,320,128]{2,1,0:T(8,128)(2,1)S(1)} %collective-permute-done.refs_1_), channel_id=1, source_target_pairs={{0,1},{1,0},{2,3},{3,2},{4,5},{5,4},{6,7},{7,6},{8,9},{9,8},{10,11... | collective-permute-start | bytes 245768 | tf_op jit(solution)/shard_map/ppermute | solution.py:247
  37.7 15.0 %copy-start = (bf16[1024,576]{0,1:T(8,128)(2,1)S(1)}, bf16[1024,576]{0,1:T(8,128)(2,1)}, u32[]{:S(2)}) copy-start(bf16[1024,576]{0,1:T(8,128)(2,1)} %param.7) | copy-start | bytes 3538948
  38.3 1.0 copy-start.1
  40.8 14.2 %collective-permute-start.2 = (f32[16,1024]{1,0:T(8,128)}, f32[16,1024]{1,0:T(8,128)S(1)}, u32[]{:S(2)}, u32[]{:S(2)}) collective-permute-start(f32[16,1024]{1,0:T(8,128)} %get-tuple-element.37), channel_id=1, source_target_pairs={{0,128},{64,192},{128,0},{192,64},{256,384},{320,448},{384,256},{4... | collective-permute-start | bytes 196616 | tf_op jit(solution)/shard_map/ppermute | solution.py:218
  43.9 11.1 %collective-permute-start.3 = (f32[16,1024]{1,0:T(8,128)}, f32[16,1024]{1,0:T(8,128)S(1)}, u32[]{:S(2)}, u32[]{:S(2)}) collective-permute-start(f32[16,1024]{1,0:T(8,128)} %get-tuple-element.36), channel_id=1, source_target_pairs={{0,256},{64,320},{128,384},{192,448},{256,0},{320,64},{384,128},{4... | collective-permute-start | bytes 196616 | tf_op jit(solution)/shard_map/ppermute | solution.py:218
  48.3 6.7 %collective-permute-start.4 = (f32[16,1024]{1,0:T(8,128)}, f32[16,1024]{1,0:T(8,128)}, u32[]{:S(2)}, u32[]{:S(2)}) collective-permute-start(f32[16,1024]{1,0:T(8,128)} %get-tuple-element.35), channel_id=1, source_target_pairs={{0,384},{64,448},{128,256},{192,320},{256,128},{320,192},{384,0},{... | collective-permute-start | bytes 196616 | tf_op jit(solution)/shard_map/ppermute | solution.py:218
  89.8 30.7 %copy-start.2 = (bf16[1024,128]{1,0:T(8,128)(2,1)S(1)}, bf16[1024,128]{1,0:T(8,128)(2,1)}, u32[]{:S(2)}) copy-start(bf16[1024,128]{1,0:T(8,128)(2,1)} %refs_1_.3) | copy-start | bytes 786436
  98.8 13.7 %collective-permute-start.5 = (f32[16,1024]{1,0:T(8,128)S(1)}, f32[16,1024]{1,0:T(8,128)S(1)}, u32[]{:S(2)}, u32[]{:S(2)}) collective-permute-start(f32[16,1024]{1,0:T(8,128)S(1)} %reduce_sum.9.one_ref), channel_id=1, source_target_pairs={{0,64},{64,0},{128,192},{192,128},{256,320},{320,256},{384,448},{4... | collective-permute-start | bytes 196616 | tf_op jit(solution)/shard_map/ppermute | solution.py:287
  136.5 19.0 %all-to-all-start.7 = ((f32[8,72,128]{2,1,0:T(8,128)}), f32[8,72,128]{2,1,0:T(8,128)S(1)}, u32[]{:S(2)}, u32[]{:S(2)}) async-start(f32[8,72,128]{2,1,0:T(8,128)} %shard_map.92), calls=%async_computation.7 | async-start | bytes 589824 | tf_op jit(solution)/shard_map/all_to_all | solution.py:42
  140.5 10.5 %collective-permute-start.6 = (bf16[4,320,128]{2,1,0:T(8,128)(2,1)S(1)}, bf16[4,320,128]{2,1,0:T(8,128)(2,1)S(1)}, u32[]{:S(2)}, u32[]{:S(2)}) collective-permute-start(bf16[4,320,128]{2,1,0:T(8,128)(2,1)S(1)} %pad_maximum_fusion), channel_id=1, source_target_pairs={{0,128},{64,192},{128,0},{192,64},{256,384},{320,448},{384,256},{4... | collective-permute-start | bytes 983048 | tf_op jit(solution)/shard_map/ppermute | solution.py:293
  151.0 18.1 %collective-permute-start.7 = (bf16[8,320,128]{2,1,0:T(8,128)(2,1)S(1)}, bf16[8,320,128]{2,1,0:T(8,128)(2,1)S(1)}, u32[]{:S(2)}, u32[]{:S(2)}) collective-permute-start(bf16[8,320,128]{2,1,0:T(8,128)(2,1)S(1)} %constant_dynamic-update-slice_fusion.refs_2_), channel_id=1, source_target_pairs={{0,256},{64,320},{128,384},{192,448},{256,0},{320,64},{384,128},{4... | collective-permute-start | bytes 1966088 | tf_op jit(solution)/shard_map/ppermute | solution.py:306
  156.2 15.7 %all-to-all-start.8 = ((f32[8,72,128]{2,1,0:T(8,128)}), f32[8,72,128]{2,1,0:T(8,128)S(1)}, u32[]{:S(2)}, u32[]{:S(2)}) async-start(f32[8,72,128]{2,1,0:T(8,128)} %shard_map.93), calls=%async_computation.8 | async-start | bytes 589824 | tf_op jit(solution)/shard_map/all_to_all | solution.py:42

commit v13 on v11

--- a/solution.py
+++ b/solution.py
@@ -117,7 +117,7 @@
     out_ref[...] = logits
 
 
-def index_stats_kernel(limit_ref, *refs):
+def index_stats_kernel(limit_ref, max_ref, total_ref, *refs):
     pieces, (logits_ref, stat_ref) = refs[:-2], refs[-2:]
     logits = sum(piece[...] for piece in pieces)
     key = lax.broadcasted_iota(jnp.int32, (1, logits.shape[1]), 1)
@@ -125,7 +125,9 @@
     m = jnp.max(logits, axis=1, keepdims=True)
     l = jnp.sum(jnp.exp(logits - m), axis=1, keepdims=True)
     logits_ref[...] = logits
-    stat_ref[...] = jnp.concatenate([as_row(m), as_row(l), jnp.zeros((6, 128), f32)], axis=0)
+    index_lines = [as_row(m), as_row(l), jnp.zeros((6, 128), f32)]
+    lines = jnp.concatenate([max_ref[...], total_ref[...], *index_lines], axis=0)
+    stat_ref[...] = jnp.broadcast_to(lines[None], stat_ref.shape)
 
 
 def joined(stats):
@@ -274,16 +276,14 @@
 
     local_max, *pieces = lax.optimization_barrier((local_max, *pieces))
     share_limit = lax.dynamic_slice_in_dim(limit, x * share_rows, share_rows, 0)
-    logits, index_stats = call(
+    logits, stats = call(
         index_stats_kernel,
-        (shape((share_rows, key_count), f32), shape((8, 128), f32)),
+        (shape((share_rows, key_count), f32), shape((NZ, 2 * NYC + 8, 128), f32)),
         flops=index_flops,
         moved=1 << 20,
-    )(share_limit[:, None], *pieces)
-
-    stats = jnp.concatenate([local_max, local_total, index_stats])
-
-    stats = gathered(stats, "tokens", groups_z)
+    )(share_limit[:, None], local_max, local_total, *pieces)
+
+    stats = exchanged(stats, "tokens", groups_z)
     stats = call(join_kernel, shape((NYC, *stats.shape[1:]), f32))(stats)
     stats = exchanged(stats, "tokens", groups_yc)
 

time: 174 us -> 174 us (level)
  no operation moved by 1% of the time
where the time goes in v13:
time: 174 us; the launch traced here: 173 us
  starting transfers between devices  74.5 us (43%)
  blocking collectives  50.2 us (29%)
  waiting for transfers between devices  26.1 us (15%)
  Pallas kernels  14 us (8%)
  local copies, waits for them, and re-layouts  6.38 us (4%)
    all_to_all x4, blocking collectives, exchanged(): lax.all_to_all(parts, axis, 0, 0, tiled=True, axis_index_groups=groups)  50.2 us
    all_to_all x5, starting transfers between devices, exchanged(): lax.all_to_all(parts, axis, 0, 0, tiled=True, axis_index_groups=groups)  39.8 us
    all_to_all x5, waiting for transfers between devices, exchanged(): lax.all_to_all(parts, axis, 0, 0, tiled=True, axis_index_groups=groups)  12.2 us
    ppermute x3, starting transfers between devices, x_scatter(): lax.ppermute(pieces[flip], 'heads', pairs_x(flip))  9.57 us
    ppermute x1, starting transfers between devices, local(): other = lax.ppermute(over_x, 'heads', pairs_zh)  8.07 us
    ppermute x1, starting transfers between devices, local(): lax.ppermute(lax.dynamic_index_in_dim(mine, core, 0), 'heads', pairs_zh)  7.94 us
    ppermute x1, waiting for transfers between devices, local(): other = lax.ppermute(piece, 'tokens', pairs_z4)  7.47 us
    ppermute x1, waiting for transfers between devices, local(): other = lax.ppermute(over_x, 'heads', pairs_zh)  5.78 us
  transfers between devices with their start and end apart: 14, of which 8 were waited for; matrix products, arithmetic and copies ran while one was open for 3% of the time, Pallas kernels for 6%

profile of v13, /device:TPU:1, one launch (start us, length us, event | category | flops | bytes accessed | tf_op | source)
XLA Modules:
  0.0 172.9 jit_solution(4867159044363984650)
XLA Ops:
  0.6 1.4 broadcast_in_dim.22
  2.0 13.1 %all-to-all-start = ((bf16[8,16,576]{2,1,0:T(8,128)(2,1)}), bf16[8,16,576]{2,1,0:T(8,128)(2,1)S(1)}, u32[]{:S(2)}, u32[]{:S(2)}) async-start(bf16[8,16,576]{2,1,0:T(8,128)(2,1)} %broadcast_in_dim.22), calls=%async_computation | async-start | bytes 327680 | tf_op jit(solution)/shard_map/all_to_all | solution.py:46
  17.1 7.9 %collective-permute-start = (bf16[1,320,128]{2,1,0:T(8,128)(2,1)S(1)}, bf16[1,320,128]{2,1,0:T(8,128)(2,1)S(1)}, u32[]{:S(2)}, u32[]{:S(2)}) collective-permute-start(bf16[1,320,128]{2,1,0:T(8,128)(2,1)S(1)} %constant_dynamic-slice_fusion), channel_id=1, source_target_pairs={{0,64},{64,0},{128,192},{192,128},{256,320},{320,256},{384,448},{4... | collective-permute-start | bytes 245768 | tf_op jit(solution)/shard_map/ppermute | solution.py:256
  25.8 1.2 broadcast_in_dim.23
  26.9 7.9 %all-to-all-start.1 = ((bf16[8,8,16,576]{3,2,1,0:T(8,128)(2,1)}), bf16[8,8,16,576]{3,2,1,0:T(8,128)(2,1)S(1)}, u32[]{:S(2)}, u32[]{:S(2)}) async-start(bf16[8,8,16,576]{3,2,1,0:T(8,128)(2,1)} %broadcast_in_dim.23), calls=%async_computation.1 | async-start | bytes 2621440 | tf_op jit(solution)/shard_map/all_to_all | solution.py:46
  35.2 1.9 %collective-permute-start.1 = (bf16[1,320,128]{2,1,0:T(8,128)(2,1)S(1)}, bf16[1,320,128]{2,1,0:T(8,128)(2,1)S(1)}, u32[]{:S(2)}, u32[]{:S(2)}) collective-permute-start(bf16[1,320,128]{2,1,0:T(8,128)(2,1)S(1)} %collective-permute-done.refs_1_), channel_id=1, source_target_pairs={{0,1},{1,0},{2,3},{3,2},{4,5},{5,4},{6,7},{7,6},{8,9},{9,8},{10,11... | collective-permute-start | bytes 245768 | tf_op jit(solution)/shard_map/ppermute | solution.py:257
  38.4 0.9 copy-done.1
  40.8 3.1 %collective-permute-start.2 = (f32[16,1024]{1,0:T(8,128)}, f32[16,1024]{1,0:T(8,128)S(1)}, u32[]{:S(2)}, u32[]{:S(2)}) collective-permute-start(f32[16,1024]{1,0:T(8,128)} %get-tuple-element.37), channel_id=1, source_target_pairs={{0,128},{64,192},{128,0},{192,64},{256,384},{320,448},{384,256},{4... | collective-permute-start | bytes 196616 | tf_op jit(solution)/shard_map/ppermute | solution.py:228
  43.9 4.4 %collective-permute-start.3 = (f32[16,1024]{1,0:T(8,128)}, f32[16,1024]{1,0:T(8,128)S(1)}, u32[]{:S(2)}, u32[]{:S(2)}) collective-permute-start(f32[16,1024]{1,0:T(8,128)} %get-tuple-element.36), channel_id=1, source_target_pairs={{0,256},{64,320},{128,384},{192,448},{256,0},{320,64},{384,128},{4... | collective-permute-start | bytes 196616 | tf_op jit(solution)/shard_map/ppermute | solution.py:228
  48.3 2.1 %collective-permute-start.4 = (f32[16,1024]{1,0:T(8,128)}, f32[16,1024]{1,0:T(8,128)}, u32[]{:S(2)}, u32[]{:S(2)}) collective-permute-start(f32[16,1024]{1,0:T(8,128)} %get-tuple-element.35), channel_id=1, source_target_pairs={{0,384},{64,448},{128,256},{192,320},{256,128},{320,192},{384,0},{... | collective-permute-start | bytes 196616 | tf_op jit(solution)/shard_map/ppermute | solution.py:228
  50.4 2.3 %all-to-all-done.1 = bf16[8,8,16,576]{3,2,1,0:T(8,128)(2,1)S(1)} async-done(((bf16[8,8,16,576]{3,2,1,0:T(8,128)(2,1)}), bf16[8,8,16,576]{3,2,1,0:T(8,128)(2,1)S(1)}, u32[]{:S(2)}, u32[]{:S(2)}) %all-to-all-start.1) | async-done | bytes 1179680 | tf_op jit(solution)/shard_map/all_to_all | solution.py:46
  52.6 2.3 %shard_map.85 = (f32[1024,1024]{1,0:T(8,128)S(1)}, f32[8,128]{1,0:T(8,128)S(1)}, f32[8,128]{1,0:T(8,128)S(1)}) custom-call(s32[1024,1]{1,0:T(8,128)S(1)} %broadcast_in_dim_reshape.5.limit_ref, bf16[1024,576]{1,0:T(8,128)(2,1)S(1)} %bitcast.38, bf16[576,1024]{1,0:T(8,128)(2,1)S(1)} %bitcast.45), custom_call_target="tpu_custom_call" | custom-call | flops 1207959552 | bytes 4194304 | tf_op jit(solution)/shard_map/pallas_call | solution.py:270
  55.0 1.1 shard_map.87
  56.1 20.1 %all_to_all.45.stats_ref = f32[8,24,128]{2,1,0:T(8,128)S(1)} all-to-all(f32[8,24,128]{2,1,0:T(8,128)S(1)} %get-tuple-element.26), channel_id=1, replica_groups={{0,2,4,6,8,10,12,14},{1,3,5,7,9,11,13,15},{16,18,20,22,24,26,28,30},{17..., dimensions={0} | all-to-all | bytes 196608 | tf_op jit(solution)/shard_map/all_to_all | solution.py:46
  76.3 12.7 %all_to_all.46.stats_ref = f32[8,24,128]{2,1,0:T(8,128)S(1)} all-to-all(f32[8,24,128]{2,1,0:T(8,128)S(1)} %shard_map.88), channel_id=1, replica_groups={{0,16,32,48,1,17,33,49},{2,18,34,50,3,19,35,51},{4,20,36,52,5,21,37,53}..., dimensions={0} | all-to-all | bytes 196608 | tf_op jit(solution)/shard_map/all_to_all | solution.py:46
  89.8 8.8 %all_to_all.47 = f32[4,16,1024]{2,1,0:T(8,128)S(1)} all-to-all(f32[4,16,1024]{2,1,0:T(8,128)S(1)} %bitcast.40), channel_id=1, replica_groups={{0,128,256,384},{64,192,320,448},{1,129,257,385},{65,193,321,449},{2,13..., dimensions={0} | all-to-all | bytes 524288 | tf_op jit(solution)/shard_map/all_to_all | solution.py:46
  98.6 8.1 %collective-permute-start.5 = (f32[16,1024]{1,0:T(8,128)S(1)}, f32[16,1024]{1,0:T(8,128)S(1)}, u32[]{:S(2)}, u32[]{:S(2)}) collective-permute-start(f32[16,1024]{1,0:T(8,128)S(1)} %reduce_sum.18.one_ref), channel_id=1, source_target_pairs={{0,64},{64,0},{128,192},{192,128},{256,320},{320,256},{384,448},{4... | collective-permute-start | bytes 196616 | tf_op jit(solution)/shard_map/ppermute | solution.py:295
  106.7 5.8 %collective-permute-done.5.two_ref = f32[16,1024]{1,0:T(8,128)S(1)} collective-permute-done((f32[16,1024]{1,0:T(8,128)S(1)}, f32[16,1024]{1,0:T(8,128)S(1)}, u32[]{:S(2)}, u32[]{:S(2)}) %collective-permute-start.5) | collective-permute-done | bytes 65568 | tf_op jit(solution)/shard_map/ppermute | solution.py:295
  113.3 3.4 %all-to-all-start.5 = ((f32[4,16,1024]{2,1,0:T(8,128)}), f32[4,16,1024]{2,1,0:T(8,128)S(1)}, u32[]{:S(2)}, u32[]{:S(2)}) async-start(f32[4,16,1024]{2,1,0:T(8,128)} %shard_map.90), calls=%async_computation.5 | async-start | bytes 524288 | tf_op jit(solution)/shard_map/all_to_all | solution.py:46
  116.7 3.3 %collective-permute-start.7 = (bf16[4,320,128]{2,1,0:T(8,128)(2,1)S(1)}, bf16[4,320,128]{2,1,0:T(8,128)(2,1)S(1)}, u32[]{:S(2)}, u32[]{:S(2)}) collective-permute-start(bf16[4,320,128]{2,1,0:T(8,128)(2,1)S(1)} %pad_maximum_fusion), channel_id=1, source_target_pairs={{0,128},{64,192},{128,0},{192,64},{256,384},{320,448},{384,256},{4... | collective-permute-start | bytes 983048 | tf_op jit(solution)/shard_map/ppermute | solution.py:301
  120.1 2.1 %all-to-all-done.5 = f32[4,16,1024]{2,1,0:T(8,128)S(1)} async-done(((f32[4,16,1024]{2,1,0:T(8,128)}), f32[4,16,1024]{2,1,0:T(8,128)S(1)}, u32[]{:S(2)}, u32[]{:S(2)}) %all-to-all-start.5) | async-done | bytes 262176 | tf_op jit(solution)/shard_map/all_to_all | solution.py:46
  122.2 1.8 %shard_map.91 = f32[576,128]{1,0:T(8,128)} custom-call(f32[64,1024]{1,0:T(8,128)S(1)} %bitcast.41, bf16[2,320,128]{2,1,0:T(8,128)(2,1)S(1)} %fusion.1.refs_0_.refs_1_, bf16[1024,128]{1,0:T(8,128)(2,1)S(1)} %copy-done.2), custom_call_target="tpu_custom_call" | custom-call | flops 268435456 | bytes 2097152 | tf_op jit(solution)/shard_map/pallas_call | solution.py:305
  123.9 9.2 %all-to-all-start.6 = ((f32[8,72,128]{2,1,0:T(8,128)}), f32[8,72,128]{2,1,0:T(8,128)S(1)}, u32[]{:S(2)}, u32[]{:S(2)}) async-start(f32[8,72,128]{2,1,0:T(8,128)} %bitcast.24), calls=%async_computation.6 | async-start | bytes 589824 | tf_op jit(solution)/shard_map/all_to_all | solution.py:46
  133.2 1.9 %collective-permute-start.8 = (bf16[8,320,128]{2,1,0:T(8,128)(2,1)S(1)}, bf16[8,320,128]{2,1,0:T(8,128)(2,1)S(1)}, u32[]{:S(2)}, u32[]{:S(2)}) collective-permute-start(bf16[8,320,128]{2,1,0:T(8,128)(2,1)S(1)} %constant_dynamic-update-slice_fusion.refs_2_), channel_id=1, source_target_pairs={{0,256},{64,320},{128,384},{192,448},{256,0},{320,64},{384,128},{4... | collective-permute-start | bytes 1966088 | tf_op jit(solution)/shard_map/ppermute | solution.py:314
  135.2 5.2 %all-to-all-done.6.parts_ref = f32[8,72,128]{2,1,0:T(8,128)S(1)} async-done(((f32[8,72,128]{2,1,0:T(8,128)}), f32[8,72,128]{2,1,0:T(8,128)S(1)}, u32[]{:S(2)}, u32[]{:S(2)}) %all-to-all-start.6) | async-done | bytes 294944 | tf_op jit(solution)/shard_map/all_to_all | solution.py:46
  140.4 8.6 %all_to_all.48 = f32[4,72,128]{2,1,0:T(8,128)S(1)} all-to-all(f32[4,72,128]{2,1,0:T(8,128)S(1)} %shard_map.92), channel_id=1, replica_groups={{0,2,4,6},{1,3,5,7},{16,18,20,22},{17,19,21,23},{32,34,36,38},{33,35,37..., dimensions={0} | all-to-all | bytes 294912 | tf_op jit(solution)/shard_map/all_to_all | solution.py:46
  148.9 1.9 %collective-permute-start.6 = (f32[72,128]{1,0:T(8,128)S(1)}, f32[72,128]{1,0:T(8,128)S(1)}, u32[]{:S(2)}, u32[]{:S(2)}) collective-permute-start(f32[72,128]{1,0:T(8,128)S(1)} %reduce_sum.19.one_ref), channel_id=1, source_target_pairs={{0,8},{1,9},{2,10},{3,11},{4,12},{5,13},{6,14},{7,15},{8,0},{9,1},... | collective-permute-start | bytes 110600 | tf_op jit(solution)/shard_map/ppermute | solution.py:317
  150.9 7.5 %collective-permute-done.6.two_ref = f32[72,128]{1,0:T(8,128)S(1)} collective-permute-done((f32[72,128]{1,0:T(8,128)S(1)}, f32[72,128]{1,0:T(8,128)S(1)}, u32[]{:S(2)}, u32[]{:S(2)}) %collective-permute-start.6) | collective-permute-done | bytes 36896 | tf_op jit(solution)/shard_map/ppermute | solution.py:317
  159.1 6.2 %all-to-all-start.8 = ((f32[8,72,128]{2,1,0:T(8,128)}), f32[8,72,128]{2,1,0:T(8,128)S(1)}, u32[]{:S(2)}, u32[]{:S(2)}) async-start(f32[8,72,128]{2,1,0:T(8,128)} %shard_map.93), calls=%async_computation.8 | async-start | bytes 589824 | tf_op jit(solution)/shard_map/all_to_all | solution.py:46
  165.3 2.1 %shard_map.95.refs_3_ = f32[1024,128]{1,0:T(8,128)S(1)} custom-call(f32[64,1024]{1,0:T(8,128)S(1)} %bitcast.42, bf16[1024,128]{1,0:T(8,128)(2,1)S(1)} %copy-done.2, bf16[8,320,128]{2,1,0:T(8,128)(2,1)S(1)} %constant_dynamic-update-slice_fusion.refs_2_), custom_call_target="tpu_custom_call" | custom-call | flops 1073741824 | bytes 2097152 | tf_op jit(solution)/shard_map/pallas_call | solution.py:329
  167.4 2.9 %shard_map.96 = f32[1024,128]{1,0:T(8,128)} custom-call(f32[64,1024]{1,0:T(8,128)S(1)} %bitcast.43, bf16[1024,128]{1,0:T(8,128)(2,1)S(1)} %copy-done.2, bf16[8,320,128]{2,1,0:T(8,128)(2,1)S(1)} %collective-permute-done.8.refs_2_, f32[1024,128]{1,0:T(8,128)S(1)} %shard_map.95.refs_3_), custom_call_target="tpu_custom_call" | custom-call | flops 1073741824 | bytes 2097152 | tf_op jit(solution)/shard_map/pallas_call | solution.py:329
  170.2 2.0 %all-to-all-done.8 = f32[8,72,128]{2,1,0:T(8,128)S(1)} async-done(((f32[8,72,128]{2,1,0:T(8,128)}), f32[8,72,128]{2,1,0:T(8,128)S(1)}, u32[]{:S(2)}, u32[]{:S(2)}) %all-to-all-start.8) | async-done | bytes 294944 | tf_op jit(solution)/shard_map/all_to_all | solution.py:46
  (46 shorter events, 8.9 us)
Async XLA Ops:
  2.0 23.7 %all-to-all-start = ((bf16[8,16,576]{2,1,0:T(8,128)(2,1)}), bf16[8,16,576]{2,1,0:T(8,128)(2,1)S(1)}, u32[]{:S(2)}, u32[]{:S(2)}) async-start(bf16[8,16,576]{2,1,0:T(8,128)(2,1)} %broadcast_in_dim.22), calls=%async_computation | async-start | bytes 327680 | tf_op jit(solution)/shard_map/all_to_all | solution.py:46
  17.1 18.0 %collective-permute-start = (bf16[1,320,128]{2,1,0:T(8,128)(2,1)S(1)}, bf16[1,320,128]{2,1,0:T(8,128)(2,1)S(1)}, u32[]{:S(2)}, u32[]{:S(2)}) collective-permute-start(bf16[1,320,128]{2,1,0:T(8,128)(2,1)S(1)} %constant_dynamic-slice_fusion), channel_id=1, source_target_pairs={{0,64},{64,0},{128,192},{192,128},{256,320},{320,256},{384,448},{4... | collective-permute-start | bytes 245768 | tf_op jit(solution)/shard_map/ppermute | solution.py:256
  26.9 7.9 %copy-start.3 = (s32[64]{0:T(128)S(1)}, s32[64]{0:T(128)}, u32[]{:S(2)}) copy-start(s32[64]{0:T(128)} %param.11) | copy-start | bytes 772
  26.9 25.7 %all-to-all-start.1 = ((bf16[8,8,16,576]{3,2,1,0:T(8,128)(2,1)}), bf16[8,8,16,576]{3,2,1,0:T(8,128)(2,1)S(1)}, u32[]{:S(2)}, u32[]{:S(2)}) async-start(bf16[8,8,16,576]{3,2,1,0:T(8,128)(2,1)} %broadcast_in_dim.23), calls=%async_computation.1 | async-start | bytes 2621440 | tf_op jit(solution)/shard_map/all_to_all | solution.py:46
  35.2 3.2 %collective-permute-start.1 = (bf16[1,320,128]{2,1,0:T(8,128)(2,1)S(1)}, bf16[1,320,128]{2,1,0:T(8,128)(2,1)S(1)}, u32[]{:S(2)}, u32[]{:S(2)}) collective-permute-start(bf16[1,320,128]{2,1,0:T(8,128)(2,1)S(1)} %collective-permute-done.refs_1_), channel_id=1, source_target_pairs={{0,1},{1,0},{2,3},{3,2},{4,5},{5,4},{6,7},{7,6},{8,9},{9,8},{10,11... | collective-permute-start | bytes 245768 | tf_op jit(solution)/shard_map/ppermute | solution.py:257
  37.7 15.0 %copy-start = (bf16[1024,576]{0,1:T(8,128)(2,1)S(1)}, bf16[1024,576]{0,1:T(8,128)(2,1)}, u32[]{:S(2)}) copy-start(bf16[1024,576]{0,1:T(8,128)(2,1)} %param.7) | copy-start | bytes 3538948
  38.3 1.0 copy-start.1
  40.8 14.2 %collective-permute-start.2 = (f32[16,1024]{1,0:T(8,128)}, f32[16,1024]{1,0:T(8,128)S(1)}, u32[]{:S(2)}, u32[]{:S(2)}) collective-permute-start(f32[16,1024]{1,0:T(8,128)} %get-tuple-element.37), channel_id=1, source_target_pairs={{0,128},{64,192},{128,0},{192,64},{256,384},{320,448},{384,256},{4... | collective-permute-start | bytes 196616 | tf_op jit(solution)/shard_map/ppermute | solution.py:228
  43.9 11.1 %collective-permute-start.3 = (f32[16,1024]{1,0:T(8,128)}, f32[16,1024]{1,0:T(8,128)S(1)}, u32[]{:S(2)}, u32[]{:S(2)}) collective-permute-start(f32[16,1024]{1,0:T(8,128)} %get-tuple-element.36), channel_id=1, source_target_pairs={{0,256},{64,320},{128,384},{192,448},{256,0},{320,64},{384,128},{4... | collective-permute-start | bytes 196616 | tf_op jit(solution)/shard_map/ppermute | solution.py:228
  48.3 6.7 %collective-permute-start.4 = (f32[16,1024]{1,0:T(8,128)}, f32[16,1024]{1,0:T(8,128)}, u32[]{:S(2)}, u32[]{:S(2)}) collective-permute-start(f32[16,1024]{1,0:T(8,128)} %get-tuple-element.35), channel_id=1, source_target_pairs={{0,384},{64,448},{128,256},{192,320},{256,128},{320,192},{384,0},{... | collective-permute-start | bytes 196616 | tf_op jit(solution)/shard_map/ppermute | solution.py:228
  98.6 23.6 %copy-start.2 = (bf16[1024,128]{1,0:T(8,128)(2,1)S(1)}, bf16[1024,128]{1,0:T(8,128)(2,1)}, u32[]{:S(2)}) copy-start(bf16[1024,128]{1,0:T(8,128)(2,1)} %refs_1_.3) | copy-start | bytes 786436
  98.6 13.9 %collective-permute-start.5 = (f32[16,1024]{1,0:T(8,128)S(1)}, f32[16,1024]{1,0:T(8,128)S(1)}, u32[]{:S(2)}, u32[]{:S(2)}) collective-permute-start(f32[16,1024]{1,0:T(8,128)S(1)} %reduce_sum.18.one_ref), channel_id=1, source_target_pairs={{0,64},{64,0},{128,192},{192,128},{256,320},{320,256},{384,448},{4... | collective-permute-start | bytes 196616 | tf_op jit(solution)/shard_map/ppermute | solution.py:295
  113.3 8.9 %all-to-all-start.5 = ((f32[4,16,1024]{2,1,0:T(8,128)}), f32[4,16,1024]{2,1,0:T(8,128)S(1)}, u32[]{:S(2)}, u32[]{:S(2)}) async-start(f32[4,16,1024]{2,1,0:T(8,128)} %shard_map.90), calls=%async_computation.5 | async-start | bytes 524288 | tf_op jit(solution)/shard_map/all_to_all | solution.py:46
  116.7 16.4 %collective-permute-start.7 = (bf16[4,320,128]{2,1,0:T(8,128)(2,1)S(1)}, bf16[4,320,128]{2,1,0:T(8,128)(2,1)S(1)}, u32[]{:S(2)}, u32[]{:S(2)}) collective-permute-start(bf16[4,320,128]{2,1,0:T(8,128)(2,1)S(1)} %pad_maximum_fusion), channel_id=1, source_target_pairs={{0,128},{64,192},{128,0},{192,64},{256,384},{320,448},{384,256},{4... | collective-permute-start | bytes 983048 | tf_op jit(solution)/shard_map/ppermute | solution.py:301
  123.9 16.4 %all-to-all-start.6 = ((f32[8,72,128]{2,1,0:T(8,128)}), f32[8,72,128]{2,1,0:T(8,128)S(1)}, u32[]{:S(2)}, u32[]{:S(2)}) async-start(f32[8,72,128]{2,1,0:T(8,128)} %bitcast.24), calls=%async_computation.6 | async-start | bytes 589824 | tf_op jit(solution)/shard_map/all_to_all | solution.py:46
  133.2 34.1 %collective-permute-start.8 = (bf16[8,320,128]{2,1,0:T(8,128)(2,1)S(1)}, bf16[8,320,128]{2,1,0:T(8,128)(2,1)S(1)}, u32[]{:S(2)}, u32[]{:S(2)}) collective-permute-start(bf16[8,320,128]{2,1,0:T(8,128)(2,1)S(1)} %constant_dynamic-update-slice_fusion.refs_2_), channel_id=1, source_target_pairs={{0,256},{64,320},{128,384},{192,448},{256,0},{320,64},{384,128},{4... | collective-permute-start | bytes 1966088 | tf_op jit(solution)/shard_map/ppermute | solution.py:314
  148.9 9.4 %collective-permute-start.6 = (f32[72,128]{1,0:T(8,128)S(1)}, f32[72,128]{1,0:T(8,128)S(1)}, u32[]{:S(2)}, u32[]{:S(2)}) collective-permute-start(f32[72,128]{1,0:T(8,128)S(1)} %reduce_sum.19.one_ref), channel_id=1, source_target_pairs={{0,8},{1,9},{2,10},{3,11},{4,12},{5,13},{6,14},{7,15},{8,0},{9,1},... | collective-permute-start | bytes 110600 | tf_op jit(solution)/shard_map/ppermute | solution.py:317
  159.1 13.1 %all-to-all-start.8 = ((f32[8,72,128]{2,1,0:T(8,128)}), f32[8,72,128]{2,1,0:T(8,128)S(1)}, u32[]{:S(2)}, u32[]{:S(2)}) async-start(f32[8,72,128]{2,1,0:T(8,128)} %shard_map.93), calls=%async_computation.8 | async-start | bytes 589824 | tf_op jit(solution)/shard_map/all_to_all | solution.py:46

commit v14 on v13

--- a/solution.py
+++ b/solution.py
@@ -104,16 +104,15 @@
     return lax.dot_general(iq, ik, (((1,), (1,)), ((), ())), preferred_element_type=f32)
 
 
-def logits_kernel(heads, scale, mine_ref, one_ref, two_ref, ik_ref, out_ref):
+def logits_kernel(heads, scale, one_ref, two_ref, ik_ref, *refs):
+    before, out_ref = refs[:-1], refs[-1]
     tokens = out_ref.shape[0]
-    ik = ik_ref[...]
-    logits = jnp.zeros(out_ref.shape, f32)
-    for pair in ((mine_ref.at[0], mine_ref.at[1]), (one_ref.at[0], two_ref.at[0])):
-        iq, weights = message_parts(*pair, tokens, heads)
-        active = index_dot(iq, ik)
-        for j, w in enumerate(weights):
-            here = active[j * tokens : (j + 1) * tokens] * scale
-            logits = logits + w * jnp.maximum(here, 0.0)
+    logits = before[0][...] if before else jnp.zeros(out_ref.shape, f32)
+    iq, weights = message_parts(one_ref.at[0], two_ref.at[0], tokens, heads)
+    active = index_dot(iq, ik_ref[...])
+    for j, w in enumerate(weights):
+        here = active[j * tokens : (j + 1) * tokens] * scale
+        logits = logits + w * jnp.maximum(here, 0.0)
     out_ref[...] = logits
 
 
@@ -254,15 +253,22 @@
     mine = jnp.concatenate([by_head, lines.astype(bf16)], axis=1)
 
     first = lax.ppermute(lax.dynamic_index_in_dim(mine, core, 0), "heads", pairs_zh)
+    index_flops = 2 * query_count * index_heads * key_count * index_width
+    own = call(
+        lambda *refs: logits_kernel(half, index_scale, *refs),
+        shape((query_count, key_count), f32),
+        flops=index_flops,
+        moved=1 << 20,
+    )(mine[:1], mine[1:], index_keys)
+    first, own = lax.optimization_barrier((first, own))
     second = lax.ppermute(first, "tokens", pairs_c)
 
-    index_flops = 2 * query_count * index_heads * key_count * index_width
     partial = call(
         lambda *refs: logits_kernel(half, index_scale, *refs),
         shape((query_count, key_count), f32),
         flops=WEIGHT * index_flops,
         moved=1 << 20,
-    )(mine, first, second, index_keys)
+    )(first, second, index_keys, own)
     pieces = x_scatter(partial.reshape(NX, share_rows, key_count), x)
     rows = gathered(along_z, "tokens", groups_yc).reshape(-1, width)
     row_count = rows.shape[0]

time: 174 us -> 171 us (0.983)
  blocking collectives: 50.2 us -> 47 us
    all_to_all x4, blocking collectives: 50.2 us -> 47 us  [exchanged(): lax.all_to_all(parts, axis, 0, 0, tiled=True, axis_index_groups=groups)]
  transfers between devices with their start and end apart: 14 -> 14, of which waited for: 8 -> 8; matrix products, arithmetic and copies ran while one was open for 3% -> 2% of each run, Pallas kernels for 6% -> 6%
where the time goes in v14:
time: 171 us; the launch traced here: 170 us
  starting transfers between devices  73.8 us (43%)
  blocking collectives  47 us (27%)
  waiting for transfers between devices  27.7 us (16%)
  Pallas kernels  13.3 us (8%)
  local copies, waits for them, and re-layouts  6.05 us (4%)
    all_to_all x4, blocking collectives, exchanged(): lax.all_to_all(parts, axis, 0, 0, tiled=True, axis_index_groups=groups)  47 us
    all_to_all x5, starting transfers between devices, exchanged(): lax.all_to_all(parts, axis, 0, 0, tiled=True, axis_index_groups=groups)  39.3 us
    all_to_all x5, waiting for transfers between devices, exchanged(): lax.all_to_all(parts, axis, 0, 0, tiled=True, axis_index_groups=groups)  13.6 us
    ppermute x3, starting transfers between devices, x_scatter(): lax.ppermute(pieces[flip], 'heads', pairs_x(flip))  9.58 us
    ppermute x1, starting transfers between devices, local(): other = lax.ppermute(over_x, 'heads', pairs_zh)  7.94 us
    ppermute x1, starting transfers between devices, local(): lax.ppermute(lax.dynamic_index_in_dim(mine, core, 0), 'heads', pairs_zh)  7.94 us
    ppermute x1, waiting for transfers between devices, local(): other = lax.ppermute(piece, 'tokens', pairs_z4)  7.47 us
    ppermute x1, waiting for transfers between devices, local(): other = lax.ppermute(over_x, 'heads', pairs_zh)  5.87 us
  transfers between devices with their start and end apart: 14, of which 8 were waited for; matrix products, arithmetic and copies ran while one was open for 2% of the time, Pallas kernels for 6%

profile of v14, /device:TPU:1, one launch (start us, length us, event | category | flops | bytes accessed | tf_op | source)
XLA Modules:
  0.0 169.6 jit_solution(11758320379444918644)
XLA Ops:
  0.6 1.4 broadcast_in_dim.22
  2.0 13.1 %all-to-all-start = ((bf16[8,16,576]{2,1,0:T(8,128)(2,1)}), bf16[8,16,576]{2,1,0:T(8,128)(2,1)S(1)}, u32[]{:S(2)}, u32[]{:S(2)}) async-start(bf16[8,16,576]{2,1,0:T(8,128)(2,1)} %broadcast_in_dim.22), calls=%async_computation | async-start | bytes 327680 | tf_op jit(solution)/shard_map/all_to_all | solution.py:46
  16.1 0.9 copy.22
  17.1 7.9 %collective-permute-start = (bf16[1,320,128]{2,1,0:T(8,128)(2,1)S(1)}, bf16[1,320,128]{2,1,0:T(8,128)(2,1)S(1)}, u32[]{:S(2)}, u32[]{:S(2)}) collective-permute-start(bf16[1,320,128]{2,1,0:T(8,128)(2,1)S(1)} %get-tuple-element.45), channel_id=1, source_target_pairs={{0,64},{64,0},{128,192},{192,128},{256,320},{320,256},{384,448},{4... | collective-permute-start | bytes 245768 | tf_op jit(solution)/shard_map/ppermute | solution.py:255
  25.8 1.2 broadcast_in_dim.23
  26.9 7.9 %all-to-all-start.1 = ((bf16[8,8,16,576]{3,2,1,0:T(8,128)(2,1)}), bf16[8,8,16,576]{3,2,1,0:T(8,128)(2,1)S(1)}, u32[]{:S(2)}, u32[]{:S(2)}) async-start(bf16[8,8,16,576]{3,2,1,0:T(8,128)(2,1)} %broadcast_in_dim.23), calls=%async_computation.1 | async-start | bytes 2621440 | tf_op jit(solution)/shard_map/all_to_all | solution.py:46
  35.6 1.9 %collective-permute-start.1 = (bf16[1,320,128]{2,1,0:T(8,128)(2,1)S(1)}, bf16[1,320,128]{2,1,0:T(8,128)(2,1)S(1)}, u32[]{:S(2)}, u32[]{:S(2)}) collective-permute-start(bf16[1,320,128]{2,1,0:T(8,128)(2,1)S(1)} %collective-permute-done.refs_0_), channel_id=1, source_target_pairs={{0,1},{1,0},{2,3},{3,2},{4,5},{5,4},{6,7},{7,6},{8,9},{9,8},{10,11... | collective-permute-start | bytes 245768 | tf_op jit(solution)/shard_map/ppermute | solution.py:264
  39.3 3.1 %collective-permute-start.2 = (f32[16,1024]{1,0:T(8,128)S(1)}, f32[16,1024]{1,0:T(8,128)S(1)}, u32[]{:S(2)}, u32[]{:S(2)}) collective-permute-start(f32[16,1024]{1,0:T(8,128)S(1)} %get-tuple-element.41), channel_id=1, source_target_pairs={{0,128},{64,192},{128,0},{192,64},{256,384},{320,448},{384,256},{4... | collective-permute-start | bytes 196616 | tf_op jit(solution)/shard_map/ppermute | solution.py:227
  42.4 4.4 %collective-permute-start.3 = (f32[16,1024]{1,0:T(8,128)S(1)}, f32[16,1024]{1,0:T(8,128)S(1)}, u32[]{:S(2)}, u32[]{:S(2)}) collective-permute-start(f32[16,1024]{1,0:T(8,128)S(1)} %get-tuple-element.40), channel_id=1, source_target_pairs={{0,256},{64,320},{128,384},{192,448},{256,0},{320,64},{384,128},{4... | collective-permute-start | bytes 196616 | tf_op jit(solution)/shard_map/ppermute | solution.py:227
  46.8 2.1 %collective-permute-start.4 = (f32[16,1024]{1,0:T(8,128)S(1)}, f32[16,1024]{1,0:T(8,128)S(1)}, u32[]{:S(2)}, u32[]{:S(2)}) collective-permute-start(f32[16,1024]{1,0:T(8,128)S(1)} %get-tuple-element.39), channel_id=1, source_target_pairs={{0,384},{64,448},{128,256},{192,320},{256,128},{320,192},{384,0},{... | collective-permute-start | bytes 196616 | tf_op jit(solution)/shard_map/ppermute | solution.py:227
  48.9 3.7 %all-to-all-done.1 = bf16[8,8,16,576]{3,2,1,0:T(8,128)(2,1)S(1)} async-done(((bf16[8,8,16,576]{3,2,1,0:T(8,128)(2,1)}), bf16[8,8,16,576]{3,2,1,0:T(8,128)(2,1)S(1)}, u32[]{:S(2)}, u32[]{:S(2)}) %all-to-all-start.1) | async-done | bytes 1179680 | tf_op jit(solution)/shard_map/all_to_all | solution.py:46
  52.6 1.3 copy-done.1
  53.9 2.3 %shard_map.85 = (f32[1024,1024]{1,0:T(8,128)S(1)}, f32[8,128]{1,0:T(8,128)S(1)}, f32[8,128]{1,0:T(8,128)S(1)}) custom-call(s32[1024,1]{1,0:T(8,128)S(1)} %broadcast_in_dim_reshape.5.limit_ref, bf16[1024,576]{1,0:T(8,128)(2,1)S(1)} %bitcast.38, bf16[576,1024]{1,0:T(8,128)(2,1)S(1)} %bitcast.45), custom_call_target="tpu_custom_call" | custom-call | flops 1207959552 | bytes 4194304 | tf_op jit(solution)/shard_map/pallas_call | solution.py:276
  56.5 16.8 %all_to_all.45.stats_ref = f32[8,24,128]{2,1,0:T(8,128)S(1)} all-to-all(f32[8,24,128]{2,1,0:T(8,128)S(1)} %get-tuple-element.30), channel_id=1, replica_groups={{0,2,4,6,8,10,12,14},{1,3,5,7,9,11,13,15},{16,18,20,22,24,26,28,30},{17..., dimensions={0} | all-to-all | bytes 196608 | tf_op jit(solution)/shard_map/all_to_all | solution.py:46
  73.3 12.6 %all_to_all.46.stats_ref = f32[8,24,128]{2,1,0:T(8,128)S(1)} all-to-all(f32[8,24,128]{2,1,0:T(8,128)S(1)} %shard_map.89), channel_id=1, replica_groups={{0,16,32,48,1,17,33,49},{2,18,34,50,3,19,35,51},{4,20,36,52,5,21,37,53}..., dimensions={0} | all-to-all | bytes 196608 | tf_op jit(solution)/shard_map/all_to_all | solution.py:46
  86.7 8.7 %all_to_all.47 = f32[4,16,1024]{2,1,0:T(8,128)S(1)} all-to-all(f32[4,16,1024]{2,1,0:T(8,128)S(1)} %bitcast.40), channel_id=1, replica_groups={{0,128,256,384},{64,192,320,448},{1,129,257,385},{65,193,321,449},{2,13..., dimensions={0} | all-to-all | bytes 524288 | tf_op jit(solution)/shard_map/all_to_all | solution.py:46
  95.4 7.9 %collective-permute-start.5 = (f32[16,1024]{1,0:T(8,128)S(1)}, f32[16,1024]{1,0:T(8,128)S(1)}, u32[]{:S(2)}, u32[]{:S(2)}) collective-permute-start(f32[16,1024]{1,0:T(8,128)S(1)} %reduce_sum.18.one_ref), channel_id=1, source_target_pairs={{0,64},{64,0},{128,192},{192,128},{256,320},{320,256},{384,448},{4... | collective-permute-start | bytes 196616 | tf_op jit(solution)/shard_map/ppermute | solution.py:301
  103.3 5.9 %collective-permute-done.5.two_ref = f32[16,1024]{1,0:T(8,128)S(1)} collective-permute-done((f32[16,1024]{1,0:T(8,128)S(1)}, f32[16,1024]{1,0:T(8,128)S(1)}, u32[]{:S(2)}, u32[]{:S(2)}) %collective-permute-start.5) | collective-permute-done | bytes 65568 | tf_op jit(solution)/shard_map/ppermute | solution.py:301
  110.0 3.4 %all-to-all-start.5 = ((f32[4,16,1024]{2,1,0:T(8,128)}), f32[4,16,1024]{2,1,0:T(8,128)S(1)}, u32[]{:S(2)}, u32[]{:S(2)}) async-start(f32[4,16,1024]{2,1,0:T(8,128)} %shard_map.91), calls=%async_computation.5 | async-start | bytes 524288 | tf_op jit(solution)/shard_map/all_to_all | solution.py:46
  113.5 3.3 %collective-permute-start.7 = (bf16[4,320,128]{2,1,0:T(8,128)(2,1)S(1)}, bf16[4,320,128]{2,1,0:T(8,128)(2,1)S(1)}, u32[]{:S(2)}, u32[]{:S(2)}) collective-permute-start(bf16[4,320,128]{2,1,0:T(8,128)(2,1)S(1)} %pad_maximum_fusion), channel_id=1, source_target_pairs={{0,128},{64,192},{128,0},{192,64},{256,384},{320,448},{384,256},{4... | collective-permute-start | bytes 983048 | tf_op jit(solution)/shard_map/ppermute | solution.py:307
  116.9 2.1 %all-to-all-done.5 = f32[4,16,1024]{2,1,0:T(8,128)S(1)} async-done(((f32[4,16,1024]{2,1,0:T(8,128)}), f32[4,16,1024]{2,1,0:T(8,128)S(1)}, u32[]{:S(2)}, u32[]{:S(2)}) %all-to-all-start.5) | async-done | bytes 262176 | tf_op jit(solution)/shard_map/all_to_all | solution.py:46
  118.9 1.8 %shard_map.92 = f32[576,128]{1,0:T(8,128)} custom-call(f32[64,1024]{1,0:T(8,128)S(1)} %bitcast.41, bf16[2,320,128]{2,1,0:T(8,128)(2,1)S(1)} %fusion.1.refs_1_, bf16[1024,128]{1,0:T(8,128)(2,1)S(1)} %copy-done), custom_call_target="tpu_custom_call" | custom-call | flops 268435456 | bytes 2097152 | tf_op jit(solution)/shard_map/pallas_call | solution.py:311
  120.7 8.7 %all-to-all-start.6 = ((f32[8,72,128]{2,1,0:T(8,128)}), f32[8,72,128]{2,1,0:T(8,128)S(1)}, u32[]{:S(2)}, u32[]{:S(2)}) async-start(f32[8,72,128]{2,1,0:T(8,128)} %bitcast.24), calls=%async_computation.6 | async-start | bytes 589824 | tf_op jit(solution)/shard_map/all_to_all | solution.py:46
  129.5 1.9 %collective-permute-start.8 = (bf16[8,320,128]{2,1,0:T(8,128)(2,1)S(1)}, bf16[8,320,128]{2,1,0:T(8,128)(2,1)S(1)}, u32[]{:S(2)}, u32[]{:S(2)}) collective-permute-start(bf16[8,320,128]{2,1,0:T(8,128)(2,1)S(1)} %constant_dynamic-update-slice_fusion.refs_2_), channel_id=1, source_target_pairs={{0,256},{64,320},{128,384},{192,448},{256,0},{320,64},{384,128},{4... | collective-permute-start | bytes 1966088 | tf_op jit(solution)/shard_map/ppermute | solution.py:320
  131.4 5.2 %all-to-all-done.6.parts_ref = f32[8,72,128]{2,1,0:T(8,128)S(1)} async-done(((f32[8,72,128]{2,1,0:T(8,128)}), f32[8,72,128]{2,1,0:T(8,128)S(1)}, u32[]{:S(2)}, u32[]{:S(2)}) %all-to-all-start.6) | async-done | bytes 294944 | tf_op jit(solution)/shard_map/all_to_all | solution.py:46
  136.6 9.0 %all_to_all.48 = f32[4,72,128]{2,1,0:T(8,128)S(1)} all-to-all(f32[4,72,128]{2,1,0:T(8,128)S(1)} %shard_map.93), channel_id=1, replica_groups={{0,2,4,6},{1,3,5,7},{16,18,20,22},{17,19,21,23},{32,34,36,38},{33,35,37..., dimensions={0} | all-to-all | bytes 294912 | tf_op jit(solution)/shard_map/all_to_all | solution.py:46
  145.6 1.9 %collective-permute-start.6 = (f32[72,128]{1,0:T(8,128)S(1)}, f32[72,128]{1,0:T(8,128)S(1)}, u32[]{:S(2)}, u32[]{:S(2)}) collective-permute-start(f32[72,128]{1,0:T(8,128)S(1)} %reduce_sum.19.one_ref), channel_id=1, source_target_pairs={{0,8},{1,9},{2,10},{3,11},{4,12},{5,13},{6,14},{7,15},{8,0},{9,1},... | collective-permute-start | bytes 110600 | tf_op jit(solution)/shard_map/ppermute | solution.py:323
  147.5 7.5 %collective-permute-done.6.two_ref = f32[72,128]{1,0:T(8,128)S(1)} collective-permute-done((f32[72,128]{1,0:T(8,128)S(1)}, f32[72,128]{1,0:T(8,128)S(1)}, u32[]{:S(2)}, u32[]{:S(2)}) %collective-permute-start.6) | collective-permute-done | bytes 36896 | tf_op jit(solution)/shard_map/ppermute | solution.py:323
  155.8 6.2 %all-to-all-start.8 = ((f32[8,72,128]{2,1,0:T(8,128)}), f32[8,72,128]{2,1,0:T(8,128)S(1)}, u32[]{:S(2)}, u32[]{:S(2)}) async-start(f32[8,72,128]{2,1,0:T(8,128)} %shard_map.94), calls=%async_computation.8 | async-start | bytes 589824 | tf_op jit(solution)/shard_map/all_to_all | solution.py:46
  162.0 2.1 %shard_map.96.refs_3_ = f32[1024,128]{1,0:T(8,128)S(1)} custom-call(f32[64,1024]{1,0:T(8,128)S(1)} %bitcast.42, bf16[1024,128]{1,0:T(8,128)(2,1)S(1)} %copy-done, bf16[8,320,128]{2,1,0:T(8,128)(2,1)S(1)} %constant_dynamic-update-slice_fusion.refs_2_), custom_call_target="tpu_custom_call" | custom-call | flops 1073741824 | bytes 2097152 | tf_op jit(solution)/shard_map/pallas_call | solution.py:335
  164.0 2.9 %shard_map.97 = f32[1024,128]{1,0:T(8,128)} custom-call(f32[64,1024]{1,0:T(8,128)S(1)} %bitcast.43, bf16[1024,128]{1,0:T(8,128)(2,1)S(1)} %copy-done, bf16[8,320,128]{2,1,0:T(8,128)(2,1)S(1)} %collective-permute-done.8.refs_2_, f32[1024,128]{1,0:T(8,128)S(1)} %shard_map.96.refs_3_), custom_call_target="tpu_custom_call" | custom-call | flops 1073741824 | bytes 2097152 | tf_op jit(solution)/shard_map/pallas_call | solution.py:335
  166.9 2.0 %all-to-all-done.8 = f32[8,72,128]{2,1,0:T(8,128)S(1)} async-done(((f32[8,72,128]{2,1,0:T(8,128)}), f32[8,72,128]{2,1,0:T(8,128)S(1)}, u32[]{:S(2)}, u32[]{:S(2)}) %all-to-all-start.8) | async-done | bytes 294944 | tf_op jit(solution)/shard_map/all_to_all | solution.py:46
  (45 shorter events, 7.7 us)
Async XLA Ops:
  2.0 23.7 %all-to-all-start = ((bf16[8,16,576]{2,1,0:T(8,128)(2,1)}), bf16[8,16,576]{2,1,0:T(8,128)(2,1)S(1)}, u32[]{:S(2)}, u32[]{:S(2)}) async-start(bf16[8,16,576]{2,1,0:T(8,128)(2,1)} %broadcast_in_dim.22), calls=%async_computation | async-start | bytes 327680 | tf_op jit(solution)/shard_map/all_to_all | solution.py:46
  17.1 18.5 %collective-permute-start = (bf16[1,320,128]{2,1,0:T(8,128)(2,1)S(1)}, bf16[1,320,128]{2,1,0:T(8,128)(2,1)S(1)}, u32[]{:S(2)}, u32[]{:S(2)}) collective-permute-start(bf16[1,320,128]{2,1,0:T(8,128)(2,1)S(1)} %get-tuple-element.45), channel_id=1, source_target_pairs={{0,64},{64,0},{128,192},{192,128},{256,320},{320,256},{384,448},{4... | collective-permute-start | bytes 245768 | tf_op jit(solution)/shard_map/ppermute | solution.py:255
  26.9 7.9 %copy-start.2 = (s32[64]{0:T(128)S(1)}, s32[64]{0:T(128)}, u32[]{:S(2)}) copy-start(s32[64]{0:T(128)} %param.11) | copy-start | bytes 772
  26.9 8.2 %copy-start = (bf16[1024,128]{1,0:T(8,128)(2,1)S(1)}, bf16[1024,128]{1,0:T(8,128)(2,1)}, u32[]{:S(2)}) copy-start(bf16[1024,128]{1,0:T(8,128)(2,1)} %refs_1_.3) | copy-start | bytes 786436
  26.9 25.7 %all-to-all-start.1 = ((bf16[8,8,16,576]{3,2,1,0:T(8,128)(2,1)}), bf16[8,8,16,576]{3,2,1,0:T(8,128)(2,1)S(1)}, u32[]{:S(2)}, u32[]{:S(2)}) async-start(bf16[8,8,16,576]{3,2,1,0:T(8,128)(2,1)} %broadcast_in_dim.23), calls=%async_computation.1 | async-start | bytes 2621440 | tf_op jit(solution)/shard_map/all_to_all | solution.py:46
  35.6 3.2 %collective-permute-start.1 = (bf16[1,320,128]{2,1,0:T(8,128)(2,1)S(1)}, bf16[1,320,128]{2,1,0:T(8,128)(2,1)S(1)}, u32[]{:S(2)}, u32[]{:S(2)}) collective-permute-start(bf16[1,320,128]{2,1,0:T(8,128)(2,1)S(1)} %collective-permute-done.refs_0_), channel_id=1, source_target_pairs={{0,1},{1,0},{2,3},{3,2},{4,5},{5,4},{6,7},{7,6},{8,9},{9,8},{10,11... | collective-permute-start | bytes 245768 | tf_op jit(solution)/shard_map/ppermute | solution.py:264
  39.3 16.9 %collective-permute-start.2 = (f32[16,1024]{1,0:T(8,128)S(1)}, f32[16,1024]{1,0:T(8,128)S(1)}, u32[]{:S(2)}, u32[]{:S(2)}) collective-permute-start(f32[16,1024]{1,0:T(8,128)S(1)} %get-tuple-element.41), channel_id=1, source_target_pairs={{0,128},{64,192},{128,0},{192,64},{256,384},{320,448},{384,256},{4... | collective-permute-start | bytes 196616 | tf_op jit(solution)/shard_map/ppermute | solution.py:227
  42.4 13.8 %collective-permute-start.3 = (f32[16,1024]{1,0:T(8,128)S(1)}, f32[16,1024]{1,0:T(8,128)S(1)}, u32[]{:S(2)}, u32[]{:S(2)}) collective-permute-start(f32[16,1024]{1,0:T(8,128)S(1)} %get-tuple-element.40), channel_id=1, source_target_pairs={{0,256},{64,320},{128,384},{192,448},{256,0},{320,64},{384,128},{4... | collective-permute-start | bytes 196616 | tf_op jit(solution)/shard_map/ppermute | solution.py:227
  46.8 9.4 %collective-permute-start.4 = (f32[16,1024]{1,0:T(8,128)S(1)}, f32[16,1024]{1,0:T(8,128)S(1)}, u32[]{:S(2)}, u32[]{:S(2)}) collective-permute-start(f32[16,1024]{1,0:T(8,128)S(1)} %get-tuple-element.39), channel_id=1, source_target_pairs={{0,384},{64,448},{128,256},{192,320},{256,128},{320,192},{384,0},{... | collective-permute-start | bytes 196616 | tf_op jit(solution)/shard_map/ppermute | solution.py:227
  52.6 1.3 copy-start.1
  95.4 13.8 %collective-permute-start.5 = (f32[16,1024]{1,0:T(8,128)S(1)}, f32[16,1024]{1,0:T(8,128)S(1)}, u32[]{:S(2)}, u32[]{:S(2)}) collective-permute-start(f32[16,1024]{1,0:T(8,128)S(1)} %reduce_sum.18.one_ref), channel_id=1, source_target_pairs={{0,64},{64,0},{128,192},{192,128},{256,320},{320,256},{384,448},{4... | collective-permute-start | bytes 196616 | tf_op jit(solution)/shard_map/ppermute | solution.py:301
  110.0 8.9 %all-to-all-start.5 = ((f32[4,16,1024]{2,1,0:T(8,128)}), f32[4,16,1024]{2,1,0:T(8,128)S(1)}, u32[]{:S(2)}, u32[]{:S(2)}) async-start(f32[4,16,1024]{2,1,0:T(8,128)} %shard_map.91), calls=%async_computation.5 | async-start | bytes 524288 | tf_op jit(solution)/shard_map/all_to_all | solution.py:46
  113.5 15.9 %collective-permute-start.7 = (bf16[4,320,128]{2,1,0:T(8,128)(2,1)S(1)}, bf16[4,320,128]{2,1,0:T(8,128)(2,1)S(1)}, u32[]{:S(2)}, u32[]{:S(2)}) collective-permute-start(bf16[4,320,128]{2,1,0:T(8,128)(2,1)S(1)} %pad_maximum_fusion), channel_id=1, source_target_pairs={{0,128},{64,192},{128,0},{192,64},{256,384},{320,448},{384,256},{4... | collective-permute-start | bytes 983048 | tf_op jit(solution)/shard_map/ppermute | solution.py:307
  120.7 15.9 %all-to-all-start.6 = ((f32[8,72,128]{2,1,0:T(8,128)}), f32[8,72,128]{2,1,0:T(8,128)S(1)}, u32[]{:S(2)}, u32[]{:S(2)}) async-start(f32[8,72,128]{2,1,0:T(8,128)} %bitcast.24), calls=%async_computation.6 | async-start | bytes 589824 | tf_op jit(solution)/shard_map/all_to_all | solution.py:46
  129.5 34.5 %collective-permute-start.8 = (bf16[8,320,128]{2,1,0:T(8,128)(2,1)S(1)}, bf16[8,320,128]{2,1,0:T(8,128)(2,1)S(1)}, u32[]{:S(2)}, u32[]{:S(2)}) collective-permute-start(bf16[8,320,128]{2,1,0:T(8,128)(2,1)S(1)} %constant_dynamic-update-slice_fusion.refs_2_), channel_id=1, source_target_pairs={{0,256},{64,320},{128,384},{192,448},{256,0},{320,64},{384,128},{4... | collective-permute-start | bytes 1966088 | tf_op jit(solution)/shard_map/ppermute | solution.py:320
  145.6 9.4 %collective-permute-start.6 = (f32[72,128]{1,0:T(8,128)S(1)}, f32[72,128]{1,0:T(8,128)S(1)}, u32[]{:S(2)}, u32[]{:S(2)}) collective-permute-start(f32[72,128]{1,0:T(8,128)S(1)} %reduce_sum.19.one_ref), channel_id=1, source_target_pairs={{0,8},{1,9},{2,10},{3,11},{4,12},{5,13},{6,14},{7,15},{8,0},{9,1},... | collective-permute-start | bytes 110600 | tf_op jit(solution)/shard_map/ppermute | solution.py:323
  155.8 13.1 %all-to-all-start.8 = ((f32[8,72,128]{2,1,0:T(8,128)}), f32[8,72,128]{2,1,0:T(8,128)S(1)}, u32[]{:S(2)}, u32[]{:S(2)}) async-start(f32[8,72,128]{2,1,0:T(8,128)} %shard_map.94), calls=%async_computation.8 | async-start | bytes 589824 | tf_op jit(solution)/shard_map/all_to_all | solution.py:46
